TPU v7x, 32 devices: a whole 2x2x4 slice. The times are simulated.
32 devices in a mesh: gx: 4 (over z), gy: 2 (over x), gz: 4 (over y, core).
Axes of the slice: x: 2, y: 2, z: 4, core: 2. Of those that a mesh axis runs over, the one named last changes fastest.
Arguments:
- positions: float32 [3, 8, 2, 8, 8], P(None, 'gx', 'gy', 'gz'), as said below
- features: float32 [8, 2, 8, 8, 128], P('gx', 'gy', 'gz'), may hold values from -6 to 6
- species: int32 [8, 2, 8, 8], P('gx', 'gy', 'gz'), may hold values from 0 to 4
- centers: int32 [1024], P(('gx', 'gy', 'gz')), may hold values from 0 to 32, as said below
- neighbours: int32 [1024, 32], P(('gx', 'gy', 'gz')), may hold values from 0 to 384, as said below
- counts: int32 [32], P(('gx', 'gy', 'gz')), may hold values from 0 to 32, as said below
- species_scale: float32 [5], replicated, may hold values from 0.5 to 2
- species_shift: float32 [5], replicated, may hold values from -4 to 4
- center_weight: float32 [128, 128], replicated, may hold values from -0.5 to 0.5
- near_weight: float32 [128, 128], replicated, may hold values from -0.5 to 0.5
- basis_weight: float32 [8, 128], replicated, may hold values from -12 to 12
- path_weight: float32 [3, 128], replicated, may hold values from -6 to 6
- value_weight: float32 [128, 256], replicated, may hold values from -0.5 to 0.5
- latent_weight: float32 [256, 128], replicated, may hold values from -0.375 to 0.375
- out_weight: float32 [128], replicated, may hold values from -0.5 to 0.5
Outputs:
- site_energy: float32 [8, 2, 8, 8], P('gx', 'gy', 'gz')
- forces: float32 [3, 8, 2, 8, 8], P(None, 'gx', 'gy', 'gz')
- virial: float32 [9, 8, 2, 8, 8], P(None, 'gx', 'gy', 'gz')
Inputs may be any that keep to these rules, and one draw needn't show every extreme that they name: `positions`: a listed neighbour lies within two lattice steps of its center, closer than 4.95 Angstrom; coordinates are the site's place in the cell plus a small jitter. `centers`: domain d's block of 32 entries lists its occupied own slots in increasing order, then 32 in the rest. `neighbours`: row k of domain d's block holds the frame rows of the occupied sites within two lattice steps of center k, in any order, and 384 in the other entries; rows of padding centers are all 384. counts[d] is the number of entries of domain d's block of centers that are not 32; some domain holds 32.
All inputs are finite; a program needn't handle non-finite values.
Results may differ from a plain program's by a relative error of at most 0.0003.
Values sent between devices are 32-bit elements; how exact they have to be, the bound alone decides.
No kernel may reach another device: no remote copies, remote signals or barrier semaphores. Data moves between devices by JAX's collectives and lax.ppermute only.
A program may use at most 64 MiB of HBM per device.

v0:
```python
import math

import jax
import jax.numpy as jnp
from jax import lax
from jax.sharding import PartitionSpec as P

EXACT_DOT = lax.Precision.HIGHEST
CUTOFF = 5.0
CELL_SIDE = 4.6
ROOT_HALF = 0.7071067811865476


def padded(array, sides, width):
    for axis, dim in sides:
        size, length = (lax.axis_size(axis), array.shape[dim])
        up = [(i, (i + 1) % size) for i in range(size)]
        down = [(j, i) for i, j in up]
        last = lax.slice_in_dim(array, length - width, length, axis=dim)
        leading = lax.slice_in_dim(array, 0, width, axis=dim)
        before = lax.ppermute(last, axis, up)
        after = lax.ppermute(leading, axis, down)
        array = jnp.concatenate([before, array, after], axis=dim)
    return array


def envelope(ratio):
    polynomial = 1.0 - 28.0 * ratio**6 + 48.0 * ratio**7 - 21.0 * ratio**8
    return jnp.where(ratio < 1.0, polynomial, 0.0)


def harmonics(unit):
    along_x = unit[..., 0]
    along_y = unit[..., 1]
    along_z = unit[..., 2]
    root_three = math.sqrt(3.0)
    root_fifteen = math.sqrt(15.0)
    root_five = math.sqrt(5.0)
    return jnp.stack(
        [
            jnp.ones_like(along_x),
            root_three * along_x,
            root_three * along_y,
            root_three * along_z,
            root_fifteen * along_x * along_y,
            root_fifteen * along_y * along_z,
            0.5 * root_five * (3.0 * along_z * along_z - 1.0),
            root_fifteen * along_x * along_z,
            0.5 * root_fifteen * (along_x * along_x - along_y * along_y),
        ],
        axis=-1,
    )


def path_table(path_weight):
    width = path_weight.shape[1]
    return jnp.concatenate(
        [
            path_weight[0:1],
            jnp.broadcast_to(path_weight[1:2], (3, width)),
            jnp.broadcast_to(path_weight[2:3], (5, width)),
        ],
        axis=0,
    )


def center_energy(
    displace,
    live,
    center_proj,
    near_proj,
    scale,
    shift,
    active,
    basis_weight,
    paths,
    value_weight,
    latent_weight,
    out_weight,
):
    width = center_proj.shape[-1]
    neighbours_count = displace.shape[1]
    length = jnp.sqrt(jnp.sum(displace * displace, axis=-1))
    ratio = length / CUTOFF
    weight = envelope(ratio) * live
    frequency = jnp.arange(1, basis_weight.shape[0] + 1).astype(jnp.float32) * math.pi
    basis = math.sqrt(2.0 / CUTOFF) * jnp.sin(ratio[..., None] * frequency) / length[..., None]
    angular = harmonics(displace / length[..., None])
    radial = jnp.einsum("knb,bc->knc", basis, basis_weight, precision=EXACT_DOT)
    latent = weight[..., None] * jax.nn.silu(radial + center_proj[:, None, :] + near_proj)
    mixed = jnp.einsum("knc,cd->knd", latent, value_weight, precision=EXACT_DOT)
    values = mixed[..., :width]
    env_weight = mixed[..., width:]
    embed = jnp.einsum("knc,knm->kcm", env_weight, angular, precision=EXACT_DOT) / math.sqrt(
        neighbours_count
    )
    weighted = embed * jnp.transpose(paths)[None]
    inner = jnp.einsum("knm,kcm->knc", angular, weighted, precision=EXACT_DOT)
    scalars = values * inner
    joined = jnp.concatenate([latent, scalars], axis=-1)
    update = jax.nn.silu(jnp.einsum("knc,cd->knd", joined, latent_weight, precision=EXACT_DOT))
    final = (latent + weight[..., None] * update) * ROOT_HALF
    pair_energy = jnp.einsum("knc,c->kn", final, out_weight, precision=EXACT_DOT)
    return active * (scale * jnp.sum(pair_energy, axis=1) / math.sqrt(neighbours_count) + shift)


def own_to_frame(slots, cells_x, cells_y, cells_z, sites):
    owned = cells_x * cells_y * cells_z * sites
    frame_count = (cells_x + 2) * (cells_y + 2) * (cells_z + 2) * sites
    site = slots % sites
    cell = slots // sites
    cell_z = cell % cells_z
    cell_y = cell // cells_z % cells_y
    cell_x = cell // (cells_z * cells_y)
    frame = (
        ((cell_x + 1) * (cells_y + 2) + cell_y + 1) * (cells_z + 2) + cell_z + 1
    ) * sites + site
    return jnp.where(slots < owned, frame, frame_count)


def cell_corner(span_x, span_y, span_z):
    grid_x = jnp.broadcast_to(
        jnp.arange(span_x).astype(jnp.float32)[:, None, None], (span_x, span_y, span_z)
    )
    grid_y = jnp.broadcast_to(
        jnp.arange(span_y).astype(jnp.float32)[None, :, None], (span_x, span_y, span_z)
    )
    grid_z = jnp.broadcast_to(
        jnp.arange(span_z).astype(jnp.float32)[None, None, :], (span_x, span_y, span_z)
    )
    return (jnp.stack([grid_x, grid_y, grid_z], axis=-1) * CELL_SIDE)[:, :, :, None, :]


def pair_return(totals, centre_rows, near_rows, displace, pair_grad):
    block = displace.shape[0]
    slots_count = displace.shape[1]
    pair_virial = -(displace[..., :, None] * pair_grad[..., None, :]).reshape(block, slots_count, 9)
    centre_part = jnp.concatenate(
        [jnp.sum(pair_grad, axis=1), 0.5 * jnp.sum(pair_virial, axis=1)], axis=-1
    )
    near_part = jnp.concatenate([-pair_grad, 0.5 * pair_virial], axis=-1).reshape(
        block * slots_count, 12
    )
    totals = totals.at[centre_rows].add(centre_part)
    return totals.at[near_rows.reshape(-1)].add(near_part)


def local(
    positions,
    features,
    species,
    centers,
    neighbours,
    counts,
    species_scale,
    species_shift,
    center_weight,
    near_weight,
    basis_weight,
    path_weight,
    value_weight,
    latent_weight,
    out_weight,
):
    cells_x, cells_y, cells_z, sites, width = features.shape
    owned = cells_x * cells_y * cells_z * sites
    span_x = cells_x + 2
    span_y = cells_y + 2
    span_z = cells_z + 2
    frame_count = span_x * span_y * span_z * sites
    coords = jnp.transpose(positions, (1, 2, 3, 4, 0)).reshape(
        cells_x, cells_y, cells_z, 1, sites * 3
    )
    coords = jnp.pad(coords, ((0, 0), (0, 0), (0, 0), (0, 0), (0, width - sites * 3)))
    payload = jnp.concatenate([features, coords], axis=3)
    framed = padded(payload, (("gx", 0), ("gy", 1), ("gz", 2)), 1)
    frame_feat = framed[:, :, :, :sites, :].reshape(frame_count, width)
    in_cell = framed[:, :, :, sites, : sites * 3].reshape(span_x, span_y, span_z, sites, 3)
    frame_position = (in_cell + cell_corner(span_x, span_y, span_z)).reshape(frame_count, 3)
    frame_position = jnp.concatenate([frame_position, jnp.zeros((1, 3), jnp.float32)], axis=0)
    near = jnp.dot(frame_feat, near_weight, precision=EXACT_DOT, preferred_element_type=jnp.float32)
    near = jnp.concatenate([near, jnp.zeros((1, width), jnp.float32)], axis=0)
    own_center = jnp.dot(
        features.reshape(owned, width),
        center_weight,
        precision=EXACT_DOT,
        preferred_element_type=jnp.float32,
    )
    own_center = jnp.concatenate([own_center, jnp.zeros((1, width), jnp.float32)], axis=0)
    own_species = jnp.concatenate([species.reshape(owned), jnp.zeros((1,), jnp.int32)], axis=0)
    kinds = jnp.arange(species_scale.shape[0])
    paths = path_table(path_weight)
    dead_shift = jnp.array([6.0, 0.0, 0.0], jnp.float32)
    block = min(32, owned)

    def visit(step_index, carry):
        totals, energy = carry
        start = (jnp.asarray(step_index) * block).astype(jnp.int32)
        active = (start + jnp.arange(block) < counts[0]).astype(jnp.float32)
        kind = own_species[centers]
        matches = (kind[:, None] == kinds[None, :]).astype(jnp.float32)
        scale = jnp.sum(matches * species_scale[None, :], axis=1)
        shift = jnp.sum(matches * species_shift[None, :], axis=1)
        centre_rows = own_to_frame(centers, cells_x, cells_y, cells_z, sites)
        live = (neighbours != frame_count).astype(jnp.float32)
        separation = frame_position[neighbours] - frame_position[centre_rows][:, None, :]
        displace = jnp.where(live[..., None] > 0.0, separation, dead_shift)
        center_proj = own_center[centers]
        near_proj = near[neighbours]

        def energy_of(moved):
            return center_energy(
                moved,
                live,
                center_proj,
                near_proj,
                scale,
                shift,
                active,
                basis_weight,
                paths,
                value_weight,
                latent_weight,
                out_weight,
            )

        energies, pull = jax.vjp(energy_of, displace)
        pair_grad = pull(jnp.ones_like(energies))[0]
        totals = pair_return(totals, centre_rows, neighbours, displace, pair_grad)
        energy = energy.at[centers].add(energies)
        return (totals, energy)

    initial = (jnp.zeros((frame_count + 1, 12), jnp.float32), jnp.zeros((owned + 1,), jnp.float32))
    limit = owned // block
    totals, energy = lax.fori_loop(0, limit, visit, initial)
    grid = totals[:frame_count].reshape(span_x, span_y, span_z, sites * 12)
    outgoing = jnp.stack([grid[:, :, 0], grid[:, :, span_z - 1]], axis=2)
    incoming = padded(outgoing, (("gz", 2),), 1)
    grid = grid[:, :, 1 : span_z - 1]
    grid = grid.at[:, :, 0].add(incoming[:, :, 0])
    grid = grid.at[:, :, cells_z - 1].add(incoming[:, :, 3])
    outgoing = jnp.stack([grid[:, 0], grid[:, span_y - 1]], axis=1)
    incoming = padded(outgoing, (("gy", 1),), 1)
    grid = grid[:, 1 : span_y - 1]
    grid = grid.at[:, 0].add(incoming[:, 0])
    grid = grid.at[:, cells_y - 1].add(incoming[:, 3])
    outgoing = jnp.stack([grid[0], grid[span_x - 1]], axis=0)
    incoming = padded(outgoing, (("gx", 0),), 1)
    grid = grid[1 : span_x - 1]
    grid = grid.at[0].add(incoming[0])
    grid = grid.at[cells_x - 1].add(incoming[3])
    grid = grid.reshape(cells_x, cells_y, cells_z, sites, 12)
    forces = jnp.transpose(grid[..., 0:3], (4, 0, 1, 2, 3))
    virial = jnp.transpose(grid[..., 3:12], (4, 0, 1, 2, 3))
    site_energy = energy[:owned].reshape(cells_x, cells_y, cells_z, sites)
    return (site_energy, forces, virial)


def solution(mesh):
    placed = (
        P(None, "gx", "gy", "gz", None),
        P("gx", "gy", "gz", None, None),
        P("gx", "gy", "gz", None),
        P(("gx", "gy", "gz")),
        P(("gx", "gy", "gz"), None),
        P(("gx", "gy", "gz")),
        P(),
        P(),
        P(),
        P(),
        P(),
        P(),
        P(),
        P(),
        P(),
    )
    return jax.shard_map(
        local,
        mesh=mesh,
        in_specs=placed,
        out_specs=(
            P("gx", "gy", "gz", None),
            P(None, "gx", "gy", "gz", None),
            P(None, "gx", "gy", "gz", None),
        ),
        check_vma=False,
    )
```

profile of v0, /device:TPU:0, one launch (start us, length us, event | category | flops | bytes accessed | tf_op | source)
XLA Modules:
  0.0 71.8 jit_solution(12245250420275676102)
XLA Ops:
  0.6 0.8 %copy.75 = f32[2,1,2,8,3]{4,3,2,0,1:T(8,128)S(1)} copy(f32[2,1,2,8,3]{3,2,1,0,4:T(2,128)} %bitcast.83) | data formatting | bytes 768 | tf_op jit(solution)/shard_map/transpose | solution.py:171
  2.2 3.1 %collective-permute-start = (f32[1,1,2,9,128]{4,3,2,1,0:T(8,128)S(1)}, f32[1,1,2,9,128]{4,3,2,1,0:T(8,128)S(1)}, u32[]{:S(2)}, u32[]{:S(2)}) collective-permute-start(f32[1,1,2,9,128]{4,3,2,1,0:T(8,128)S(1)} %get-tuple-element.173), channel_id=1, source_target_pairs={{0,8},{8,16},{16,24},{24,0},{1,9},{9,17},{17,25},{25,1},{2,10},{10... | collective-permute-start | bytes 27656 | tf_op jit(solution)/shard_map/ppermute | solution.py:21
  5.3 2.1 %collective-permute-start.1 = (f32[1,1,2,9,128]{4,3,2,1,0:T(8,128)S(1)}, f32[1,1,2,9,128]{4,3,2,1,0:T(8,128)S(1)}, u32[]{:S(2)}, u32[]{:S(2)}) collective-permute-start(f32[1,1,2,9,128]{4,3,2,1,0:T(8,128)S(1)} %get-tuple-element.174), channel_id=1, source_target_pairs={{8,0},{16,8},{24,16},{0,24},{9,1},{17,9},{25,17},{1,25},{10,2},{18... | collective-permute-start | bytes 27656 | tf_op jit(solution)/shard_map/ppermute | solution.py:22
  11.0 1.7 %collective-permute-start.3 = (f32[4,1,2,9,128]{4,3,2,1,0:T(8,128)S(1)}, f32[4,1,2,9,128]{4,3,2,1,0:T(8,128)S(1)}, u32[]{:S(2)}, u32[]{:S(2)}) collective-permute-start(f32[4,1,2,9,128]{4,3,2,1,0:T(8,128)S(1)} %pad_maximum_fusion.3), channel_id=1, source_target_pairs={{4,0},{0,4},{5,1},{1,5},{6,2},{2,6},{7,3},{3,7},{12,8},{8,12},{13,... | collective-permute-start | bytes 110600 | tf_op jit(solution)/shard_map/ppermute | solution.py:22
  13.1 2.7 %collective-permute-done.3 = f32[4,1,2,9,128]{4,3,2,1,0:T(8,128)S(1)} collective-permute-done((f32[4,1,2,9,128]{4,3,2,1,0:T(8,128)S(1)}, f32[4,1,2,9,128]{4,3,2,1,0:T(8,128)S(1)}, u32[]{:S(2)}, u32[]{:S(2)}) %collective-permute-start.3) | collective-permute-done | bytes 36896 | tf_op jit(solution)/shard_map/ppermute | solution.py:22
  15.9 1.1 %collective-permute-done.2 = f32[4,1,2,9,128]{4,3,2,1,0:T(8,128)S(1)} collective-permute-done((f32[4,1,2,9,128]{4,3,2,1,0:T(8,128)S(1)}, f32[4,1,2,9,128]{4,3,2,1,0:T(8,128)S(1)}, u32[]{:S(2)}, u32[]{:S(2)}) %collective-permute-start.2) | collective-permute-done | bytes 36896 | tf_op jit(solution)/shard_map/ppermute | solution.py:21
  17.1 1.7 %collective-permute-start.5 = (f32[4,3,1,9,128]{4,3,2,1,0:T(8,128)S(1)}, f32[4,3,1,9,128]{4,3,2,1,0:T(8,128)S(1)}, u32[]{:S(2)}, u32[]{:S(2)}) collective-permute-start(f32[4,3,1,9,128]{4,3,2,1,0:T(8,128)S(1)} %get-tuple-element.168), channel_id=1, source_target_pairs={{1,0},{2,1},{3,2},{0,3},{5,4},{6,5},{7,6},{4,7},{9,8},{10,9},{11,1... | collective-permute-start | bytes 165896 | tf_op jit(solution)/shard_map/ppermute | solution.py:22
  20.1 1.1 %collective-permute-done.4 = f32[4,3,1,9,128]{4,3,2,1,0:T(8,128)S(1)} collective-permute-done((f32[4,3,1,9,128]{4,3,2,1,0:T(8,128)S(1)}, f32[4,3,1,9,128]{4,3,2,1,0:T(8,128)S(1)}, u32[]{:S(2)}, u32[]{:S(2)}) %collective-permute-start.4) | collective-permute-done | bytes 55328 | tf_op jit(solution)/shard_map/ppermute | solution.py:21
  21.4 0.8 %copy-done.4 = f32[128,128]{1,0:T(8,128)S(1)} copy-done((f32[128,128]{1,0:T(8,128)S(1)}, f32[128,128]{1,0:T(8,128)}, u32[]{:S(2)}) %copy-start.4) | copy-done | bytes 65560
  23.4 2.8 %gather_fusion.1 = f32[1024,3]{1,0:T(8,128)S(1)} fusion(f32[385,3]{1,0:T(8,128)S(1)} %concatenate.60, s32[1024]{0:T(1024)S(1)} %broadcast_clamp_fusion), kind=kCustom, calls=%fused_computation.1 | custom fusion | bytes 28672 | tf_op jit(solution)/shard_map/while/body/eval_jaxpr/gather | solution.py:206
  27.4 3.0 %gather_fusion.4 = f32[1024,128]{1,0:T(8,128)S(1)} fusion(f32[385,128]{1,0:T(8,128)S(1)} %concatenate.62, s32[1024]{0:T(1024)S(1)} %broadcast_clamp_fusion), kind=kCustom, calls=%fused_computation.4 | custom fusion | bytes 1052672 | tf_op jit(solution)/shard_map/while/body/eval_jaxpr/gather | solution.py:209
  31.1 1.5 %broadcast_multiply_fusion = (f32[32,32,128]{2,1,0:T(8,128)S(1)}, f32[32,32,128]{2,1,0:T(8,128)S(1)}) fusion(f32[32,32]{1,0:T(8,128)S(1)} %get-tuple-element.178, f32[32,32,128]{2,1,0:T(8,128)S(1)} %bitcast.73, f32[32,128]{1,0:T(8,128)S(1)} %gather_fusion.3, f32[8,128]{1,0:T(8,128)S(1)} %copy-done.12, f32[32,32]{1,0:T(8,128)S(1)} %get-tuple-element.179, ...), kind=kOutput, calls=%fused_computation.69 | convolution fusion | flops 13524992 | bytes 1605664 | tf_op jit(solution)/shard_map/while/body/eval_jaxpr/jvp(knb,bc->knc)/dot_general | solution.py:89
  32.6 1.0 %fusion.62 = f32[32,32,256]{2,1,0:T(8,128)S(1)} fusion(f32[32,32,128]{2,1,0:T(8,128)S(1)} %get-tuple-element.191, f32[128,256]{1,0:T(8,128)S(1)} %copy-done), kind=kOutput, calls=%fused_computation.90 | convolution fusion | flops 402653184 | bytes 1703936 | tf_op jit(solution)/shard_map/while/body/eval_jaxpr/jvp(knc,cd->knd)/dot_general | solution.py:91
  34.2 1.1 %slice_multiply_fusion.2 = (f32[32,32,128]{2,1,0:T(8,128)S(1)}, f32[32,32,128]{2,1,0:T(8,128)S(1)}) fusion(f32[32,32,256]{2,1,0:T(8,128)S(1)} %fusion.62, f32[32,128,9]{1,2,0:T(8,128)S(1)} %convolution_multiply_fusion.1, f32[32,32,9]{1,0,2:T(8,128)S(1)} %constant_dynamic-update-slice_fusion), kind=kOutput, calls=%fused_computation.53 | convolution fusion | flops 14286848 | bytes 1757184 | tf_op jit(solution)/shard_map/while/body/eval_jaxpr/jvp(knm,kcm->knc)/dot_general | solution.py:98
  35.3 1.0 %fusion.2 = f32[32,32,128]{2,1,0:T(8,128)S(1)} fusion(f32[32,32,128]{2,1,0:T(8,128)S(1)} %get-tuple-element.193, f32[32,32,128]{2,1,0:T(8,128)S(1)} %get-tuple-element.191, f32[256,128]{1,0:T(8,128)S(1)} %copy-done.3), kind=kOutput, calls=%fused_computation.14 | convolution fusion | flops 402915328 | bytes 1703936 | tf_op jit(solution)/shard_map/while/body/eval_jaxpr/jvp(knc,cd->knd)/dot_general | solution.py:101
  36.3 2.2 %fusion.26 = f32[1,32,32]{2,0,1:T(1,128)S(1)} fusion(f32[32,32,128]{2,1,0:T(8,128)S(1)} %get-tuple-element.191, f32[32,32]{1,0:T(8,128)S(1)} %get-tuple-element.178, f32[32,32,128]{2,1,0:T(8,128)S(1)} %fusion.2, f32[128]{0:T(128)S(1)} %copy-done.11), kind=kOutput, calls=%fused_computation.40 | convolution fusion | flops 2490368 | bytes 1057280 | tf_op jit(solution)/shard_map/while/body/eval_jaxpr/jvp(knc,c->kn)/dot_general | solution.py:103
  39.0 1.0 %fusion.15 = f32[32,32,256]{2,1,0:T(8,128)S(1)} fusion(f32[32,32,128]{2,1,0:T(8,128)S(1)} %fusion.2, f32[32,32]{1,0:T(8,128)S(1)} %get-tuple-element.177, f32[128]{0:T(128)S(1)} %copy-done.11, f32[32]{0:T(128)S(1)} %get-tuple-element.187, f32[256,128]{1,0:T(8,128)S(1)} %copy-done.3), kind=kOutput, calls=%fused_computation.31 | convolution fusion | flops 404094976 | bytes 1708672 | tf_op jit(solution)/shard_map/while/body/eval_jaxpr/transpose(jvp(knc,cd->knd))/dot_general | solution.py:101
  40.0 0.9 %fusion.49 = f32[32,32,9]{1,2,0:T(8,128)S(1)} fusion(f32[32,128,9]{1,2,0:T(8,128)S(1)} %convolution_multiply_fusion.1, f32[32,32,256]{2,1,0:T(8,128)S(1)} %fusion.15, f32[32,32,256]{2,1,0:T(8,128)S(1)} %fusion.62), kind=kOutput, calls=%fused_computation.77 | convolution fusion | flops 14286848 | bytes 1347584 | tf_op jit(solution)/shard_map/while/body/eval_jaxpr/transpose(jvp(knm,kcm->knc))/dot_general | solution.py:98
  41.6 0.9 %fusion.32 = f32[32,32,9]{1,2,0:T(8,128)S(1)} fusion(f32[32,128,9]{1,2,0:T(8,128)S(1)} %fusion.1, f32[32,32,256]{2,1,0:T(8,128)S(1)} %fusion.62), kind=kOutput, calls=%fused_computation.50 | convolution fusion | flops 14155776 | bytes 823296 | tf_op jit(solution)/shard_map/while/body/eval_jaxpr/transpose(jvp(knc,knm->kcm))/dot_general | solution.py:94
  42.6 1.1 %fusion.35 = f32[32,32,128]{2,1,0:T(8,128)S(1)} fusion(f32[32,128,9]{1,2,0:T(8,128)S(1)} %fusion.1, f32[32,32,9]{1,0,2:T(8,128)S(1)} %constant_dynamic-update-slice_fusion), kind=kOutput, calls=%fused_computation.55 | convolution fusion | flops 14155776 | bytes 708608 | tf_op jit(solution)/shard_map/while/body/eval_jaxpr/transpose(jvp(knc,knm->kcm))/dot_general | solution.py:94
  43.8 1.1 %multiply_reduce_fusion = (f32[32,32]{1,0:T(8,128)S(1)}, f32[32,32,128]{2,1,0:T(8,128)S(1)}) fusion(f32[32,32,128]{2,1,0:T(8,128)S(1)} %get-tuple-element.192, f32[128,256]{1,0:T(8,128)S(1)} %copy-done, f32[32,32,128]{2,1,0:T(8,128)S(1)} %slice_multiply_fusion, f32[32,32,128]{2,1,0:T(8,128)S(1)} %fusion.35, f32[32,32,256]{2,1,0:T(8,128)S(1)} %fusion.15, ...), kind=kOutput, calls=%fused_computation.36 | convolution fusion | flops 404225024 | bytes 2757248 | tf_op jit(solution)/shard_map/while/body/eval_jaxpr/transpose(jvp(knc,cd->knd))/dot_general | solution.py:91
  44.9 2.7 %fusion.55 = (f32[32,32]{1,0:T(8,128)S(1)}, f32[32,32]{1,0:T(8,128)S(1)}) fusion(f32[32,32]{1,0:T(8,128)S(1)} %get-tuple-element.175, f32[8]{0:T(128)S(1)} %convert_multiply_fusion, f32[32,32]{1,0:T(8,128)S(1)} %get-tuple-element.176, f32[32,32]{1,0:T(8,128)S(1)} %get-tuple-element.179, f32[8,128]{1,0:T(8,128)S(1)} %copy-done.12, ...), kind=kOutput, calls=%fused_computation.83 | convolution fusion | flops 13973504 | bytes 1077280 | tf_op jit(solution)/shard_map/while/body/eval_jaxpr/transpose(jvp(knb,bc->knc))/dot_general | solution.py:89
  48.0 0.7 %scatter_custom_fusion.1 = f32[385,12]{1,0:T(8,128)S(1)} fusion(s32[32]{0:T(128)S(1)} %get-tuple-element.189, f32[32,12]{1,0:T(8,128)S(1)} %copy.87, f32[]{:T(128)} %constant.293.clone.1), kind=kCustom, calls=%fused_computation.92 | custom fusion | flops 384 | bytes 18484 | tf_op jit(solution)/shard_map/while/body/eval_jaxpr/scatter-add | solution.py:144
  49.0 6.1 %scatter_fusion = f32[385,12]{1,0:T(8,128)S(1)} fusion(f32[385,12]{1,0:T(8,128)S(1)} %scatter_custom_fusion.1, s32[1024]{0:T(1024)S(1)} %bitcast.81, f32[1024,12]{1,0:T(8,128)S(1)} %bitcast.69), kind=kCustom, calls=%fused_computation.7 | custom fusion | flops 12288 | bytes 151552 | tf_op jit(solution)/shard_map/while/body/eval_jaxpr/scatter-add | solution.py:145
  55.2 1.9 %collective-permute-start.6 = (f32[4,3,1,96]{3,2,1,0:T(1,128)S(1)}, f32[4,3,1,96]{3,2,1,0:T(1,128)S(1)}, u32[]{:S(2)}, u32[]{:S(2)}) collective-permute-start(f32[4,3,1,96]{3,2,1,0:T(1,128)S(1)} %get-tuple-element.172), channel_id=1, source_target_pairs={{0,1},{1,2},{2,3},{3,0},{4,5},{5,6},{6,7},{7,4},{8,9},{9,10},{10,1... | collective-permute-start | bytes 13832 | tf_op jit(solution)/shard_map/ppermute | solution.py:21
  57.3 1.2 %collective-permute-done.6 = f32[4,3,1,96]{3,2,1,0:T(1,128)S(1)} collective-permute-done((f32[4,3,1,96]{3,2,1,0:T(1,128)S(1)}, f32[4,3,1,96]{3,2,1,0:T(1,128)S(1)}, u32[]{:S(2)}, u32[]{:S(2)}) %collective-permute-start.6) | collective-permute-done | bytes 4640 | tf_op jit(solution)/shard_map/ppermute | solution.py:21
  58.7 1.4 %collective-permute-start.8 = (f32[4,1,2,96]{3,2,1,0:T(2,128)S(1)}, f32[4,1,2,96]{3,2,1,0:T(2,128)S(1)}, u32[]{:S(2)}, u32[]{:S(2)}) collective-permute-start(f32[4,1,2,96]{3,2,1,0:T(2,128)S(1)} %get-tuple-element.180), channel_id=1, source_target_pairs={{0,4},{4,0},{1,5},{5,1},{2,6},{6,2},{3,7},{7,3},{8,12},{12,8},{9,1... | collective-permute-start | bytes 9224 | tf_op jit(solution)/shard_map/ppermute | solution.py:21
  60.8 1.6 %collective-permute-done.8 = f32[4,1,2,96]{3,2,1,0:T(2,128)S(1)} collective-permute-done((f32[4,1,2,96]{3,2,1,0:T(2,128)S(1)}, f32[4,1,2,96]{3,2,1,0:T(2,128)S(1)}, u32[]{:S(2)}, u32[]{:S(2)}) %collective-permute-start.8) | collective-permute-done | bytes 3104 | tf_op jit(solution)/shard_map/ppermute | solution.py:21
  62.4 1.3 %collective-permute-done.9 = f32[4,1,2,96]{3,2,1,0:T(2,128)S(1)} collective-permute-done((f32[4,1,2,96]{3,2,1,0:T(2,128)S(1)}, f32[4,1,2,96]{3,2,1,0:T(2,128)S(1)}, u32[]{:S(2)}, u32[]{:S(2)}) %collective-permute-start.9) | collective-permute-done | bytes 3104 | tf_op jit(solution)/shard_map/ppermute | solution.py:22
  63.8 0.8 %scatter_custom_fusion = f32[33]{0:T(128)S(1)} fusion(s32[32]{0:T(128)S(1)} %get-tuple-element.190, f32[32]{0:T(128)S(1)} %get-tuple-element.188, f32[]{:T(128)} %constant.293.clone.1), kind=kCustom, calls=%fused_computation.210 | custom fusion | flops 32 | bytes 136 | tf_op jit(solution)/shard_map/while/body/eval_jaxpr/scatter-add | solution.py:230
  65.2 3.8 %collective-permute-start.11 = (f32[1,1,2,96]{3,2,1,0:T(2,128)S(1)}, f32[1,1,2,96]{3,2,1,0:T(2,128)S(1)}, u32[]{:S(2)}, u32[]{:S(2)}) collective-permute-start(f32[1,1,2,96]{3,2,1,0:T(2,128)S(1)} %get-tuple-element.182), channel_id=1, source_target_pairs={{8,0},{16,8},{24,16},{0,24},{9,1},{17,9},{25,17},{1,25},{10,2},{18... | collective-permute-start | bytes 2312 | tf_op jit(solution)/shard_map/ppermute | solution.py:22
  69.2 1.2 %collective-permute-done.11 = f32[1,1,2,96]{3,2,1,0:T(2,128)S(1)} collective-permute-done((f32[1,1,2,96]{3,2,1,0:T(2,128)S(1)}, f32[1,1,2,96]{3,2,1,0:T(2,128)S(1)}, u32[]{:S(2)}, u32[]{:S(2)}) %collective-permute-start.11) | collective-permute-done | bytes 800 | tf_op jit(solution)/shard_map/ppermute | solution.py:22
  (131 shorter events, 14.5 us)
Async XLA Ops:
  0.6 31.9 %copy-start = (f32[128,256]{1,0:T(8,128)S(1)}, f32[128,256]{1,0:T(8,128)}, u32[]{:S(2)}) copy-start(f32[128,256]{1,0:T(8,128)} %param.40) | copy-start | bytes 393220
  1.5 0.7 copy-start.1
  2.2 5.2 %copy-start.2 = (s32[32,32]{1,0:T(8,128)S(1)}, s32[32,32]{1,0:T(8,128)}, u32[]{:S(2)}) copy-start(s32[32,32]{1,0:T(8,128)} %param.32) | copy-start | bytes 12292
  2.2 8.8 %collective-permute-start = (f32[1,1,2,9,128]{4,3,2,1,0:T(8,128)S(1)}, f32[1,1,2,9,128]{4,3,2,1,0:T(8,128)S(1)}, u32[]{:S(2)}, u32[]{:S(2)}) collective-permute-start(f32[1,1,2,9,128]{4,3,2,1,0:T(8,128)S(1)} %get-tuple-element.173), channel_id=1, source_target_pairs={{0,8},{8,16},{16,24},{24,0},{1,9},{9,17},{17,25},{25,1},{2,10},{10... | collective-permute-start | bytes 27656 | tf_op jit(solution)/shard_map/ppermute | solution.py:21
  5.3 5.7 %collective-permute-start.1 = (f32[1,1,2,9,128]{4,3,2,1,0:T(8,128)S(1)}, f32[1,1,2,9,128]{4,3,2,1,0:T(8,128)S(1)}, u32[]{:S(2)}, u32[]{:S(2)}) collective-permute-start(f32[1,1,2,9,128]{4,3,2,1,0:T(8,128)S(1)} %get-tuple-element.174), channel_id=1, source_target_pairs={{8,0},{16,8},{24,16},{0,24},{9,1},{17,9},{25,17},{1,25},{10,2},{18... | collective-permute-start | bytes 27656 | tf_op jit(solution)/shard_map/ppermute | solution.py:22
  7.5 0.7 copy-start.6
  8.2 0.7 copy-start.13
  8.2 0.7 copy-start.7
  9.0 0.8 %copy-start.5 = (f32[128,128]{1,0:T(8,128)S(1)}, f32[128,128]{1,0:T(8,128)}, u32[]{:S(2)}) copy-start(f32[128,128]{1,0:T(8,128)} %param.36) | copy-start | bytes 196612
  9.9 0.7 copy-start.9
  9.9 0.7 copy-start.10
  11.0 4.8 %collective-permute-start.3 = (f32[4,1,2,9,128]{4,3,2,1,0:T(8,128)S(1)}, f32[4,1,2,9,128]{4,3,2,1,0:T(8,128)S(1)}, u32[]{:S(2)}, u32[]{:S(2)}) collective-permute-start(f32[4,1,2,9,128]{4,3,2,1,0:T(8,128)S(1)} %pad_maximum_fusion.3), channel_id=1, source_target_pairs={{4,0},{0,4},{5,1},{1,5},{6,2},{2,6},{7,3},{3,7},{12,8},{8,12},{13,... | collective-permute-start | bytes 110600 | tf_op jit(solution)/shard_map/ppermute | solution.py:22
  12.7 4.3 %collective-permute-start.2 = (f32[4,1,2,9,128]{4,3,2,1,0:T(8,128)S(1)}, f32[4,1,2,9,128]{4,3,2,1,0:T(8,128)S(1)}, u32[]{:S(2)}, u32[]{:S(2)}) collective-permute-start(f32[4,1,2,9,128]{4,3,2,1,0:T(8,128)S(1)} %pad_maximum_fusion.3), channel_id=1, source_target_pairs={{0,4},{4,0},{1,5},{5,1},{2,6},{6,2},{3,7},{7,3},{8,12},{12,8},{9,1... | collective-permute-start | bytes 110600 | tf_op jit(solution)/shard_map/ppermute | solution.py:21
  17.0 4.1 %collective-permute-start.4 = (f32[4,3,1,9,128]{4,3,2,1,0:T(8,128)S(1)}, f32[4,3,1,9,128]{4,3,2,1,0:T(8,128)S(1)}, u32[]{:S(2)}, u32[]{:S(2)}) collective-permute-start(f32[4,3,1,9,128]{4,3,2,1,0:T(8,128)S(1)} %get-tuple-element.167), channel_id=1, source_target_pairs={{0,1},{1,2},{2,3},{3,0},{4,5},{5,6},{6,7},{7,4},{8,9},{9,10},{10,1... | collective-permute-start | bytes 165896 | tf_op jit(solution)/shard_map/ppermute | solution.py:21
  17.1 4.1 %collective-permute-start.5 = (f32[4,3,1,9,128]{4,3,2,1,0:T(8,128)S(1)}, f32[4,3,1,9,128]{4,3,2,1,0:T(8,128)S(1)}, u32[]{:S(2)}, u32[]{:S(2)}) collective-permute-start(f32[4,3,1,9,128]{4,3,2,1,0:T(8,128)S(1)} %get-tuple-element.168), channel_id=1, source_target_pairs={{1,0},{2,1},{3,2},{0,3},{5,4},{6,5},{7,6},{4,7},{9,8},{10,9},{11,1... | collective-permute-start | bytes 165896 | tf_op jit(solution)/shard_map/ppermute | solution.py:22
  21.3 0.8 %copy-start.4 = (f32[128,128]{1,0:T(8,128)S(1)}, f32[128,128]{1,0:T(8,128)}, u32[]{:S(2)}) copy-start(f32[128,128]{1,0:T(8,128)} %param.37) | copy-start | bytes 196612
  26.4 0.7 copy-start.8
  30.4 0.7 copy-start.12
  34.2 1.1 %copy-start.3 = (f32[256,128]{1,0:T(8,128)S(1)}, f32[256,128]{1,0:T(8,128)}, u32[]{:S(2)}) copy-start(f32[256,128]{1,0:T(8,128)} %param.41) | copy-start | bytes 393220
  35.3 1.0 %copy-start.11 = (f32[128]{0:T(128)S(1)}, f32[128]{0:T(128)}, u32[]{:S(2)}) copy-start(f32[128]{0:T(128)} %param.42) | copy-start | bytes 1540
  55.2 3.3 %collective-permute-start.6 = (f32[4,3,1,96]{3,2,1,0:T(1,128)S(1)}, f32[4,3,1,96]{3,2,1,0:T(1,128)S(1)}, u32[]{:S(2)}, u32[]{:S(2)}) collective-permute-start(f32[4,3,1,96]{3,2,1,0:T(1,128)S(1)} %get-tuple-element.172), channel_id=1, source_target_pairs={{0,1},{1,2},{2,3},{3,0},{4,5},{5,6},{6,7},{7,4},{8,9},{9,10},{10,1... | collective-permute-start | bytes 13832 | tf_op jit(solution)/shard_map/ppermute | solution.py:21
  57.2 1.4 %collective-permute-start.7 = (f32[4,3,1,96]{3,2,1,0:T(1,128)S(1)}, f32[4,3,1,96]{3,2,1,0:T(1,128)S(1)}, u32[]{:S(2)}, u32[]{:S(2)}) collective-permute-start(f32[4,3,1,96]{3,2,1,0:T(1,128)S(1)} %get-tuple-element.171), channel_id=1, source_target_pairs={{1,0},{2,1},{3,2},{0,3},{5,4},{6,5},{7,6},{4,7},{9,8},{10,9},{11,1... | collective-permute-start | bytes 13832 | tf_op jit(solution)/shard_map/ppermute | solution.py:22
  58.7 3.7 %collective-permute-start.8 = (f32[4,1,2,96]{3,2,1,0:T(2,128)S(1)}, f32[4,1,2,96]{3,2,1,0:T(2,128)S(1)}, u32[]{:S(2)}, u32[]{:S(2)}) collective-permute-start(f32[4,1,2,96]{3,2,1,0:T(2,128)S(1)} %get-tuple-element.180), channel_id=1, source_target_pairs={{0,4},{4,0},{1,5},{5,1},{2,6},{6,2},{3,7},{7,3},{8,12},{12,8},{9,1... | collective-permute-start | bytes 9224 | tf_op jit(solution)/shard_map/ppermute | solution.py:21
  60.1 3.6 %collective-permute-start.9 = (f32[4,1,2,96]{3,2,1,0:T(2,128)S(1)}, f32[4,1,2,96]{3,2,1,0:T(2,128)S(1)}, u32[]{:S(2)}, u32[]{:S(2)}) collective-permute-start(f32[4,1,2,96]{3,2,1,0:T(2,128)S(1)} %get-tuple-element.181), channel_id=1, source_target_pairs={{4,0},{0,4},{5,1},{1,5},{6,2},{2,6},{7,3},{3,7},{12,8},{8,12},{13,... | collective-permute-start | bytes 9224 | tf_op jit(solution)/shard_map/ppermute | solution.py:22
  63.7 5.4 %collective-permute-start.10 = (f32[1,1,2,96]{3,2,1,0:T(2,128)S(1)}, f32[1,1,2,96]{3,2,1,0:T(2,128)S(1)}, u32[]{:S(2)}, u32[]{:S(2)}) collective-permute-start(f32[1,1,2,96]{3,2,1,0:T(2,128)S(1)} %get-tuple-element.183), channel_id=1, source_target_pairs={{0,8},{8,16},{16,24},{24,0},{1,9},{9,17},{17,25},{25,1},{2,10},{10... | collective-permute-start | bytes 2312 | tf_op jit(solution)/shard_map/ppermute | solution.py:21
  65.2 5.1 %collective-permute-start.11 = (f32[1,1,2,96]{3,2,1,0:T(2,128)S(1)}, f32[1,1,2,96]{3,2,1,0:T(2,128)S(1)}, u32[]{:S(2)}, u32[]{:S(2)}) collective-permute-start(f32[1,1,2,96]{3,2,1,0:T(2,128)S(1)} %get-tuple-element.182), channel_id=1, source_target_pairs={{8,0},{16,8},{24,16},{0,24},{9,1},{17,9},{25,17},{1,25},{10,2},{18... | collective-permute-start | bytes 2312 | tf_op jit(solution)/shard_map/ppermute | solution.py:22
where the time goes:
time: 72 us; the launch traced here: 71.8 us
  local copies, waits for them, and re-layouts  17.1 us (24%)
  starting transfers between devices  17 us (24%)
  matrix products  16.1 us (22%)
  waiting for transfers between devices  10.5 us (15%)
  other arithmetic  9.15 us (13%)
  between operations  1.9 us (3%)
    ppermute x6, starting transfers between devices, padded(): after = lax.ppermute(leading, axis, down)  10.1 us
    ppermute x6, starting transfers between devices, padded(): before = lax.ppermute(last, axis, up)  6.89 us
    scatter-add x1, other arithmetic, pair_return(): return totals.at[near_rows.reshape(-1)].add(near_part)  6.06 us
    unnamed x30, local copies, waits for them, and re-layouts  5.41 us
    ppermute x6, waiting for transfers between devices, padded(): after = lax.ppermute(leading, axis, down)  5.39 us
    ppermute x6, waiting for transfers between devices, padded(): before = lax.ppermute(last, axis, up)  5.12 us
    dot_general x2, matrix products, center_energy(): radial = jnp.einsum('knb,bc->knc', basis, basis_weight, precision=EXACT_DOT)  4.16 us
    gather x2, local copies, waits for them, and re-layouts, visit(): frame_position[neighbours] - frame_position[centre_rows][:, None, :]  3.08 us
  transfers between devices with their start and end apart: 12, of which 9 were waited for; matrix products, arithmetic and copies ran while one was open for 5% of the time, Pallas kernels for 0%

commit v1 on v0

v1 whole, which is shorter than its diff:
```python
import math

import jax
import jax.numpy as jnp
import numpy as np
from jax import lax
from jax.experimental import pallas as pl
from jax.experimental.pallas import tpu as pltpu
from jax.sharding import PartitionSpec as P

EXACT_DOT = lax.Precision.HIGHEST
CUTOFF = 5.0
CELL_SIDE = 4.6
ROOT_HALF = 0.7071067811865476
GROUP = 8
ORDERS = 16
F32 = jnp.float32
BF16 = jnp.bfloat16


def padded(array, sides, width):
    for axis, dim in sides:
        size, length = (lax.axis_size(axis), array.shape[dim])
        up = [(i, (i + 1) % size) for i in range(size)]
        down = [(j, i) for i, j in up]
        last = lax.slice_in_dim(array, length - width, length, axis=dim)
        leading = lax.slice_in_dim(array, 0, width, axis=dim)
        before = lax.ppermute(last, axis, up)
        if size == 2 and length == width:
            after = before
        else:
            after = lax.ppermute(leading, axis, down)
        array = jnp.concatenate([before, array, after], axis=dim)
    return array


def cell_corner(span_x, span_y, span_z):
    grid = np.stack(
        np.meshgrid(np.arange(span_x), np.arange(span_y), np.arange(span_z), indexing="ij"),
        axis=-1,
    ).astype(np.float32)
    return grid * np.float32(CELL_SIDE)


def split(value):
    high = value.astype(BF16)
    low = (value - high.astype(F32)).astype(BF16)
    return high, low


def split3(value):
    high = value.astype(BF16)
    rest = value - high.astype(F32)
    middle = rest.astype(BF16)
    low = (rest - middle.astype(F32)).astype(BF16)
    return high, middle, low


def mm(a, b):
    return lax.dot_general(a, b, (((1,), (0,)), ((), ())), preferred_element_type=F32)


def mm_nt(a, b):
    return lax.dot_general(a, b, (((1,), (1,)), ((), ())), preferred_element_type=F32)


def stacked(high, low):
    top = jnp.concatenate([high, high], axis=1)
    bottom = jnp.concatenate([low, jnp.zeros_like(low)], axis=1)
    return jnp.concatenate([top, bottom], axis=0)


def folded(product):
    half = product.shape[0] // 2
    return product[:half] + product[half:]


def half_depth(weights, value):
    return folded(mm(weights, jnp.concatenate(split(value), axis=0)))


def full_depth(both, high, value_high, value_low):
    return folded(mm(both, value_high)) + mm(high, value_low)


def sin_cos_pi(turns):
    near = turns - 2.0 * jnp.round(turns * 0.5)
    quarter = jnp.round(near * 2.0)
    v = (near - 0.5 * quarter) * math.pi
    v2 = v * v
    s = v * (
        1.0
        + v2
        * (-1.0 / 6 + v2 * (1.0 / 120 + v2 * (-1.0 / 5040 + v2 * (1.0 / 362880 - v2 / 39916800))))
    )
    c = 1.0 + v2 * (
        -0.5
        + v2
        * (1.0 / 24 + v2 * (-1.0 / 720 + v2 * (1.0 / 40320 + v2 * (-1.0 / 3628800 + v2 / 479001600))))
    )
    odd = jnp.abs(quarter) == 1.0
    sine = jnp.where(odd, quarter * c, jnp.where(quarter == 0.0, s, -s))
    cosine = jnp.where(odd, -quarter * s, jnp.where(quarter == 0.0, c, -c))
    return sine, cosine


def force_kernel(
    feats_ref,
    coords_ref,
    own_ref,
    near_row_ref,
    center_row_ref,
    center_slot_ref,
    center_list_ref,
    species_ref,
    scale_ref,
    shift_ref,
    center_weight_ref,
    near_weight_ref,
    basis_weight_ref,
    path_weight_ref,
    value_weight_ref,
    latent_weight_ref,
    out_weight_ref,
    totals_ref,
    energy_ref,
):
    frame, width = feats_ref.shape
    owned = own_ref.shape[0]
    pairs = near_row_ref.shape[1]
    nbr = pairs // owned
    radial = basis_weight_ref.shape[0]
    sites = frame // coords_ref.shape[0]
    span = GROUP * nbr
    root_count = math.sqrt(nbr)
    root_three = math.sqrt(3.0)
    root_fifteen = math.sqrt(15.0)
    root_five = math.sqrt(5.0)

    value_t = jnp.transpose(value_weight_ref[...])
    latent_t = jnp.transpose(latent_weight_ref[...])
    value_rows = stacked(*split(value_t))
    latent_high_t, latent_low_t = split(latent_t)
    latent_both_t = jnp.concatenate([latent_high_t, latent_low_t], axis=0)
    latent_rows = stacked(*split(latent_weight_ref[...]))
    value_high, value_low = split(value_weight_ref[...])
    value_both = jnp.concatenate([value_high, value_low], axis=0)
    basis_t = jnp.transpose(basis_weight_ref[...])
    basis_high_t, basis_low_t = split(basis_t)
    basis_rows = stacked(*split(basis_weight_ref[...]))

    def project(weight, rows):
        weight_t = jnp.transpose(weight)
        high, low = split(rows)
        return folded(
            mm_nt(stacked(*split(weight_t)), jnp.concatenate([high, low], axis=1))
        )

    near_t = project(near_weight_ref[...], feats_ref[...])
    own_t = project(center_weight_ref[...], own_ref[...])
    near_high, near_low = split(near_t)
    own_high, own_low = split(own_t)
    lookup = jnp.concatenate(
        [
            jnp.concatenate([near_high, own_high, basis_high_t, basis_high_t], axis=1),
            jnp.concatenate([near_low, own_low, basis_low_t, jnp.zeros_like(basis_low_t)], axis=1),
        ],
        axis=0,
    )

    cells = frame // sites
    spread = jnp.broadcast_to(coords_ref[...][:, None, :], (cells, sites, 128)).reshape(frame, 128)
    lane = lax.broadcasted_iota(jnp.int32, (frame, 128), 1)
    row = lax.broadcasted_iota(jnp.int32, (frame, 128), 0)
    keep = (lane % sites == row % sites) & (lane < 3 * sites)
    spread = jnp.where(keep, spread, 0.0)
    place_t = jnp.concatenate(
        [jnp.transpose(spread)[: 3 * sites]], axis=0
    )
    place_parts = jnp.concatenate(split3(place_t), axis=0)

    species = species_ref[...]
    scale_slot = jnp.zeros(species.shape, F32)
    shift_slot = jnp.zeros(species.shape, F32)
    for s in range(scale_ref.shape[0]):
        scale_slot = jnp.where(species == s, scale_ref[s], scale_slot)
        shift_slot = jnp.where(species == s, shift_ref[s], shift_slot)
    scale_parts = jnp.concatenate(
        [*split3(scale_slot), jnp.zeros((13, owned), BF16)], axis=0
    )

    kind = lax.broadcasted_iota(jnp.int32, (ORDERS, width), 0)
    path_rows = jnp.where(
        kind == 0,
        path_weight_ref[0:1, :],
        jnp.where(
            kind < 4,
            path_weight_ref[1:2, :],
            jnp.where(kind < 9, path_weight_ref[2:3, :], 0.0),
        ),
    )
    paths_t = jnp.transpose(jnp.concatenate([path_rows] * GROUP, axis=0)) * (1.0 / root_count)
    out_column = jnp.transpose(jnp.broadcast_to(out_weight_ref[...], (width, width)))
    out_column = jnp.concatenate([out_column] * (span // width), axis=1)

    frame_ids = lax.broadcasted_iota(jnp.int32, (frame, span), 0)
    slot_ids = lax.broadcasted_iota(jnp.int32, (owned, span), 0)
    block_row = lax.broadcasted_iota(jnp.int32, (GROUP * ORDERS, span), 0) // ORDERS
    block_lane = lax.broadcasted_iota(jnp.int32, (GROUP * ORDERS, span), 1) // nbr
    block_mask = (block_row == block_lane).astype(F32)
    block_half = block_mask.astype(BF16)
    order = lax.broadcasted_iota(jnp.int32, (radial, span), 0).astype(F32) + 1.0

    totals = jnp.zeros((frame, 2 * ORDERS), F32)
    own_sums = jnp.zeros((4 * ORDERS, owned), F32)
    for g in range(owned // GROUP):
        lanes = slice(g * span, (g + 1) * span)
        near_row = near_row_ref[:, lanes]
        hit = frame_ids == near_row
        pick = jnp.where(hit, 1.0, 0.0)
        from_center = jnp.where(frame_ids == center_row_ref[:, lanes], 1.0, 0.0)
        pick_half = pick.astype(BF16)
        slot_half = jnp.where(slot_ids == center_slot_ref[:, lanes], 1.0, 0.0).astype(BF16)
        live = near_row != frame

        moved = mm(place_parts, (pick - from_center).astype(BF16))
        moved = moved[: 3 * sites] + moved[3 * sites : 6 * sites] + moved[6 * sites :]
        dx = jnp.sum(moved[:sites], axis=0, keepdims=True)
        dy = jnp.sum(moved[sites : 2 * sites], axis=0, keepdims=True)
        dz = jnp.sum(moved[2 * sites :], axis=0, keepdims=True)
        dx = jnp.where(live, dx, 6.0)
        dy = jnp.where(live, dy, 0.0)
        dz = jnp.where(live, dz, 0.0)
        length = jnp.sqrt(dx * dx + dy * dy + dz * dz)
        inverse = 1.0 / length
        ratio = length * (1.0 / CUTOFF)
        inside = live & (ratio < 1.0)
        r2 = ratio * ratio
        r5 = r2 * r2 * ratio
        r6 = r5 * ratio
        weight = jnp.where(inside, 1.0 - r6 * (28.0 - 48.0 * ratio + 21.0 * r2), 0.0)
        slope = jnp.where(inside, -168.0 * r5 * (1.0 - 2.0 * ratio + r2), 0.0)
        sine, cosine = sin_cos_pi(order * ratio)
        basis = (math.sqrt(2.0 / CUTOFF) * inverse) * sine
        basis_slope = (math.sqrt(2.0 / CUTOFF) * inverse) * (
            (math.pi / CUTOFF) * order * cosine - sine * inverse
        )
        ex = dx * inverse
        ey = dy * inverse
        ez = dz * inverse
        angular = jnp.concatenate(
            [
                jnp.ones_like(ex),
                root_three * ex,
                root_three * ey,
                root_three * ez,
                root_fifteen * ex * ey,
                root_fifteen * ey * ez,
                0.5 * root_five * (3.0 * ez * ez - 1.0),
                root_fifteen * ex * ez,
                0.5 * root_fifteen * (ex * ex - ey * ey),
                jnp.zeros((ORDERS - 9, span), F32),
            ],
            axis=0,
        )
        angular_high, angular_low = split(angular)
        block_high = jnp.concatenate([angular_high] * GROUP, axis=0) * block_half
        block_low = jnp.concatenate([angular_low] * GROUP, axis=0) * block_half
        block_pair = jnp.concatenate([block_high, block_low], axis=0)

        basis_high, basis_low = split(basis)
        before = folded(
            mm(lookup, jnp.concatenate([pick_half, slot_half, basis_high, basis_low], axis=0))
        )
        gate = 0.5 * jnp.tanh(0.5 * before) + 0.5
        active = before * gate
        latent = weight * active
        mixed = half_depth(value_rows, latent)
        values = mixed[:width]
        env = mixed[width:]
        env_high, env_low = split(env)
        env_pair = jnp.concatenate([env_high, env_low], axis=0)
        quad = mm_nt(env_pair, block_pair)
        wide = GROUP * ORDERS
        embed = quad[:width, :wide] + quad[:width, wide:] + quad[width:, :wide]
        weighted = embed * paths_t
        weighted_high, weighted_low = split(weighted)
        inner = folded(mm(stacked(weighted_high, weighted_low), block_pair))
        scalars = values * inner
        joined_high, joined_low = split(jnp.concatenate([latent, scalars], axis=0))
        z = full_depth(latent_both_t, latent_high_t, joined_high, joined_low)
        z_gate = 0.5 * jnp.tanh(0.5 * z) + 0.5
        update = z * z_gate
        update_out = update * out_column
        pair_energy = jnp.sum(latent * out_column + weight * update_out, axis=0, keepdims=True)

        scale = mm(scale_parts, slot_half)
        scale = (scale[0:1] + scale[1:2] + scale[2:3]) * (1.0 / root_count)
        pair_energy = pair_energy * (ROOT_HALF * scale)
        pull = ROOT_HALF * scale
        dz_full = (pull * weight) * out_column * (z_gate + update * (1.0 - z_gate))
        spread_back = half_depth(latent_rows, dz_full)
        d_scalars = spread_back[width:]
        d_values = d_scalars * inner
        d_inner = d_scalars * values
        dinner_high, dinner_low = split(d_inner)
        quad = mm_nt(jnp.concatenate([dinner_high, dinner_low], axis=0), block_pair)
        d_weighted = quad[:width, :wide] + quad[:width, wide:] + quad[width:, :wide]
        d_embed = d_weighted * paths_t
        dembed_high, dembed_low = split(d_embed)
        d_env = folded(mm(stacked(dembed_high, dembed_low), block_pair))

        sides = jnp.transpose(jnp.concatenate([weighted, d_embed], axis=0))
        sides_high, sides_low = split(sides)
        d_block = full_depth(
            jnp.concatenate([sides_high, sides_low], axis=0),
            sides_high,
            jnp.concatenate([dinner_high, env_high], axis=0),
            jnp.concatenate([dinner_low, env_low], axis=0),
        )
        d_block = d_block * block_mask
        d_angular = d_block[:ORDERS]
        for k in range(1, GROUP):
            d_angular = d_angular + d_block[k * ORDERS : (k + 1) * ORDERS]

        mixed_high, mixed_low = split(jnp.concatenate([d_values, d_env], axis=0))
        d_latent = (
            full_depth(value_both, value_high, mixed_high, mixed_low)
            + spread_back[:width]
            + pull * out_column
        )
        d_weight = jnp.sum(d_latent * active + pull * update_out, axis=0, keepdims=True)
        d_before = d_latent * weight * (gate + active * (1.0 - gate))
        d_basis = half_depth(basis_rows, d_before)

        d_length = (
            jnp.sum(d_basis * basis_slope, axis=0, keepdims=True)
            + d_weight * slope * (1.0 / CUTOFF)
        )
        a1 = d_angular[1:2]
        a2 = d_angular[2:3]
        a3 = d_angular[3:4]
        a4 = d_angular[4:5]
        a5 = d_angular[5:6]
        a6 = d_angular[6:7]
        a7 = d_angular[7:8]
        a8 = d_angular[8:9]
        ux = root_three * a1 + root_fifteen * (ey * a4 + ez * a7 + ex * a8)
        uy = root_three * a2 + root_fifteen * (ex * a4 + ez * a5 - ey * a8)
        uz = root_three * a3 + root_fifteen * (ey * a5 + ex * a7) + 3.0 * root_five * ez * a6
        along = ex * ux + ey * uy + ez * uz
        radial_part = d_length - along * inverse
        gx = ux * inverse + ex * radial_part
        gy = uy * inverse + ey * radial_part
        gz = uz * inverse + ez * radial_part
        hx = -0.5 * dx
        hy = -0.5 * dy
        hz = -0.5 * dz
        virial = [hx * gx, hx * gy, hx * gz, hy * gx, hy * gy, hy * gz, hz * gx, hz * gy, hz * gz]
        near_terms = jnp.concatenate(
            [-gx, -gy, -gz, *virial, pair_energy, jnp.ones_like(gx), jnp.zeros((2, span), F32)],
            axis=0,
        )
        near_high, near_low = split(near_terms)
        totals = totals + mm_nt(pick_half, jnp.concatenate([near_high, near_low], axis=0))
        own_sums = own_sums + mm_nt(
            jnp.concatenate([*split3(near_terms), jnp.zeros((ORDERS, span), BF16)], axis=0),
            slot_half,
        )

    sums = own_sums[:ORDERS] + own_sums[ORDERS : 2 * ORDERS] + own_sums[2 * ORDERS : 3 * ORDERS]
    energy_ref[...] = sums[12:13] + jnp.where(sums[13:14] > 0.5, shift_slot, 0.0)
    sign_row = lax.broadcasted_iota(jnp.int32, (ORDERS, owned), 0)
    center_terms = jnp.where(sign_row < 3, -sums, sums)
    center_high, center_low = split(center_terms)
    own_rows = jnp.where(
        lax.broadcasted_iota(jnp.int32, (frame, owned), 0) == center_list_ref[...], 1.0, 0.0
    ).astype(BF16)
    totals = totals + mm_nt(own_rows, jnp.concatenate([center_high, center_low], axis=0))
    both = totals[:, :ORDERS] + totals[:, ORDERS:]
    totals_ref[...] = jnp.concatenate([both, jnp.zeros((frame, 128 - ORDERS), F32)], axis=1)


def own_frame_rows(cells_x, cells_y, cells_z, sites):
    slots = np.arange(cells_x * cells_y * cells_z * sites)
    site = slots % sites
    cell = slots // sites
    cell_z = cell % cells_z
    cell_y = cell // cells_z % cells_y
    cell_x = cell // (cells_z * cells_y)
    return (
        ((cell_x + 1) * (cells_y + 2) + cell_y + 1) * (cells_z + 2) + cell_z + 1
    ) * sites + site


def own_to_frame(slots, cells_x, cells_y, cells_z, sites):
    owned = cells_x * cells_y * cells_z * sites
    frame_count = (cells_x + 2) * (cells_y + 2) * (cells_z + 2) * sites
    site = slots % sites
    cell = slots // sites
    cell_z = cell % cells_z
    cell_y = cell // cells_z % cells_y
    cell_x = cell // (cells_z * cells_y)
    frame = (
        ((cell_x + 1) * (cells_y + 2) + cell_y + 1) * (cells_z + 2) + cell_z + 1
    ) * sites + site
    return jnp.where(slots < owned, frame, frame_count)


def frame_terms(
    frame_feat,
    coords,
    features,
    species,
    centers,
    neighbours,
    species_scale,
    species_shift,
    center_weight,
    near_weight,
    basis_weight,
    path_weight,
    value_weight,
    latent_weight,
    out_weight,
):
    cells_x, cells_y, cells_z, sites, width = features.shape
    owned = cells_x * cells_y * cells_z * sites
    frame_count = frame_feat.shape[0]
    pairs = neighbours.size
    nbr = pairs // owned
    near_row = neighbours.reshape(1, pairs)
    rows = own_to_frame(centers, cells_x, cells_y, cells_z, sites)
    center_row = jnp.broadcast_to(rows[:, None], (owned, nbr)).reshape(1, pairs)
    center_slot = jnp.broadcast_to(centers[:, None], (owned, nbr)).reshape(1, pairs)
    own_rows = jnp.asarray(own_frame_rows(cells_x, cells_y, cells_z, sites), jnp.int32)
    vmem = pl.BlockSpec(memory_space=pltpu.VMEM)
    smem = pl.BlockSpec(memory_space=pltpu.SMEM)
    return pl.pallas_call(
        force_kernel,
        out_shape=(
            jax.ShapeDtypeStruct((frame_count, 128), F32),
            jax.ShapeDtypeStruct((1, owned), F32),
        ),
        in_specs=[vmem] * 8 + [smem] * 2 + [vmem] * 7,
        out_specs=(vmem, vmem),
        compiler_params=pltpu.CompilerParams(vmem_limit_bytes=32 * 1024 * 1024),
        name="pair_forces",
    )(
        frame_feat,
        coords,
        features.reshape(owned, width),
        near_row,
        center_row,
        center_slot,
        own_rows.reshape(1, owned),
        species.reshape(1, owned),
        species_scale,
        species_shift,
        center_weight,
        near_weight,
        basis_weight,
        path_weight,
        value_weight,
        latent_weight,
        out_weight.reshape(1, width),
    )


def local(
    positions,
    features,
    species,
    centers,
    neighbours,
    counts,
    species_scale,
    species_shift,
    center_weight,
    near_weight,
    basis_weight,
    path_weight,
    value_weight,
    latent_weight,
    out_weight,
):
    cells_x, cells_y, cells_z, sites, width = features.shape
    owned = cells_x * cells_y * cells_z * sites
    span_x = cells_x + 2
    span_y = cells_y + 2
    span_z = cells_z + 2
    frame_count = span_x * span_y * span_z * sites
    coords = jnp.transpose(positions, (1, 2, 3, 0, 4)).reshape(
        cells_x, cells_y, cells_z, 1, sites * 3
    )
    coords = jnp.pad(coords, ((0, 0), (0, 0), (0, 0), (0, 0), (0, width - sites * 3)))
    payload = jnp.concatenate([features, coords], axis=3)
    framed = padded(payload, (("gy", 1), ("gz", 2), ("gx", 0)), 1)
    frame_feat = framed[:, :, :, :sites, :].reshape(frame_count, width)
    corner = np.repeat(cell_corner(span_x, span_y, span_z), sites, axis=-1)
    corner = np.pad(corner, ((0, 0), (0, 0), (0, 0), (0, width - sites * 3)))
    frame_coords = (framed[:, :, :, sites, :] + jnp.asarray(corner)).reshape(-1, width)
    totals, energy = frame_terms(
        frame_feat,
        frame_coords,
        features,
        species,
        centers,
        neighbours,
        species_scale,
        species_shift,
        center_weight,
        near_weight,
        basis_weight,
        path_weight,
        value_weight,
        latent_weight,
        out_weight,
    )
    grid = totals.reshape(span_x, span_y, span_z, sites, totals.shape[-1])
    for axis, dim, cells in (("gx", 0, cells_x), ("gz", 2, cells_z), ("gy", 1, cells_y)):
        size = lax.axis_size(axis)
        up = [(i, (i + 1) % size) for i in range(size)]
        down = [(j, i) for i, j in up]
        first = lax.slice_in_dim(grid, 0, 1, axis=dim)
        last = lax.slice_in_dim(grid, cells + 1, cells + 2, axis=dim)
        inner = lax.slice_in_dim(grid, 1, cells + 1, axis=dim)
        if size == 2 and cells == 1:
            grid = inner + lax.ppermute(first + last, axis, up)
            continue
        to_last = lax.ppermute(first, axis, down)
        to_first = lax.ppermute(last, axis, up)
        low = lax.slice_in_dim(inner, 0, 1, axis=dim) + to_first
        if cells == 1:
            grid = low + to_last
            continue
        high = lax.slice_in_dim(inner, cells - 1, cells, axis=dim) + to_last
        middle = lax.slice_in_dim(inner, 1, cells - 1, axis=dim)
        grid = jnp.concatenate([low, middle, high], axis=dim)
    forces = jnp.transpose(grid[..., 0:3], (4, 0, 1, 2, 3))
    virial = jnp.transpose(grid[..., 3:12], (4, 0, 1, 2, 3))
    site_energy = energy.reshape(cells_x, cells_y, cells_z, sites)
    return (site_energy, forces, virial)


def solution(mesh):
    placed = (
        P(None, "gx", "gy", "gz", None),
        P("gx", "gy", "gz", None, None),
        P("gx", "gy", "gz", None),
        P(("gx", "gy", "gz")),
        P(("gx", "gy", "gz"), None),
        P(("gx", "gy", "gz")),
        P(),
        P(),
        P(),
        P(),
        P(),
        P(),
        P(),
        P(),
        P(),
    )
    return jax.shard_map(
        local,
        mesh=mesh,
        in_specs=placed,
        out_specs=(
            P("gx", "gy", "gz", None),
            P(None, "gx", "gy", "gz", None),
            P(None, "gx", "gy", "gz", None),
        ),
        check_vma=False,
    )
```

time: 72 us -> 46.9 us (0.65)
  matrix products: 16.1 us -> 0 us
  local copies, waits for them, and re-layouts: 17.1 us -> 6.54 us
  Pallas kernels: 0 us -> 10.1 us
  other arithmetic: 9.15 us -> 0.82 us
  waiting for transfers between devices: 10.5 us -> 12.1 us
  between operations: 1.9 us -> 0.86 us
  starting transfers between devices: 17 us -> 16 us
    dot_general x15 -> x0, matrix products: 16.1 us -> none  [the longest x2 4.16 us: center_energy(): radial = jnp.einsum('knb,bc->knc', basis, basis_weight, precision=EXACT_DOT)]
    pallas_call x0 -> x1, Pallas kernels: none -> 10.1 us  [frame_terms(): pl.pallas_call(force_kernel, out_shape=(jax.ShapeDtypeStruct((frame_count...]
    gather x7 -> x0, local copies, waits for them, and re-layouts: 8 us -> none  [the longest x2 3.08 us: visit(): frame_position[neighbours] - frame_position[centre_rows][:, None, :]]
    scatter-add x5 -> x0, other arithmetic: 7.57 us -> none  [the longest x1 6.06 us: pair_return(): return totals.at[near_rows.reshape(-1)].add(near_part)]
    ppermute x0 -> x5, starting transfers between devices: none -> 7.08 us  [the longest x2 4.95 us: local(): to_last = lax.ppermute(first, axis, down)]
    ppermute x6 -> x2, starting transfers between devices: 10.1 us -> 3.82 us  [padded(): after = lax.ppermute(leading, axis, down)]
    ppermute x0 -> x5, waiting for transfers between devices: none -> 4.48 us  [the longest x2 3.77 us: local(): to_first = lax.ppermute(last, axis, up)]
    ppermute x6 -> x2, waiting for transfers between devices: 5.39 us -> 2.86 us  [padded(): after = lax.ppermute(leading, axis, down)]
  transfers between devices with their start and end apart: 12 -> 10, of which waited for: 9 -> 8; matrix products, arithmetic and copies ran while one was open for 5% -> 5% of each run, Pallas kernels for 0% -> 0%
where the time goes in v1:
time: 46.9 us; the launch traced here: 46.5 us
  starting transfers between devices  16 us (34%)
  waiting for transfers between devices  12.1 us (26%)
  Pallas kernels  10.1 us (22%)
  local copies, waits for them, and re-layouts  6.54 us (14%)
  between operations  0.86 us (2%)
  other arithmetic  0.82 us (2%)
    pallas_call x1, Pallas kernels, frame_terms(): pl.pallas_call(force_kernel, out_shape=(jax.ShapeDtypeStruct((frame_count...  10.1 us
    ppermute x3, starting transfers between devices, padded(): before = lax.ppermute(last, axis, up)  5.13 us
    ppermute x2, starting transfers between devices, local(): to_last = lax.ppermute(first, axis, down)  4.95 us
    ppermute x3, waiting for transfers between devices, padded(): before = lax.ppermute(last, axis, up)  4.81 us
    ppermute x2, starting transfers between devices, padded(): after = lax.ppermute(leading, axis, down)  3.82 us
    ppermute x2, waiting for transfers between devices, local(): to_first = lax.ppermute(last, axis, up)  3.77 us
    unnamed x31, local copies, waits for them, and re-layouts  3.37 us
    ppermute x2, waiting for transfers between devices, padded(): after = lax.ppermute(leading, axis, down)  2.86 us
  transfers between devices with their start and end apart: 10, of which 8 were waited for; matrix products, arithmetic and copies ran while one was open for 5% of the time, Pallas kernels for 0%

profile of v1, /device:TPU:0, one launch (start us, length us, event | category | flops | bytes accessed | tf_op | source)
XLA Modules:
  0.0 46.5 jit_solution(8380161119930388918)
XLA Ops:
  0.6 0.7 %copy.23 = f32[2,1,2,3,8]{4,3,2,0,1:T(4,128)S(1)} copy(f32[2,1,2,3,8]{4,2,1,0,3:T(2,128)} %bitcast.29) | data formatting | bytes 768 | tf_op jit(solution)/shard_map/transpose | solution.py:493
  1.3 0.1 reshape.47
  1.4 3.0 %collective-permute-start = (f32[2,1,2,9,128]{4,3,2,1,0:T(8,128)S(1)}, f32[2,1,2,9,128]{4,3,2,1,0:T(8,128)S(1)}, u32[]{:S(2)}, u32[]{:S(2)}) collective-permute-start(f32[2,1,2,9,128]{4,3,2,1,0:T(8,128)S(1)} %pad_maximum_fusion.3), channel_id=1, source_target_pairs={{0,4},{4,0},{1,5},{5,1},{2,6},{6,2},{3,7},{7,3},{8,12},{12,8},{9,1... | collective-permute-start | bytes 55304 | tf_op jit(solution)/shard_map/ppermute | solution.py:28
  4.5 1.9 %collective-permute-done = f32[2,1,2,9,128]{4,3,2,1,0:T(8,128)S(1)} collective-permute-done((f32[2,1,2,9,128]{4,3,2,1,0:T(8,128)S(1)}, f32[2,1,2,9,128]{4,3,2,1,0:T(8,128)S(1)}, u32[]{:S(2)}, u32[]{:S(2)}) %collective-permute-start) | collective-permute-done | bytes 18464 | tf_op jit(solution)/shard_map/ppermute | solution.py:28
  6.4 1.7 %collective-permute-start.2 = (f32[2,3,1,9,128]{4,3,2,1,0:T(8,128)S(1)}, f32[2,3,1,9,128]{4,3,2,1,0:T(8,128)S(1)}, u32[]{:S(2)}, u32[]{:S(2)}) collective-permute-start(f32[2,3,1,9,128]{4,3,2,1,0:T(8,128)S(1)} %get-tuple-element.24), channel_id=1, source_target_pairs={{1,0},{2,1},{3,2},{0,3},{5,4},{6,5},{7,6},{4,7},{9,8},{10,9},{11,1... | collective-permute-start | bytes 82952 | tf_op jit(solution)/shard_map/ppermute | solution.py:32
  8.2 1.8 %collective-permute-done.1 = f32[2,3,1,9,128]{4,3,2,1,0:T(8,128)S(1)} collective-permute-done((f32[2,3,1,9,128]{4,3,2,1,0:T(8,128)S(1)}, f32[2,3,1,9,128]{4,3,2,1,0:T(8,128)S(1)}, u32[]{:S(2)}, u32[]{:S(2)}) %collective-permute-start.1) | collective-permute-done | bytes 27680 | tf_op jit(solution)/shard_map/ppermute | solution.py:28
  9.9 0.1 collective-permute-done.2
  10.1 2.1 %collective-permute-start.3 = (f32[1,3,4,9,128]{4,3,2,1,0:T(8,128)S(1)}, f32[1,3,4,9,128]{4,3,2,1,0:T(8,128)S(1)}, u32[]{:S(2)}, u32[]{:S(2)}) collective-permute-start(f32[1,3,4,9,128]{4,3,2,1,0:T(8,128)S(1)} %get-tuple-element.17), channel_id=1, source_target_pairs={{0,8},{8,16},{16,24},{24,0},{1,9},{9,17},{17,25},{25,1},{2,10},{10... | collective-permute-start | bytes 165896 | tf_op jit(solution)/shard_map/ppermute | solution.py:28
  12.2 2.1 %collective-permute-start.4 = (f32[1,3,4,9,128]{4,3,2,1,0:T(8,128)S(1)}, f32[1,3,4,9,128]{4,3,2,1,0:T(8,128)S(1)}, u32[]{:S(2)}, u32[]{:S(2)}) collective-permute-start(f32[1,3,4,9,128]{4,3,2,1,0:T(8,128)S(1)} %get-tuple-element.18), channel_id=1, source_target_pairs={{8,0},{16,8},{24,16},{0,24},{9,1},{17,9},{25,17},{1,25},{10,2},{18... | collective-permute-start | bytes 165896 | tf_op jit(solution)/shard_map/ppermute | solution.py:32
  14.4 0.1 reshape.52.center_row_ref
  14.5 0.1 reshape.53.center_slot_ref
  14.6 0.6 %copy-done.12 = s32[32,32]{1,0:T(8,128)S(1)} copy-done((s32[32,32]{1,0:T(8,128)S(1)}, s32[32,32]{1,0:T(8,128)}, u32[]{:S(2)}) %copy-start.12) | copy-done | bytes 4120
  15.2 0.6 %copy-done.13 = s32[2,1,2,8]{3,2,1,0:T(2,128)S(1)} copy-done((s32[2,1,2,8]{3,2,1,0:T(2,128)S(1)}, s32[2,1,2,8]{3,2,1,0:T(2,128)}, u32[]{:S(2)}) %copy-start.13) | copy-done | bytes 152
  15.8 0.1 reshape.55.species_ref
  15.9 1.1 %collective-permute-done.3 = f32[1,3,4,9,128]{4,3,2,1,0:T(8,128)S(1)} collective-permute-done((f32[1,3,4,9,128]{4,3,2,1,0:T(8,128)S(1)}, f32[1,3,4,9,128]{4,3,2,1,0:T(8,128)S(1)}, u32[]{:S(2)}, u32[]{:S(2)}) %collective-permute-start.3) | collective-permute-done | bytes 55328 | tf_op jit(solution)/shard_map/ppermute | solution.py:28
  17.1 2.8 %collective-permute-done.4 = f32[1,3,4,9,128]{4,3,2,1,0:T(8,128)S(1)} collective-permute-done((f32[1,3,4,9,128]{4,3,2,1,0:T(8,128)S(1)}, f32[1,3,4,9,128]{4,3,2,1,0:T(8,128)S(1)}, u32[]{:S(2)}, u32[]{:S(2)}) %collective-permute-start.4) | collective-permute-done | bytes 55328 | tf_op jit(solution)/shard_map/ppermute | solution.py:32
  19.9 0.7 %copy-done.11 = f32[4,3,4,1,128]{4,3,2,1,0:T(1,128)S(1)} copy-done((f32[4,3,4,1,128]{4,3,2,1,0:T(1,128)S(1)}, f32[4,3,4,1,128]{4,3,2,1,0:T(1,128)}, u32[]{:S(2)}) %copy-start.11) | copy-done | bytes 24600
  20.7 0.1 copy-done.1
  20.9 0.6 %copy-done.3 = f32[128,128]{1,0:T(8,128)S(1)} copy-done((f32[128,128]{1,0:T(8,128)S(1)}, f32[128,128]{1,0:T(8,128)}, u32[]{:S(2)}) %copy-start.3) | copy-done | bytes 65560
  21.5 10.1 %pair_forces.1 = (f32[384,128]{1,0:T(8,128)S(1)}, f32[1,32]{1,0:T(1,128)S(1)}) custom-call(f32[384,128]{1,0:T(8,128)S(1)} %bitcast.17, f32[48,128]{1,0:T(8,128)S(1)} %bitcast.19, f32[32,128]{1,0:T(8,128)S(1)} %bitcast.18, s32[1,1024]{1,0:T(1,128)S(1)} %reshape.51.near_row_ref, s32[1,1024]{1,0:T(1,128)S(1)} %reshape.52.center_row_ref, ...), custom_call_target="tpu_custom_call" | custom-call | tf_op jit(solution)/shard_map/pair_forces/pallas_call | solution.py:439
  31.6 0.7 %collective-permute-start.5 = (f32[1,3,4,8,128]{4,3,2,1,0:T(8,128)S(1)}, f32[1,3,4,8,128]{4,3,2,1,0:T(8,128)S(1)}, u32[]{:S(2)}, u32[]{:S(2)}) collective-permute-start(f32[1,3,4,8,128]{4,3,2,1,0:T(8,128)S(1)} %bitcast.28), channel_id=1, source_target_pairs={{0,8},{8,16},{16,24},{24,0},{1,9},{9,17},{17,25},{25,1},{2,10},{10... | collective-permute-start | bytes 147464 | tf_op jit(solution)/shard_map/ppermute | solution.py:532
  32.3 3.2 %collective-permute-start.6 = (f32[1,3,4,8,128]{4,3,2,1,0:T(8,128)S(1)}, f32[1,3,4,8,128]{4,3,2,1,0:T(8,128)S(1)}, u32[]{:S(2)}, u32[]{:S(2)}) collective-permute-start(f32[1,3,4,8,128]{4,3,2,1,0:T(8,128)S(1)} %bitcast.27), channel_id=1, source_target_pairs={{8,0},{16,8},{24,16},{0,24},{9,1},{17,9},{25,17},{1,25},{10,2},{18... | collective-permute-start | bytes 147464 | tf_op jit(solution)/shard_map/ppermute | solution.py:531
  35.5 2.3 %collective-permute-done.5 = f32[1,3,4,8,128]{4,3,2,1,0:T(8,128)S(1)} collective-permute-done((f32[1,3,4,8,128]{4,3,2,1,0:T(8,128)S(1)}, f32[1,3,4,8,128]{4,3,2,1,0:T(8,128)S(1)}, u32[]{:S(2)}, u32[]{:S(2)}) %collective-permute-start.5) | collective-permute-done | bytes 49184 | tf_op jit(solution)/shard_map/ppermute | solution.py:532
  37.9 1.7 %collective-permute-start.8 = (f32[2,3,1,8,128]{4,3,2,1,0:T(8,128)S(1)}, f32[2,3,1,8,128]{4,3,2,1,0:T(8,128)S(1)}, u32[]{:S(2)}, u32[]{:S(2)}) collective-permute-start(f32[2,3,1,8,128]{4,3,2,1,0:T(8,128)S(1)} %get-tuple-element.21), channel_id=1, source_target_pairs={{1,0},{2,1},{3,2},{0,3},{5,4},{6,5},{7,6},{4,7},{9,8},{10,9},{11,1... | collective-permute-start | bytes 73736 | tf_op jit(solution)/shard_map/ppermute | solution.py:531
  39.6 1.5 %collective-permute-done.7 = f32[2,3,1,8,128]{4,3,2,1,0:T(8,128)S(1)} collective-permute-done((f32[2,3,1,8,128]{4,3,2,1,0:T(8,128)S(1)}, f32[2,3,1,8,128]{4,3,2,1,0:T(8,128)S(1)}, u32[]{:S(2)}, u32[]{:S(2)}) %collective-permute-start.7) | collective-permute-done | bytes 24608 | tf_op jit(solution)/shard_map/ppermute | solution.py:532
  41.2 1.4 %collective-permute-start.9 = (f32[2,1,2,8,128]{4,3,2,1,0:T(8,128)S(1)}, f32[2,1,2,8,128]{4,3,2,1,0:T(8,128)S(1)}, u32[]{:S(2)}, u32[]{:S(2)}) collective-permute-start(f32[2,1,2,8,128]{4,3,2,1,0:T(8,128)S(1)} %fusion.6), channel_id=1, source_target_pairs={{0,4},{4,0},{1,5},{5,1},{2,6},{6,2},{3,7},{7,3},{8,12},{12,8},{9,1... | collective-permute-start | bytes 49160 | tf_op jit(solution)/shard_map/ppermute | solution.py:529
  42.6 0.5 %broadcast.36 = f32[]{:T(128)} broadcast(f32[]{:T(128)} %constant.129), dimensions={} | broadcast | bytes 8 | tf_op jit(solution)/shard_map/pair_forces/pallas_call | solution.py:439
  43.1 0.7 %reduce.3 = f32[32]{0:T(128)S(1)} reduce(f32[1,32]{1,0:T(1,128)S(1)} %get-tuple-element.5, f32[]{:T(128)} %broadcast.36), dimensions={0}, to_apply=%get-tuple-element.5.reduce_sub_computation.3 | reduce | bytes 260 | tf_op jit(solution)/shard_map/pair_forces/pallas_call | solution.py:439
  43.8 0.7 %reshape.57 = f32[2,1,2,8]{3,2,0,1:T(2,128)} reshape(f32[32]{0:T(128)S(1)} %reduce.3) | data formatting | bytes 256 | tf_op jit(solution)/shard_map/reshape | solution.py:542
  44.4 0.7 %collective-permute-done.9 = f32[2,1,2,8,128]{4,3,2,1,0:T(8,128)S(1)} collective-permute-done((f32[2,1,2,8,128]{4,3,2,1,0:T(8,128)S(1)}, f32[2,1,2,8,128]{4,3,2,1,0:T(8,128)S(1)}, u32[]{:S(2)}, u32[]{:S(2)}) %collective-permute-start.9) | collective-permute-done | bytes 16416 | tf_op jit(solution)/shard_map/ppermute | solution.py:529
  45.1 0.7 %slice_bitcast_fusion = f32[9,2,1,2,8]{0,4,3,2,1:T(8,128)} fusion(f32[2,1,2,8,128]{4,3,2,1,0:T(8,128)S(1)} %fusion.8), kind=kLoop, calls=%fused_computation.25 | loop fusion | bytes 2304 | tf_op jit(solution)/shard_map/transpose | solution.py:541
  45.8 0.7 %copy.26 = f32[3,2,1,2,8]{4,3,2,1,0:T(2,128)} copy(f32[3,2,1,2,8]{0,4,3,2,1:T(8,128)S(1)} %slice_bitcast_fusion.1) | data formatting | bytes 768
  (50 shorter events, 0.7 us)
Async XLA Ops:
  0.6 0.8 %copy-start = (f32[2,1,2,8,128]{4,3,2,1,0:T(8,128)S(1)}, f32[2,1,2,8,128]{4,3,2,1,0:T(8,128)}, u32[]{:S(2)}) copy-start(f32[2,1,2,8,128]{4,3,2,1,0:T(8,128)} %param.18) | copy-start | bytes 49156
  1.4 4.9 %collective-permute-start = (f32[2,1,2,9,128]{4,3,2,1,0:T(8,128)S(1)}, f32[2,1,2,9,128]{4,3,2,1,0:T(8,128)S(1)}, u32[]{:S(2)}, u32[]{:S(2)}) collective-permute-start(f32[2,1,2,9,128]{4,3,2,1,0:T(8,128)S(1)} %pad_maximum_fusion.3), channel_id=1, source_target_pairs={{0,4},{4,0},{1,5},{5,1},{2,6},{6,2},{3,7},{7,3},{8,12},{12,8},{9,1... | collective-permute-start | bytes 55304 | tf_op jit(solution)/shard_map/ppermute | solution.py:28
  6.4 3.6 %collective-permute-start.1 = (f32[2,3,1,9,128]{4,3,2,1,0:T(8,128)S(1)}, f32[2,3,1,9,128]{4,3,2,1,0:T(8,128)S(1)}, u32[]{:S(2)}, u32[]{:S(2)}) collective-permute-start(f32[2,3,1,9,128]{4,3,2,1,0:T(8,128)S(1)} %get-tuple-element.23), channel_id=1, source_target_pairs={{0,1},{1,2},{2,3},{3,0},{4,5},{5,6},{6,7},{7,4},{8,9},{9,10},{10,1... | collective-permute-start | bytes 82952 | tf_op jit(solution)/shard_map/ppermute | solution.py:28
  6.4 3.6 %collective-permute-start.2 = (f32[2,3,1,9,128]{4,3,2,1,0:T(8,128)S(1)}, f32[2,3,1,9,128]{4,3,2,1,0:T(8,128)S(1)}, u32[]{:S(2)}, u32[]{:S(2)}) collective-permute-start(f32[2,3,1,9,128]{4,3,2,1,0:T(8,128)S(1)} %get-tuple-element.24), channel_id=1, source_target_pairs={{1,0},{2,1},{3,2},{0,3},{5,4},{6,5},{7,6},{4,7},{9,8},{10,9},{11,1... | collective-permute-start | bytes 82952 | tf_op jit(solution)/shard_map/ppermute | solution.py:32
  10.1 4.2 %copy-start.14 = (s32[32]{0:T(128)S(1)}, s32[32]{0:T(128)}, u32[]{:S(2)}) copy-start(s32[32]{0:T(128)} %param.20) | copy-start | bytes 388
  10.1 7.0 %collective-permute-start.3 = (f32[1,3,4,9,128]{4,3,2,1,0:T(8,128)S(1)}, f32[1,3,4,9,128]{4,3,2,1,0:T(8,128)S(1)}, u32[]{:S(2)}, u32[]{:S(2)}) collective-permute-start(f32[1,3,4,9,128]{4,3,2,1,0:T(8,128)S(1)} %get-tuple-element.17), channel_id=1, source_target_pairs={{0,8},{8,16},{16,24},{24,0},{1,9},{9,17},{17,25},{25,1},{2,10},{10... | collective-permute-start | bytes 165896 | tf_op jit(solution)/shard_map/ppermute | solution.py:28
  12.2 7.7 %collective-permute-start.4 = (f32[1,3,4,9,128]{4,3,2,1,0:T(8,128)S(1)}, f32[1,3,4,9,128]{4,3,2,1,0:T(8,128)S(1)}, u32[]{:S(2)}, u32[]{:S(2)}) collective-permute-start(f32[1,3,4,9,128]{4,3,2,1,0:T(8,128)S(1)} %get-tuple-element.18), channel_id=1, source_target_pairs={{8,0},{16,8},{24,16},{0,24},{9,1},{17,9},{25,17},{1,25},{10,2},{18... | collective-permute-start | bytes 165896 | tf_op jit(solution)/shard_map/ppermute | solution.py:32
  14.4 0.7 %copy-start.12 = (s32[32,32]{1,0:T(8,128)S(1)}, s32[32,32]{1,0:T(8,128)}, u32[]{:S(2)}) copy-start(s32[32,32]{1,0:T(8,128)} %param.21) | copy-start | bytes 12292
  15.2 0.7 %copy-start.13 = (s32[2,1,2,8]{3,2,1,0:T(2,128)S(1)}, s32[2,1,2,8]{3,2,1,0:T(2,128)}, u32[]{:S(2)}) copy-start(s32[2,1,2,8]{3,2,1,0:T(2,128)} %param.19) | copy-start | bytes 388
  19.9 0.7 %copy-start.11 = (f32[4,3,4,1,128]{4,3,2,1,0:T(1,128)S(1)}, f32[4,3,4,1,128]{4,3,2,1,0:T(1,128)}, u32[]{:S(2)}) copy-start(f32[4,3,4,1,128]{4,3,2,1,0:T(1,128)} %constant.82) | copy-start | bytes 73732
  19.9 0.9 %copy-start.1 = (f32[128,256]{1,0:T(8,128)S(1)}, f32[128,256]{1,0:T(8,128)}, u32[]{:S(2)}) copy-start(f32[128,256]{1,0:T(8,128)} %value_weight_ref.1) | copy-start | bytes 393220
  19.9 1.0 %copy-start.2 = (f32[256,128]{1,0:T(8,128)S(1)}, f32[256,128]{1,0:T(8,128)}, u32[]{:S(2)}) copy-start(f32[256,128]{1,0:T(8,128)} %latent_weight_ref.1) | copy-start | bytes 393220
  19.9 1.0 %copy-start.4 = (f32[128,128]{1,0:T(8,128)S(1)}, f32[128,128]{1,0:T(8,128)}, u32[]{:S(2)}) copy-start(f32[128,128]{1,0:T(8,128)} %near_weight_ref.1) | copy-start | bytes 196612
  20.6 0.9 %copy-start.3 = (f32[128,128]{1,0:T(8,128)S(1)}, f32[128,128]{1,0:T(8,128)}, u32[]{:S(2)}) copy-start(f32[128,128]{1,0:T(8,128)} %center_weight_ref.1) | copy-start | bytes 196612
  20.6 0.9 %copy-start.10 = (s32[1,32]{1,0:T(1,128)S(1)}, s32[1,32]{1,0:T(1,128)}, u32[]{:S(2)}) copy-start(s32[1,32]{1,0:T(1,128)} %constant.81.center_list_ref) | copy-start | bytes 388
  20.6 0.8 %copy-start.5 = (f32[8,128]{1,0:T(8,128)S(1)}, f32[8,128]{1,0:T(8,128)}, u32[]{:S(2)}) copy-start(f32[8,128]{1,0:T(8,128)} %basis_weight_ref.1) | copy-start | bytes 12292
  20.7 0.8 %copy-start.6 = (f32[3,128]{1,0:T(4,128)S(1)}, f32[3,128]{1,0:T(4,128)}, u32[]{:S(2)}) copy-start(f32[3,128]{1,0:T(4,128)} %path_weight_ref.1) | copy-start | bytes 4612
  20.7 0.8 %copy-start.7 = (f32[5]{0:T(128)S(1)}, f32[5]{0:T(128)}, u32[]{:S(2)}) copy-start(f32[5]{0:T(128)} %scale_ref.1) | copy-start | bytes 64
  20.7 0.8 %copy-start.8 = (f32[5]{0:T(128)S(1)}, f32[5]{0:T(128)}, u32[]{:S(2)}) copy-start(f32[5]{0:T(128)} %shift_ref.1) | copy-start | bytes 64
  20.7 0.8 %copy-start.9 = (f32[128]{0:T(128)S(1)}, f32[128]{0:T(128)}, u32[]{:S(2)}) copy-start(f32[128]{0:T(128)} %param.30) | copy-start | bytes 1540
  31.6 6.1 %collective-permute-start.5 = (f32[1,3,4,8,128]{4,3,2,1,0:T(8,128)S(1)}, f32[1,3,4,8,128]{4,3,2,1,0:T(8,128)S(1)}, u32[]{:S(2)}, u32[]{:S(2)}) collective-permute-start(f32[1,3,4,8,128]{4,3,2,1,0:T(8,128)S(1)} %bitcast.28), channel_id=1, source_target_pairs={{0,8},{8,16},{16,24},{24,0},{1,9},{9,17},{17,25},{25,1},{2,10},{10... | collective-permute-start | bytes 147464 | tf_op jit(solution)/shard_map/ppermute | solution.py:532
  32.3 5.5 %collective-permute-start.6 = (f32[1,3,4,8,128]{4,3,2,1,0:T(8,128)S(1)}, f32[1,3,4,8,128]{4,3,2,1,0:T(8,128)S(1)}, u32[]{:S(2)}, u32[]{:S(2)}) collective-permute-start(f32[1,3,4,8,128]{4,3,2,1,0:T(8,128)S(1)} %bitcast.27), channel_id=1, source_target_pairs={{8,0},{16,8},{24,16},{0,24},{9,1},{17,9},{25,17},{1,25},{10,2},{18... | collective-permute-start | bytes 147464 | tf_op jit(solution)/shard_map/ppermute | solution.py:531
  37.8 3.3 %collective-permute-start.7 = (f32[2,3,1,8,128]{4,3,2,1,0:T(8,128)S(1)}, f32[2,3,1,8,128]{4,3,2,1,0:T(8,128)S(1)}, u32[]{:S(2)}, u32[]{:S(2)}) collective-permute-start(f32[2,3,1,8,128]{4,3,2,1,0:T(8,128)S(1)} %get-tuple-element.22), channel_id=1, source_target_pairs={{0,1},{1,2},{2,3},{3,0},{4,5},{5,6},{6,7},{7,4},{8,9},{9,10},{10,1... | collective-permute-start | bytes 73736 | tf_op jit(solution)/shard_map/ppermute | solution.py:532
  37.9 3.3 %collective-permute-start.8 = (f32[2,3,1,8,128]{4,3,2,1,0:T(8,128)S(1)}, f32[2,3,1,8,128]{4,3,2,1,0:T(8,128)S(1)}, u32[]{:S(2)}, u32[]{:S(2)}) collective-permute-start(f32[2,3,1,8,128]{4,3,2,1,0:T(8,128)S(1)} %get-tuple-element.21), channel_id=1, source_target_pairs={{1,0},{2,1},{3,2},{0,3},{5,4},{6,5},{7,6},{4,7},{9,8},{10,9},{11,1... | collective-permute-start | bytes 73736 | tf_op jit(solution)/shard_map/ppermute | solution.py:531
  41.2 3.9 %collective-permute-start.9 = (f32[2,1,2,8,128]{4,3,2,1,0:T(8,128)S(1)}, f32[2,1,2,8,128]{4,3,2,1,0:T(8,128)S(1)}, u32[]{:S(2)}, u32[]{:S(2)}) collective-permute-start(f32[2,1,2,8,128]{4,3,2,1,0:T(8,128)S(1)} %fusion.6), channel_id=1, source_target_pairs={{0,4},{4,0},{1,5},{5,1},{2,6},{6,2},{3,7},{7,3},{8,12},{12,8},{9,1... | collective-permute-start | bytes 49160 | tf_op jit(solution)/shard_map/ppermute | solution.py:529

commit v2 on v1

v2 whole, which is shorter than its diff:
```python
import functools
import math

import jax
import jax.numpy as jnp
import numpy as np
from jax import lax
from jax.experimental import pallas as pl
from jax.experimental.pallas import tpu as pltpu
from jax.sharding import PartitionSpec as P

EXACT_DOT = lax.Precision.HIGHEST
CUTOFF = 5.0
CELL_SIDE = 4.6
ROOT_HALF = 0.7071067811865476
GROUP = 8
ORDERS = 16
F32 = jnp.float32
BF16 = jnp.bfloat16


def split(value):
    high = value.astype(BF16)
    low = (value - high.astype(F32)).astype(BF16)
    return high, low


def split3(value):
    high = value.astype(BF16)
    rest = value - high.astype(F32)
    middle = rest.astype(BF16)
    low = (rest - middle.astype(F32)).astype(BF16)
    return high, middle, low


def mm(a, b):
    return lax.dot_general(a, b, (((1,), (0,)), ((), ())), preferred_element_type=F32)


def mm_nt(a, b):
    return lax.dot_general(a, b, (((1,), (1,)), ((), ())), preferred_element_type=F32)


def stacked(high, low):
    top = jnp.concatenate([high, high], axis=1)
    bottom = jnp.concatenate([low, jnp.zeros_like(low)], axis=1)
    return jnp.concatenate([top, bottom], axis=0)


def folded(product):
    half = product.shape[0] // 2
    return product[:half] + product[half:]


def half_depth(weights, value):
    return folded(mm(weights, jnp.concatenate(split(value), axis=0)))


def full_depth(both, high, value_high, value_low):
    return folded(mm(both, value_high)) + mm(high, value_low)


def sin_cos_pi(turns):
    near = turns - 2.0 * jnp.round(turns * 0.5)
    quarter = jnp.round(near * 2.0)
    v = (near - 0.5 * quarter) * math.pi
    v2 = v * v
    s = v * (
        1.0
        + v2
        * (-1.0 / 6 + v2 * (1.0 / 120 + v2 * (-1.0 / 5040 + v2 * (1.0 / 362880 - v2 / 39916800))))
    )
    c = 1.0 + v2 * (
        -0.5
        + v2
        * (1.0 / 24 + v2 * (-1.0 / 720 + v2 * (1.0 / 40320 + v2 * (-1.0 / 3628800 + v2 / 479001600))))
    )
    odd = jnp.abs(quarter) == 1.0
    sine = jnp.where(odd, quarter * c, jnp.where(quarter == 0.0, s, -s))
    cosine = jnp.where(odd, -quarter * s, jnp.where(quarter == 0.0, c, -c))
    return sine, cosine


def center_rows(slots, cells, sites):
    cells_x, cells_y, cells_z = cells
    owned = cells_x * cells_y * cells_z * sites
    frame_count = (cells_x + 2) * (cells_y + 2) * (cells_z + 2) * sites
    site = slots % sites
    cell = slots // sites
    cell_z = cell % cells_z
    cell_y = cell // cells_z % cells_y
    cell_x = cell // (cells_z * cells_y)
    frame = (
        ((cell_x + 1) * (cells_y + 2) + cell_y + 1) * (cells_z + 2) + cell_z + 1
    ) * sites + site
    return jnp.where(slots < owned, frame, frame_count)


def target_rows(rows, cells, sites, kinds):
    spans = [count + 2 for count in cells]
    site = rows % sites
    cell = rows // sites
    places = (cell // (spans[1] * spans[2]), cell // spans[2] % spans[1], cell % spans[2])
    block = jnp.zeros_like(rows)
    slot = jnp.zeros_like(rows)
    for place, count, kind in zip(places, cells, kinds):
        above = place > count
        below = place < 1
        step = jnp.where(below, kind - 1, jnp.where(above, 1, 0))
        inside = jnp.where(below, count - 1, jnp.where(above, 0, place - 1))
        block = block * kind + step
        slot = slot * count + inside
    owned = cells[0] * cells[1] * cells[2] * sites
    target = block * owned + slot * sites + site
    return jnp.where(rows < spans[0] * spans[1] * spans[2] * sites, target, -1)


def force_kernel(
    cells,
    axes,
    kinds,
    gathered_ref,
    place_ref,
    own_ref,
    near_row_ref,
    target_row_ref,
    center_row_ref,
    center_slot_ref,
    species_ref,
    scale_ref,
    shift_ref,
    center_weight_ref,
    near_weight_ref,
    basis_weight_ref,
    path_weight_ref,
    value_weight_ref,
    latent_weight_ref,
    out_weight_ref,
    parts_ref,
    energy_ref,
    feats_ref,
    coords_ref,
):
    frame, width = feats_ref.shape
    owned = own_ref.shape[0]
    pairs = near_row_ref.shape[1]
    nbr = pairs // owned
    radial = basis_weight_ref.shape[0]
    spans = [count + 2 for count in cells]
    sites = frame // (spans[0] * spans[1] * spans[2])
    stride = gathered_ref.shape[0] // (axes[0] * axes[1] * axes[2])
    span = GROUP * nbr
    groups = owned // GROUP
    wide = GROUP * ORDERS
    root_count = math.sqrt(nbr)
    root_three = math.sqrt(3.0)
    root_fifteen = math.sqrt(15.0)
    root_five = math.sqrt(5.0)
    here = [place_ref[i] for i in range(3)]

    def shifted(axis, step):
        moved = here[axis] + step
        size = axes[axis]
        moved = jnp.where(moved >= size, moved - size, moved)
        return jnp.where(moved < 0, moved + size, moved)

    steps = [[shifted(axis, step) for step in (-1, 0, 1)] for axis in range(3)]

    def device(x, y, z):
        return (steps[0][x + 1] * axes[1] + steps[1][y + 1]) * axes[2] + steps[2][z + 1]

    tile_lane = lax.broadcasted_iota(jnp.int32, (sites, 128), 1)
    tile_row = lax.broadcasted_iota(jnp.int32, (sites, 128), 0)
    keep = (tile_lane % sites == tile_row) & (tile_lane < 3 * sites)
    component = tile_lane // sites
    for cell in range(spans[0] * spans[1] * spans[2]):
        place = (cell // (spans[1] * spans[2]), cell // spans[2] % spans[1], cell % spans[2])
        step = [(p > c) * 1 - (p < 1) * 1 for p, c in zip(place, cells)]
        inside = [(p - 1) % c for p, c in zip(place, cells)]
        local_cell = (inside[0] * cells[1] + inside[1]) * cells[2] + inside[2]
        base = device(*step) * stride
        start = pl.multiple_of(base + local_cell * sites, 8)
        feats_ref[cell * sites : (cell + 1) * sites, :] = gathered_ref[pl.ds(start, sites), :]
        row = gathered_ref[pl.ds(base + (owned + local_cell), 1), :]
        corner = [np.float32(p) * np.float32(CELL_SIDE) for p in place]
        offset = jnp.where(
            component == 0, corner[0], jnp.where(component == 1, corner[1], corner[2])
        )
        coords_ref[cell * sites : (cell + 1) * sites, :] = jnp.where(keep, row + offset, 0.0)

    value_t = jnp.transpose(value_weight_ref[...])
    latent_t = jnp.transpose(latent_weight_ref[...])
    value_rows = stacked(*split(value_t))
    latent_high_t, latent_low_t = split(latent_t)
    latent_both_t = jnp.concatenate([latent_high_t, latent_low_t], axis=0)
    latent_rows = stacked(*split(latent_weight_ref[...]))
    value_high, value_low = split(value_weight_ref[...])
    value_both = jnp.concatenate([value_high, value_low], axis=0)
    basis_t = jnp.transpose(basis_weight_ref[...])
    basis_high_t, basis_low_t = split(basis_t)
    basis_rows = stacked(*split(basis_weight_ref[...]))

    def project(weight, rows):
        high, low = split(rows)
        return folded(
            mm_nt(stacked(*split(jnp.transpose(weight))), jnp.concatenate([high, low], axis=1))
        )

    near_t = project(near_weight_ref[...], feats_ref[...])
    own_t = project(center_weight_ref[...], own_ref[...])
    near_high, near_low = split(near_t)
    own_high, own_low = split(own_t)
    lookup = jnp.concatenate(
        [
            jnp.concatenate([near_high, own_high, basis_high_t, basis_high_t], axis=1),
            jnp.concatenate([near_low, own_low, basis_low_t, jnp.zeros_like(basis_low_t)], axis=1),
        ],
        axis=0,
    )
    place_parts = jnp.concatenate(
        split3(jnp.transpose(coords_ref[...])[: 3 * sites]), axis=0
    )

    species = species_ref[...]
    scale_slot = jnp.zeros(species.shape, F32)
    shift_slot = jnp.zeros(species.shape, F32)
    for s in range(scale_ref.shape[0]):
        scale_slot = jnp.where(species == s, scale_ref[s], scale_slot)
        shift_slot = jnp.where(species == s, shift_ref[s], shift_slot)
    scale_parts = jnp.concatenate([*split3(scale_slot), jnp.zeros((13, owned), BF16)], axis=0)

    kind = lax.broadcasted_iota(jnp.int32, (ORDERS, width), 0)
    path_rows = jnp.where(
        kind == 0,
        path_weight_ref[0:1, :],
        jnp.where(
            kind < 4,
            path_weight_ref[1:2, :],
            jnp.where(kind < 9, path_weight_ref[2:3, :], 0.0),
        ),
    )
    paths_t = jnp.transpose(jnp.concatenate([path_rows] * GROUP, axis=0)) * (1.0 / root_count)
    out_column = jnp.transpose(jnp.broadcast_to(out_weight_ref[...], (width, width)))
    out_column = jnp.concatenate([out_column] * (pairs // width), axis=1)

    frame_ids = lax.broadcasted_iota(jnp.int32, (frame, pairs), 0)
    slot_ids = lax.broadcasted_iota(jnp.int32, (owned, pairs), 0)
    block_row = lax.broadcasted_iota(jnp.int32, (wide, span), 0) // ORDERS
    block_lane = lax.broadcasted_iota(jnp.int32, (wide, span), 1) // nbr
    block_mask = (block_row == block_lane).astype(F32)
    block_half = block_mask.astype(BF16)
    order = lax.broadcasted_iota(jnp.int32, (radial, pairs), 0).astype(F32) + 1.0
    lanes = [slice(g * span, (g + 1) * span) for g in range(groups)]

    near_row = near_row_ref[...]
    pick = jnp.where(frame_ids == near_row, 1.0, 0.0)
    from_center = jnp.where(frame_ids == center_row_ref[...], 1.0, 0.0)
    pick_half = pick.astype(BF16)
    slot_half = jnp.where(slot_ids == center_slot_ref[...], 1.0, 0.0).astype(BF16)
    live = near_row != frame

    moved = mm(place_parts, (pick - from_center).astype(BF16))
    moved = moved[: 3 * sites] + moved[3 * sites : 6 * sites] + moved[6 * sites :]
    dx = jnp.where(live, jnp.sum(moved[:sites], axis=0, keepdims=True), 6.0)
    dy = jnp.where(live, jnp.sum(moved[sites : 2 * sites], axis=0, keepdims=True), 0.0)
    dz = jnp.where(live, jnp.sum(moved[2 * sites :], axis=0, keepdims=True), 0.0)
    length = jnp.sqrt(dx * dx + dy * dy + dz * dz)
    inverse = 1.0 / length
    ratio = length * (1.0 / CUTOFF)
    inside = live & (ratio < 1.0)
    r2 = ratio * ratio
    r5 = r2 * r2 * ratio
    r6 = r5 * ratio
    weight = jnp.where(inside, 1.0 - r6 * (28.0 - 48.0 * ratio + 21.0 * r2), 0.0)
    slope = jnp.where(inside, -168.0 * r5 * (1.0 - 2.0 * ratio + r2), 0.0)
    sine, cosine = sin_cos_pi(order * ratio)
    basis = (math.sqrt(2.0 / CUTOFF) * inverse) * sine
    basis_slope = (math.sqrt(2.0 / CUTOFF) * inverse) * (
        (math.pi / CUTOFF) * order * cosine - sine * inverse
    )
    ex = dx * inverse
    ey = dy * inverse
    ez = dz * inverse
    angular = jnp.concatenate(
        [
            jnp.ones_like(ex),
            root_three * ex,
            root_three * ey,
            root_three * ez,
            root_fifteen * ex * ey,
            root_fifteen * ey * ez,
            0.5 * root_five * (3.0 * ez * ez - 1.0),
            root_fifteen * ex * ez,
            0.5 * root_fifteen * (ex * ex - ey * ey),
            jnp.zeros((ORDERS - 9, pairs), F32),
        ],
        axis=0,
    )
    angular_high, angular_low = split(angular)
    blocks = [
        jnp.concatenate(
            [
                jnp.concatenate([angular_high[:, cut]] * GROUP, axis=0) * block_half,
                jnp.concatenate([angular_low[:, cut]] * GROUP, axis=0) * block_half,
            ],
            axis=0,
        )
        for cut in lanes
    ]
    scale = mm(scale_parts, slot_half)
    scale = (scale[0:1] + scale[1:2] + scale[2:3]) * (1.0 / root_count)
    pull = ROOT_HALF * scale

    basis_high, basis_low = split(basis)
    before = folded(
        mm(lookup, jnp.concatenate([pick_half, slot_half, basis_high, basis_low], axis=0))
    )
    gate = 0.5 * jnp.tanh(0.5 * before) + 0.5
    active = before * gate
    latent = weight * active
    mixed = half_depth(value_rows, latent)
    values = mixed[:width]
    env_high, env_low = split(mixed[width:])

    def over_pairs(high, low):
        sums = []
        for cut, block in zip(lanes, blocks):
            quad = mm_nt(jnp.concatenate([high[:, cut], low[:, cut]], axis=0), block)
            sums.append((quad[:width, :wide] + quad[:width, wide:] + quad[width:, :wide]) * paths_t)
        return sums

    def over_orders(tables):
        parts = [folded(mm(stacked(*split(t)), block)) for t, block in zip(tables, blocks)]
        return jnp.concatenate(parts, axis=1)

    weighted = over_pairs(env_high, env_low)
    inner = over_orders(weighted)
    scalars = values * inner
    joined_high, joined_low = split(jnp.concatenate([latent, scalars], axis=0))
    z = full_depth(latent_both_t, latent_high_t, joined_high, joined_low)
    z_gate = 0.5 * jnp.tanh(0.5 * z) + 0.5
    update = z * z_gate
    update_out = update * out_column
    pair_energy = jnp.sum(latent * out_column + weight * update_out, axis=0, keepdims=True)
    pair_energy = pair_energy * pull
    d_z = (pull * weight) * out_column * (z_gate + update * (1.0 - z_gate))
    spread_back = half_depth(latent_rows, d_z)
    d_scalars = spread_back[width:]
    d_values = d_scalars * inner
    dinner_high, dinner_low = split(d_scalars * values)
    d_embed = over_pairs(dinner_high, dinner_low)
    d_env = over_orders(d_embed)

    d_angular = []
    for g, cut in enumerate(lanes):
        sides = jnp.transpose(jnp.concatenate([weighted[g], d_embed[g]], axis=0))
        sides_high, sides_low = split(sides)
        d_block = full_depth(
            jnp.concatenate([sides_high, sides_low], axis=0),
            sides_high,
            jnp.concatenate([dinner_high[:, cut], env_high[:, cut]], axis=0),
            jnp.concatenate([dinner_low[:, cut], env_low[:, cut]], axis=0),
        )
        d_block = d_block * block_mask
        total = d_block[:ORDERS]
        for k in range(1, GROUP):
            total = total + d_block[k * ORDERS : (k + 1) * ORDERS]
        d_angular.append(total)
    d_angular = jnp.concatenate(d_angular, axis=1)

    mixed_high, mixed_low = split(jnp.concatenate([d_values, d_env], axis=0))
    d_latent = (
        full_depth(value_both, value_high, mixed_high, mixed_low)
        + spread_back[:width]
        + pull * out_column
    )
    d_weight = jnp.sum(d_latent * active + pull * update_out, axis=0, keepdims=True)
    d_before = d_latent * weight * (gate + active * (1.0 - gate))
    d_basis = half_depth(basis_rows, d_before)

    d_length = jnp.sum(d_basis * basis_slope, axis=0, keepdims=True) + d_weight * slope * (
        1.0 / CUTOFF
    )
    a1, a2, a3, a4, a5, a6, a7, a8 = [d_angular[m : m + 1] for m in range(1, 9)]
    ux = root_three * a1 + root_fifteen * (ey * a4 + ez * a7 + ex * a8)
    uy = root_three * a2 + root_fifteen * (ex * a4 + ez * a5 - ey * a8)
    uz = root_three * a3 + root_fifteen * (ey * a5 + ex * a7) + 3.0 * root_five * ez * a6
    along = ex * ux + ey * uy + ez * uz
    radial_part = d_length - along * inverse
    gx = ux * inverse + ex * radial_part
    gy = uy * inverse + ey * radial_part
    gz = uz * inverse + ez * radial_part
    hx = -0.5 * dx
    hy = -0.5 * dy
    hz = -0.5 * dz
    virial = [hx * gx, hx * gy, hx * gz, hy * gx, hy * gy, hy * gz, hz * gx, hz * gy, hz * gz]
    near_terms = jnp.concatenate(
        [-gx, -gy, -gz, *virial, pair_energy, jnp.ones_like(gx), jnp.zeros((2, pairs), F32)],
        axis=0,
    )
    terms_high, terms_middle, terms_low = split3(near_terms)
    count = kinds[0] * kinds[1] * kinds[2]
    target_ids = lax.broadcasted_iota(jnp.int32, (count * owned, pairs), 0)
    reach = jnp.where(target_ids == target_row_ref[...], 1.0, 0.0).astype(BF16)
    totals = folded(mm_nt(jnp.concatenate([terms_high, terms_middle], axis=0), reach))
    own_sums = mm_nt(
        jnp.concatenate(
            [terms_high, terms_middle, terms_low, jnp.zeros((ORDERS, pairs), BF16)], axis=0
        ),
        slot_half,
    )
    sums = own_sums[:ORDERS] + own_sums[ORDERS : 2 * ORDERS] + own_sums[2 * ORDERS : 3 * ORDERS]
    energy_ref[...] = sums[12:13] + jnp.where(sums[13:14] > 0.5, shift_slot, 0.0)
    sign_row = lax.broadcasted_iota(jnp.int32, (ORDERS, owned), 0)
    center_terms = jnp.where(sign_row < 3, -sums, sums)
    center_terms = jnp.concatenate(
        [center_terms, jnp.zeros((ORDERS, 128 - owned), F32)], axis=1
    )

    parts_ref[...] = jnp.zeros(parts_ref.shape, F32)
    per_tile = 128 // owned
    half = ORDERS // 2
    padding = -count % per_tile * owned
    if padding:
        totals = jnp.concatenate([totals, jnp.zeros((ORDERS, padding), F32)], axis=1)
    lane = lax.broadcasted_iota(jnp.int32, (half, 128), 1)
    for block in range(count):
        choice = (block // (kinds[1] * kinds[2]), block // kinds[2] % kinds[1], block % kinds[2])
        step = [-1 if c == 2 else c for c in choice]
        column = block // per_tile * 128
        tile = totals[:, column : column + 128]
        if block == 0:
            tile = tile + center_terms
        turn = block % per_tile * owned
        first = tile[:half] if turn == 0 else pltpu.roll(tile[:half], 128 - turn, 1)
        back = (128 - turn + owned) % 128
        second = tile[half:] if back == 0 else pltpu.roll(tile[half:], back, 1)
        packed = jnp.where(lane < owned, first, jnp.where(lane < 2 * owned, second, 0.0))
        parts_ref[pl.ds(device(*step), 1)] = packed[None]


def local(
    positions,
    features,
    species,
    centers,
    neighbours,
    counts,
    species_scale,
    species_shift,
    center_weight,
    near_weight,
    basis_weight,
    path_weight,
    value_weight,
    latent_weight,
    out_weight,
):
    names = ("gx", "gy", "gz")
    cells_x, cells_y, cells_z, sites, width = features.shape
    cells = (cells_x, cells_y, cells_z)
    cell_count = cells_x * cells_y * cells_z
    owned = cell_count * sites
    frame_count = (cells_x + 2) * (cells_y + 2) * (cells_z + 2) * sites
    axes = tuple(lax.axis_size(name) for name in names)
    kinds = tuple(min(3, size) for size in axes)
    devices = axes[0] * axes[1] * axes[2]
    pairs = neighbours.size
    nbr = pairs // owned

    coords = jnp.transpose(positions, (1, 2, 3, 0, 4)).reshape(cell_count, 3 * sites)
    coords = jnp.pad(coords, ((0, -cell_count % 8), (0, width - 3 * sites)))
    payload = jnp.concatenate([features.reshape(owned, width), coords], axis=0)
    gathered = lax.all_gather(payload, names, tiled=True)

    near_row = neighbours.reshape(1, pairs)
    rows = center_rows(centers, cells, sites)
    center_row = jnp.broadcast_to(rows[:, None], (owned, nbr)).reshape(1, pairs)
    center_slot = jnp.broadcast_to(centers[:, None], (owned, nbr)).reshape(1, pairs)
    target_row = target_rows(near_row, cells, sites, kinds)
    place = jnp.stack([lax.axis_index(name) for name in names]).astype(jnp.int32)
    vmem = pl.BlockSpec(memory_space=pltpu.VMEM)
    smem = pl.BlockSpec(memory_space=pltpu.SMEM)
    parts, energy = pl.pallas_call(
        functools.partial(force_kernel, cells, axes, kinds),
        out_shape=(
            jax.ShapeDtypeStruct((devices, 8, 128), F32),
            jax.ShapeDtypeStruct((1, owned), F32),
        ),
        in_specs=[vmem, smem] + [vmem] * 6 + [smem] * 2 + [vmem] * 7,
        out_specs=(vmem, vmem),
        scratch_shapes=[
            pltpu.VMEM((frame_count, width), F32),
            pltpu.VMEM((frame_count, 128), F32),
        ],
        compiler_params=pltpu.CompilerParams(vmem_limit_bytes=40 * 1024 * 1024),
        name="pair_forces",
    )(
        gathered,
        place,
        features.reshape(owned, width),
        near_row,
        target_row,
        center_row,
        center_slot,
        species.reshape(1, owned),
        species_scale,
        species_shift,
        center_weight,
        near_weight,
        basis_weight,
        path_weight,
        value_weight,
        latent_weight,
        out_weight.reshape(1, width),
    )
    returned = lax.all_to_all(parts, names, split_axis=0, concat_axis=0, tiled=True)
    summed = jnp.sum(returned, axis=0)
    terms = jnp.concatenate([summed[:, :owned], summed[:, owned : 2 * owned]], axis=0)
    forces = terms[0:3].reshape(3, cells_x, cells_y, cells_z, sites)
    virial = terms[3:12].reshape(9, cells_x, cells_y, cells_z, sites)
    site_energy = energy.reshape(cells_x, cells_y, cells_z, sites)
    return (site_energy, forces, virial)


def solution(mesh):
    placed = (
        P(None, "gx", "gy", "gz", None),
        P("gx", "gy", "gz", None, None),
        P("gx", "gy", "gz", None),
        P(("gx", "gy", "gz")),
        P(("gx", "gy", "gz"), None),
        P(("gx", "gy", "gz")),
        P(),
        P(),
        P(),
        P(),
        P(),
        P(),
        P(),
        P(),
        P(),
    )
    return jax.shard_map(
        local,
        mesh=mesh,
        in_specs=placed,
        out_specs=(
            P("gx", "gy", "gz", None),
            P(None, "gx", "gy", "gz", None),
            P(None, "gx", "gy", "gz", None),
        ),
        check_vma=False,
    )
```

time: 46.9 us -> 66.8 us (1.42)
  blocking collectives: 0 us -> 45.1 us
  starting transfers between devices: 16 us -> 2.56 us
  waiting for transfers between devices: 12.1 us -> 6.39 us
  Pallas kernels: 10.1 us -> 5.54 us
  local copies, waits for them, and re-layouts: 6.54 us -> 5.14 us
    all_gather x0 -> x1, blocking collectives: none -> 45.1 us  [local(): gathered = lax.all_gather(payload, names, tiled=True)]
    ppermute x10 -> x0, starting transfers between devices: 16 us -> none  [the longest x3 5.13 us: padded(): before = lax.ppermute(last, axis, up)]
    ppermute x10 -> x0, waiting for transfers between devices: 12.1 us -> none  [the longest x3 4.81 us: padded(): before = lax.ppermute(last, axis, up)]
    all_to_all x0 -> x1, waiting for transfers between devices: none -> 6.39 us  [local(): lax.all_to_all(parts, names, split_axis=0, concat_axis=0, tiled=True)]
    pallas_call x1, Pallas kernels: 10.1 us -> 5.54 us  [local(): pl.pallas_call(functools.partial(force_kernel, cells, axes, kinds), out_s...]
    all_to_all x0 -> x1, starting transfers between devices: none -> 2.56 us  [local(): lax.all_to_all(parts, names, split_axis=0, concat_axis=0, tiled=True)]
    unnamed x31 -> x28, local copies, waits for them, and re-layouts: 3.37 us -> 1.97 us
    transpose x3 -> x1, local copies, waits for them, and re-layouts: 1.38 us -> 0.01 us  [local(): jnp.transpose(positions, (1, 2, 3, 0, 4)).reshape(cell_count, 3 * sites)]
  transfers between devices with their start and end apart: 10 -> 1, of which waited for: 8 -> 1; matrix products, arithmetic and copies ran while one was open for 5% -> 3% of each run, Pallas kernels for 0% -> 0%
where the time goes in v2:
time: 66.8 us; the launch traced here: 66.5 us
  blocking collectives  45.1 us (68%)
  waiting for transfers between devices  6.39 us (10%)
  Pallas kernels  5.54 us (8%)
  local copies, waits for them, and re-layouts  5.14 us (8%)
  starting transfers between devices  2.56 us (4%)
  other arithmetic  0.95 us (1%)
  between operations  0.76 us (1%)
    all_gather x1, blocking collectives, local(): gathered = lax.all_gather(payload, names, tiled=True)  45.1 us
    all_to_all x1, waiting for transfers between devices, local(): lax.all_to_all(parts, names, split_axis=0, concat_axis=0, tiled=True)  6.39 us
    pallas_call x1, Pallas kernels, local(): pl.pallas_call(functools.partial(force_kernel, cells, axes, kinds), out_s...  5.54 us
    all_to_all x1, starting transfers between devices, local(): lax.all_to_all(parts, names, split_axis=0, concat_axis=0, tiled=True)  2.56 us
    unnamed x28, local copies, waits for them, and re-layouts  1.97 us
  transfers between devices with their start and end apart: 1, of which 1 were waited for; matrix products, arithmetic and copies ran while one was open for 3% of the time, Pallas kernels for 0%

profile of v2, /device:TPU:0, one launch (start us, length us, event | category | flops | bytes accessed | tf_op | source)
XLA Modules:
  0.0 66.5 jit_solution(8278113212042000447)
XLA Ops:
  0.7 0.7 %copy-done.11 = f32[3,2,1,2,8]{4,3,2,1,0:T(2,128)S(1)} copy-done((f32[3,2,1,2,8]{4,3,2,1,0:T(2,128)S(1)}, f32[3,2,1,2,8]{4,3,2,1,0:T(2,128)}, u32[]{:S(2)}) %copy-start.11) | copy-done | bytes 408
  1.3 0.1 reshape.455
  1.4 0.0 copy-done.2
  1.4 0.0 copy-start.10
  1.4 0.0 copy-start.13
  1.4 0.0 copy-start
  1.5 0.0 copy-start.1
  1.5 0.0 copy-start.4
  1.5 45.1 %all_gather.3.gathered_ref = f32[1280,128]{1,0:T(8,128)S(1)} all-gather(f32[40,128]{1,0:T(8,128)S(1)} %select_maximum_fusion), channel_id=1, replica_groups=mesh['gx'=4,'gy'=2,'gz'=4] {'gx','gy','gz'}, dimensions={0}, use_global_device_ids=true | all-gather | bytes 675840 | tf_op jit(solution)/shard_map/all_gather | solution.py:474
  46.6 0.1 reshape.456.near_row_ref
  46.7 0.1 compare_select_fusion.target_row_ref
  46.9 0.1 broadcast_in_dim.41
  47.0 0.1 reshape.457.center_row_ref
  47.0 0.1 broadcast_in_dim.42
  47.1 0.1 reshape.458.center_slot_ref
  47.2 0.6 copy-done.12
  47.8 0.1 reshape.459.species_ref
  47.9 0.1 pad_add_fusion.place_ref
  48.0 0.6 copy-done.5
  48.6 0.0 copy-done.6
  48.6 0.0 copy-done.7
  48.6 0.0 copy-done.8
  48.6 0.0 copy-done.9
  48.7 5.5 %pair_forces.1 = (f32[32,8,128]{2,1,0:T(8,128)}, f32[1,32]{1,0:T(1,128)S(1)}) custom-call(f32[1280,128]{1,0:T(8,128)S(1)} %all_gather.3.gathered_ref, s32[3]{0:T(128)S(1)} %pad_add_fusion.place_ref, f32[32,128]{1,0:T(8,128)S(1)} %bitcast.12, s32[1,1024]{1,0:T(1,128)S(1)} %reshape.456.near_row_ref, s32[1,1024]{1,0:T(1,128)S(1)} %compare_select_fusion.target_row_ref, ...), custom_call_target="tpu_custom_call" | custom-call | tf_op jit(solution)/shard_map/pair_forces/pallas_call | solution.py:484
  54.2 2.6 %all-to-all-start = ((f32[32,8,128]{2,1,0:T(8,128)}), f32[32,8,128]{2,1,0:T(8,128)S(1)}, u32[]{:S(2)}, u32[]{:S(2)}) async-start(f32[32,8,128]{2,1,0:T(8,128)} %get-tuple-element.6), calls=%async_computation | async-start | bytes 262144 | tf_op jit(solution)/shard_map/all_to_all | solution.py:517
  56.8 0.5 broadcast.538
  57.3 0.7 reduce.3
  57.9 0.7 reshape.461
  58.6 6.4 %all-to-all-done = f32[32,8,128]{2,1,0:T(8,128)S(1)} async-done(((f32[32,8,128]{2,1,0:T(8,128)}), f32[32,8,128]{2,1,0:T(8,128)S(1)}, u32[]{:S(2)}, u32[]{:S(2)}) %all-to-all-start) | async-done | bytes 131104 | tf_op jit(solution)/shard_map/all_to_all | solution.py:517
  65.0 0.1 fusion.8
  65.1 0.7 %copy.22 = f32[9,32]{0,1:T(8,128)} copy(f32[9,32]{1,0:T(8,128)S(1)} %pad_maximum_fusion) | data formatting | bytes 2304 | tf_op jit(solution)/shard_map/slice | solution.py:521
  65.8 0.7 %reshape.462 = f32[3,2,1,2,8]{4,3,1,0,2:T(2,128)} reshape(f32[3,32]{1,0:T(4,128)S(1)} %slice.13) | data formatting | bytes 768 | tf_op jit(solution)/shard_map/reshape | solution.py:520
  (21 shorter events, 0.1 us)
Async XLA Ops:
  0.6 0.7 %copy-start.11 = (f32[3,2,1,2,8]{4,3,2,1,0:T(2,128)S(1)}, f32[3,2,1,2,8]{4,3,2,1,0:T(2,128)}, u32[]{:S(2)}) copy-start(f32[3,2,1,2,8]{4,3,2,1,0:T(2,128)} %param.15) | copy-start | bytes 1156
  0.6 0.8 %copy-start.2 = (f32[2,1,2,8,128]{4,3,2,1,0:T(8,128)S(1)}, f32[2,1,2,8,128]{4,3,2,1,0:T(8,128)}, u32[]{:S(2)}) copy-start(f32[2,1,2,8,128]{4,3,2,1,0:T(8,128)} %param.16) | copy-start | bytes 49156
  1.4 45.2 %copy-start.10 = (s32[32,32]{1,0:T(8,128)S(1)}, s32[32,32]{1,0:T(8,128)}, u32[]{:S(2)}) copy-start(s32[32,32]{1,0:T(8,128)} %param.19) | copy-start | bytes 12292
  1.4 45.4 %copy-start.13 = (s32[32]{0:T(128)S(1)}, s32[32]{0:T(128)}, u32[]{:S(2)}) copy-start(s32[32]{0:T(128)} %param.18) | copy-start | bytes 388
  1.4 46.5 %copy-start = (f32[128,256]{1,0:T(8,128)S(1)}, f32[128,256]{1,0:T(8,128)}, u32[]{:S(2)}) copy-start(f32[128,256]{1,0:T(8,128)} %value_weight_ref.1) | copy-start | bytes 393220
  1.5 46.5 %copy-start.1 = (f32[256,128]{1,0:T(8,128)S(1)}, f32[256,128]{1,0:T(8,128)}, u32[]{:S(2)}) copy-start(f32[256,128]{1,0:T(8,128)} %latent_weight_ref.1) | copy-start | bytes 393220
  1.5 46.5 %copy-start.4 = (f32[128,128]{1,0:T(8,128)S(1)}, f32[128,128]{1,0:T(8,128)}, u32[]{:S(2)}) copy-start(f32[128,128]{1,0:T(8,128)} %near_weight_ref.1) | copy-start | bytes 196612
  46.6 1.4 %copy-start.3 = (f32[128,128]{1,0:T(8,128)S(1)}, f32[128,128]{1,0:T(8,128)}, u32[]{:S(2)}) copy-start(f32[128,128]{1,0:T(8,128)} %center_weight_ref.1) | copy-start | bytes 196612
  47.1 0.7 %copy-start.12 = (s32[2,1,2,8]{3,2,1,0:T(2,128)S(1)}, s32[2,1,2,8]{3,2,1,0:T(2,128)}, u32[]{:S(2)}) copy-start(s32[2,1,2,8]{3,2,1,0:T(2,128)} %param.17) | copy-start | bytes 388
  47.9 0.7 %copy-start.5 = (f32[8,128]{1,0:T(8,128)S(1)}, f32[8,128]{1,0:T(8,128)}, u32[]{:S(2)}) copy-start(f32[8,128]{1,0:T(8,128)} %basis_weight_ref.1) | copy-start | bytes 12292
  47.9 0.7 %copy-start.6 = (f32[3,128]{1,0:T(4,128)S(1)}, f32[3,128]{1,0:T(4,128)}, u32[]{:S(2)}) copy-start(f32[3,128]{1,0:T(4,128)} %path_weight_ref.1) | copy-start | bytes 4612
  48.0 0.7 copy-start.7
  48.0 0.7 %copy-start.8 = (f32[5]{0:T(128)S(1)}, f32[5]{0:T(128)}, u32[]{:S(2)}) copy-start(f32[5]{0:T(128)} %shift_ref.1) | copy-start | bytes 64
  48.0 0.7 %copy-start.9 = (f32[128]{0:T(128)S(1)}, f32[128]{0:T(128)}, u32[]{:S(2)}) copy-start(f32[128]{0:T(128)} %param.28) | copy-start | bytes 1540
  54.2 10.8 %all-to-all-start = ((f32[32,8,128]{2,1,0:T(8,128)}), f32[32,8,128]{2,1,0:T(8,128)S(1)}, u32[]{:S(2)}, u32[]{:S(2)}) async-start(f32[32,8,128]{2,1,0:T(8,128)} %get-tuple-element.6), calls=%async_computation | async-start | bytes 262144 | tf_op jit(solution)/shard_map/all_to_all | solution.py:517

commit v3 on v2

--- a/solution.py
+++ b/solution.py
@@ -119,7 +119,17 @@
     cells,
     axes,
     kinds,
-    gathered_ref,
+    *refs,
+):
+    pieces = refs[: kinds[0] * kinds[1] * kinds[2]]
+    force_body(cells, axes, kinds, pieces, *refs[len(pieces) :])
+
+
+def force_body(
+    cells,
+    axes,
+    kinds,
+    pieces,
     place_ref,
     own_ref,
     near_row_ref,
@@ -148,7 +158,6 @@
     radial = basis_weight_ref.shape[0]
     spans = [count + 2 for count in cells]
     sites = frame // (spans[0] * spans[1] * spans[2])
-    stride = gathered_ref.shape[0] // (axes[0] * axes[1] * axes[2])
     span = GROUP * nbr
     groups = owned // GROUP
     wide = GROUP * ORDERS
@@ -175,13 +184,19 @@
     component = tile_lane // sites
     for cell in range(spans[0] * spans[1] * spans[2]):
         place = (cell // (spans[1] * spans[2]), cell // spans[2] % spans[1], cell % spans[2])
-        step = [(p > c) * 1 - (p < 1) * 1 for p, c in zip(place, cells)]
-        inside = [(p - 1) % c for p, c in zip(place, cells)]
-        local_cell = (inside[0] * cells[1] + inside[1]) * cells[2] + inside[2]
-        base = device(*step) * stride
-        start = pl.multiple_of(base + local_cell * sites, 8)
-        feats_ref[cell * sites : (cell + 1) * sites, :] = gathered_ref[pl.ds(start, sites), :]
-        row = gathered_ref[pl.ds(base + (owned + local_cell), 1), :]
+        piece = 0
+        inside = 0
+        for p, count, kind in zip(place, cells, kinds):
+            step = (p > count) * 1 - (p < 1) * 1
+            whole = step == 0 or kind == 2
+            piece = piece * kind + step % kind
+            inside = inside * (count if whole else 1) + ((p - 1) % count if whole else 0)
+        source = pieces[piece]
+        total = (source.shape[0] - 8) // sites
+        feats_ref[cell * sites : (cell + 1) * sites, :] = source[
+            inside * sites : (inside + 1) * sites, :
+        ]
+        row = source[total * sites + inside : total * sites + inside + 1, :]
         corner = [np.float32(p) * np.float32(CELL_SIDE) for p in place]
         offset = jnp.where(
             component == 0, corner[0], jnp.where(component == 1, corner[1], corner[2])
@@ -419,11 +434,11 @@
 
     parts_ref[...] = jnp.zeros(parts_ref.shape, F32)
     per_tile = 128 // owned
-    half = ORDERS // 2
+    quarter = parts_ref.shape[1]
     padding = -count % per_tile * owned
     if padding:
         totals = jnp.concatenate([totals, jnp.zeros((ORDERS, padding), F32)], axis=1)
-    lane = lax.broadcasted_iota(jnp.int32, (half, 128), 1)
+    lane = lax.broadcasted_iota(jnp.int32, (quarter, 128), 1)
     for block in range(count):
         choice = (block // (kinds[1] * kinds[2]), block // kinds[2] % kinds[1], block % kinds[2])
         step = [-1 if c == 2 else c for c in choice]
@@ -431,11 +446,13 @@
         tile = totals[:, column : column + 128]
         if block == 0:
             tile = tile + center_terms
-        turn = block % per_tile * owned
-        first = tile[:half] if turn == 0 else pltpu.roll(tile[:half], 128 - turn, 1)
-        back = (128 - turn + owned) % 128
-        second = tile[half:] if back == 0 else pltpu.roll(tile[half:], back, 1)
-        packed = jnp.where(lane < owned, first, jnp.where(lane < 2 * owned, second, 0.0))
+        packed = jnp.zeros((quarter, 128), F32)
+        for part in range(12 // quarter):
+            turn = (part - block % per_tile) * owned % 128
+            rows = tile[part * quarter : (part + 1) * quarter]
+            rows = pltpu.roll(rows, turn, 1) if turn else rows
+            mine = (lane >= part * owned) & (lane < (part + 1) * owned)
+            packed = jnp.where(mine, rows, packed)
         parts_ref[pl.ds(device(*step), 1)] = packed[None]
 
 
@@ -459,8 +476,7 @@
     names = ("gx", "gy", "gz")
     cells_x, cells_y, cells_z, sites, width = features.shape
     cells = (cells_x, cells_y, cells_z)
-    cell_count = cells_x * cells_y * cells_z
-    owned = cell_count * sites
+    owned = cells_x * cells_y * cells_z * sites
     frame_count = (cells_x + 2) * (cells_y + 2) * (cells_z + 2) * sites
     axes = tuple(lax.axis_size(name) for name in names)
     kinds = tuple(min(3, size) for size in axes)
@@ -468,10 +484,34 @@
     pairs = neighbours.size
     nbr = pairs // owned
 
-    coords = jnp.transpose(positions, (1, 2, 3, 0, 4)).reshape(cell_count, 3 * sites)
-    coords = jnp.pad(coords, ((0, -cell_count % 8), (0, width - 3 * sites)))
-    payload = jnp.concatenate([features.reshape(owned, width), coords], axis=0)
-    gathered = lax.all_gather(payload, names, tiled=True)
+    coords = jnp.transpose(positions, (1, 2, 3, 0, 4)).reshape(*cells, 3 * sites)
+    coords = jnp.pad(coords, ((0, 0), (0, 0), (0, 0), (0, width - 3 * sites)))
+    pieces = []
+    for choice in np.ndindex(*kinds):
+        feats = features
+        rows = coords
+        step = [-1 if c == 2 else c for c in choice]
+        for dim, (c, kind, count) in enumerate(zip(choice, kinds, cells)):
+            if c == 0 or kind == 2:
+                continue
+            first = 0 if c == 1 else count - 1
+            feats = lax.slice_in_dim(feats, first, first + 1, axis=dim)
+            rows = lax.slice_in_dim(rows, first, first + 1, axis=dim)
+        rows = rows.reshape(-1, width)
+        rows = jnp.pad(rows, ((0, 8 - rows.shape[0]), (0, 0)))
+        piece = jnp.concatenate([feats.reshape(-1, width), rows], axis=0)
+        if any(step):
+            route = []
+            for at in np.ndindex(*axes):
+                to = [(p - q) % size for p, q, size in zip(at, step, axes)]
+                route.append(
+                    (
+                        (at[0] * axes[1] + at[1]) * axes[2] + at[2],
+                        (to[0] * axes[1] + to[1]) * axes[2] + to[2],
+                    )
+                )
+            piece = lax.ppermute(piece, names, route)
+        pieces.append(piece)
 
     near_row = neighbours.reshape(1, pairs)
     rows = center_rows(centers, cells, sites)
@@ -484,10 +524,10 @@
     parts, energy = pl.pallas_call(
         functools.partial(force_kernel, cells, axes, kinds),
         out_shape=(
-            jax.ShapeDtypeStruct((devices, 8, 128), F32),
+            jax.ShapeDtypeStruct((devices, 4, 128), F32),
             jax.ShapeDtypeStruct((1, owned), F32),
         ),
-        in_specs=[vmem, smem] + [vmem] * 6 + [smem] * 2 + [vmem] * 7,
+        in_specs=[vmem] * len(pieces) + [smem] + [vmem] * 6 + [smem] * 2 + [vmem] * 7,
         out_specs=(vmem, vmem),
         scratch_shapes=[
             pltpu.VMEM((frame_count, width), F32),
@@ -496,7 +536,7 @@
         compiler_params=pltpu.CompilerParams(vmem_limit_bytes=40 * 1024 * 1024),
         name="pair_forces",
     )(
-        gathered,
+        *pieces,
         place,
         features.reshape(owned, width),
         near_row,
@@ -516,7 +556,9 @@
     )
     returned = lax.all_to_all(parts, names, split_axis=0, concat_axis=0, tiled=True)
     summed = jnp.sum(returned, axis=0)
-    terms = jnp.concatenate([summed[:, :owned], summed[:, owned : 2 * owned]], axis=0)
+    terms = jnp.concatenate(
+        [summed[:, :owned], summed[:, owned : 2 * owned], summed[:, 2 * owned : 3 * owned]], axis=0
+    )
     forces = terms[0:3].reshape(3, cells_x, cells_y, cells_z, sites)
     virial = terms[3:12].reshape(9, cells_x, cells_y, cells_z, sites)
     site_energy = energy.reshape(cells_x, cells_y, cells_z, sites)

time: 66.8 us -> 53.7 us (0.80)
  blocking collectives: 45.1 us -> 0 us
  starting transfers between devices: 2.56 us -> 32.8 us
  waiting for transfers between devices: 6.39 us -> 9.14 us
  local copies, waits for them, and re-layouts: 5.14 us -> 3.96 us
    all_gather x1 -> x0, blocking collectives: 45.1 us -> none  [local(): gathered = lax.all_gather(payload, names, tiled=True)]
    ppermute x0 -> x17, starting transfers between devices: none -> 30.1 us  [local(): piece = lax.ppermute(piece, names, route)]
    ppermute x0 -> x17, waiting for transfers between devices: none -> 3.57 us  [local(): piece = lax.ppermute(piece, names, route)]
    unnamed x28 -> x26, local copies, waits for them, and re-layouts: 1.97 us -> 0.06 us
    all_to_all x1, waiting for transfers between devices: 6.39 us -> 5.57 us  [local(): lax.all_to_all(parts, names, split_axis=0, concat_axis=0, tiled=True)]
    transpose x1, local copies, waits for them, and re-layouts: 0.01 us -> 0.7 us  [local(): jnp.transpose(positions, (1, 2, 3, 0, 4)).reshape(*cells, 3 * sites)]
  transfers between devices with their start and end apart: 1 -> 18, of which waited for: 1 -> 3; matrix products, arithmetic and copies ran while one was open for 3% -> 5% of each run, Pallas kernels for 0% -> 0%
where the time goes in v3:
time: 53.7 us; the launch traced here: 53.4 us
  starting transfers between devices  32.8 us (61%)
  waiting for transfers between devices  9.14 us (17%)
  Pallas kernels  5.54 us (10%)
  local copies, waits for them, and re-layouts  3.96 us (7%)
  other arithmetic  1.01 us (2%)
  between operations  0.9 us (2%)
    ppermute x17, starting transfers between devices, local(): piece = lax.ppermute(piece, names, route)  30.1 us
    all_to_all x1, waiting for transfers between devices, local(): lax.all_to_all(parts, names, split_axis=0, concat_axis=0, tiled=True)  5.57 us
    pallas_call x1, Pallas kernels, local(): pl.pallas_call(functools.partial(force_kernel, cells, axes, kinds), out_s...  5.54 us
    ppermute x17, waiting for transfers between devices, local(): piece = lax.ppermute(piece, names, route)  3.57 us
    all_to_all x1, starting transfers between devices, local(): lax.all_to_all(parts, names, split_axis=0, concat_axis=0, tiled=True)  2.76 us
  transfers between devices with their start and end apart: 18, of which 3 were waited for; matrix products, arithmetic and copies ran while one was open for 5% of the time, Pallas kernels for 0%

profile of v3, /device:TPU:0, one launch (start us, length us, event | category | flops | bytes accessed | tf_op | source)
XLA Modules:
  0.0 53.4 jit_solution(16541632971678430325)
XLA Ops:
  0.6 0.7 %copy.22 = f32[2,1,2,3,8]{4,3,2,0,1:T(4,128)S(1)} copy(f32[2,1,2,3,8]{4,2,1,0,3:T(2,128)} %bitcast.54) | data formatting | bytes 768 | tf_op jit(solution)/shard_map/transpose | solution.py:487
  1.3 0.1 reshape.524
  1.5 3.5 %collective-permute-start.12 = (f32[16,128]{1,0:T(8,128)S(1)}, f32[16,128]{1,0:T(8,128)S(1)}, u32[]{:S(2)}, u32[]{:S(2)}) collective-permute-start(f32[16,128]{1,0:T(8,128)S(1)} %select_maximum_fusion.6), channel_id=1, source_target_pairs={{0,11},{1,8},{2,9},{3,10},{4,15},{5,12},{6,13},{7,14},{8,19},{9,16... | collective-permute-start | bytes 24584 | tf_op jit(solution)/shard_map/ppermute | solution.py:513
  4.9 2.8 %collective-permute-start.15 = (f32[16,128]{1,0:T(8,128)S(1)}, f32[16,128]{1,0:T(8,128)S(1)}, u32[]{:S(2)}, u32[]{:S(2)}) collective-permute-start(f32[16,128]{1,0:T(8,128)S(1)} %select_maximum_fusion.6), channel_id=1, source_target_pairs={{0,15},{1,12},{2,13},{3,14},{4,11},{5,8},{6,9},{7,10},{8,23},{9,20... | collective-permute-start | bytes 24584 | tf_op jit(solution)/shard_map/ppermute | solution.py:513
  7.8 1.1 %collective-permute-start.13 = (f32[16,128]{1,0:T(8,128)S(1)}, f32[16,128]{1,0:T(8,128)S(1)}, u32[]{:S(2)}, u32[]{:S(2)}) collective-permute-start(f32[16,128]{1,0:T(8,128)S(1)} %select_maximum_fusion.5), channel_id=1, source_target_pairs={{0,9},{1,10},{2,11},{3,8},{4,13},{5,14},{6,15},{7,12},{8,17},{9,18... | collective-permute-start | bytes 24584 | tf_op jit(solution)/shard_map/ppermute | solution.py:513
  8.9 4.3 %collective-permute-start.10 = (f32[16,128]{1,0:T(8,128)S(1)}, f32[16,128]{1,0:T(8,128)S(1)}, u32[]{:S(2)}, u32[]{:S(2)}) collective-permute-start(f32[16,128]{1,0:T(8,128)S(1)} %select_maximum_fusion.7), channel_id=1, source_target_pairs={{0,29},{1,30},{2,31},{3,28},{4,25},{5,26},{6,27},{7,24},{8,5},{9,6... | collective-permute-start | bytes 24584 | tf_op jit(solution)/shard_map/ppermute | solution.py:513
  13.3 0.1 reshape.542.refs_20_
  13.3 0.1 compare_select_fusion.refs_21_
  13.6 1.0 %collective-permute-done.10.refs_11_ = f32[16,128]{1,0:T(8,128)S(1)} collective-permute-done((f32[16,128]{1,0:T(8,128)S(1)}, f32[16,128]{1,0:T(8,128)S(1)}, u32[]{:S(2)}, u32[]{:S(2)}) %collective-permute-start.10) | collective-permute-done | bytes 8224 | tf_op jit(solution)/shard_map/ppermute | solution.py:513
  14.6 3.5 %collective-permute-start.7 = (f32[16,128]{1,0:T(8,128)S(1)}, f32[16,128]{1,0:T(8,128)S(1)}, u32[]{:S(2)}, u32[]{:S(2)}) collective-permute-start(f32[16,128]{1,0:T(8,128)S(1)} %select_maximum_fusion.7), channel_id=1, source_target_pairs={{0,25},{1,26},{2,27},{3,24},{4,29},{5,30},{6,31},{7,28},{8,1},{9,2... | collective-permute-start | bytes 24584 | tf_op jit(solution)/shard_map/ppermute | solution.py:513
  18.1 1.0 %collective-permute-start.6 = (f32[16,128]{1,0:T(8,128)S(1)}, f32[16,128]{1,0:T(8,128)S(1)}, u32[]{:S(2)}, u32[]{:S(2)}) collective-permute-start(f32[16,128]{1,0:T(8,128)S(1)} %select_maximum_fusion.8), channel_id=1, source_target_pairs={{0,27},{1,24},{2,25},{3,26},{4,31},{5,28},{6,29},{7,30},{8,3},{9,0... | collective-permute-start | bytes 24584 | tf_op jit(solution)/shard_map/ppermute | solution.py:513
  19.1 1.0 %collective-permute-start.9 = (f32[16,128]{1,0:T(8,128)S(1)}, f32[16,128]{1,0:T(8,128)S(1)}, u32[]{:S(2)}, u32[]{:S(2)}) collective-permute-start(f32[16,128]{1,0:T(8,128)S(1)} %select_maximum_fusion.8), channel_id=1, source_target_pairs={{0,31},{1,28},{2,29},{3,30},{4,27},{5,24},{6,25},{7,26},{8,7},{9,4... | collective-permute-start | bytes 24584 | tf_op jit(solution)/shard_map/ppermute | solution.py:513
  20.1 3.2 %collective-permute-start.11 = (f32[24,128]{1,0:T(8,128)S(1)}, f32[24,128]{1,0:T(8,128)S(1)}, u32[]{:S(2)}, u32[]{:S(2)}) collective-permute-start(f32[24,128]{1,0:T(8,128)S(1)} %select_maximum_fusion.1), channel_id=1, source_target_pairs={{0,8},{1,9},{2,10},{3,11},{4,12},{5,13},{6,14},{7,15},{8,16},{9,17... | collective-permute-start | bytes 36872 | tf_op jit(solution)/shard_map/ppermute | solution.py:513
  23.2 0.6 %collective-permute-start.14 = (f32[24,128]{1,0:T(8,128)S(1)}, f32[24,128]{1,0:T(8,128)S(1)}, u32[]{:S(2)}, u32[]{:S(2)}) collective-permute-start(f32[24,128]{1,0:T(8,128)S(1)} %select_maximum_fusion.1), channel_id=1, source_target_pairs={{0,12},{1,13},{2,14},{3,15},{4,8},{5,9},{6,10},{7,11},{8,20},{9,21... | collective-permute-start | bytes 36872 | tf_op jit(solution)/shard_map/ppermute | solution.py:513
  23.8 2.1 %collective-permute-start = (f32[24,128]{1,0:T(8,128)S(1)}, f32[24,128]{1,0:T(8,128)S(1)}, u32[]{:S(2)}, u32[]{:S(2)}) collective-permute-start(f32[24,128]{1,0:T(8,128)S(1)} %select_maximum_fusion.4), channel_id=1, source_target_pairs={{0,3},{1,0},{2,1},{3,2},{4,7},{5,4},{6,5},{7,6},{8,11},{9,8},{10,9... | collective-permute-start | bytes 36872 | tf_op jit(solution)/shard_map/ppermute | solution.py:513
  25.9 2.7 %collective-permute-start.3 = (f32[24,128]{1,0:T(8,128)S(1)}, f32[24,128]{1,0:T(8,128)S(1)}, u32[]{:S(2)}, u32[]{:S(2)}) collective-permute-start(f32[24,128]{1,0:T(8,128)S(1)} %select_maximum_fusion.4), channel_id=1, source_target_pairs={{0,7},{1,4},{2,5},{3,6},{4,3},{5,0},{6,1},{7,2},{8,15},{9,12},{10,... | collective-permute-start | bytes 36872 | tf_op jit(solution)/shard_map/ppermute | solution.py:513
  28.6 0.7 %collective-permute-start.4 = (f32[24,128]{1,0:T(8,128)S(1)}, f32[24,128]{1,0:T(8,128)S(1)}, u32[]{:S(2)}, u32[]{:S(2)}) collective-permute-start(f32[24,128]{1,0:T(8,128)S(1)} %select_maximum_fusion.3), channel_id=1, source_target_pairs={{0,5},{1,6},{2,7},{3,4},{4,1},{5,2},{6,3},{7,0},{8,13},{9,14},{10,... | collective-permute-start | bytes 36872 | tf_op jit(solution)/shard_map/ppermute | solution.py:513
  29.3 2.2 %collective-permute-start.5 = (f32[24,128]{1,0:T(8,128)S(1)}, f32[24,128]{1,0:T(8,128)S(1)}, u32[]{:S(2)}, u32[]{:S(2)}) collective-permute-start(f32[24,128]{1,0:T(8,128)S(1)} %select_maximum_fusion.2), channel_id=1, source_target_pairs={{0,24},{1,25},{2,26},{3,27},{4,28},{5,29},{6,30},{7,31},{8,0},{9,1... | collective-permute-start | bytes 36872 | tf_op jit(solution)/shard_map/ppermute | solution.py:513
  31.5 0.1 collective-permute-start.8
  31.6 1.4 %collective-permute-start.2 = (f32[40,128]{1,0:T(8,128)S(1)}, f32[40,128]{1,0:T(8,128)S(1)}, u32[]{:S(2)}, u32[]{:S(2)}) collective-permute-start(f32[40,128]{1,0:T(8,128)S(1)} %select_maximum_fusion.refs_0_), channel_id=1, source_target_pairs={{0,4},{1,5},{2,6},{3,7},{4,0},{5,1},{6,2},{7,3},{8,12},{9,13},{10,... | collective-permute-start | bytes 61448 | tf_op jit(solution)/shard_map/ppermute | solution.py:513
  33.2 0.1 reshape.543.refs_22_
  33.3 0.1 reshape.544.refs_23_
  33.4 0.1 reshape.545.refs_24_
  33.5 2.6 %collective-permute-done.8.refs_9_ = f32[24,128]{1,0:T(8,128)S(1)} collective-permute-done((f32[24,128]{1,0:T(8,128)S(1)}, f32[24,128]{1,0:T(8,128)S(1)}, u32[]{:S(2)}, u32[]{:S(2)}) %collective-permute-start.8) | collective-permute-done | bytes 12320 | tf_op jit(solution)/shard_map/ppermute | solution.py:513
  36.2 5.5 %pair_forces.1 = (f32[32,4,128]{2,1,0:T(4,128)}, f32[1,32]{1,0:T(1,128)S(1)}) custom-call(f32[40,128]{1,0:T(8,128)S(1)} %select_maximum_fusion.refs_0_, f32[24,128]{1,0:T(8,128)S(1)} %collective-permute-done.refs_1_, f32[24,128]{1,0:T(8,128)S(1)} %collective-permute-done.1.refs_2_, f32[40,128]{1,0:T(8,128)S(1)} %collective-permute-done.2.refs_3_, ...), custom_call_target="tpu_custom_call" | custom-call | tf_op jit(solution)/shard_map/pair_forces/pallas_call | solution.py:524
  41.7 2.8 %all-to-all-start = ((f32[32,4,128]{2,1,0:T(4,128)}), f32[32,4,128]{2,1,0:T(4,128)S(1)}, u32[]{:S(2)}, u32[]{:S(2)}) async-start(f32[32,4,128]{2,1,0:T(4,128)} %get-tuple-element.6), calls=%async_computation | async-start | bytes 131072 | tf_op jit(solution)/shard_map/all_to_all | solution.py:557
  44.5 0.5 broadcast.588
  45.0 0.7 %reduce.3 = f32[32]{0:T(128)S(1)} reduce(f32[1,32]{1,0:T(1,128)S(1)} %get-tuple-element.5, f32[]{:T(128)} %broadcast.588), dimensions={0}, to_apply=%get-tuple-element.5.reduce_sub_computation.3 | reduce | bytes 260 | tf_op jit(solution)/shard_map/pair_forces/pallas_call | solution.py:524
  45.7 0.7 %reshape.547 = f32[2,1,2,8]{3,2,0,1:T(2,128)} reshape(f32[32]{0:T(128)S(1)} %reduce.3) | data formatting | bytes 256 | tf_op jit(solution)/shard_map/reshape | solution.py:564
  46.3 5.6 %all-to-all-done = f32[32,4,128]{2,1,0:T(4,128)S(1)} async-done(((f32[32,4,128]{2,1,0:T(4,128)}), f32[32,4,128]{2,1,0:T(4,128)S(1)}, u32[]{:S(2)}, u32[]{:S(2)}) %all-to-all-start) | async-done | bytes 65568 | tf_op jit(solution)/shard_map/all_to_all | solution.py:557
  52.0 0.7 %copy.24 = f32[9,32]{0,1:T(8,128)} copy(f32[9,32]{1,0:T(8,128)S(1)} %pad_maximum_fusion) | data formatting | bytes 2304 | tf_op jit(solution)/shard_map/slice | solution.py:563
  52.7 0.7 %reshape.548 = f32[3,2,1,2,8]{4,3,1,0,2:T(2,128)} reshape(f32[3,32]{1,0:T(4,128)S(1)} %bitcast.51) | data formatting | bytes 768 | tf_op jit(solution)/shard_map/reshape | solution.py:562
  (66 shorter events, 0.6 us)
Async XLA Ops:
  0.6 0.8 %copy-start = (f32[2,1,2,8,128]{4,3,2,1,0:T(8,128)S(1)}, f32[2,1,2,8,128]{4,3,2,1,0:T(8,128)}, u32[]{:S(2)}) copy-start(f32[2,1,2,8,128]{4,3,2,1,0:T(8,128)} %param.16) | copy-start | bytes 49156
  1.4 11.8 %copy-start.10 = (s32[32,32]{1,0:T(8,128)S(1)}, s32[32,32]{1,0:T(8,128)}, u32[]{:S(2)}) copy-start(s32[32,32]{1,0:T(8,128)} %param.19) | copy-start | bytes 12292
  1.5 16.6 %collective-permute-start.12 = (f32[16,128]{1,0:T(8,128)S(1)}, f32[16,128]{1,0:T(8,128)S(1)}, u32[]{:S(2)}, u32[]{:S(2)}) collective-permute-start(f32[16,128]{1,0:T(8,128)S(1)} %select_maximum_fusion.6), channel_id=1, source_target_pairs={{0,11},{1,8},{2,9},{3,10},{4,15},{5,12},{6,13},{7,14},{8,19},{9,16... | collective-permute-start | bytes 24584 | tf_op jit(solution)/shard_map/ppermute | solution.py:513
  4.9 15.1 %collective-permute-start.15 = (f32[16,128]{1,0:T(8,128)S(1)}, f32[16,128]{1,0:T(8,128)S(1)}, u32[]{:S(2)}, u32[]{:S(2)}) collective-permute-start(f32[16,128]{1,0:T(8,128)S(1)} %select_maximum_fusion.6), channel_id=1, source_target_pairs={{0,15},{1,12},{2,13},{3,14},{4,11},{5,8},{6,9},{7,10},{8,23},{9,20... | collective-permute-start | bytes 24584 | tf_op jit(solution)/shard_map/ppermute | solution.py:513
  7.7 5.8 %copy-start.12 = (s32[32]{0:T(128)S(1)}, s32[32]{0:T(128)}, u32[]{:S(2)}) copy-start(s32[32]{0:T(128)} %param.18) | copy-start | bytes 388
  7.7 25.7 %copy-start.11 = (s32[2,1,2,8]{3,2,1,0:T(2,128)S(1)}, s32[2,1,2,8]{3,2,1,0:T(2,128)}, u32[]{:S(2)}) copy-start(s32[2,1,2,8]{3,2,1,0:T(2,128)} %param.17) | copy-start | bytes 388
  7.7 28.4 %copy-start.5 = (f32[8,128]{1,0:T(8,128)S(1)}, f32[8,128]{1,0:T(8,128)}, u32[]{:S(2)}) copy-start(f32[8,128]{1,0:T(8,128)} %refs_29_.1) | copy-start | bytes 12292
  7.7 28.4 %copy-start.6 = (f32[3,128]{1,0:T(4,128)S(1)}, f32[3,128]{1,0:T(4,128)}, u32[]{:S(2)}) copy-start(f32[3,128]{1,0:T(4,128)} %refs_30_.1) | copy-start | bytes 4612
  7.8 11.3 %collective-permute-start.13 = (f32[16,128]{1,0:T(8,128)S(1)}, f32[16,128]{1,0:T(8,128)S(1)}, u32[]{:S(2)}, u32[]{:S(2)}) collective-permute-start(f32[16,128]{1,0:T(8,128)S(1)} %select_maximum_fusion.5), channel_id=1, source_target_pairs={{0,9},{1,10},{2,11},{3,8},{4,13},{5,14},{6,15},{7,12},{8,17},{9,18... | collective-permute-start | bytes 24584 | tf_op jit(solution)/shard_map/ppermute | solution.py:513
  8.8 14.4 %collective-permute-start.16 = (f32[16,128]{1,0:T(8,128)S(1)}, f32[16,128]{1,0:T(8,128)S(1)}, u32[]{:S(2)}, u32[]{:S(2)}) collective-permute-start(f32[16,128]{1,0:T(8,128)S(1)} %select_maximum_fusion.5), channel_id=1, source_target_pairs={{0,13},{1,14},{2,15},{3,12},{4,9},{5,10},{6,11},{7,8},{8,21},{9,22... | collective-permute-start | bytes 24584 | tf_op jit(solution)/shard_map/ppermute | solution.py:513
  8.9 27.2 %copy-start.4 = (f32[128,128]{1,0:T(8,128)S(1)}, f32[128,128]{1,0:T(8,128)}, u32[]{:S(2)}) copy-start(f32[128,128]{1,0:T(8,128)} %refs_28_.1) | copy-start | bytes 196612
  8.9 5.7 %collective-permute-start.10 = (f32[16,128]{1,0:T(8,128)S(1)}, f32[16,128]{1,0:T(8,128)S(1)}, u32[]{:S(2)}, u32[]{:S(2)}) collective-permute-start(f32[16,128]{1,0:T(8,128)S(1)} %select_maximum_fusion.7), channel_id=1, source_target_pairs={{0,29},{1,30},{2,31},{3,28},{4,25},{5,26},{6,27},{7,24},{8,5},{9,6... | collective-permute-start | bytes 24584 | tf_op jit(solution)/shard_map/ppermute | solution.py:513
  13.2 22.9 %copy-start.3 = (f32[128,128]{1,0:T(8,128)S(1)}, f32[128,128]{1,0:T(8,128)}, u32[]{:S(2)}) copy-start(f32[128,128]{1,0:T(8,128)} %refs_27_.1) | copy-start | bytes 196612
  13.5 22.6 %copy-start.2 = (f32[256,128]{1,0:T(8,128)S(1)}, f32[256,128]{1,0:T(8,128)}, u32[]{:S(2)}) copy-start(f32[256,128]{1,0:T(8,128)} %refs_32_.1) | copy-start | bytes 393220
  13.5 22.6 %copy-start.1 = (f32[128,256]{1,0:T(8,128)S(1)}, f32[128,256]{1,0:T(8,128)}, u32[]{:S(2)}) copy-start(f32[128,256]{1,0:T(8,128)} %refs_31_.1) | copy-start | bytes 393220
  14.6 11.3 %collective-permute-start.7 = (f32[16,128]{1,0:T(8,128)S(1)}, f32[16,128]{1,0:T(8,128)S(1)}, u32[]{:S(2)}, u32[]{:S(2)}) collective-permute-start(f32[16,128]{1,0:T(8,128)S(1)} %select_maximum_fusion.7), channel_id=1, source_target_pairs={{0,25},{1,26},{2,27},{3,24},{4,29},{5,30},{6,31},{7,28},{8,1},{9,2... | collective-permute-start | bytes 24584 | tf_op jit(solution)/shard_map/ppermute | solution.py:513
  18.1 5.7 %collective-permute-start.6 = (f32[16,128]{1,0:T(8,128)S(1)}, f32[16,128]{1,0:T(8,128)S(1)}, u32[]{:S(2)}, u32[]{:S(2)}) collective-permute-start(f32[16,128]{1,0:T(8,128)S(1)} %select_maximum_fusion.8), channel_id=1, source_target_pairs={{0,27},{1,24},{2,25},{3,26},{4,31},{5,28},{6,29},{7,30},{8,3},{9,0... | collective-permute-start | bytes 24584 | tf_op jit(solution)/shard_map/ppermute | solution.py:513
  19.1 6.8 %collective-permute-start.9 = (f32[16,128]{1,0:T(8,128)S(1)}, f32[16,128]{1,0:T(8,128)S(1)}, u32[]{:S(2)}, u32[]{:S(2)}) collective-permute-start(f32[16,128]{1,0:T(8,128)S(1)} %select_maximum_fusion.8), channel_id=1, source_target_pairs={{0,31},{1,28},{2,29},{3,30},{4,27},{5,24},{6,25},{7,26},{8,7},{9,4... | collective-permute-start | bytes 24584 | tf_op jit(solution)/shard_map/ppermute | solution.py:513
  20.1 11.4 %collective-permute-start.11 = (f32[24,128]{1,0:T(8,128)S(1)}, f32[24,128]{1,0:T(8,128)S(1)}, u32[]{:S(2)}, u32[]{:S(2)}) collective-permute-start(f32[24,128]{1,0:T(8,128)S(1)} %select_maximum_fusion.1), channel_id=1, source_target_pairs={{0,8},{1,9},{2,10},{3,11},{4,12},{5,13},{6,14},{7,15},{8,16},{9,17... | collective-permute-start | bytes 36872 | tf_op jit(solution)/shard_map/ppermute | solution.py:513
  23.2 8.4 %collective-permute-start.14 = (f32[24,128]{1,0:T(8,128)S(1)}, f32[24,128]{1,0:T(8,128)S(1)}, u32[]{:S(2)}, u32[]{:S(2)}) collective-permute-start(f32[24,128]{1,0:T(8,128)S(1)} %select_maximum_fusion.1), channel_id=1, source_target_pairs={{0,12},{1,13},{2,14},{3,15},{4,8},{5,9},{6,10},{7,11},{8,20},{9,21... | collective-permute-start | bytes 36872 | tf_op jit(solution)/shard_map/ppermute | solution.py:513
  23.8 4.8 %collective-permute-start = (f32[24,128]{1,0:T(8,128)S(1)}, f32[24,128]{1,0:T(8,128)S(1)}, u32[]{:S(2)}, u32[]{:S(2)}) collective-permute-start(f32[24,128]{1,0:T(8,128)S(1)} %select_maximum_fusion.4), channel_id=1, source_target_pairs={{0,3},{1,0},{2,1},{3,2},{4,7},{5,4},{6,5},{7,6},{8,11},{9,8},{10,9... | collective-permute-start | bytes 36872 | tf_op jit(solution)/shard_map/ppermute | solution.py:513
  25.8 3.5 %collective-permute-start.1 = (f32[24,128]{1,0:T(8,128)S(1)}, f32[24,128]{1,0:T(8,128)S(1)}, u32[]{:S(2)}, u32[]{:S(2)}) collective-permute-start(f32[24,128]{1,0:T(8,128)S(1)} %select_maximum_fusion.3), channel_id=1, source_target_pairs={{0,1},{1,2},{2,3},{3,0},{4,5},{5,6},{6,7},{7,4},{8,9},{9,10},{10,1... | collective-permute-start | bytes 36872 | tf_op jit(solution)/shard_map/ppermute | solution.py:513
  25.9 7.6 %collective-permute-start.3 = (f32[24,128]{1,0:T(8,128)S(1)}, f32[24,128]{1,0:T(8,128)S(1)}, u32[]{:S(2)}, u32[]{:S(2)}) collective-permute-start(f32[24,128]{1,0:T(8,128)S(1)} %select_maximum_fusion.4), channel_id=1, source_target_pairs={{0,7},{1,4},{2,5},{3,6},{4,3},{5,0},{6,1},{7,2},{8,15},{9,12},{10,... | collective-permute-start | bytes 36872 | tf_op jit(solution)/shard_map/ppermute | solution.py:513
  28.6 4.9 %collective-permute-start.4 = (f32[24,128]{1,0:T(8,128)S(1)}, f32[24,128]{1,0:T(8,128)S(1)}, u32[]{:S(2)}, u32[]{:S(2)}) collective-permute-start(f32[24,128]{1,0:T(8,128)S(1)} %select_maximum_fusion.3), channel_id=1, source_target_pairs={{0,5},{1,6},{2,7},{3,4},{4,1},{5,2},{6,3},{7,0},{8,13},{9,14},{10,... | collective-permute-start | bytes 36872 | tf_op jit(solution)/shard_map/ppermute | solution.py:513
  29.3 4.2 %collective-permute-start.5 = (f32[24,128]{1,0:T(8,128)S(1)}, f32[24,128]{1,0:T(8,128)S(1)}, u32[]{:S(2)}, u32[]{:S(2)}) collective-permute-start(f32[24,128]{1,0:T(8,128)S(1)} %select_maximum_fusion.2), channel_id=1, source_target_pairs={{0,24},{1,25},{2,26},{3,27},{4,28},{5,29},{6,30},{7,31},{8,0},{9,1... | collective-permute-start | bytes 36872 | tf_op jit(solution)/shard_map/ppermute | solution.py:513
  31.5 4.6 %collective-permute-start.8 = (f32[24,128]{1,0:T(8,128)S(1)}, f32[24,128]{1,0:T(8,128)S(1)}, u32[]{:S(2)}, u32[]{:S(2)}) collective-permute-start(f32[24,128]{1,0:T(8,128)S(1)} %select_maximum_fusion.2), channel_id=1, source_target_pairs={{0,28},{1,29},{2,30},{3,31},{4,24},{5,25},{6,26},{7,27},{8,4},{9,5... | collective-permute-start | bytes 36872 | tf_op jit(solution)/shard_map/ppermute | solution.py:513
  31.6 4.5 %collective-permute-start.2 = (f32[40,128]{1,0:T(8,128)S(1)}, f32[40,128]{1,0:T(8,128)S(1)}, u32[]{:S(2)}, u32[]{:S(2)}) collective-permute-start(f32[40,128]{1,0:T(8,128)S(1)} %select_maximum_fusion.refs_0_), channel_id=1, source_target_pairs={{0,4},{1,5},{2,6},{3,7},{4,0},{5,1},{6,2},{7,3},{8,12},{9,13},{10,... | collective-permute-start | bytes 61448 | tf_op jit(solution)/shard_map/ppermute | solution.py:513
  33.5 2.7 %copy-start.7 = (f32[5]{0:T(128)S(1)}, f32[5]{0:T(128)}, u32[]{:S(2)}) copy-start(f32[5]{0:T(128)} %refs_25_.1) | copy-start | bytes 64
  33.5 2.7 %copy-start.8 = (f32[5]{0:T(128)S(1)}, f32[5]{0:T(128)}, u32[]{:S(2)}) copy-start(f32[5]{0:T(128)} %refs_26_.1) | copy-start | bytes 64
  33.5 2.7 %copy-start.9 = (f32[128]{0:T(128)S(1)}, f32[128]{0:T(128)}, u32[]{:S(2)}) copy-start(f32[128]{0:T(128)} %param.28) | copy-start | bytes 1540
  41.7 10.2 %all-to-all-start = ((f32[32,4,128]{2,1,0:T(4,128)}), f32[32,4,128]{2,1,0:T(4,128)S(1)}, u32[]{:S(2)}, u32[]{:S(2)}) async-start(f32[32,4,128]{2,1,0:T(4,128)} %get-tuple-element.6), calls=%async_computation | async-start | bytes 131072 | tf_op jit(solution)/shard_map/all_to_all | solution.py:557

commit v4 on v2

--- a/solution.py
+++ b/solution.py
@@ -115,11 +115,58 @@
     return jnp.where(rows < spans[0] * spans[1] * spans[2] * sites, target, -1)
 
 
+def frame_places(count, kind):
+    places = []
+    for p in range(count + 2):
+        if p < 1:
+            places.append((kind - 1, count - 1))
+        elif p > count:
+            places.append((1, 0))
+        else:
+            places.append((0, p - 1))
+    return places
+
+
+def plane_cells(cells, kinds):
+    sides = [list(dict.fromkeys(frame_places(cells[i], kinds[i]))) for i in (1, 2)]
+    return [(y, z) for y in sides[0] for z in sides[1]]
+
+
+def axis_place(place_ref, axis, step, size):
+    moved = place_ref[axis] + (step if step < 2 else -1)
+    moved = jnp.where(moved >= size, moved - size, moved)
+    return jnp.where(moved < 0, moved + size, moved)
+
+
+def plane_kernel(cells, axes, kinds, place_ref, group_ref, slabs_ref, send_ref):
+    sites = 8
+    owned = cells[0] * cells[1] * cells[2] * sites
+    plane = plane_cells(cells, kinds)
+    slabs_ref[...] = jnp.zeros(slabs_ref.shape, F32)
+    for j, ((y, inside_y), (z, inside_z)) in enumerate(plane):
+        member = axis_place(place_ref, 1, y, axes[1]) * axes[2] + axis_place(
+            place_ref, 2, z, axes[2]
+        )
+        for x in range(cells[0]):
+            cell = (x * cells[1] + inside_y) * cells[2] + inside_z
+            slabs_ref[x, j * sites : (j + 1) * sites, :] = group_ref[
+                pl.ds(member, 1), cell * sites : (cell + 1) * sites, :
+            ][0]
+            row = len(plane) * sites + j
+            slabs_ref[x, row : row + 1, :] = group_ref[
+                pl.ds(member, 1), owned + cell : owned + cell + 1, :
+            ][0]
+    for x in range(axes[0]):
+        send_ref[x] = slabs_ref[0]
+    send_ref[pl.ds(axis_place(place_ref, 0, 1, axes[0]), 1)] = slabs_ref[cells[0] - 1 :]
+
+
 def force_kernel(
     cells,
     axes,
     kinds,
-    gathered_ref,
+    slabs_ref,
+    around_ref,
     place_ref,
     own_ref,
     near_row_ref,
@@ -148,7 +195,6 @@
     radial = basis_weight_ref.shape[0]
     spans = [count + 2 for count in cells]
     sites = frame // (spans[0] * spans[1] * spans[2])
-    stride = gathered_ref.shape[0] // (axes[0] * axes[1] * axes[2])
     span = GROUP * nbr
     groups = owned // GROUP
     wide = GROUP * ORDERS
@@ -156,32 +202,29 @@
     root_three = math.sqrt(3.0)
     root_fifteen = math.sqrt(15.0)
     root_five = math.sqrt(5.0)
-    here = [place_ref[i] for i in range(3)]
-
-    def shifted(axis, step):
-        moved = here[axis] + step
-        size = axes[axis]
-        moved = jnp.where(moved >= size, moved - size, moved)
-        return jnp.where(moved < 0, moved + size, moved)
-
-    steps = [[shifted(axis, step) for step in (-1, 0, 1)] for axis in range(3)]
-
     def device(x, y, z):
-        return (steps[0][x + 1] * axes[1] + steps[1][y + 1]) * axes[2] + steps[2][z + 1]
+        where = [axis_place(place_ref, i, step, axes[i]) for i, step in enumerate((x, y, z))]
+        return (where[0] * axes[1] + where[1]) * axes[2] + where[2]
 
     tile_lane = lax.broadcasted_iota(jnp.int32, (sites, 128), 1)
     tile_row = lax.broadcasted_iota(jnp.int32, (sites, 128), 0)
     keep = (tile_lane % sites == tile_row) & (tile_lane < 3 * sites)
     component = tile_lane // sites
+    plane = plane_cells(cells, kinds)
+    beside = [axis_place(place_ref, 0, step, axes[0]) for step in range(3)]
     for cell in range(spans[0] * spans[1] * spans[2]):
         place = (cell // (spans[1] * spans[2]), cell // spans[2] % spans[1], cell % spans[2])
-        step = [(p > c) * 1 - (p < 1) * 1 for p, c in zip(place, cells)]
-        inside = [(p - 1) % c for p, c in zip(place, cells)]
-        local_cell = (inside[0] * cells[1] + inside[1]) * cells[2] + inside[2]
-        base = device(*step) * stride
-        start = pl.multiple_of(base + local_cell * sites, 8)
-        feats_ref[cell * sites : (cell + 1) * sites, :] = gathered_ref[pl.ds(start, sites), :]
-        row = gathered_ref[pl.ds(base + (owned + local_cell), 1), :]
+        around = [frame_places(c, k)[p] for p, c, k in zip(place, cells, kinds)]
+        index = plane.index((around[1], around[2]))
+        tile = slice(index * sites, (index + 1) * sites)
+        mark = slice(len(plane) * sites + index, len(plane) * sites + index + 1)
+        if around[0][0] == 0:
+            feats = slabs_ref[around[0][1], tile, :]
+            row = slabs_ref[around[0][1], mark, :]
+        else:
+            feats = around_ref[pl.ds(beside[around[0][0]], 1), tile, :][0]
+            row = around_ref[pl.ds(beside[around[0][0]], 1), mark, :][0]
+        feats_ref[cell * sites : (cell + 1) * sites, :] = feats
         corner = [np.float32(p) * np.float32(CELL_SIDE) for p in place]
         offset = jnp.where(
             component == 0, corner[0], jnp.where(component == 1, corner[1], corner[2])
@@ -419,24 +462,25 @@
 
     parts_ref[...] = jnp.zeros(parts_ref.shape, F32)
     per_tile = 128 // owned
-    half = ORDERS // 2
+    quarter = parts_ref.shape[1]
     padding = -count % per_tile * owned
     if padding:
         totals = jnp.concatenate([totals, jnp.zeros((ORDERS, padding), F32)], axis=1)
-    lane = lax.broadcasted_iota(jnp.int32, (half, 128), 1)
+    lane = lax.broadcasted_iota(jnp.int32, (quarter, 128), 1)
     for block in range(count):
         choice = (block // (kinds[1] * kinds[2]), block // kinds[2] % kinds[1], block % kinds[2])
-        step = [-1 if c == 2 else c for c in choice]
         column = block // per_tile * 128
         tile = totals[:, column : column + 128]
         if block == 0:
             tile = tile + center_terms
-        turn = block % per_tile * owned
-        first = tile[:half] if turn == 0 else pltpu.roll(tile[:half], 128 - turn, 1)
-        back = (128 - turn + owned) % 128
-        second = tile[half:] if back == 0 else pltpu.roll(tile[half:], back, 1)
-        packed = jnp.where(lane < owned, first, jnp.where(lane < 2 * owned, second, 0.0))
-        parts_ref[pl.ds(device(*step), 1)] = packed[None]
+        packed = jnp.zeros((quarter, 128), F32)
+        for part in range(12 // quarter):
+            turn = (part - block % per_tile) * owned % 128
+            rows = tile[part * quarter : (part + 1) * quarter]
+            rows = pltpu.roll(rows, turn, 1) if turn else rows
+            mine = (lane >= part * owned) & (lane < (part + 1) * owned)
+            packed = jnp.where(mine, rows, packed)
+        parts_ref[pl.ds(device(*choice), 1)] = packed[None]
 
 
 def local(
@@ -459,8 +503,7 @@
     names = ("gx", "gy", "gz")
     cells_x, cells_y, cells_z, sites, width = features.shape
     cells = (cells_x, cells_y, cells_z)
-    cell_count = cells_x * cells_y * cells_z
-    owned = cell_count * sites
+    owned = cells_x * cells_y * cells_z * sites
     frame_count = (cells_x + 2) * (cells_y + 2) * (cells_z + 2) * sites
     axes = tuple(lax.axis_size(name) for name in names)
     kinds = tuple(min(3, size) for size in axes)
@@ -468,26 +511,41 @@
     pairs = neighbours.size
     nbr = pairs // owned
 
+    place = jnp.stack([lax.axis_index(name) for name in names]).astype(jnp.int32)
+    vmem = pl.BlockSpec(memory_space=pltpu.VMEM)
+    smem = pl.BlockSpec(memory_space=pltpu.SMEM)
+    cell_count = cells_x * cells_y * cells_z
     coords = jnp.transpose(positions, (1, 2, 3, 0, 4)).reshape(cell_count, 3 * sites)
     coords = jnp.pad(coords, ((0, -cell_count % 8), (0, width - 3 * sites)))
     payload = jnp.concatenate([features.reshape(owned, width), coords], axis=0)
-    gathered = lax.all_gather(payload, names, tiled=True)
+    payload = jnp.broadcast_to(payload[None], (axes[1] * axes[2], *payload.shape))
+    group = lax.all_to_all(payload, ("gy", "gz"), split_axis=0, concat_axis=0, tiled=True)
+    plane = len(plane_cells(cells, kinds))
+    height = plane * sites + plane + -plane % 8
+    slabs, send = pl.pallas_call(
+        functools.partial(plane_kernel, cells, axes, kinds),
+        out_shape=(
+            jax.ShapeDtypeStruct((cells_x, height, width), F32),
+            jax.ShapeDtypeStruct((axes[0], height, width), F32),
+        ),
+        in_specs=[smem, vmem],
+        out_specs=(vmem, vmem),
+        name="x_slabs",
+    )(place, group)
+    around = lax.all_to_all(send, "gx", split_axis=0, concat_axis=0, tiled=True)
 
     near_row = neighbours.reshape(1, pairs)
     rows = center_rows(centers, cells, sites)
     center_row = jnp.broadcast_to(rows[:, None], (owned, nbr)).reshape(1, pairs)
     center_slot = jnp.broadcast_to(centers[:, None], (owned, nbr)).reshape(1, pairs)
     target_row = target_rows(near_row, cells, sites, kinds)
-    place = jnp.stack([lax.axis_index(name) for name in names]).astype(jnp.int32)
-    vmem = pl.BlockSpec(memory_space=pltpu.VMEM)
-    smem = pl.BlockSpec(memory_space=pltpu.SMEM)
     parts, energy = pl.pallas_call(
         functools.partial(force_kernel, cells, axes, kinds),
         out_shape=(
-            jax.ShapeDtypeStruct((devices, 8, 128), F32),
+            jax.ShapeDtypeStruct((devices, 4, 128), F32),
             jax.ShapeDtypeStruct((1, owned), F32),
         ),
-        in_specs=[vmem, smem] + [vmem] * 6 + [smem] * 2 + [vmem] * 7,
+        in_specs=[vmem] * 2 + [smem] + [vmem] * 6 + [smem] * 2 + [vmem] * 7,
         out_specs=(vmem, vmem),
         scratch_shapes=[
             pltpu.VMEM((frame_count, width), F32),
@@ -496,7 +554,8 @@
         compiler_params=pltpu.CompilerParams(vmem_limit_bytes=40 * 1024 * 1024),
         name="pair_forces",
     )(
-        gathered,
+        slabs,
+        around,
         place,
         features.reshape(owned, width),
         near_row,
@@ -516,7 +575,9 @@
     )
     returned = lax.all_to_all(parts, names, split_axis=0, concat_axis=0, tiled=True)
     summed = jnp.sum(returned, axis=0)
-    terms = jnp.concatenate([summed[:, :owned], summed[:, owned : 2 * owned]], axis=0)
+    terms = jnp.concatenate(
+        [summed[:, :owned], summed[:, owned : 2 * owned], summed[:, 2 * owned : 3 * owned]], axis=0
+    )
     forces = terms[0:3].reshape(3, cells_x, cells_y, cells_z, sites)
     virial = terms[3:12].reshape(9, cells_x, cells_y, cells_z, sites)
     site_energy = energy.reshape(cells_x, cells_y, cells_z, sites)

time: 66.8 us -> 45.6 us (0.68)
  blocking collectives: 45.1 us -> 0 us
  starting transfers between devices: 2.56 us -> 12.9 us
  waiting for transfers between devices: 6.39 us -> 14.7 us
  local copies, waits for them, and re-layouts: 5.14 us -> 8 us
  Pallas kernels: 5.54 us -> 7.19 us
    all_gather x1 -> x0, blocking collectives: 45.1 us -> none  [local(): gathered = lax.all_gather(payload, names, tiled=True)]
    all_to_all x0 -> x2, starting transfers between devices: none -> 10.3 us  [the longest x1 5.3 us: local(): lax.all_to_all(payload, ('gy', 'gz'), split_axis=0, concat_axis=0, tiled=...]
    all_to_all x0 -> x2, waiting for transfers between devices: none -> 9.12 us  [the longest x1 6.1 us: local(): around = lax.all_to_all(send, 'gx', split_axis=0, concat_axis=0, tiled=True)]
    pallas_call x0 -> x1, Pallas kernels: none -> 1.67 us  [local(): pl.pallas_call(functools.partial(plane_kernel, cells, axes, kinds), out_s...]
    unnamed x28 -> x32, local copies, waits for them, and re-layouts: 1.97 us -> 3.47 us
    all_to_all x1, waiting for transfers between devices: 6.39 us -> 5.57 us  [local(): lax.all_to_all(parts, names, split_axis=0, concat_axis=0, tiled=True)]
    transpose x1, local copies, waits for them, and re-layouts: 0.01 us -> 0.7 us  [local(): jnp.transpose(positions, (1, 2, 3, 0, 4)).reshape(cell_count, 3 * sites)]
    broadcast_in_dim x0 -> x1, local copies, waits for them, and re-layouts: none -> 0.67 us  [local(): jnp.broadcast_to(payload[None], (axes[1] * axes[2], *payload.shape))]
  transfers between devices with their start and end apart: 1 -> 3, of which waited for: 1 -> 3; matrix products, arithmetic and copies ran while one was open for 3% -> 7% of each run, Pallas kernels for 0% -> 0%
where the time goes in v4:
time: 45.6 us; the launch traced here: 45 us
  waiting for transfers between devices  14.7 us (32%)
  starting transfers between devices  12.9 us (28%)
  local copies, waits for them, and re-layouts  8 us (18%)
  Pallas kernels  7.19 us (16%)
  other arithmetic  1.51 us (3%)
  between operations  0.75 us (2%)
    all_to_all x1, waiting for transfers between devices, local(): around = lax.all_to_all(send, 'gx', split_axis=0, concat_axis=0, tiled=True)  6.1 us
    all_to_all x1, waiting for transfers between devices, local(): lax.all_to_all(parts, names, split_axis=0, concat_axis=0, tiled=True)  5.57 us
    pallas_call x1, Pallas kernels, local(): pl.pallas_call(functools.partial(force_kernel, cells, axes, kinds), out_s...  5.52 us
    all_to_all x1, starting transfers between devices, local(): lax.all_to_all(payload, ('gy', 'gz'), split_axis=0, concat_axis=0, tiled=...  5.3 us
    all_to_all x1, starting transfers between devices, local(): around = lax.all_to_all(send, 'gx', split_axis=0, concat_axis=0, tiled=True)  5.01 us
    unnamed x32, local copies, waits for them, and re-layouts  3.47 us
    all_to_all x1, waiting for transfers between devices, local(): lax.all_to_all(payload, ('gy', 'gz'), split_axis=0, concat_axis=0, tiled=...  3.02 us
    all_to_all x1, starting transfers between devices, local(): lax.all_to_all(parts, names, split_axis=0, concat_axis=0, tiled=True)  2.56 us
  transfers between devices with their start and end apart: 3, of which 3 were waited for; matrix products, arithmetic and copies ran while one was open for 7% of the time, Pallas kernels for 0%

profile of v4, /device:TPU:0, one launch (start us, length us, event | category | flops | bytes accessed | tf_op | source)
XLA Modules:
  0.0 45.0 jit_solution(9817351834654940515)
XLA Ops:
  0.6 0.7 %copy.21 = f32[2,1,2,3,8]{4,3,2,0,1:T(4,128)S(1)} copy(f32[2,1,2,3,8]{4,2,1,0,3:T(2,128)} %bitcast.17) | data formatting | bytes 768 | tf_op jit(solution)/shard_map/transpose | solution.py:518
  1.3 0.1 reshape.456
  1.4 0.7 %broadcast_in_dim.45 = f32[8,40,128]{2,1,0:T(8,128)} broadcast(f32[40,128]{1,0:T(8,128)S(1)} %select_maximum_fusion), dimensions={1,2} | broadcast | bytes 184320 | tf_op jit(solution)/shard_map/broadcast_in_dim | solution.py:521
  2.1 5.3 %all-to-all-start = ((f32[8,40,128]{2,1,0:T(8,128)}), f32[8,40,128]{2,1,0:T(8,128)S(1)}, u32[]{:S(2)}, u32[]{:S(2)}) async-start(f32[8,40,128]{2,1,0:T(8,128)} %broadcast_in_dim.45), calls=%async_computation | async-start | bytes 327680 | tf_op jit(solution)/shard_map/all_to_all | solution.py:522
  7.5 0.7 %copy-done.13 = s32[32,32]{1,0:T(8,128)S(1)} copy-done((s32[32,32]{1,0:T(8,128)S(1)}, s32[32,32]{1,0:T(8,128)}, u32[]{:S(2)}) %copy-start.13) | copy-done | bytes 4120
  8.1 0.1 reshape.457.near_row_ref
  8.2 0.1 broadcast_in_dim.48
  8.3 0.1 reshape.458.center_row_ref
  8.4 0.1 broadcast_in_dim.49
  8.4 0.1 reshape.459.center_slot_ref
  8.5 0.6 %copy-done.14 = s32[2,1,2,8]{3,2,1,0:T(2,128)S(1)} copy-done((s32[2,1,2,8]{3,2,1,0:T(2,128)S(1)}, s32[2,1,2,8]{3,2,1,0:T(2,128)}, u32[]{:S(2)}) %copy-start.14) | copy-done | bytes 152
  9.1 0.1 reshape.460.species_ref
  9.2 0.6 %pad_add_fusion.place_ref = s32[3]{0:T(128)} fusion(s32[1]{0:T(128)} %bitcast.2, s32[1]{0:T(128)} %bitcast.1, s32[1]{0:T(128)} %bitcast), kind=kLoop, calls=%fused_computation.48 | loop fusion | flops 6 | bytes 24 | tf_op jit(solution)/shard_map/stack | solution.py:514
  9.8 3.0 %all-to-all-done.group_ref = f32[8,40,128]{2,1,0:T(8,128)S(1)} async-done(((f32[8,40,128]{2,1,0:T(8,128)}), f32[8,40,128]{2,1,0:T(8,128)S(1)}, u32[]{:S(2)}, u32[]{:S(2)}) %all-to-all-start) | async-done | bytes 163872 | tf_op jit(solution)/shard_map/all_to_all | solution.py:522
  12.9 0.7 %copy-done.12 = f32[8,40,128]{2,1,0:T(8,128)} copy-done((f32[8,40,128]{2,1,0:T(8,128)}, f32[8,40,128]{2,1,0:T(8,128)S(1)}, u32[]{:S(2)}) %copy-start.12) | copy-done | bytes 163864
  13.5 1.7 %x_slabs.1 = (f32[2,72,128]{2,1,0:T(8,128)}, f32[4,72,128]{2,1,0:T(8,128)}) custom-call(s32[3]{0:T(128)} %pad_add_fusion.place_ref, f32[8,40,128]{2,1,0:T(8,128)} %copy-done.12), custom_call_target="tpu_custom_call" | custom-call | tf_op jit(solution)/shard_map/x_slabs/pallas_call | solution.py:525
  15.2 5.0 %all-to-all-start.1 = ((f32[4,72,128]{2,1,0:T(8,128)}), f32[4,72,128]{2,1,0:T(8,128)S(1)}, u32[]{:S(2)}, u32[]{:S(2)}) async-start(f32[4,72,128]{2,1,0:T(8,128)} %get-tuple-element.8), calls=%async_computation.1 | async-start | bytes 294912 | tf_op jit(solution)/shard_map/all_to_all | solution.py:535
  20.2 0.1 compare_select_fusion.target_row_ref
  20.4 6.1 %all-to-all-done.1.around_ref = f32[4,72,128]{2,1,0:T(8,128)S(1)} async-done(((f32[4,72,128]{2,1,0:T(8,128)}), f32[4,72,128]{2,1,0:T(8,128)S(1)}, u32[]{:S(2)}, u32[]{:S(2)}) %all-to-all-start.1) | async-done | bytes 147488 | tf_op jit(solution)/shard_map/all_to_all | solution.py:535
  26.5 0.6 %copy-done.6 = s32[3]{0:T(128)S(1)} copy-done((s32[3]{0:T(128)S(1)}, s32[3]{0:T(128)}, u32[]{:S(2)}) %copy-start.6) | copy-done | bytes 36
  27.1 0.0 copy-done.9
  27.1 0.0 copy-done.10
  27.1 0.9 %copy-done.2 = f32[2,72,128]{2,1,0:T(8,128)S(1)} copy-done((f32[2,72,128]{2,1,0:T(8,128)S(1)}, f32[2,72,128]{2,1,0:T(8,128)}, u32[]{:S(2)}) %copy-start.2) | copy-done | bytes 73752
  28.0 5.5 %pair_forces.1 = (f32[32,4,128]{2,1,0:T(4,128)}, f32[1,32]{1,0:T(1,128)S(1)}) custom-call(f32[2,72,128]{2,1,0:T(8,128)S(1)} %copy-done.2, f32[4,72,128]{2,1,0:T(8,128)S(1)} %all-to-all-done.1.around_ref, s32[3]{0:T(128)S(1)} %copy-done.6, f32[32,128]{1,0:T(8,128)S(1)} %bitcast.13, s32[1,1024]{1,0:T(1,128)S(1)} %reshape.457.near_row_ref, ...), custom_call_target="tpu_custom_call" | custom-call | tf_op jit(solution)/shard_map/pair_forces/pallas_call | solution.py:542
  33.5 2.6 %all-to-all-start.2 = ((f32[32,4,128]{2,1,0:T(4,128)}), f32[32,4,128]{2,1,0:T(4,128)S(1)}, u32[]{:S(2)}, u32[]{:S(2)}) async-start(f32[32,4,128]{2,1,0:T(4,128)} %get-tuple-element.10), calls=%async_computation.2 | async-start | bytes 131072 | tf_op jit(solution)/shard_map/all_to_all | solution.py:576
  36.1 0.5 %broadcast.539 = f32[]{:T(128)} broadcast(f32[]{:T(128)} %constant.199), dimensions={} | broadcast | bytes 8 | tf_op jit(solution)/shard_map/pair_forces/pallas_call | solution.py:542
  36.6 0.7 %reduce.3 = f32[32]{0:T(128)S(1)} reduce(f32[1,32]{1,0:T(1,128)S(1)} %get-tuple-element.9, f32[]{:T(128)} %broadcast.539), dimensions={0}, to_apply=%get-tuple-element.9.reduce_sub_computation.3 | reduce | bytes 260 | tf_op jit(solution)/shard_map/pair_forces/pallas_call | solution.py:542
  37.3 0.7 %reshape.462 = f32[2,1,2,8]{3,2,0,1:T(2,128)} reshape(f32[32]{0:T(128)S(1)} %reduce.3) | data formatting | bytes 256 | tf_op jit(solution)/shard_map/reshape | solution.py:583
  37.9 5.6 %all-to-all-done.2 = f32[32,4,128]{2,1,0:T(4,128)S(1)} async-done(((f32[32,4,128]{2,1,0:T(4,128)}), f32[32,4,128]{2,1,0:T(4,128)S(1)}, u32[]{:S(2)}, u32[]{:S(2)}) %all-to-all-start.2) | async-done | bytes 65568 | tf_op jit(solution)/shard_map/all_to_all | solution.py:576
  43.6 0.1 fusion.8
  43.6 0.7 %copy.22 = f32[9,32]{0,1:T(8,128)} copy(f32[9,32]{1,0:T(8,128)S(1)} %pad_maximum_fusion) | data formatting | bytes 2304 | tf_op jit(solution)/shard_map/slice | solution.py:582
  44.3 0.7 %reshape.463 = f32[3,2,1,2,8]{4,3,1,0,2:T(2,128)} reshape(f32[3,32]{1,0:T(4,128)S(1)} %bitcast.15) | data formatting | bytes 768 | tf_op jit(solution)/shard_map/reshape | solution.py:581
  (29 shorter events, 0.1 us)
Async XLA Ops:
  0.6 0.8 %copy-start.5 = (f32[2,1,2,8,128]{4,3,2,1,0:T(8,128)S(1)}, f32[2,1,2,8,128]{4,3,2,1,0:T(8,128)}, u32[]{:S(2)}) copy-start(f32[2,1,2,8,128]{4,3,2,1,0:T(8,128)} %param.16) | copy-start | bytes 49156
  2.1 5.3 %copy-start.15 = (s32[32]{0:T(128)S(1)}, s32[32]{0:T(128)}, u32[]{:S(2)}) copy-start(s32[32]{0:T(128)} %param.18) | copy-start | bytes 388
  2.1 10.7 %all-to-all-start = ((f32[8,40,128]{2,1,0:T(8,128)}), f32[8,40,128]{2,1,0:T(8,128)S(1)}, u32[]{:S(2)}, u32[]{:S(2)}) async-start(f32[8,40,128]{2,1,0:T(8,128)} %broadcast_in_dim.45), calls=%async_computation | async-start | bytes 327680 | tf_op jit(solution)/shard_map/all_to_all | solution.py:522
  7.4 0.7 %copy-start.13 = (s32[32,32]{1,0:T(8,128)S(1)}, s32[32,32]{1,0:T(8,128)}, u32[]{:S(2)}) copy-start(s32[32,32]{1,0:T(8,128)} %param.19) | copy-start | bytes 12292
  8.4 0.7 %copy-start.14 = (s32[2,1,2,8]{3,2,1,0:T(2,128)S(1)}, s32[2,1,2,8]{3,2,1,0:T(2,128)}, u32[]{:S(2)}) copy-start(s32[2,1,2,8]{3,2,1,0:T(2,128)} %param.17) | copy-start | bytes 388
  12.9 0.7 %copy-start.12 = (f32[8,40,128]{2,1,0:T(8,128)}, f32[8,40,128]{2,1,0:T(8,128)S(1)}, u32[]{:S(2)}) copy-start(f32[8,40,128]{2,1,0:T(8,128)S(1)} %all-to-all-done.group_ref) | copy-start | bytes 491524
  13.5 13.0 %copy-start.3 = (f32[128,128]{1,0:T(8,128)S(1)}, f32[128,128]{1,0:T(8,128)}, u32[]{:S(2)}) copy-start(f32[128,128]{1,0:T(8,128)} %center_weight_ref.1) | copy-start | bytes 196612
  13.5 13.0 %copy-start.4 = (f32[128,128]{1,0:T(8,128)S(1)}, f32[128,128]{1,0:T(8,128)}, u32[]{:S(2)}) copy-start(f32[128,128]{1,0:T(8,128)} %near_weight_ref.1) | copy-start | bytes 196612
  15.2 11.3 %copy-start = (f32[128,256]{1,0:T(8,128)S(1)}, f32[128,256]{1,0:T(8,128)}, u32[]{:S(2)}) copy-start(f32[128,256]{1,0:T(8,128)} %value_weight_ref.1) | copy-start | bytes 393220
  15.2 11.3 %copy-start.1 = (f32[256,128]{1,0:T(8,128)S(1)}, f32[256,128]{1,0:T(8,128)}, u32[]{:S(2)}) copy-start(f32[256,128]{1,0:T(8,128)} %latent_weight_ref.1) | copy-start | bytes 393220
  15.2 11.3 %copy-start.11 = (f32[128]{0:T(128)S(1)}, f32[128]{0:T(128)}, u32[]{:S(2)}) copy-start(f32[128]{0:T(128)} %param.28) | copy-start | bytes 1540
  15.2 11.3 %all-to-all-start.1 = ((f32[4,72,128]{2,1,0:T(8,128)}), f32[4,72,128]{2,1,0:T(8,128)S(1)}, u32[]{:S(2)}, u32[]{:S(2)}) async-start(f32[4,72,128]{2,1,0:T(8,128)} %get-tuple-element.8), calls=%async_computation.1 | async-start | bytes 294912 | tf_op jit(solution)/shard_map/all_to_all | solution.py:535
  20.2 6.3 %copy-start.7 = (f32[8,128]{1,0:T(8,128)S(1)}, f32[8,128]{1,0:T(8,128)}, u32[]{:S(2)}) copy-start(f32[8,128]{1,0:T(8,128)} %basis_weight_ref.1) | copy-start | bytes 12292
  20.3 6.2 %copy-start.8 = (f32[3,128]{1,0:T(4,128)S(1)}, f32[3,128]{1,0:T(4,128)}, u32[]{:S(2)}) copy-start(f32[3,128]{1,0:T(4,128)} %path_weight_ref.1) | copy-start | bytes 4612
  26.5 0.6 %copy-start.6 = (s32[3]{0:T(128)S(1)}, s32[3]{0:T(128)}, u32[]{:S(2)}) copy-start(s32[3]{0:T(128)} %pad_add_fusion.place_ref) | copy-start | bytes 40
  26.5 0.7 %copy-start.9 = (f32[5]{0:T(128)S(1)}, f32[5]{0:T(128)}, u32[]{:S(2)}) copy-start(f32[5]{0:T(128)} %scale_ref.1) | copy-start | bytes 64
  26.5 0.7 %copy-start.10 = (f32[5]{0:T(128)S(1)}, f32[5]{0:T(128)}, u32[]{:S(2)}) copy-start(f32[5]{0:T(128)} %shift_ref.1) | copy-start | bytes 64
  27.1 0.9 %copy-start.2 = (f32[2,72,128]{2,1,0:T(8,128)S(1)}, f32[2,72,128]{2,1,0:T(8,128)}, u32[]{:S(2)}) copy-start(f32[2,72,128]{2,1,0:T(8,128)} %get-tuple-element.7.slabs_ref) | copy-start | bytes 221188
  33.5 10.0 %all-to-all-start.2 = ((f32[32,4,128]{2,1,0:T(4,128)}), f32[32,4,128]{2,1,0:T(4,128)S(1)}, u32[]{:S(2)}, u32[]{:S(2)}) async-start(f32[32,4,128]{2,1,0:T(4,128)} %get-tuple-element.10), calls=%async_computation.2 | async-start | bytes 131072 | tf_op jit(solution)/shard_map/all_to_all | solution.py:576

commit v5 on v2

v5 whole, which is shorter than its diff:
```python
import functools
import math

import jax
import jax.numpy as jnp
import numpy as np
from jax import lax
from jax.experimental import pallas as pl
from jax.experimental.pallas import tpu as pltpu
from jax.sharding import PartitionSpec as P

EXACT_DOT = lax.Precision.HIGHEST
CUTOFF = 5.0
CELL_SIDE = 4.6
ROOT_HALF = 0.7071067811865476
GROUP = 8
ORDERS = 16
SITES = 8
OWN_CELLS = 4
FRAME_CELLS = 48
F32 = jnp.float32
BF16 = jnp.bfloat16


def split(value):
    high = value.astype(BF16)
    low = (value - high.astype(F32)).astype(BF16)
    return high, low


def split3(value):
    high = value.astype(BF16)
    rest = value - high.astype(F32)
    middle = rest.astype(BF16)
    low = (rest - middle.astype(F32)).astype(BF16)
    return high, middle, low


def mm(a, b):
    return lax.dot_general(a, b, (((1,), (0,)), ((), ())), preferred_element_type=F32)


def mm_nt(a, b):
    return lax.dot_general(a, b, (((1,), (1,)), ((), ())), preferred_element_type=F32)


def stacked(high, low):
    top = jnp.concatenate([high, high], axis=1)
    bottom = jnp.concatenate([low, jnp.zeros_like(low)], axis=1)
    return jnp.concatenate([top, bottom], axis=0)


def folded(product):
    half = product.shape[0] // 2
    return product[:half] + product[half:]


def half_depth(weights, value):
    return folded(mm(weights, jnp.concatenate(split(value), axis=0)))


def full_depth(both, high, value_high, value_low):
    return folded(mm(both, value_high)) + mm(high, value_low)


def sin_cos_pi(turns):
    near = turns - 2.0 * jnp.round(turns * 0.5)
    quarter = jnp.round(near * 2.0)
    v = (near - 0.5 * quarter) * math.pi
    v2 = v * v
    s = v * (
        1.0
        + v2
        * (-1.0 / 6 + v2 * (1.0 / 120 + v2 * (-1.0 / 5040 + v2 * (1.0 / 362880 - v2 / 39916800))))
    )
    c = 1.0 + v2 * (
        -0.5
        + v2
        * (1.0 / 24 + v2 * (-1.0 / 720 + v2 * (1.0 / 40320 + v2 * (-1.0 / 3628800 + v2 / 479001600))))
    )
    odd = jnp.abs(quarter) == 1.0
    sine = jnp.where(odd, quarter * c, jnp.where(quarter == 0.0, s, -s))
    cosine = jnp.where(odd, -quarter * s, jnp.where(quarter == 0.0, c, -c))
    return sine, cosine


def exact(a, b):
    return jnp.dot(a, b, precision=EXACT_DOT, preferred_element_type=F32)


def list_kernel(kind, centers_ref, neighbours_ref, codes_ref):
    owned, nbr = neighbours_ref.shape
    per_row = 128 // nbr
    chosen = lax.broadcasted_iota(jnp.int32, (owned, owned), 0) == centers_ref[...]
    chosen = jnp.where(chosen, 1.0, 0.0)
    occupied = jnp.sum(chosen, axis=1, keepdims=True) > 0.5
    rows = exact(chosen, neighbours_ref[...].astype(F32)).astype(jnp.int32)
    live = occupied & (rows < FRAME_CELLS * SITES)
    slot = lax.broadcasted_iota(jnp.int32, (owned, nbr), 0)
    cell = slot >> 3
    site = rows & 7
    place = rows >> 3
    near_z = (place & 3) + 1 - 2 * (cell & 1)
    column = place >> 2
    frame_x = (column * 11) >> 5
    frame_y = column - 3 * frame_x
    near_x = frame_x + 1 - 2 * (cell >> 1)
    side = jnp.where(frame_y == 1, 0, jnp.where(frame_y == 2, 1, kind - 1))
    block = (near_z >> 1) * 2 + (near_x >> 1)
    where = (block * kind + side) * owned + (near_x & 1) * 16 + (near_z & 1) * 8 + site
    code = jnp.where(live, 1 + where + (frame_y << 10), 0).astype(F32)
    lane = lax.broadcasted_iota(jnp.int32, (nbr, 128), 1)
    spread = jnp.where(lax.broadcasted_iota(jnp.int32, (nbr, 128), 0) == lane % nbr, 1.0, 0.0)
    wide = exact(code, spread)
    row = lax.broadcasted_iota(jnp.int32, (owned, 128), 0)
    lane = lax.broadcasted_iota(jnp.int32, (owned, 128), 1)
    wide = jnp.where(row % per_row == lane // nbr, wide, 0.0)
    fold = lax.broadcasted_iota(jnp.int32, (owned // per_row, owned), 1) // per_row
    fold = jnp.where(
        fold == lax.broadcasted_iota(jnp.int32, (owned // per_row, owned), 0), 1.0, 0.0
    )
    codes_ref[...] = exact(fold, wide)


def force_kernel(
    kind,
    nbr,
    here_ref,
    next_x_ref,
    next_z_ref,
    center_weight_ref,
    near_weight_ref,
    basis_weight_ref,
    path_weight_ref,
    value_weight_ref,
    latent_weight_ref,
    out_weight_ref,
    totals_ref,
):
    height, width = here_ref.shape
    owned = OWN_CELLS * SITES
    feats_rows = kind * owned
    coord_rows = kind * OWN_CELLS + -kind * OWN_CELLS % 8
    pairs = owned * nbr
    radial = basis_weight_ref.shape[0]
    span = GROUP * nbr
    groups = owned // GROUP
    wide = GROUP * ORDERS
    sites = SITES
    blocks_in = [
        here_ref[...],
        next_x_ref[...],
        next_z_ref[:height],
        next_z_ref[height:],
    ]
    root_count = math.sqrt(nbr)
    root_three = math.sqrt(3.0)
    root_fifteen = math.sqrt(15.0)
    root_five = math.sqrt(5.0)
    feats = jnp.concatenate([block[:feats_rows] for block in blocks_in], axis=0)
    known = feats.shape[0]
    center_feats = []
    coords = []
    scales = []
    codes = []
    cell_row = lax.broadcasted_iota(jnp.int32, (kind * OWN_CELLS, 128), 0) % OWN_CELLS
    tile_lane = lax.broadcasted_iota(jnp.int32, (kind * OWN_CELLS, 128), 1)
    for g, block in enumerate(blocks_in):
        ahead_x, ahead_z = g % 2, g // 2
        cell = (1 - ahead_x) * 2 + 1 - ahead_z
        center_feats.append(block[cell * sites : (cell + 1) * sites])
        rows = block[feats_rows : feats_rows + kind * OWN_CELLS]
        scales.append(rows[cell : cell + 1])
        corner_x = (cell_row // 2 + 2 * ahead_x).astype(F32) * CELL_SIDE
        corner_z = (cell_row % 2 + 2 * ahead_z).astype(F32) * CELL_SIDE
        corner = jnp.where(
            tile_lane < sites, corner_x, jnp.where(tile_lane < 2 * sites, 0.0, corner_z)
        )
        coords.append(rows + corner)
        start = feats_rows + coord_rows + cell * span // 128
        codes.extend(block[start + r : start + r + 1] for r in range(span // 128))
    center_feats = jnp.concatenate(center_feats, axis=0)
    coords = jnp.concatenate(coords, axis=0)
    code = jnp.concatenate(codes, axis=1).astype(jnp.int32)
    live = code > 0
    code = jnp.maximum(code - 1, 0)
    side_y = ((code >> 10) - 1).astype(F32)
    near_row = jnp.where(live, code & 1023, known)

    spread = jnp.broadcast_to(coords[:, None, :], (coords.shape[0], sites, 128))
    spread = spread.reshape(known, 128)
    keep_lane = lax.broadcasted_iota(jnp.int32, (known, 128), 1)
    keep_row = lax.broadcasted_iota(jnp.int32, (known, 128), 0)
    keep = (keep_lane % sites == keep_row % sites) & (keep_lane < 3 * sites)
    spread = jnp.where(keep, spread, 0.0)
    place_parts = jnp.concatenate(split3(jnp.transpose(spread)[: 3 * sites]), axis=0)

    value_t = jnp.transpose(value_weight_ref[...])
    latent_t = jnp.transpose(latent_weight_ref[...])
    value_rows = stacked(*split(value_t))
    latent_high_t, latent_low_t = split(latent_t)
    latent_both_t = jnp.concatenate([latent_high_t, latent_low_t], axis=0)
    latent_rows = stacked(*split(latent_weight_ref[...]))
    value_high, value_low = split(value_weight_ref[...])
    value_both = jnp.concatenate([value_high, value_low], axis=0)
    basis_t = jnp.transpose(basis_weight_ref[...])
    basis_high_t, basis_low_t = split(basis_t)
    basis_rows = stacked(*split(basis_weight_ref[...]))

    def project(weight, rows):
        high, low = split(rows)
        return folded(
            mm_nt(stacked(*split(jnp.transpose(weight))), jnp.concatenate([high, low], axis=1))
        )

    near_t = project(near_weight_ref[...], feats)
    own_t = project(center_weight_ref[...], center_feats)
    near_high, near_low = split(near_t)
    own_high, own_low = split(own_t)
    lookup = jnp.concatenate(
        [
            jnp.concatenate([near_high, own_high, basis_high_t, basis_high_t], axis=1),
            jnp.concatenate([near_low, own_low, basis_low_t, jnp.zeros_like(basis_low_t)], axis=1),
        ],
        axis=0,
    )
    scale_rows = jnp.concatenate(scales, axis=0)
    scale_parts = jnp.concatenate(
        [*split3(scale_rows), jnp.zeros((16 - 3 * groups, 128), BF16)], axis=0
    )

    level = lax.broadcasted_iota(jnp.int32, (ORDERS, width), 0)
    path_rows = jnp.where(
        level == 0,
        path_weight_ref[0:1, :],
        jnp.where(
            level < 4,
            path_weight_ref[1:2, :],
            jnp.where(level < 9, path_weight_ref[2:3, :], 0.0),
        ),
    )
    paths_t = jnp.transpose(jnp.concatenate([path_rows] * GROUP, axis=0)) * (1.0 / root_count)
    out_column = jnp.transpose(jnp.broadcast_to(out_weight_ref[...], (width, width)))
    out_column = jnp.concatenate([out_column] * (pairs // width), axis=1)

    site_ids = lax.broadcasted_iota(jnp.int32, (known, pairs), 0)
    slot_ids = lax.broadcasted_iota(jnp.int32, (owned, pairs), 0)
    slot_row = lax.broadcasted_iota(jnp.int32, (1, pairs), 1) // nbr
    group_row = slot_row // GROUP
    center_cell = (1 - group_row % 2) * 2 + 1 - group_row // 2
    center_row = group_row * feats_rows + center_cell * sites + slot_row % GROUP
    block_row = lax.broadcasted_iota(jnp.int32, (wide, span), 0) // ORDERS
    block_lane = lax.broadcasted_iota(jnp.int32, (wide, span), 1) // nbr
    block_mask = (block_row == block_lane).astype(F32)
    block_half = block_mask.astype(BF16)
    order = lax.broadcasted_iota(jnp.int32, (radial, pairs), 0).astype(F32) + 1.0
    lanes = [slice(g * span, (g + 1) * span) for g in range(groups)]

    pick = jnp.where(site_ids == near_row, 1.0, 0.0)
    from_center = jnp.where(site_ids == center_row, 1.0, 0.0)
    pick_half = pick.astype(BF16)
    center_half = from_center.astype(BF16)
    slot_half = jnp.where(slot_ids == slot_row, 1.0, 0.0).astype(BF16)

    moved = mm(place_parts, (pick - from_center).astype(BF16))
    moved = moved[: 3 * sites] + moved[3 * sites : 6 * sites] + moved[6 * sites :]
    dx = jnp.where(live, jnp.sum(moved[:sites], axis=0, keepdims=True), 6.0)
    dy = jnp.sum(moved[sites : 2 * sites], axis=0, keepdims=True) + CELL_SIDE * side_y
    dy = jnp.where(live, dy, 0.0)
    dz = jnp.where(live, jnp.sum(moved[2 * sites :], axis=0, keepdims=True), 0.0)
    length = jnp.sqrt(dx * dx + dy * dy + dz * dz)
    inverse = 1.0 / length
    ratio = length * (1.0 / CUTOFF)
    inside = live & (ratio < 1.0)
    r2 = ratio * ratio
    r5 = r2 * r2 * ratio
    r6 = r5 * ratio
    weight = jnp.where(inside, 1.0 - r6 * (28.0 - 48.0 * ratio + 21.0 * r2), 0.0)
    slope = jnp.where(inside, -168.0 * r5 * (1.0 - 2.0 * ratio + r2), 0.0)
    sine, cosine = sin_cos_pi(order * ratio)
    basis = (math.sqrt(2.0 / CUTOFF) * inverse) * sine
    basis_slope = (math.sqrt(2.0 / CUTOFF) * inverse) * (
        (math.pi / CUTOFF) * order * cosine - sine * inverse
    )
    ex = dx * inverse
    ey = dy * inverse
    ez = dz * inverse
    angular = jnp.concatenate(
        [
            jnp.ones_like(ex),
            root_three * ex,
            root_three * ey,
            root_three * ez,
            root_fifteen * ex * ey,
            root_fifteen * ey * ez,
            0.5 * root_five * (3.0 * ez * ez - 1.0),
            root_fifteen * ex * ez,
            0.5 * root_fifteen * (ex * ex - ey * ey),
            jnp.zeros((ORDERS - 9, pairs), F32),
        ],
        axis=0,
    )
    angular_high, angular_low = split(angular)
    blocks = [
        jnp.concatenate(
            [
                jnp.concatenate([angular_high[:, cut]] * GROUP, axis=0) * block_half,
                jnp.concatenate([angular_low[:, cut]] * GROUP, axis=0) * block_half,
            ],
            axis=0,
        )
        for cut in lanes
    ]
    lane_ids = lax.broadcasted_iota(jnp.int32, (128, span), 0)
    lane_slot = lax.broadcasted_iota(jnp.int32, (128, span), 1) // nbr + 3 * sites
    scale = mm(scale_parts, jnp.where(lane_ids == lane_slot, 1.0, 0.0).astype(BF16))
    scale = scale[:groups] + scale[groups : 2 * groups] + scale[2 * groups : 3 * groups]
    scale = jnp.concatenate([scale[g : g + 1] for g in range(groups)], axis=1)
    scale = scale * (1.0 / root_count)
    pull = ROOT_HALF * scale

    basis_high, basis_low = split(basis)
    before = folded(
        mm(lookup, jnp.concatenate([pick_half, slot_half, basis_high, basis_low], axis=0))
    )
    gate = 0.5 * jnp.tanh(0.5 * before) + 0.5
    active = before * gate
    latent = weight * active
    mixed = half_depth(value_rows, latent)
    values = mixed[:width]
    env_high, env_low = split(mixed[width:])

    def over_pairs(high, low):
        sums = []
        for cut, block in zip(lanes, blocks):
            quad = mm_nt(jnp.concatenate([high[:, cut], low[:, cut]], axis=0), block)
            sums.append((quad[:width, :wide] + quad[:width, wide:] + quad[width:, :wide]) * paths_t)
        return sums

    def over_orders(tables):
        parts = [folded(mm(stacked(*split(t)), block)) for t, block in zip(tables, blocks)]
        return jnp.concatenate(parts, axis=1)

    weighted = over_pairs(env_high, env_low)
    inner = over_orders(weighted)
    scalars = values * inner
    joined_high, joined_low = split(jnp.concatenate([latent, scalars], axis=0))
    z = full_depth(latent_both_t, latent_high_t, joined_high, joined_low)
    z_gate = 0.5 * jnp.tanh(0.5 * z) + 0.5
    update = z * z_gate
    update_out = update * out_column
    pair_energy = jnp.sum(latent * out_column + weight * update_out, axis=0, keepdims=True)
    pair_energy = pair_energy * pull
    d_z = (pull * weight) * out_column * (z_gate + update * (1.0 - z_gate))
    spread_back = half_depth(latent_rows, d_z)
    d_scalars = spread_back[width:]
    d_values = d_scalars * inner
    dinner_high, dinner_low = split(d_scalars * values)
    d_embed = over_pairs(dinner_high, dinner_low)
    d_env = over_orders(d_embed)

    d_angular = []
    for g, cut in enumerate(lanes):
        sides = jnp.transpose(jnp.concatenate([weighted[g], d_embed[g]], axis=0))
        sides_high, sides_low = split(sides)
        d_block = full_depth(
            jnp.concatenate([sides_high, sides_low], axis=0),
            sides_high,
            jnp.concatenate([dinner_high[:, cut], env_high[:, cut]], axis=0),
            jnp.concatenate([dinner_low[:, cut], env_low[:, cut]], axis=0),
        )
        d_block = d_block * block_mask
        total = d_block[:ORDERS]
        for k in range(1, GROUP):
            total = total + d_block[k * ORDERS : (k + 1) * ORDERS]
        d_angular.append(total)
    d_angular = jnp.concatenate(d_angular, axis=1)

    mixed_high, mixed_low = split(jnp.concatenate([d_values, d_env], axis=0))
    d_latent = (
        full_depth(value_both, value_high, mixed_high, mixed_low)
        + spread_back[:width]
        + pull * out_column
    )
    d_weight = jnp.sum(d_latent * active + pull * update_out, axis=0, keepdims=True)
    d_before = d_latent * weight * (gate + active * (1.0 - gate))
    d_basis = half_depth(basis_rows, d_before)

    d_length = jnp.sum(d_basis * basis_slope, axis=0, keepdims=True) + d_weight * slope * (
        1.0 / CUTOFF
    )
    a1, a2, a3, a4, a5, a6, a7, a8 = [d_angular[m : m + 1] for m in range(1, 9)]
    ux = root_three * a1 + root_fifteen * (ey * a4 + ez * a7 + ex * a8)
    uy = root_three * a2 + root_fifteen * (ex * a4 + ez * a5 - ey * a8)
    uz = root_three * a3 + root_fifteen * (ey * a5 + ex * a7) + 3.0 * root_five * ez * a6
    along = ex * ux + ey * uy + ez * uz
    radial_part = d_length - along * inverse
    gx = ux * inverse + ex * radial_part
    gy = uy * inverse + ey * radial_part
    gz = uz * inverse + ez * radial_part
    hx = -0.5 * dx
    hy = -0.5 * dy
    hz = -0.5 * dz
    virial = [hx * gx, hx * gy, hx * gz, hy * gx, hy * gy, hy * gz, hz * gx, hz * gy, hz * gz]
    rest = [jnp.zeros((ORDERS - 13, pairs), F32)]
    near_terms = jnp.concatenate(
        [-gx, -gy, -gz, *virial, jnp.zeros_like(gx), *rest], axis=0
    )
    center_terms = jnp.concatenate([gx, gy, gz, *virial, pair_energy, *rest], axis=0)
    near_sums = mm_nt(jnp.concatenate(split(near_terms), axis=0), pick_half)
    center_sums = mm_nt(jnp.concatenate(split(center_terms), axis=0), center_half)
    totals_ref[...] = folded(near_sums + center_sums)


def local(
    positions,
    features,
    species,
    centers,
    neighbours,
    counts,
    species_scale,
    species_shift,
    center_weight,
    near_weight,
    basis_weight,
    path_weight,
    value_weight,
    latent_weight,
    out_weight,
):
    cells_x, cells_y, cells_z, sites, width = features.shape
    cell_count = cells_x * cells_y * cells_z
    owned = cell_count * sites
    assert (cells_x, cells_y, cells_z, sites) == (2, 1, 2, SITES)
    pairs = neighbours.size
    nbr = pairs // owned
    kind = min(3, lax.axis_size("gy"))

    def from_next(array, axis):
        size = lax.axis_size(axis)
        return lax.ppermute(array, axis, [((i + 1) % size, i) for i in range(size)])

    def from_last(array, axis):
        size = lax.axis_size(axis)
        return lax.ppermute(array, axis, [(i, (i + 1) % size) for i in range(size)])

    vmem = pl.BlockSpec(memory_space=pltpu.VMEM)
    kinds = jnp.arange(species_scale.shape[0])
    chosen = species.reshape(cell_count, sites, 1) == kinds
    scale = jnp.sum(jnp.where(chosen, species_scale, 0.0), axis=-1)
    shift = jnp.sum(jnp.where(chosen, species_shift, 0.0), axis=-1).reshape(owned)
    coords = jnp.transpose(positions, (1, 2, 3, 0, 4)).reshape(cell_count, 3 * sites)
    coords = jnp.concatenate([coords, scale], axis=1)
    coords = jnp.pad(coords, ((0, -cell_count % 8), (0, width - 4 * sites)))
    payload = jnp.concatenate([features.reshape(owned, width), coords], axis=0)
    sides = [payload, from_next(payload, "gy")]
    if kind == 3:
        sides.append(from_last(payload, "gy"))
    codes = pl.pallas_call(
        functools.partial(list_kernel, kind),
        out_shape=jax.ShapeDtypeStruct((pairs // 128, 128), F32),
        in_specs=[vmem, vmem],
        out_specs=vmem,
        name="neighbour_codes",
    )(centers.reshape(1, owned), neighbours)
    spare = jnp.zeros((-kind * cell_count % 8, width), F32)
    here = jnp.concatenate(
        [side[:owned] for side in sides]
        + [side[owned : owned + cell_count] for side in sides]
        + [spare, codes],
        axis=0,
    )
    next_x = from_next(here, "gx")
    next_z = from_next(jnp.concatenate([here, next_x], axis=0), "gz")
    totals = pl.pallas_call(
        functools.partial(force_kernel, kind, nbr),
        out_shape=jax.ShapeDtypeStruct((ORDERS, 4 * kind * owned), F32),
        in_specs=[vmem] * 10,
        out_specs=vmem,
        compiler_params=pltpu.CompilerParams(vmem_limit_bytes=40 * 1024 * 1024),
        name="pair_forces",
    )(
        here,
        next_x,
        next_z,
        center_weight,
        near_weight,
        basis_weight,
        path_weight,
        value_weight,
        latent_weight,
        out_weight.reshape(1, width),
    )
    half = 2 * kind * owned
    totals = totals[:, :half] + from_last(totals[:, half:], "gz")
    half = kind * owned
    totals = totals[:, :half] + from_last(totals[:, half:], "gx")
    own = totals[:, :owned] + from_last(totals[:, owned : 2 * owned], "gy")
    if kind == 3:
        own = own + from_next(totals[:, 2 * owned :], "gy")
    forces = own[0:3].reshape(3, cells_x, cells_y, cells_z, sites)
    virial = own[3:12].reshape(9, cells_x, cells_y, cells_z, sites)
    occupied = jnp.any(centers[None, :] == jnp.arange(owned)[:, None], axis=1)
    site_energy = own[12] + jnp.where(occupied, shift, 0.0)
    site_energy = site_energy.reshape(cells_x, cells_y, cells_z, sites)
    return (site_energy, forces, virial)


def solution(mesh):
    placed = (
        P(None, "gx", "gy", "gz", None),
        P("gx", "gy", "gz", None, None),
        P("gx", "gy", "gz", None),
        P(("gx", "gy", "gz")),
        P(("gx", "gy", "gz"), None),
        P(("gx", "gy", "gz")),
        P(),
        P(),
        P(),
        P(),
        P(),
        P(),
        P(),
        P(),
        P(),
    )
    return jax.shard_map(
        local,
        mesh=mesh,
        in_specs=placed,
        out_specs=(
            P("gx", "gy", "gz", None),
            P(None, "gx", "gy", "gz", None),
            P(None, "gx", "gy", "gz", None),
        ),
        check_vma=False,
    )
```

time: 66.8 us -> 39.5 us (0.59)
  blocking collectives: 45.1 us -> 0 us
  starting transfers between devices: 2.56 us -> 10.5 us
  waiting for transfers between devices: 6.39 us -> 12.6 us
  local copies, waits for them, and re-layouts: 5.14 us -> 6.75 us
  other arithmetic: 0.95 us -> 2.3 us
    all_gather x1 -> x0, blocking collectives: 45.1 us -> none  [local(): gathered = lax.all_gather(payload, names, tiled=True)]
    ppermute x0 -> x6, waiting for transfers between devices: none -> 12.6 us  [the longest x3 8.86 us: from_last(): return lax.ppermute(array, axis, [(i, (i + 1) % size) for i in range(size)])]
    ppermute x0 -> x6, starting transfers between devices: none -> 10.5 us  [the longest x3 7.01 us: from_next(): return lax.ppermute(array, axis, [((i + 1) % size, i) for i in range(size)])]
    all_to_all x1 -> x0, waiting for transfers between devices: 6.39 us -> none  [local(): lax.all_to_all(parts, names, split_axis=0, concat_axis=0, tiled=True)]
    concatenate x0 -> x2, local copies, waits for them, and re-layouts: none -> 2.92 us  [the longest x1 1.48 us: local(): jnp.concatenate([side[:owned] for side in sides] + [side[owned:owned + ce...]
    all_to_all x1 -> x0, starting transfers between devices: 2.56 us -> none  [local(): lax.all_to_all(parts, names, split_axis=0, concat_axis=0, tiled=True)]
    reshape x6 -> x1, local copies, waits for them, and re-layouts: 1.66 us -> 0.68 us  [local(): forces = own[0:3].reshape(3, cells_x, cells_y, cells_z, sites)]
    concatenate x1, other arithmetic: 0.01 us -> 0.76 us  [local(): payload = jnp.concatenate([features.reshape(owned, width), coords], axis=0)]
  transfers between devices with their start and end apart: 1 -> 6, of which waited for: 1 -> 5; matrix products, arithmetic and copies ran while one was open for 3% -> 1% of each run, Pallas kernels for 0% -> 5%
where the time goes in v5:
time: 39.5 us; the launch traced here: 38.8 us
  waiting for transfers between devices  12.6 us (32%)
  starting transfers between devices  10.5 us (27%)
  local copies, waits for them, and re-layouts  6.75 us (17%)
  Pallas kernels  5.89 us (15%)
  other arithmetic  2.3 us (6%)
  between operations  0.73 us (2%)
    ppermute x3, waiting for transfers between devices, from_last(): return lax.ppermute(array, axis, [(i, (i + 1) % size) for i in range(size)])  8.86 us
    ppermute x3, starting transfers between devices, from_next(): return lax.ppermute(array, axis, [((i + 1) % size, i) for i in range(size)])  7.01 us
    pallas_call x1, Pallas kernels, local(): pl.pallas_call(functools.partial(force_kernel, kind, nbr), out_shape=jax....  4.1 us
    ppermute x3, waiting for transfers between devices, from_next(): return lax.ppermute(array, axis, [((i + 1) % size, i) for i in range(size)])  3.73 us
    ppermute x3, starting transfers between devices, from_last(): return lax.ppermute(array, axis, [(i, (i + 1) % size) for i in range(size)])  3.53 us
    unnamed x21, local copies, waits for them, and re-layouts  1.99 us
    pallas_call x1, Pallas kernels, local(): pl.pallas_call(functools.partial(list_kernel, kind), out_shape=jax.ShapeD...  1.8 us
    concatenate x1, local copies, waits for them, and re-layouts, local(): jnp.concatenate([side[:owned] for side in sides] + [side[owned:owned + ce...  1.48 us
  transfers between devices with their start and end apart: 6, of which 5 were waited for; matrix products, arithmetic and copies ran while one was open for 1% of the time, Pallas kernels for 5%

profile of v5, /device:TPU:0, one launch (start us, length us, event | category | flops | bytes accessed | tf_op | source)
XLA Modules:
  0.0 38.8 jit_solution(6312589542737378023)
XLA Ops:
  0.7 0.7 %copy.25 = f32[2,1,2,3,8]{4,3,2,0,1:T(4,128)S(1)} copy(f32[2,1,2,3,8]{4,2,1,0,3:T(2,128)} %bitcast.18) | data formatting | bytes 768 | tf_op jit(solution)/shard_map/transpose | solution.py:453
  1.4 0.1 reshape.59
  1.5 0.8 %select_reduce_fusion = (f32[4,8]{1,0:T(4,128)S(1)}, f32[4,8]{1,0:T(4,128)S(1)}) fusion(f32[5]{0:T(128)} %param.21, s32[4,8]{1,0:T(4,128)S(1)} %bitcast.20, f32[5]{0:T(128)} %param.20), kind=kLoop, calls=%fused_computation.3 | loop fusion | flops 736 | bytes 424 | tf_op jit(solution)/shard_map/reduce_sum | solution.py:452
  2.2 0.1 select_maximum_fusion
  2.3 0.8 %pad_maximum_fusion = f32[40,128]{1,0:T(8,128)S(1)} fusion(f32[8,128]{1,0:T(8,128)S(1)} %select_maximum_fusion, f32[32,128]{1,0:T(8,128)} %bitcast.13), kind=kLoop, calls=%fused_computation | loop fusion | flops 5120 | bytes 40960 | tf_op jit(solution)/shard_map/concatenate | solution.py:456
  3.1 2.9 %collective-permute-start = (f32[40,128]{1,0:T(8,128)S(1)}, f32[40,128]{1,0:T(8,128)S(1)}, u32[]{:S(2)}, u32[]{:S(2)}) collective-permute-start(f32[40,128]{1,0:T(8,128)S(1)} %pad_maximum_fusion), channel_id=1, source_target_pairs={{4,0},{0,4},{5,1},{1,5},{6,2},{2,6},{7,3},{3,7},{12,8},{8,12},{13,... | collective-permute-start | bytes 61448 | tf_op jit(solution)/shard_map/ppermute | solution.py:442
  6.0 1.8 %neighbour_codes.1 = f32[8,128]{1,0:T(8,128)} custom-call(s32[1,32]{1,0:T(1,128)} %bitcast.21, s32[32,32]{1,0:T(8,128)} %neighbours_ref.1), custom_call_target="tpu_custom_call" | custom-call | tf_op jit(solution)/shard_map/neighbour_codes/pallas_call | solution.py:460
  7.8 0.0 copy-start
  7.8 1.5 %concatenate.15.here_ref = f32[80,128]{1,0:T(8,128)S(1)} concatenate(f32[32,128]{1,0:T(8,128)} %bitcast.14, f32[32,128]{1,0:T(8,128)S(1)} %slice.48, f32[4,128]{1,0:T(4,128)S(1)} %slice.37, f32[4,128]{1,0:T(4,128)S(1)} %slice.49, f32[8,128]{1,0:T(8,128)} %neighbour_codes.1), dimensions={0} | concatenate | bytes 81920 | tf_op jit(solution)/shard_map/concatenate | solution.py:468
  9.3 4.1 %collective-permute-start.1 = (f32[80,128]{1,0:T(8,128)S(1)}, f32[80,128]{1,0:T(8,128)S(1)}, u32[]{:S(2)}, u32[]{:S(2)}) collective-permute-start(f32[80,128]{1,0:T(8,128)S(1)} %concatenate.15.here_ref), channel_id=1, source_target_pairs={{8,0},{16,8},{24,16},{0,24},{9,1},{17,9},{25,17},{1,25},{10,2},{18... | collective-permute-start | bytes 122888 | tf_op jit(solution)/shard_map/ppermute | solution.py:442
  13.4 1.7 %collective-permute-done.1.next_x_ref = f32[80,128]{1,0:T(8,128)S(1)} collective-permute-done((f32[80,128]{1,0:T(8,128)S(1)}, f32[80,128]{1,0:T(8,128)S(1)}, u32[]{:S(2)}, u32[]{:S(2)}) %collective-permute-start.1) | collective-permute-done | bytes 40992 | tf_op jit(solution)/shard_map/ppermute | solution.py:442
  15.1 1.4 %concatenate.16 = f32[160,128]{1,0:T(8,128)S(1)} concatenate(f32[32,128]{1,0:T(8,128)} %bitcast.15, f32[32,128]{1,0:T(8,128)S(1)} %slice.48, f32[4,128]{1,0:T(4,128)S(1)} %slice.37, f32[4,128]{1,0:T(4,128)S(1)} %slice.49, f32[8,128]{1,0:T(8,128)} %neighbour_codes.1, f32[80,128]{1,0:T(8,128)S(1)} %collective-permute-done.1.next_x_ref), dimensions={0} | concatenate | bytes 163840 | tf_op jit(solution)/shard_map/concatenate | solution.py:475
  16.5 0.0 collective-permute-start.2
  16.5 2.1 %collective-permute-done.2.next_z_ref = f32[160,128]{1,0:T(8,128)S(1)} collective-permute-done((f32[160,128]{1,0:T(8,128)S(1)}, f32[160,128]{1,0:T(8,128)S(1)}, u32[]{:S(2)}, u32[]{:S(2)}) %collective-permute-start.2) | collective-permute-done | bytes 81952 | tf_op jit(solution)/shard_map/ppermute | solution.py:442
  18.6 0.0 copy-start.5
  18.6 0.7 %copy-done.5 = f32[3,128]{1,0:T(4,128)S(1)} copy-done((f32[3,128]{1,0:T(4,128)S(1)}, f32[3,128]{1,0:T(4,128)}, u32[]{:S(2)}) %copy-start.5) | copy-done | bytes 1560
  19.3 4.1 %pair_forces.1 = f32[16,256]{1,0:T(8,128)S(1)} custom-call(f32[80,128]{1,0:T(8,128)S(1)} %concatenate.15.here_ref, f32[80,128]{1,0:T(8,128)S(1)} %collective-permute-done.1.next_x_ref, f32[160,128]{1,0:T(8,128)S(1)} %collective-permute-done.2.next_z_ref, f32[128,128]{1,0:T(8,128)S(1)} %copy-done.2, f32[128,128]{1,0:T(8,128)S(1)} %copy-done.3, ...), custom_call_target="tpu_custom_call" | custom-call | tf_op jit(solution)/shard_map/pair_forces/pallas_call | solution.py:476
  23.4 1.7 %collective-permute-start.3 = (f32[16,128]{1,0:T(8,128)S(1)}, f32[16,128]{1,0:T(8,128)S(1)}, u32[]{:S(2)}, u32[]{:S(2)}) collective-permute-start(f32[16,128]{1,0:T(8,128)S(1)} %slice.51), channel_id=1, source_target_pairs={{0,1},{1,2},{2,3},{3,0},{4,5},{5,6},{6,7},{7,4},{8,9},{9,10},{10,1... | collective-permute-start | bytes 24584 | tf_op jit(solution)/shard_map/ppermute | solution.py:446
  25.1 1.4 %collective-permute-done.3 = f32[16,128]{1,0:T(8,128)S(1)} collective-permute-done((f32[16,128]{1,0:T(8,128)S(1)}, f32[16,128]{1,0:T(8,128)S(1)}, u32[]{:S(2)}, u32[]{:S(2)}) %collective-permute-start.3) | collective-permute-done | bytes 8224 | tf_op jit(solution)/shard_map/ppermute | solution.py:446
  26.6 0.1 slice.53
  26.7 0.3 collective-permute-start.4
  27.0 5.5 %collective-permute-done.4 = f32[16,64]{1,0:T(8,128)S(1)} collective-permute-done((f32[16,64]{1,0:T(8,128)S(1)}, f32[16,64]{1,0:T(8,128)S(1)}, u32[]{:S(2)}, u32[]{:S(2)}) %collective-permute-start.4) | collective-permute-done | bytes 4128 | tf_op jit(solution)/shard_map/ppermute | solution.py:446
  32.4 0.1 slice.55
  32.5 1.5 %collective-permute-start.5 = (f32[16,32]{1,0:T(8,128)S(1)}, f32[16,32]{1,0:T(8,128)S(1)}, u32[]{:S(2)}, u32[]{:S(2)}) collective-permute-start(f32[16,32]{1,0:T(8,128)S(1)} %slice.55), channel_id=1, source_target_pairs={{0,4},{4,0},{1,5},{5,1},{2,6},{6,2},{3,7},{7,3},{8,12},{12,8},{9,1... | collective-permute-start | bytes 6152 | tf_op jit(solution)/shard_map/ppermute | solution.py:446
  34.0 0.1 fusion
  34.1 0.1 reduce_or.12
  34.2 2.0 %collective-permute-done.5 = f32[16,32]{1,0:T(8,128)S(1)} collective-permute-done((f32[16,32]{1,0:T(8,128)S(1)}, f32[16,32]{1,0:T(8,128)S(1)}, u32[]{:S(2)}, u32[]{:S(2)}) %collective-permute-start.5) | collective-permute-done | bytes 2080 | tf_op jit(solution)/shard_map/ppermute | solution.py:446
  36.2 0.6 %copy-done.7 = f32[16,32]{1,0:T(8,128)} copy-done((f32[16,32]{1,0:T(8,128)}, f32[16,32]{1,0:T(8,128)S(1)}, u32[]{:S(2)}) %copy-start.7) | copy-done | bytes 2072
  36.8 0.7 %copy.29 = f32[9,32]{0,1:T(8,128)} copy(f32[9,32]{1,0:T(8,128)S(1)} %slice.58) | data formatting | bytes 2304
  37.5 0.7 %reshape.63 = f32[3,2,1,2,8]{4,3,1,0,2:T(2,128)} reshape(f32[3,32]{1,0:T(4,128)S(1)} %slice-done) | data formatting | bytes 768 | tf_op jit(solution)/shard_map/reshape | solution.py:502
  38.1 0.1 squeeze.3
  38.2 0.6 %add_bitcast_fusion = f32[2,1,2,8]{3,2,1,0:T(2,128)} fusion(f32[2,1,2,8]{3,2,0,1:T(2,128)S(1)} %squeeze.3, pred[2,1,2,8]{3,2,0,1:T(4,128)(4,1)S(1)} %reduce_or.12, f32[2,1,2,8]{3,2,0,1:T(2,128)S(1)} %bitcast.17), kind=kLoop, calls=%fused_computation.12 | loop fusion | flops 64 | bytes 416
  (28 shorter events, 0.1 us)
Async XLA Ops:
  0.6 0.8 %copy-start.8 = (s32[2,1,2,8]{3,2,1,0:T(2,128)S(1)}, s32[2,1,2,8]{3,2,1,0:T(2,128)}, u32[]{:S(2)}) copy-start(s32[2,1,2,8]{3,2,1,0:T(2,128)} %param.17) | copy-start | bytes 388
  0.6 17.9 %copy-start.3 = (f32[128,128]{1,0:T(8,128)S(1)}, f32[128,128]{1,0:T(8,128)}, u32[]{:S(2)}) copy-start(f32[128,128]{1,0:T(8,128)} %near_weight_ref.1) | copy-start | bytes 196612
  2.3 16.3 %copy-start.2 = (f32[128,128]{1,0:T(8,128)S(1)}, f32[128,128]{1,0:T(8,128)}, u32[]{:S(2)}) copy-start(f32[128,128]{1,0:T(8,128)} %center_weight_ref.1) | copy-start | bytes 196612
  3.1 4.7 %collective-permute-start = (f32[40,128]{1,0:T(8,128)S(1)}, f32[40,128]{1,0:T(8,128)S(1)}, u32[]{:S(2)}, u32[]{:S(2)}) collective-permute-start(f32[40,128]{1,0:T(8,128)S(1)} %pad_maximum_fusion), channel_id=1, source_target_pairs={{4,0},{0,4},{5,1},{1,5},{6,2},{2,6},{7,3},{3,7},{12,8},{8,12},{13,... | collective-permute-start | bytes 61448 | tf_op jit(solution)/shard_map/ppermute | solution.py:442
  7.8 10.8 %copy-start.1 = (f32[256,128]{1,0:T(8,128)S(1)}, f32[256,128]{1,0:T(8,128)}, u32[]{:S(2)}) copy-start(f32[256,128]{1,0:T(8,128)} %latent_weight_ref.1) | copy-start | bytes 393220
  7.8 10.8 %copy-start = (f32[128,256]{1,0:T(8,128)S(1)}, f32[128,256]{1,0:T(8,128)}, u32[]{:S(2)}) copy-start(f32[128,256]{1,0:T(8,128)} %value_weight_ref.1) | copy-start | bytes 393220
  9.3 5.7 %collective-permute-start.1 = (f32[80,128]{1,0:T(8,128)S(1)}, f32[80,128]{1,0:T(8,128)S(1)}, u32[]{:S(2)}, u32[]{:S(2)}) collective-permute-start(f32[80,128]{1,0:T(8,128)S(1)} %concatenate.15.here_ref), channel_id=1, source_target_pairs={{8,0},{16,8},{24,16},{0,24},{9,1},{17,9},{25,17},{1,25},{10,2},{18... | collective-permute-start | bytes 122888 | tf_op jit(solution)/shard_map/ppermute | solution.py:442
  15.1 3.5 %copy-start.4 = (f32[8,128]{1,0:T(8,128)S(1)}, f32[8,128]{1,0:T(8,128)}, u32[]{:S(2)}) copy-start(f32[8,128]{1,0:T(8,128)} %basis_weight_ref.1) | copy-start | bytes 12292
  16.5 2.1 %copy-start.6 = (f32[128]{0:T(128)S(1)}, f32[128]{0:T(128)}, u32[]{:S(2)}) copy-start(f32[128]{0:T(128)} %param.28) | copy-start | bytes 1540
  16.5 2.1 %collective-permute-start.2 = (f32[160,128]{1,0:T(8,128)S(1)}, f32[160,128]{1,0:T(8,128)S(1)}, u32[]{:S(2)}, u32[]{:S(2)}) collective-permute-start(f32[160,128]{1,0:T(8,128)S(1)} %concatenate.16), channel_id=1, source_target_pairs={{1,0},{2,1},{3,2},{0,3},{5,4},{6,5},{7,6},{4,7},{9,8},{10,9},{11,1... | collective-permute-start | bytes 245768 | tf_op jit(solution)/shard_map/ppermute | solution.py:442
  18.6 0.7 %copy-start.5 = (f32[3,128]{1,0:T(4,128)S(1)}, f32[3,128]{1,0:T(4,128)}, u32[]{:S(2)}) copy-start(f32[3,128]{1,0:T(4,128)} %path_weight_ref.1) | copy-start | bytes 4612
  23.4 3.2 %collective-permute-start.3 = (f32[16,128]{1,0:T(8,128)S(1)}, f32[16,128]{1,0:T(8,128)S(1)}, u32[]{:S(2)}, u32[]{:S(2)}) collective-permute-start(f32[16,128]{1,0:T(8,128)S(1)} %slice.51), channel_id=1, source_target_pairs={{0,1},{1,2},{2,3},{3,0},{4,5},{5,6},{6,7},{7,4},{8,9},{9,10},{10,1... | collective-permute-start | bytes 24584 | tf_op jit(solution)/shard_map/ppermute | solution.py:446
  26.7 5.8 %collective-permute-start.4 = (f32[16,64]{1,0:T(8,128)S(1)}, f32[16,64]{1,0:T(8,128)S(1)}, u32[]{:S(2)}, u32[]{:S(2)}) collective-permute-start(f32[16,64]{1,0:T(8,128)S(1)} %slice.53), channel_id=1, source_target_pairs={{0,8},{8,16},{16,24},{24,0},{1,9},{9,17},{17,25},{25,1},{2,10},{10... | collective-permute-start | bytes 12296 | tf_op jit(solution)/shard_map/ppermute | solution.py:446
  32.4 1.6 %copy-start.9 = (s32[32]{0:T(128)S(1)}, s32[32]{0:T(128)}, u32[]{:S(2)}) copy-start(s32[32]{0:T(128)} %param.18) | copy-start | bytes 388
  32.5 3.7 %collective-permute-start.5 = (f32[16,32]{1,0:T(8,128)S(1)}, f32[16,32]{1,0:T(8,128)S(1)}, u32[]{:S(2)}, u32[]{:S(2)}) collective-permute-start(f32[16,32]{1,0:T(8,128)S(1)} %slice.55), channel_id=1, source_target_pairs={{0,4},{4,0},{1,5},{5,1},{2,6},{6,2},{3,7},{7,3},{8,12},{12,8},{9,1... | collective-permute-start | bytes 6152 | tf_op jit(solution)/shard_map/ppermute | solution.py:446
  36.1 0.6 %copy-start.7 = (f32[16,32]{1,0:T(8,128)}, f32[16,32]{1,0:T(8,128)S(1)}, u32[]{:S(2)}) copy-start(f32[16,32]{1,0:T(8,128)S(1)} %slice_add_fusion) | copy-start | bytes 6148
  36.8 0.7 %slice-start = ((f32[16,32]{1,0:T(8,128)}), f32[3,32]{1,0:T(4,128)S(1)}, s32[]{:S(2)}) async-start(f32[16,32]{1,0:T(8,128)} %copy-done.7), calls=%async_computation | async-start | bytes 4096 | tf_op jit(solution)/shard_map/slice | solution.py:502

commit v6 on v5

--- a/solution.py
+++ b/solution.py
@@ -84,17 +84,53 @@
     return sine, cosine
 
 
-def exact(a, b):
-    return jnp.dot(a, b, precision=EXACT_DOT, preferred_element_type=F32)
-
-
-def list_kernel(kind, centers_ref, neighbours_ref, codes_ref):
+def lane_row(piece, offset):
+    row = jnp.concatenate([piece, jnp.zeros((1, 128 - piece.shape[1]), piece.dtype)], axis=1)
+    return pltpu.roll(row, offset, 1) if offset else row
+
+
+def pack_kernel(
+    kind,
+    positions_ref,
+    features_ref,
+    species_ref,
+    centers_ref,
+    neighbours_ref,
+    scale_ref,
+    shift_ref,
+    payload_ref,
+    shift_row_ref,
+    wide_ref,
+):
     owned, nbr = neighbours_ref.shape
     per_row = 128 // nbr
+    payload_ref[:owned] = features_ref[...]
+    payload_ref[owned : owned + 8] = jnp.zeros((8, 128), F32)
+    shift_row = jnp.zeros((1, 128), F32)
+    for cell in range(OWN_CELLS):
+        x, z = cell // 2, cell % 2
+        species = species_ref[x, 0, z : z + 1, :]
+        scale = jnp.zeros(species.shape, F32)
+        shift = jnp.zeros(species.shape, F32)
+        for s in range(scale_ref.shape[0]):
+            scale = jnp.where(species == s, scale_ref[s], scale)
+            shift = jnp.where(species == s, shift_ref[s], shift)
+        row = lane_row(scale, 3 * SITES)
+        for c in range(3):
+            row = row + lane_row(positions_ref[c, x, 0, z : z + 1, :], c * SITES)
+        payload_ref[owned + cell : owned + cell + 1] = row
+        shift_row = shift_row + lane_row(shift, cell * SITES)
+
     chosen = lax.broadcasted_iota(jnp.int32, (owned, owned), 0) == centers_ref[...]
     chosen = jnp.where(chosen, 1.0, 0.0)
     occupied = jnp.sum(chosen, axis=1, keepdims=True) > 0.5
-    rows = exact(chosen, neighbours_ref[...].astype(F32)).astype(jnp.int32)
+    column = jnp.where(occupied, jnp.ones((owned, 128), F32), 0.0)
+    shift_row_ref[...] = shift_row[:, :owned] * jnp.transpose(column)[0:1]
+    chosen = chosen.astype(BF16)
+    rows = neighbours_ref[...]
+    upper = mm(chosen, (rows >> 4).astype(F32).astype(BF16))
+    lower = mm(chosen, (rows & 15).astype(F32).astype(BF16))
+    rows = (upper * 16.0 + lower).astype(jnp.int32)
     live = occupied & (rows < FRAME_CELLS * SITES)
     slot = lax.broadcasted_iota(jnp.int32, (owned, nbr), 0)
     cell = slot >> 3
@@ -109,17 +145,67 @@
     block = (near_z >> 1) * 2 + (near_x >> 1)
     where = (block * kind + side) * owned + (near_x & 1) * 16 + (near_z & 1) * 8 + site
     code = jnp.where(live, 1 + where + (frame_y << 10), 0).astype(F32)
-    lane = lax.broadcasted_iota(jnp.int32, (nbr, 128), 1)
-    spread = jnp.where(lax.broadcasted_iota(jnp.int32, (nbr, 128), 0) == lane % nbr, 1.0, 0.0)
-    wide = exact(code, spread)
-    row = lax.broadcasted_iota(jnp.int32, (owned, 128), 0)
-    lane = lax.broadcasted_iota(jnp.int32, (owned, 128), 1)
-    wide = jnp.where(row % per_row == lane // nbr, wide, 0.0)
-    fold = lax.broadcasted_iota(jnp.int32, (owned // per_row, owned), 1) // per_row
-    fold = jnp.where(
-        fold == lax.broadcasted_iota(jnp.int32, (owned // per_row, owned), 0), 1.0, 0.0
-    )
-    codes_ref[...] = exact(fold, wide)
+    wide_ref[...] = jnp.concatenate([code, jnp.zeros((owned, 128 - nbr), F32)], axis=1)
+    codes = wide_ref[pl.ds(0, owned // per_row, stride=per_row), :]
+    for j in range(1, per_row):
+        more = wide_ref[pl.ds(j, owned // per_row, stride=per_row), :]
+        codes = codes + pltpu.roll(more, j * nbr, 1)
+    payload_ref[owned + 8 :] = codes
+
+
+def weight_kernel(
+    nbr,
+    center_weight_ref,
+    near_weight_ref,
+    path_weight_ref,
+    value_weight_ref,
+    latent_weight_ref,
+    out_weight_ref,
+    stack_ref,
+    column_ref,
+):
+    width = near_weight_ref.shape[0]
+    value_high, value_low = split(value_weight_ref[...])
+    latent_high, latent_low = split(jnp.transpose(latent_weight_ref[...]))
+    parts = [
+        stacked(*split(jnp.transpose(value_weight_ref[...]))),
+        jnp.concatenate([latent_high, latent_low], axis=0),
+        stacked(*split(latent_weight_ref[...])),
+        jnp.concatenate([value_high, value_low], axis=0),
+        stacked(*split(jnp.transpose(near_weight_ref[...]))),
+        stacked(*split(jnp.transpose(center_weight_ref[...]))),
+    ]
+    start = 0
+    for part in parts:
+        stack_ref[start : start + part.shape[0], :] = part
+        start += part.shape[0]
+    level = lax.broadcasted_iota(jnp.int32, (ORDERS, width), 0)
+    path_rows = jnp.where(
+        level == 0,
+        path_weight_ref[0:1, :],
+        jnp.where(
+            level < 4,
+            path_weight_ref[1:2, :],
+            jnp.where(level < 9, path_weight_ref[2:3, :], 0.0),
+        ),
+    )
+    paths_t = jnp.transpose(jnp.concatenate([path_rows] * GROUP, axis=0))
+    column_ref[:width] = paths_t * (1.0 / math.sqrt(nbr))
+    column_ref[width:] = jnp.transpose(jnp.broadcast_to(out_weight_ref[...], (width, width)))
+
+
+def finish_kernel(mine_ref, near_ref, shift_row_ref, energy_ref, forces_ref, virial_ref):
+    owned = near_ref.shape[1]
+    total = mine_ref[:, :owned] + near_ref[...]
+    energy = total[12:13] + shift_row_ref[...]
+    columns = jnp.transpose(jnp.concatenate([total, jnp.zeros((ORDERS, 128 - owned), F32)], axis=1))
+    for cell in range(OWN_CELLS):
+        x, z = cell // 2, cell % 2
+        lanes = slice(cell * SITES, (cell + 1) * SITES)
+        energy_ref[x, 0, z : z + 1, :] = energy[:, lanes]
+        for c in range(3):
+            forces_ref[c, x, 0, z : z + 1, :] = total[c : c + 1, lanes]
+        virial_ref[x, 0, z] = columns[lanes, 3:12]
 
 
 def force_kernel(
@@ -127,37 +213,40 @@
     nbr,
     here_ref,
     next_x_ref,
+    sides_ref,
     next_z_ref,
-    center_weight_ref,
-    near_weight_ref,
+    stack_ref,
+    column_ref,
     basis_weight_ref,
-    path_weight_ref,
-    value_weight_ref,
-    latent_weight_ref,
-    out_weight_ref,
-    totals_ref,
+    send_ref,
+    keep_ref,
 ):
     height, width = here_ref.shape
     owned = OWN_CELLS * SITES
-    feats_rows = kind * owned
-    coord_rows = kind * OWN_CELLS + -kind * OWN_CELLS % 8
+    short = owned + 8
     pairs = owned * nbr
     radial = basis_weight_ref.shape[0]
     span = GROUP * nbr
     groups = owned // GROUP
     wide = GROUP * ORDERS
     sites = SITES
-    blocks_in = [
-        here_ref[...],
-        next_x_ref[...],
-        next_z_ref[:height],
-        next_z_ref[height:],
-    ]
     root_count = math.sqrt(nbr)
     root_three = math.sqrt(3.0)
     root_fifteen = math.sqrt(15.0)
     root_five = math.sqrt(5.0)
-    feats = jnp.concatenate([block[:feats_rows] for block in blocks_in], axis=0)
+    far = next_z_ref[...]
+    mains = [here_ref[...], next_x_ref[...], far[:height], far[height : 2 * height]]
+    near_sides = sides_ref[...]
+    near_sides = [near_sides[i * short : (i + 1) * short] for i in range(2 * kind - 2)]
+    far_sides = far[2 * height :]
+    far_sides = [far_sides[i * short : (i + 1) * short] for i in range(2 * kind - 2)]
+    blocks_in = [
+        [mains[0], *near_sides[0::2]],
+        [mains[1], *near_sides[1::2]],
+        [mains[2], *far_sides[0::2]],
+        [mains[3], *far_sides[1::2]],
+    ]
+    feats = jnp.concatenate([side[:owned] for block in blocks_in for side in block], axis=0)
     known = feats.shape[0]
     center_feats = []
     coords = []
@@ -168,8 +257,8 @@
     for g, block in enumerate(blocks_in):
         ahead_x, ahead_z = g % 2, g // 2
         cell = (1 - ahead_x) * 2 + 1 - ahead_z
-        center_feats.append(block[cell * sites : (cell + 1) * sites])
-        rows = block[feats_rows : feats_rows + kind * OWN_CELLS]
+        center_feats.append(block[0][cell * sites : (cell + 1) * sites])
+        rows = jnp.concatenate([side[owned : owned + OWN_CELLS] for side in block], axis=0)
         scales.append(rows[cell : cell + 1])
         corner_x = (cell_row // 2 + 2 * ahead_x).astype(F32) * CELL_SIDE
         corner_z = (cell_row % 2 + 2 * ahead_z).astype(F32) * CELL_SIDE
@@ -177,8 +266,8 @@
             tile_lane < sites, corner_x, jnp.where(tile_lane < 2 * sites, 0.0, corner_z)
         )
         coords.append(rows + corner)
-        start = feats_rows + coord_rows + cell * span // 128
-        codes.extend(block[start + r : start + r + 1] for r in range(span // 128))
+        start = short + cell * span // 128
+        codes.extend(block[0][start + r : start + r + 1] for r in range(span // 128))
     center_feats = jnp.concatenate(center_feats, axis=0)
     coords = jnp.concatenate(coords, axis=0)
     code = jnp.concatenate(codes, axis=1).astype(jnp.int32)
@@ -195,26 +284,21 @@
     spread = jnp.where(keep, spread, 0.0)
     place_parts = jnp.concatenate(split3(jnp.transpose(spread)[: 3 * sites]), axis=0)
 
-    value_t = jnp.transpose(value_weight_ref[...])
-    latent_t = jnp.transpose(latent_weight_ref[...])
-    value_rows = stacked(*split(value_t))
-    latent_high_t, latent_low_t = split(latent_t)
-    latent_both_t = jnp.concatenate([latent_high_t, latent_low_t], axis=0)
-    latent_rows = stacked(*split(latent_weight_ref[...]))
-    value_high, value_low = split(value_weight_ref[...])
-    value_both = jnp.concatenate([value_high, value_low], axis=0)
+    value_rows = stack_ref[: 4 * width, :]
+    latent_both_t = stack_ref[4 * width : 6 * width, :]
+    latent_high_t = latent_both_t[:width]
+    latent_rows = stack_ref[6 * width : 10 * width, :]
+    value_both = stack_ref[10 * width : 12 * width, :]
+    value_high = value_both[:width]
     basis_t = jnp.transpose(basis_weight_ref[...])
     basis_high_t, basis_low_t = split(basis_t)
     basis_rows = stacked(*split(basis_weight_ref[...]))
 
     def project(weight, rows):
-        high, low = split(rows)
-        return folded(
-            mm_nt(stacked(*split(jnp.transpose(weight))), jnp.concatenate([high, low], axis=1))
-        )
-
-    near_t = project(near_weight_ref[...], feats)
-    own_t = project(center_weight_ref[...], center_feats)
+        return folded(mm_nt(weight, jnp.concatenate(split(rows), axis=1)))
+
+    near_t = project(stack_ref[12 * width : 14 * width, :], feats)
+    own_t = project(stack_ref[14 * width :, :], center_feats)
     near_high, near_low = split(near_t)
     own_high, own_low = split(own_t)
     lookup = jnp.concatenate(
@@ -229,26 +313,15 @@
         [*split3(scale_rows), jnp.zeros((16 - 3 * groups, 128), BF16)], axis=0
     )
 
-    level = lax.broadcasted_iota(jnp.int32, (ORDERS, width), 0)
-    path_rows = jnp.where(
-        level == 0,
-        path_weight_ref[0:1, :],
-        jnp.where(
-            level < 4,
-            path_weight_ref[1:2, :],
-            jnp.where(level < 9, path_weight_ref[2:3, :], 0.0),
-        ),
-    )
-    paths_t = jnp.transpose(jnp.concatenate([path_rows] * GROUP, axis=0)) * (1.0 / root_count)
-    out_column = jnp.transpose(jnp.broadcast_to(out_weight_ref[...], (width, width)))
-    out_column = jnp.concatenate([out_column] * (pairs // width), axis=1)
+    paths_t = column_ref[:width]
+    out_column = jnp.concatenate([column_ref[width:]] * (pairs // width), axis=1)
 
     site_ids = lax.broadcasted_iota(jnp.int32, (known, pairs), 0)
     slot_ids = lax.broadcasted_iota(jnp.int32, (owned, pairs), 0)
     slot_row = lax.broadcasted_iota(jnp.int32, (1, pairs), 1) // nbr
     group_row = slot_row // GROUP
     center_cell = (1 - group_row % 2) * 2 + 1 - group_row // 2
-    center_row = group_row * feats_rows + center_cell * sites + slot_row % GROUP
+    center_row = group_row * (kind * owned) + center_cell * sites + slot_row % GROUP
     block_row = lax.broadcasted_iota(jnp.int32, (wide, span), 0) // ORDERS
     block_lane = lax.broadcasted_iota(jnp.int32, (wide, span), 1) // nbr
     block_mask = (block_row == block_lane).astype(F32)
@@ -409,7 +482,20 @@
     center_terms = jnp.concatenate([gx, gy, gz, *virial, pair_energy, *rest], axis=0)
     near_sums = mm_nt(jnp.concatenate(split(near_terms), axis=0), pick_half)
     center_sums = mm_nt(jnp.concatenate(split(center_terms), axis=0), center_half)
-    totals_ref[...] = folded(near_sums + center_sums)
+    totals = folded(near_sums + center_sums)
+    keep_ref[...] = totals[:, : known // 2]
+    send_ref[...] = totals[:, known // 2 :]
+
+
+def joined(parts):
+    total = sum(part.shape[0] for part in parts)
+    start = 0
+    pads = []
+    for part in parts:
+        end = start + part.shape[0]
+        pads.append(jnp.pad(part, ((start, total - end), (0, 0))))
+        start = end
+    return functools.reduce(jnp.add, pads)
 
 
 def local(
@@ -446,65 +532,80 @@
         return lax.ppermute(array, axis, [(i, (i + 1) % size) for i in range(size)])
 
     vmem = pl.BlockSpec(memory_space=pltpu.VMEM)
-    kinds = jnp.arange(species_scale.shape[0])
-    chosen = species.reshape(cell_count, sites, 1) == kinds
-    scale = jnp.sum(jnp.where(chosen, species_scale, 0.0), axis=-1)
-    shift = jnp.sum(jnp.where(chosen, species_shift, 0.0), axis=-1).reshape(owned)
-    coords = jnp.transpose(positions, (1, 2, 3, 0, 4)).reshape(cell_count, 3 * sites)
-    coords = jnp.concatenate([coords, scale], axis=1)
-    coords = jnp.pad(coords, ((0, -cell_count % 8), (0, width - 4 * sites)))
-    payload = jnp.concatenate([features.reshape(owned, width), coords], axis=0)
-    sides = [payload, from_next(payload, "gy")]
-    if kind == 3:
-        sides.append(from_last(payload, "gy"))
-    codes = pl.pallas_call(
-        functools.partial(list_kernel, kind),
-        out_shape=jax.ShapeDtypeStruct((pairs // 128, 128), F32),
-        in_specs=[vmem, vmem],
-        out_specs=vmem,
-        name="neighbour_codes",
-    )(centers.reshape(1, owned), neighbours)
-    spare = jnp.zeros((-kind * cell_count % 8, width), F32)
-    here = jnp.concatenate(
-        [side[:owned] for side in sides]
-        + [side[owned : owned + cell_count] for side in sides]
-        + [spare, codes],
-        axis=0,
-    )
-    next_x = from_next(here, "gx")
-    next_z = from_next(jnp.concatenate([here, next_x], axis=0), "gz")
-    totals = pl.pallas_call(
-        functools.partial(force_kernel, kind, nbr),
-        out_shape=jax.ShapeDtypeStruct((ORDERS, 4 * kind * owned), F32),
-        in_specs=[vmem] * 10,
-        out_specs=vmem,
-        compiler_params=pltpu.CompilerParams(vmem_limit_bytes=40 * 1024 * 1024),
-        name="pair_forces",
+    smem = pl.BlockSpec(memory_space=pltpu.SMEM)
+    here, shift_row = pl.pallas_call(
+        functools.partial(pack_kernel, kind),
+        out_shape=(
+            jax.ShapeDtypeStruct((owned + 8 + pairs // 128, width), F32),
+            jax.ShapeDtypeStruct((1, owned), F32),
+        ),
+        in_specs=[vmem] * 5 + [smem] * 2,
+        out_specs=(vmem, vmem),
+        scratch_shapes=[pltpu.VMEM((owned, 128), F32)],
+        name="pack_payload",
     )(
-        here,
-        next_x,
-        next_z,
+        positions,
+        features.reshape(owned, width),
+        species,
+        centers.reshape(1, owned),
+        neighbours,
+        species_scale,
+        species_shift,
+    )
+    stack, column = pl.pallas_call(
+        functools.partial(weight_kernel, nbr),
+        out_shape=(
+            jax.ShapeDtypeStruct((16 * width, 2 * width), BF16),
+            jax.ShapeDtypeStruct((2 * width, width), F32),
+        ),
+        in_specs=[vmem] * 6,
+        out_specs=(vmem, vmem),
+        name="split_weights",
+    )(
         center_weight,
         near_weight,
-        basis_weight,
         path_weight,
         value_weight,
         latent_weight,
         out_weight.reshape(1, width),
     )
+    short = owned + 8
+    next_x = from_next(here, "gx")
+    both = joined([here[:short], next_x[:short]])
+    sides = from_next(both, "gy")
+    if kind == 3:
+        sides = joined([sides, from_last(both, "gy")])
+    next_z = from_next(joined([here, next_x, sides]), "gz")
     half = 2 * kind * owned
-    totals = totals[:, :half] + from_last(totals[:, half:], "gz")
+    send, keep = pl.pallas_call(
+        functools.partial(force_kernel, kind, nbr),
+        out_shape=(
+            jax.ShapeDtypeStruct((ORDERS, half), F32),
+            jax.ShapeDtypeStruct((ORDERS, half), F32),
+        ),
+        in_specs=[vmem] * 7,
+        out_specs=(vmem, vmem),
+        compiler_params=pltpu.CompilerParams(vmem_limit_bytes=40 * 1024 * 1024),
+        name="pair_forces",
+    )(here, next_x, sides, next_z, stack, column, basis_weight)
+    totals = keep + from_last(send, "gz")
     half = kind * owned
     totals = totals[:, :half] + from_last(totals[:, half:], "gx")
-    own = totals[:, :owned] + from_last(totals[:, owned : 2 * owned], "gy")
+    back = from_last(totals[:, owned : 2 * owned], "gy")
     if kind == 3:
-        own = own + from_next(totals[:, 2 * owned :], "gy")
-    forces = own[0:3].reshape(3, cells_x, cells_y, cells_z, sites)
-    virial = own[3:12].reshape(9, cells_x, cells_y, cells_z, sites)
-    occupied = jnp.any(centers[None, :] == jnp.arange(owned)[:, None], axis=1)
-    site_energy = own[12] + jnp.where(occupied, shift, 0.0)
-    site_energy = site_energy.reshape(cells_x, cells_y, cells_z, sites)
-    return (site_energy, forces, virial)
+        back = back + from_next(totals[:, 2 * owned :], "gy")
+    site_energy, forces, virial = pl.pallas_call(
+        finish_kernel,
+        out_shape=(
+            jax.ShapeDtypeStruct(species.shape, F32),
+            jax.ShapeDtypeStruct(positions.shape, F32),
+            jax.ShapeDtypeStruct((*species.shape, 9), F32),
+        ),
+        in_specs=[vmem] * 3,
+        out_specs=(vmem, vmem, vmem),
+        name="write_outputs",
+    )(totals, back, shift_row)
+    return (site_energy, forces, jnp.transpose(virial, (4, 0, 1, 2, 3)))
 
 
 def solution(mesh):

time: 39.5 us -> 37.3 us (0.944)
  Pallas kernels: 5.89 us -> 9.42 us
  local copies, waits for them, and re-layouts: 6.75 us -> 4.16 us
  other arithmetic: 2.3 us -> 0.02 us
  starting transfers between devices: 10.5 us -> 10 us
    pallas_call x2 -> x4, Pallas kernels: 5.89 us -> 9.42 us  [the longest x1 4.04 us: local(): pl.pallas_call(functools.partial(force_kernel, kind, nbr), out_shape=(jax...]
    concatenate x2 -> x0, local copies, waits for them, and re-layouts: 2.92 us -> none  [the longest x1 1.48 us: local(): jnp.concatenate([side[:owned] for side in sides] + [side[owned:owned + ce...]
    unnamed x21 -> x12, local copies, waits for them, and re-layouts: 1.99 us -> 3.24 us
    concatenate x2 -> x0, other arithmetic: 0.83 us -> none  [the longest x1 0.76 us: local(): payload = jnp.concatenate([features.reshape(owned, width), coords], axis=0)]
    reshape x2 -> x0, local copies, waits for them, and re-layouts: 0.76 us -> none  [the longest x1 0.68 us: local(): forces = own[0:3].reshape(3, cells_x, cells_y, cells_z, sites)]
    reduce_sum x1 -> x0, other arithmetic: 0.76 us -> none  [local(): jnp.sum(jnp.where(chosen, species_shift, 0.0), axis=-1).reshape(owned)]
    transpose x1 -> x0, local copies, waits for them, and re-layouts: 0.73 us -> none  [local(): jnp.transpose(positions, (1, 2, 3, 0, 4)).reshape(cell_count, 3 * sites)]
    slice x9 -> x3, local copies, waits for them, and re-layouts: 0.11 us -> 0.84 us  [the longest x2 0.77 us: local(): both = joined([here[:short], next_x[:short]])]
  transfers between devices with their start and end apart: 6 -> 6, of which waited for: 5 -> 5; matrix products, arithmetic and copies ran while one was open for 1% -> 2% of each run, Pallas kernels for 5% -> 6%
where the time goes in v6:
time: 37.3 us; the launch traced here: 36.9 us
  waiting for transfers between devices  12.6 us (34%)
  starting transfers between devices  10 us (27%)
  Pallas kernels  9.42 us (25%)
  local copies, waits for them, and re-layouts  4.16 us (11%)
  between operations  0.68 us (2%)
    ppermute x3, waiting for transfers between devices, from_last(): return lax.ppermute(array, axis, [(i, (i + 1) % size) for i in range(size)])  9.15 us
    ppermute x3, starting transfers between devices, from_next(): return lax.ppermute(array, axis, [((i + 1) % size, i) for i in range(size)])  6.66 us
    pallas_call x1, Pallas kernels, local(): pl.pallas_call(functools.partial(force_kernel, kind, nbr), out_shape=(jax...  4.04 us
    ppermute x3, waiting for transfers between devices, from_next(): return lax.ppermute(array, axis, [((i + 1) % size, i) for i in range(size)])  3.48 us
    ppermute x3, starting transfers between devices, from_last(): return lax.ppermute(array, axis, [(i, (i + 1) % size) for i in range(size)])  3.36 us
    unnamed x12, local copies, waits for them, and re-layouts  3.24 us
    pallas_call x1, Pallas kernels, local(): pl.pallas_call(functools.partial(weight_kernel, nbr), out_shape=(jax.Shap...  2.27 us
    pallas_call x1, Pallas kernels, local(): pl.pallas_call(functools.partial(pack_kernel, kind), out_shape=(jax.Shape...  1.64 us
  transfers between devices with their start and end apart: 6, of which 5 were waited for; matrix products, arithmetic and copies ran while one was open for 2% of the time, Pallas kernels for 6%

profile of v6, /device:TPU:0, one launch (start us, length us, event | category | flops | bytes accessed | tf_op | source)
XLA Modules:
  0.0 36.9 jit_solution(13828679575023875039)
XLA Ops:
  0.6 1.6 %pack_payload.1 = (f32[48,128]{1,0:T(8,128)}, f32[1,32]{1,0:T(1,128)}) custom-call(f32[3,2,1,2,8]{4,3,2,1,0:T(2,128)} %positions_ref.1, f32[32,128]{1,0:T(8,128)} %bitcast.4, s32[2,1,2,8]{3,2,1,0:T(2,128)} %species_ref.1, s32[1,32]{1,0:T(1,128)} %bitcast.5, s32[32,32]{1,0:T(8,128)} %neighbours_ref.1, f32[5]{0:T(128)} %scale_ref.1, f32[5]{0:T(128)} %shift_ref.1), custom_call_target="tpu_custom_call" | custom-call | tf_op jit(solution)/shard_map/pack_payload/pallas_call | solution.py:536
  2.3 5.0 %collective-permute-start = (f32[48,128]{1,0:T(8,128)}, f32[48,128]{1,0:T(8,128)S(1)}, u32[]{:S(2)}, u32[]{:S(2)}) collective-permute-start(f32[48,128]{1,0:T(8,128)} %get-tuple-element.12.here_ref), channel_id=1, source_target_pairs={{8,0},{16,8},{24,16},{0,24},{9,1},{17,9},{25,17},{1,25},{10,2},{18... | collective-permute-start | bytes 73736 | tf_op jit(solution)/shard_map/ppermute | solution.py:528
  7.3 0.8 %slice.15 = f32[40,128]{1,0:T(8,128)S(1)} slice(f32[48,128]{1,0:T(8,128)} %get-tuple-element.12.here_ref), slice={[0:40], [0:128]} | slice | bytes 40960 | tf_op jit(solution)/shard_map/slice | solution.py:574
  8.1 1.0 %collective-permute-done.next_x_ref = f32[48,128]{1,0:T(8,128)S(1)} collective-permute-done((f32[48,128]{1,0:T(8,128)}, f32[48,128]{1,0:T(8,128)S(1)}, u32[]{:S(2)}, u32[]{:S(2)}) %collective-permute-start) | collective-permute-done | bytes 24608 | tf_op jit(solution)/shard_map/ppermute | solution.py:528
  9.1 0.0 copy-start.1
  9.1 1.6 %collective-permute-start.1 = (f32[80,128]{1,0:T(8,128)S(1)}, f32[80,128]{1,0:T(8,128)S(1)}, u32[]{:S(2)}, u32[]{:S(2)}) collective-permute-start(f32[80,128]{1,0:T(8,128)S(1)} %pad_add_fusion.1), channel_id=1, source_target_pairs={{4,0},{0,4},{5,1},{1,5},{6,2},{2,6},{7,3},{3,7},{12,8},{8,12},{13,... | collective-permute-start | bytes 122888 | tf_op jit(solution)/shard_map/ppermute | solution.py:528
  10.6 2.5 %collective-permute-done.1.sides_ref = f32[80,128]{1,0:T(8,128)S(1)} collective-permute-done((f32[80,128]{1,0:T(8,128)S(1)}, f32[80,128]{1,0:T(8,128)S(1)}, u32[]{:S(2)}, u32[]{:S(2)}) %collective-permute-start.1) | collective-permute-done | bytes 40992 | tf_op jit(solution)/shard_map/ppermute | solution.py:528
  13.1 0.0 copy-done.1
  13.1 0.1 collective-permute-start.2
  13.2 0.0 copy-start.3
  13.2 2.3 %split_weights.1 = (bf16[2048,256]{1,0:T(8,128)(2,1)}, f32[256,128]{1,0:T(8,128)}) custom-call(f32[128,128]{1,0:T(8,128)} %center_weight_ref.1, f32[128,128]{1,0:T(8,128)} %near_weight_ref.1, f32[3,128]{1,0:T(4,128)} %path_weight_ref.1, f32[128,256]{1,0:T(8,128)} %value_weight_ref.1, f32[256,128]{1,0:T(8,128)} %latent_weight_ref.1, f32[1,128]{1,0:T(1,128)} %bitcast.6), custom_call_target="tpu_custom_call" | custom-call | tf_op jit(solution)/shard_map/split_weights/pallas_call | solution.py:555
  15.5 0.0 collective-permute-done.2.next_z_ref
  15.5 0.0 copy-done.3
  15.5 0.0 copy-start
  15.5 1.2 %copy-done = bf16[2048,256]{1,0:T(8,128)(2,1)S(1)} copy-done((bf16[2048,256]{1,0:T(8,128)(2,1)S(1)}, bf16[2048,256]{1,0:T(8,128)(2,1)}, u32[]{:S(2)}) %copy-start) | copy-done | bytes 1048600
  16.7 0.0 copy-start.2
  16.7 0.9 %copy-done.2 = f32[256,128]{1,0:T(8,128)S(1)} copy-done((f32[256,128]{1,0:T(8,128)S(1)}, f32[256,128]{1,0:T(8,128)}, u32[]{:S(2)}) %copy-start.2) | copy-done | bytes 131096
  17.6 4.0 %pair_forces.1 = (f32[16,128]{1,0:T(8,128)S(1)}, f32[16,128]{1,0:T(8,128)S(1)}) custom-call(f32[48,128]{1,0:T(8,128)S(1)} %copy-done.1, f32[48,128]{1,0:T(8,128)S(1)} %collective-permute-done.next_x_ref, f32[80,128]{1,0:T(8,128)S(1)} %collective-permute-done.1.sides_ref, f32[176,128]{1,0:T(8,128)S(1)} %collective-permute-done.2.next_z_ref, ...), custom_call_target="tpu_custom_call" | custom-call | tf_op jit(solution)/shard_map/pair_forces/pallas_call | solution.py:580
  21.7 1.6 %collective-permute-start.3 = (f32[16,128]{1,0:T(8,128)S(1)}, f32[16,128]{1,0:T(8,128)S(1)}, u32[]{:S(2)}, u32[]{:S(2)}) collective-permute-start(f32[16,128]{1,0:T(8,128)S(1)} %get-tuple-element.16), channel_id=1, source_target_pairs={{0,1},{1,2},{2,3},{3,0},{4,5},{5,6},{6,7},{7,4},{8,9},{9,10},{10,1... | collective-permute-start | bytes 24584 | tf_op jit(solution)/shard_map/ppermute | solution.py:532
  23.3 1.5 %collective-permute-done.3 = f32[16,128]{1,0:T(8,128)S(1)} collective-permute-done((f32[16,128]{1,0:T(8,128)S(1)}, f32[16,128]{1,0:T(8,128)S(1)}, u32[]{:S(2)}, u32[]{:S(2)}) %collective-permute-start.3) | collective-permute-done | bytes 8224 | tf_op jit(solution)/shard_map/ppermute | solution.py:532
  24.8 0.1 slice.22
  24.9 0.3 collective-permute-start.4
  25.2 5.5 %collective-permute-done.4 = f32[16,64]{1,0:T(8,128)S(1)} collective-permute-done((f32[16,64]{1,0:T(8,128)S(1)}, f32[16,64]{1,0:T(8,128)S(1)}, u32[]{:S(2)}, u32[]{:S(2)}) %collective-permute-start.4) | collective-permute-done | bytes 4128 | tf_op jit(solution)/shard_map/ppermute | solution.py:532
  30.6 0.0 copy-start.4
  30.6 0.1 slice.23
  30.7 0.5 %copy-done.4 = f32[16,64]{1,0:T(8,128)} copy-done((f32[16,64]{1,0:T(8,128)}, f32[16,64]{1,0:T(8,128)S(1)}, u32[]{:S(2)}) %copy-start.4) | copy-done | bytes 4120
  31.2 1.5 %collective-permute-start.5 = (f32[16,32]{1,0:T(8,128)S(1)}, f32[16,32]{1,0:T(8,128)S(1)}, u32[]{:S(2)}, u32[]{:S(2)}) collective-permute-start(f32[16,32]{1,0:T(8,128)S(1)} %slice.23), channel_id=1, source_target_pairs={{0,4},{4,0},{1,5},{5,1},{2,6},{6,2},{3,7},{7,3},{8,12},{12,8},{9,1... | collective-permute-start | bytes 6152 | tf_op jit(solution)/shard_map/ppermute | solution.py:532
  32.7 2.2 %collective-permute-done.5.near_ref = f32[16,32]{1,0:T(8,128)S(1)} collective-permute-done((f32[16,32]{1,0:T(8,128)S(1)}, f32[16,32]{1,0:T(8,128)S(1)}, u32[]{:S(2)}, u32[]{:S(2)}) %collective-permute-start.5) | collective-permute-done | bytes 2080 | tf_op jit(solution)/shard_map/ppermute | solution.py:532
  34.9 0.0 copy-start.5
  34.9 0.6 %copy-done.5 = f32[16,32]{1,0:T(8,128)} copy-done((f32[16,32]{1,0:T(8,128)}, f32[16,32]{1,0:T(8,128)S(1)}, u32[]{:S(2)}) %copy-start.5) | copy-done | bytes 2072
  35.5 1.5 %write_outputs.1 = (f32[2,1,2,8]{3,2,1,0:T(2,128)}, f32[3,2,1,2,8]{4,3,2,1,0:T(2,128)}, f32[2,1,2,8,9]{4,3,2,1,0:T(8,128)}) custom-call(f32[16,64]{1,0:T(8,128)} %copy-done.4, f32[16,32]{1,0:T(8,128)} %copy-done.5, f32[1,32]{1,0:T(1,128)} %get-tuple-element.17.shift_row_ref), custom_call_target="tpu_custom_call" | custom-call | tf_op jit(solution)/shard_map/write_outputs/pallas_call | solution.py:597
  (5 shorter events, 0.0 us)
Async XLA Ops:
  2.3 6.8 %collective-permute-start = (f32[48,128]{1,0:T(8,128)}, f32[48,128]{1,0:T(8,128)S(1)}, u32[]{:S(2)}, u32[]{:S(2)}) collective-permute-start(f32[48,128]{1,0:T(8,128)} %get-tuple-element.12.here_ref), channel_id=1, source_target_pairs={{8,0},{16,8},{24,16},{0,24},{9,1},{17,9},{25,17},{1,25},{10,2},{18... | collective-permute-start | bytes 73736 | tf_op jit(solution)/shard_map/ppermute | solution.py:528
  9.1 4.1 %copy-start.1 = (f32[48,128]{1,0:T(8,128)S(1)}, f32[48,128]{1,0:T(8,128)}, u32[]{:S(2)}) copy-start(f32[48,128]{1,0:T(8,128)} %get-tuple-element.12.here_ref) | copy-start | bytes 73732
  9.1 4.1 %collective-permute-start.1 = (f32[80,128]{1,0:T(8,128)S(1)}, f32[80,128]{1,0:T(8,128)S(1)}, u32[]{:S(2)}, u32[]{:S(2)}) collective-permute-start(f32[80,128]{1,0:T(8,128)S(1)} %pad_add_fusion.1), channel_id=1, source_target_pairs={{4,0},{0,4},{5,1},{1,5},{6,2},{2,6},{7,3},{3,7},{12,8},{8,12},{13,... | collective-permute-start | bytes 122888 | tf_op jit(solution)/shard_map/ppermute | solution.py:528
  13.1 2.4 %collective-permute-start.2 = (f32[176,128]{1,0:T(8,128)S(1)}, f32[176,128]{1,0:T(8,128)S(1)}, u32[]{:S(2)}, u32[]{:S(2)}) collective-permute-start(f32[176,128]{1,0:T(8,128)S(1)} %pad_add_fusion), channel_id=1, source_target_pairs={{1,0},{2,1},{3,2},{0,3},{5,4},{6,5},{7,6},{4,7},{9,8},{10,9},{11,1... | collective-permute-start | bytes 270344 | tf_op jit(solution)/shard_map/ppermute | solution.py:528
  13.2 2.3 %copy-start.3 = (f32[8,128]{1,0:T(8,128)S(1)}, f32[8,128]{1,0:T(8,128)}, u32[]{:S(2)}) copy-start(f32[8,128]{1,0:T(8,128)} %basis_weight_ref.1) | copy-start | bytes 12292
  15.5 1.2 %copy-start = (bf16[2048,256]{1,0:T(8,128)(2,1)S(1)}, bf16[2048,256]{1,0:T(8,128)(2,1)}, u32[]{:S(2)}) copy-start(bf16[2048,256]{1,0:T(8,128)(2,1)} %get-tuple-element.13.stack_ref) | copy-start | bytes 3145732
  16.7 0.9 %copy-start.2 = (f32[256,128]{1,0:T(8,128)S(1)}, f32[256,128]{1,0:T(8,128)}, u32[]{:S(2)}) copy-start(f32[256,128]{1,0:T(8,128)} %get-tuple-element.14.column_ref) | copy-start | bytes 393220
  21.7 3.1 %collective-permute-start.3 = (f32[16,128]{1,0:T(8,128)S(1)}, f32[16,128]{1,0:T(8,128)S(1)}, u32[]{:S(2)}, u32[]{:S(2)}) collective-permute-start(f32[16,128]{1,0:T(8,128)S(1)} %get-tuple-element.16), channel_id=1, source_target_pairs={{0,1},{1,2},{2,3},{3,0},{4,5},{5,6},{6,7},{7,4},{8,9},{9,10},{10,1... | collective-permute-start | bytes 24584 | tf_op jit(solution)/shard_map/ppermute | solution.py:532
  24.9 5.7 %collective-permute-start.4 = (f32[16,64]{1,0:T(8,128)S(1)}, f32[16,64]{1,0:T(8,128)S(1)}, u32[]{:S(2)}, u32[]{:S(2)}) collective-permute-start(f32[16,64]{1,0:T(8,128)S(1)} %slice.22), channel_id=1, source_target_pairs={{0,8},{8,16},{16,24},{24,0},{1,9},{9,17},{17,25},{25,1},{2,10},{10... | collective-permute-start | bytes 12296 | tf_op jit(solution)/shard_map/ppermute | solution.py:532
  30.6 0.6 %copy-start.4 = (f32[16,64]{1,0:T(8,128)}, f32[16,64]{1,0:T(8,128)S(1)}, u32[]{:S(2)}) copy-start(f32[16,64]{1,0:T(8,128)S(1)} %slice_add_fusion.mine_ref) | copy-start | bytes 12292
  31.2 3.7 %collective-permute-start.5 = (f32[16,32]{1,0:T(8,128)S(1)}, f32[16,32]{1,0:T(8,128)S(1)}, u32[]{:S(2)}, u32[]{:S(2)}) collective-permute-start(f32[16,32]{1,0:T(8,128)S(1)} %slice.23), channel_id=1, source_target_pairs={{0,4},{4,0},{1,5},{5,1},{2,6},{6,2},{3,7},{7,3},{8,12},{12,8},{9,1... | collective-permute-start | bytes 6152 | tf_op jit(solution)/shard_map/ppermute | solution.py:532
  34.9 0.6 %copy-start.5 = (f32[16,32]{1,0:T(8,128)}, f32[16,32]{1,0:T(8,128)S(1)}, u32[]{:S(2)}) copy-start(f32[16,32]{1,0:T(8,128)S(1)} %collective-permute-done.5.near_ref) | copy-start | bytes 6148

commit v7 on v6

--- a/solution.py
+++ b/solution.py
@@ -153,50 +153,12 @@
     payload_ref[owned + 8 :] = codes
 
 
-def weight_kernel(
-    nbr,
-    center_weight_ref,
-    near_weight_ref,
-    path_weight_ref,
-    value_weight_ref,
-    latent_weight_ref,
-    out_weight_ref,
-    stack_ref,
-    column_ref,
-):
-    width = near_weight_ref.shape[0]
-    value_high, value_low = split(value_weight_ref[...])
-    latent_high, latent_low = split(jnp.transpose(latent_weight_ref[...]))
-    parts = [
-        stacked(*split(jnp.transpose(value_weight_ref[...]))),
-        jnp.concatenate([latent_high, latent_low], axis=0),
-        stacked(*split(latent_weight_ref[...])),
-        jnp.concatenate([value_high, value_low], axis=0),
-        stacked(*split(jnp.transpose(near_weight_ref[...]))),
-        stacked(*split(jnp.transpose(center_weight_ref[...]))),
-    ]
-    start = 0
-    for part in parts:
-        stack_ref[start : start + part.shape[0], :] = part
-        start += part.shape[0]
-    level = lax.broadcasted_iota(jnp.int32, (ORDERS, width), 0)
-    path_rows = jnp.where(
-        level == 0,
-        path_weight_ref[0:1, :],
-        jnp.where(
-            level < 4,
-            path_weight_ref[1:2, :],
-            jnp.where(level < 9, path_weight_ref[2:3, :], 0.0),
-        ),
-    )
-    paths_t = jnp.transpose(jnp.concatenate([path_rows] * GROUP, axis=0))
-    column_ref[:width] = paths_t * (1.0 / math.sqrt(nbr))
-    column_ref[width:] = jnp.transpose(jnp.broadcast_to(out_weight_ref[...], (width, width)))
-
-
-def finish_kernel(mine_ref, near_ref, shift_row_ref, energy_ref, forces_ref, virial_ref):
-    owned = near_ref.shape[1]
-    total = mine_ref[:, :owned] + near_ref[...]
+def finish_kernel(mine_ref, shift_row_ref, *refs):
+    *near_refs, energy_ref, forces_ref, virial_ref = refs
+    owned = near_refs[0].shape[1]
+    total = mine_ref[:, :owned]
+    for near_ref in near_refs:
+        total = total + near_ref[...]
     energy = total[12:13] + shift_row_ref[...]
     columns = jnp.transpose(jnp.concatenate([total, jnp.zeros((ORDERS, 128 - owned), F32)], axis=1))
     for cell in range(OWN_CELLS):
@@ -208,19 +170,20 @@
         virial_ref[x, 0, z] = columns[lanes, 3:12]
 
 
-def force_kernel(
-    kind,
-    nbr,
-    here_ref,
-    next_x_ref,
-    sides_ref,
-    next_z_ref,
-    stack_ref,
-    column_ref,
-    basis_weight_ref,
-    send_ref,
-    keep_ref,
-):
+def force_kernel(kind, nbr, here_ref, next_x_ref, *refs):
+    near_side_refs = refs[: 2 * kind - 2]
+    (
+        next_z_ref,
+        center_weight_ref,
+        near_weight_ref,
+        basis_weight_ref,
+        path_weight_ref,
+        value_weight_ref,
+        latent_weight_ref,
+        out_weight_ref,
+        keep_ref,
+        send_ref,
+    ) = refs[2 * kind - 2 :]
     height, width = here_ref.shape
     owned = OWN_CELLS * SITES
     short = owned + 8
@@ -236,8 +199,7 @@
     root_five = math.sqrt(5.0)
     far = next_z_ref[...]
     mains = [here_ref[...], next_x_ref[...], far[:height], far[height : 2 * height]]
-    near_sides = sides_ref[...]
-    near_sides = [near_sides[i * short : (i + 1) * short] for i in range(2 * kind - 2)]
+    near_sides = [ref[...] for ref in near_side_refs]
     far_sides = far[2 * height :]
     far_sides = [far_sides[i * short : (i + 1) * short] for i in range(2 * kind - 2)]
     blocks_in = [
@@ -284,21 +246,22 @@
     spread = jnp.where(keep, spread, 0.0)
     place_parts = jnp.concatenate(split3(jnp.transpose(spread)[: 3 * sites]), axis=0)
 
-    value_rows = stack_ref[: 4 * width, :]
-    latent_both_t = stack_ref[4 * width : 6 * width, :]
-    latent_high_t = latent_both_t[:width]
-    latent_rows = stack_ref[6 * width : 10 * width, :]
-    value_both = stack_ref[10 * width : 12 * width, :]
-    value_high = value_both[:width]
+    value_rows = stacked(*split(jnp.transpose(value_weight_ref[...])))
+    latent_high_t, latent_low_t = split(jnp.transpose(latent_weight_ref[...]))
+    latent_both_t = jnp.concatenate([latent_high_t, latent_low_t], axis=0)
+    latent_rows = stacked(*split(latent_weight_ref[...]))
+    value_high, value_low = split(value_weight_ref[...])
+    value_both = jnp.concatenate([value_high, value_low], axis=0)
     basis_t = jnp.transpose(basis_weight_ref[...])
     basis_high_t, basis_low_t = split(basis_t)
     basis_rows = stacked(*split(basis_weight_ref[...]))
 
     def project(weight, rows):
+        weight = stacked(*split(jnp.transpose(weight)))
         return folded(mm_nt(weight, jnp.concatenate(split(rows), axis=1)))
 
-    near_t = project(stack_ref[12 * width : 14 * width, :], feats)
-    own_t = project(stack_ref[14 * width :, :], center_feats)
+    near_t = project(near_weight_ref[...], feats)
+    own_t = project(center_weight_ref[...], center_feats)
     near_high, near_low = split(near_t)
     own_high, own_low = split(own_t)
     lookup = jnp.concatenate(
@@ -313,8 +276,19 @@
         [*split3(scale_rows), jnp.zeros((16 - 3 * groups, 128), BF16)], axis=0
     )
 
-    paths_t = column_ref[:width]
-    out_column = jnp.concatenate([column_ref[width:]] * (pairs // width), axis=1)
+    level = lax.broadcasted_iota(jnp.int32, (ORDERS, width), 0)
+    path_rows = jnp.where(
+        level == 0,
+        path_weight_ref[0:1, :],
+        jnp.where(
+            level < 4,
+            path_weight_ref[1:2, :],
+            jnp.where(level < 9, path_weight_ref[2:3, :], 0.0),
+        ),
+    )
+    paths_t = jnp.transpose(jnp.concatenate([path_rows] * GROUP, axis=0)) * (1.0 / root_count)
+    out_column = jnp.transpose(jnp.broadcast_to(out_weight_ref[...], (width, width)))
+    out_column = jnp.concatenate([out_column] * (pairs // width), axis=1)
 
     site_ids = lax.broadcasted_iota(jnp.int32, (known, pairs), 0)
     slot_ids = lax.broadcasted_iota(jnp.int32, (owned, pairs), 0)
@@ -523,13 +497,16 @@
     nbr = pairs // owned
     kind = min(3, lax.axis_size("gy"))
 
-    def from_next(array, axis):
-        size = lax.axis_size(axis)
-        return lax.ppermute(array, axis, [((i + 1) % size, i) for i in range(size)])
-
-    def from_last(array, axis):
-        size = lax.axis_size(axis)
-        return lax.ppermute(array, axis, [(i, (i + 1) % size) for i in range(size)])
+    def moved(array, steps):
+        names = tuple(steps)
+        sizes = [lax.axis_size(name) for name in names]
+        route = []
+        for at in np.ndindex(*sizes):
+            to = [(p + steps[name]) % size for p, name, size in zip(at, names, sizes)]
+            route.append(
+                (int(np.ravel_multi_index(at, sizes)), int(np.ravel_multi_index(to, sizes)))
+            )
+        return lax.ppermute(array, names, route)
 
     vmem = pl.BlockSpec(memory_space=pltpu.VMEM)
     smem = pl.BlockSpec(memory_space=pltpu.SMEM)
@@ -542,6 +519,7 @@
         in_specs=[vmem] * 5 + [smem] * 2,
         out_specs=(vmem, vmem),
         scratch_shapes=[pltpu.VMEM((owned, 128), F32)],
+        compiler_params=pltpu.CompilerParams(vmem_limit_bytes=8 * 1024 * 1024),
         name="pack_payload",
     )(
         positions,
@@ -552,48 +530,46 @@
         species_scale,
         species_shift,
     )
-    stack, column = pl.pallas_call(
-        functools.partial(weight_kernel, nbr),
-        out_shape=(
-            jax.ShapeDtypeStruct((16 * width, 2 * width), BF16),
-            jax.ShapeDtypeStruct((2 * width, width), F32),
-        ),
-        in_specs=[vmem] * 6,
-        out_specs=(vmem, vmem),
-        name="split_weights",
-    )(
-        center_weight,
-        near_weight,
-        path_weight,
-        value_weight,
-        latent_weight,
-        out_weight.reshape(1, width),
-    )
-    short = owned + 8
-    next_x = from_next(here, "gx")
-    both = joined([here[:short], next_x[:short]])
-    sides = from_next(both, "gy")
-    if kind == 3:
-        sides = joined([sides, from_last(both, "gy")])
-    next_z = from_next(joined([here, next_x, sides]), "gz")
+    short = here[: owned + 8]
+    next_x = moved(here, {"gx": -1})
+    sides = []
+    for step in (-1, 1)[: kind - 1]:
+        sides.append(moved(short, {"gx": -1, "gy": step}))
+        sides.insert(-1, moved(short, {"gy": step}))
+    next_z = moved(joined([here, next_x, *sides]), {"gz": -1})
     half = 2 * kind * owned
-    send, keep = pl.pallas_call(
+    keep, send = pl.pallas_call(
         functools.partial(force_kernel, kind, nbr),
         out_shape=(
             jax.ShapeDtypeStruct((ORDERS, half), F32),
             jax.ShapeDtypeStruct((ORDERS, half), F32),
         ),
-        in_specs=[vmem] * 7,
+        in_specs=[vmem] * (8 + 2 * kind),
         out_specs=(vmem, vmem),
-        compiler_params=pltpu.CompilerParams(vmem_limit_bytes=40 * 1024 * 1024),
+        compiler_params=pltpu.CompilerParams(vmem_limit_bytes=32 * 1024 * 1024),
         name="pair_forces",
-    )(here, next_x, sides, next_z, stack, column, basis_weight)
-    totals = keep + from_last(send, "gz")
-    half = kind * owned
-    totals = totals[:, :half] + from_last(totals[:, half:], "gx")
-    back = from_last(totals[:, owned : 2 * owned], "gy")
-    if kind == 3:
-        back = back + from_next(totals[:, 2 * owned :], "gy")
+    )(
+        here,
+        next_x,
+        *sides,
+        next_z,
+        center_weight,
+        near_weight,
+        basis_weight,
+        path_weight,
+        value_weight,
+        latent_weight,
+        out_weight.reshape(1, width),
+    )
+    totals = keep + moved(send, {"gz": 1})
+
+    def part(index):
+        return totals[:, index * owned : (index + 1) * owned]
+
+    back = [moved(part(kind), {"gx": 1})]
+    for i, step in enumerate((1, -1)[: kind - 1]):
+        back.append(moved(part(kind + 1 + i), {"gx": 1, "gy": step}))
+        back.append(moved(part(1 + i), {"gy": step}))
     site_energy, forces, virial = pl.pallas_call(
         finish_kernel,
         out_shape=(
@@ -601,10 +577,11 @@
             jax.ShapeDtypeStruct(positions.shape, F32),
             jax.ShapeDtypeStruct((*species.shape, 9), F32),
         ),
-        in_specs=[vmem] * 3,
+        in_specs=[vmem] * (2 + len(back)),
         out_specs=(vmem, vmem, vmem),
+        compiler_params=pltpu.CompilerParams(vmem_limit_bytes=8 * 1024 * 1024),
         name="write_outputs",
-    )(totals, back, shift_row)
+    )(totals, shift_row, *back)
     return (site_energy, forces, jnp.transpose(virial, (4, 0, 1, 2, 3)))
 
 

time: 37.3 us -> 36.1 us (0.968)
  Pallas kernels: 9.42 us -> 5.61 us
  starting transfers between devices: 10 us -> 11.8 us
  local copies, waits for them, and re-layouts: 4.16 us -> 5.25 us
    pallas_call x1 -> x0, Pallas kernels: 2.27 us -> none  [local(): pl.pallas_call(functools.partial(weight_kernel, nbr), out_shape=(jax.Shap...]
    unnamed x12 -> x28, local copies, waits for them, and re-layouts: 3.24 us -> 5.17 us
    ppermute x6 -> x8, starting transfers between devices: 10 us -> 11.8 us  [moved(): return lax.ppermute(array, names, route)]
    pallas_call x1, Pallas kernels: 1.64 us -> 0.76 us  [local(): pl.pallas_call(functools.partial(pack_kernel, kind), out_shape=(jax.Shape...]
    slice x4 -> x2, local copies, waits for them, and re-layouts: 0.91 us -> 0.08 us  [the longest x1 0.08 us: part(): return totals[:, index * owned:(index + 1) * owned]]
    pallas_call x1, Pallas kernels: 1.46 us -> 0.75 us  [local(): pl.pallas_call(finish_kernel, out_shape=(jax.ShapeDtypeStruct(species.sha...]
    ppermute x6 -> x8, waiting for transfers between devices: 12.6 us -> 12.3 us  [moved(): return lax.ppermute(array, names, route)]
  transfers between devices with their start and end apart: 6 -> 8, of which waited for: 5 -> 7; matrix products, arithmetic and copies ran while one was open for 2% -> 0% of each run, Pallas kernels for 6% -> 0%
where the time goes in v7:
time: 36.1 us; the launch traced here: 35.7 us
  waiting for transfers between devices  12.3 us (34%)
  starting transfers between devices  11.8 us (33%)
  Pallas kernels  5.61 us (16%)
  local copies, waits for them, and re-layouts  5.25 us (15%)
  between operations  0.73 us (2%)
    ppermute x8, waiting for transfers between devices, moved(): return lax.ppermute(array, names, route)  12.3 us
    ppermute x8, starting transfers between devices, moved(): return lax.ppermute(array, names, route)  11.8 us
    unnamed x28, local copies, waits for them, and re-layouts  5.17 us
    pallas_call x1, Pallas kernels, local(): pl.pallas_call(functools.partial(force_kernel, kind, nbr), out_shape=(jax...  4.1 us
    pallas_call x1, Pallas kernels, local(): pl.pallas_call(functools.partial(pack_kernel, kind), out_shape=(jax.Shape...  0.76 us
    pallas_call x1, Pallas kernels, local(): pl.pallas_call(finish_kernel, out_shape=(jax.ShapeDtypeStruct(species.sha...  0.75 us
  transfers between devices with their start and end apart: 8, of which 7 were waited for; matrix products, arithmetic and copies ran while one was open for 0% of the time, Pallas kernels for 0%

profile of v7, /device:TPU:0, one launch (start us, length us, event | category | flops | bytes accessed | tf_op | source)
XLA Modules:
  0.0 35.7 jit_solution(284948281219708768)
XLA Ops:
  0.6 0.0 copy-start.8
  0.7 0.6 %copy-done.10 = s32[32]{0:T(128)S(1)} copy-done((s32[32]{0:T(128)S(1)}, s32[32]{0:T(128)}, u32[]{:S(2)}) %copy-start.10) | copy-done | bytes 152
  1.3 0.0 copy-done.11
  1.3 0.0 copy-done.12
  1.3 0.7 %copy-done.4 = f32[2,1,2,8,128]{4,3,2,1,0:T(8,128)S(1)} copy-done((f32[2,1,2,8,128]{4,3,2,1,0:T(8,128)S(1)}, f32[2,1,2,8,128]{4,3,2,1,0:T(8,128)}, u32[]{:S(2)}) %copy-start.4) | copy-done | bytes 16408
  2.1 0.7 %copy-done.5 = s32[32,32]{1,0:T(8,128)S(1)} copy-done((s32[32,32]{1,0:T(8,128)S(1)}, s32[32,32]{1,0:T(8,128)}, u32[]{:S(2)}) %copy-start.5) | copy-done | bytes 4120
  2.8 0.7 %copy-done.6 = f32[3,2,1,2,8]{4,3,2,1,0:T(2,128)S(1)} copy-done((f32[3,2,1,2,8]{4,3,2,1,0:T(2,128)S(1)}, f32[3,2,1,2,8]{4,3,2,1,0:T(2,128)}, u32[]{:S(2)}) %copy-start.6) | copy-done | bytes 408
  3.5 0.7 %copy-done.9 = s32[2,1,2,8]{3,2,1,0:T(2,128)S(1)} copy-done((s32[2,1,2,8]{3,2,1,0:T(2,128)S(1)}, s32[2,1,2,8]{3,2,1,0:T(2,128)}, u32[]{:S(2)}) %copy-start.9) | copy-done | bytes 152
  4.2 0.8 %pack_payload.1 = (f32[48,128]{1,0:T(8,128)S(1)}, f32[1,32]{1,0:T(1,128)S(1)}) custom-call(f32[3,2,1,2,8]{4,3,2,1,0:T(2,128)S(1)} %copy-done.6, f32[32,128]{1,0:T(8,128)S(1)} %bitcast.4, s32[2,1,2,8]{3,2,1,0:T(2,128)S(1)} %copy-done.9, s32[1,32]{1,0:T(1,128)S(1)} %bitcast.5, s32[32,32]{1,0:T(8,128)S(1)} %copy-done.5, f32[5]{0:T(128)S(1)} %copy-done.11, ...), custom_call_target="tpu_custom_call" | custom-call | tf_op jit(solution)/shard_map/pack_payload/pallas_call | solution.py:513
  4.9 5.1 %collective-permute-start = (f32[48,128]{1,0:T(8,128)S(1)}, f32[48,128]{1,0:T(8,128)S(1)}, u32[]{:S(2)}, u32[]{:S(2)}) collective-permute-start(f32[48,128]{1,0:T(8,128)S(1)} %get-tuple-element.10.here_ref), channel_id=1, source_target_pairs={{0,24},{8,0},{16,8},{24,16},{1,25},{9,1},{17,9},{25,17},{2,26},{10... | collective-permute-start | bytes 73736 | tf_op jit(solution)/shard_map/ppermute | solution.py:509
  10.0 1.4 %collective-permute-start.2 = (f32[40,128]{1,0:T(8,128)S(1)}, f32[40,128]{1,0:T(8,128)S(1)}, u32[]{:S(2)}, u32[]{:S(2)}) collective-permute-start(f32[40,128]{1,0:T(8,128)S(1)} %slice.12), channel_id=1, source_target_pairs={{0,28},{4,24},{8,4},{12,0},{16,12},{20,8},{24,20},{28,16},{1,29},{... | collective-permute-start | bytes 61448 | tf_op jit(solution)/shard_map/ppermute | solution.py:509
  11.4 0.5 %collective-permute-start.1 = (f32[40,128]{1,0:T(8,128)S(1)}, f32[40,128]{1,0:T(8,128)S(1)}, u32[]{:S(2)}, u32[]{:S(2)}) collective-permute-start(f32[40,128]{1,0:T(8,128)S(1)} %slice.12), channel_id=1, source_target_pairs={{0,4},{4,0},{1,5},{5,1},{2,6},{6,2},{3,7},{7,3},{8,12},{12,8},{9,1... | collective-permute-start | bytes 61448 | tf_op jit(solution)/shard_map/ppermute | solution.py:509
  11.9 2.8 %collective-permute-done.2.refs_1_ = f32[40,128]{1,0:T(8,128)S(1)} collective-permute-done((f32[40,128]{1,0:T(8,128)S(1)}, f32[40,128]{1,0:T(8,128)S(1)}, u32[]{:S(2)}, u32[]{:S(2)}) %collective-permute-start.2) | collective-permute-done | bytes 20512 | tf_op jit(solution)/shard_map/ppermute | solution.py:509
  14.7 0.5 %collective-permute-done.1.refs_0_ = f32[40,128]{1,0:T(8,128)S(1)} collective-permute-done((f32[40,128]{1,0:T(8,128)S(1)}, f32[40,128]{1,0:T(8,128)S(1)}, u32[]{:S(2)}, u32[]{:S(2)}) %collective-permute-start.1) | collective-permute-done | bytes 20512 | tf_op jit(solution)/shard_map/ppermute | solution.py:509
  15.2 0.0 collective-permute-done.next_x_ref
  15.2 0.0 copy-start.13
  15.2 0.1 collective-permute-start.3
  15.2 2.1 %collective-permute-done.3.refs_2_ = f32[176,128]{1,0:T(8,128)S(1)} collective-permute-done((f32[176,128]{1,0:T(8,128)S(1)}, f32[176,128]{1,0:T(8,128)S(1)}, u32[]{:S(2)}, u32[]{:S(2)}) %collective-permute-start.3) | collective-permute-done | bytes 90144 | tf_op jit(solution)/shard_map/ppermute | solution.py:509
  17.4 0.0 copy-start.2
  17.4 0.8 %copy-done.2 = f32[128,128]{1,0:T(8,128)S(1)} copy-done((f32[128,128]{1,0:T(8,128)S(1)}, f32[128,128]{1,0:T(8,128)}, u32[]{:S(2)}) %copy-start.2) | copy-done | bytes 65560
  18.2 0.8 %copy-done.3 = f32[128,128]{1,0:T(8,128)S(1)} copy-done((f32[128,128]{1,0:T(8,128)S(1)}, f32[128,128]{1,0:T(8,128)}, u32[]{:S(2)}) %copy-start.3) | copy-done | bytes 65560
  19.1 4.1 %pair_forces.1 = (f32[16,128]{1,0:T(8,128)S(1)}, f32[16,128]{1,0:T(8,128)S(1)}) custom-call(f32[48,128]{1,0:T(8,128)S(1)} %get-tuple-element.10.here_ref, f32[48,128]{1,0:T(8,128)S(1)} %collective-permute-done.next_x_ref, f32[40,128]{1,0:T(8,128)S(1)} %collective-permute-done.1.refs_0_, f32[40,128]{1,0:T(8,128)S(1)} %collective-permute-done.2.refs_1_, ...), custom_call_target="tpu_custom_call" | custom-call | tf_op jit(solution)/shard_map/pair_forces/pallas_call | solution.py:541
  23.2 1.8 %collective-permute-start.4 = (f32[16,128]{1,0:T(8,128)S(1)}, f32[16,128]{1,0:T(8,128)S(1)}, u32[]{:S(2)}, u32[]{:S(2)}) collective-permute-start(f32[16,128]{1,0:T(8,128)S(1)} %get-tuple-element.12), channel_id=1, source_target_pairs={{0,1},{1,2},{2,3},{3,0},{4,5},{5,6},{6,7},{7,4},{8,9},{9,10},{10,1... | collective-permute-start | bytes 24584 | tf_op jit(solution)/shard_map/ppermute | solution.py:509
  24.9 1.4 %collective-permute-done.4 = f32[16,128]{1,0:T(8,128)S(1)} collective-permute-done((f32[16,128]{1,0:T(8,128)S(1)}, f32[16,128]{1,0:T(8,128)S(1)}, u32[]{:S(2)}, u32[]{:S(2)}) %collective-permute-start.4) | collective-permute-done | bytes 8224 | tf_op jit(solution)/shard_map/ppermute | solution.py:509
  26.4 0.1 fusion
  26.5 1.0 %collective-permute-start.7 = (f32[16,32]{1,0:T(8,128)S(1)}, f32[16,32]{1,0:T(8,128)S(1)}, u32[]{:S(2)}, u32[]{:S(2)}) collective-permute-start(f32[16,32]{1,0:T(8,128)S(1)} %get-tuple-element.17), channel_id=1, source_target_pairs={{0,4},{4,0},{1,5},{5,1},{2,6},{6,2},{3,7},{7,3},{8,12},{12,8},{9,1... | collective-permute-start | bytes 6152 | tf_op jit(solution)/shard_map/ppermute | solution.py:509
  27.5 2.0 %collective-permute-start.6 = (f32[16,32]{1,0:T(8,128)S(1)}, f32[16,32]{1,0:T(8,128)S(1)}, u32[]{:S(2)}, u32[]{:S(2)}) collective-permute-start(f32[16,32]{1,0:T(8,128)S(1)} %get-tuple-element.18), channel_id=1, source_target_pairs={{0,12},{4,8},{8,20},{12,16},{16,28},{20,24},{24,4},{28,0},{1,13},{... | collective-permute-start | bytes 6152 | tf_op jit(solution)/shard_map/ppermute | solution.py:509
  29.5 0.0 collective-permute-start.5
  29.5 0.6 %collective-permute-done.7.refs_2_ = f32[16,32]{1,0:T(8,128)S(1)} collective-permute-done((f32[16,32]{1,0:T(8,128)S(1)}, f32[16,32]{1,0:T(8,128)S(1)}, u32[]{:S(2)}, u32[]{:S(2)}) %collective-permute-start.7) | collective-permute-done | bytes 2080 | tf_op jit(solution)/shard_map/ppermute | solution.py:509
  30.1 3.7 %collective-permute-done.6.refs_1_ = f32[16,32]{1,0:T(8,128)S(1)} collective-permute-done((f32[16,32]{1,0:T(8,128)S(1)}, f32[16,32]{1,0:T(8,128)S(1)}, u32[]{:S(2)}, u32[]{:S(2)}) %collective-permute-start.6) | collective-permute-done | bytes 2080 | tf_op jit(solution)/shard_map/ppermute | solution.py:509
  33.8 1.1 %collective-permute-done.5.refs_0_ = f32[16,32]{1,0:T(8,128)S(1)} collective-permute-done((f32[16,32]{1,0:T(8,128)S(1)}, f32[16,32]{1,0:T(8,128)S(1)}, u32[]{:S(2)}, u32[]{:S(2)}) %collective-permute-start.5) | collective-permute-done | bytes 2080 | tf_op jit(solution)/shard_map/ppermute | solution.py:509
  35.0 0.8 %write_outputs.1 = (f32[2,1,2,8]{3,2,1,0:T(2,128)}, f32[3,2,1,2,8]{4,3,2,1,0:T(2,128)}, f32[2,1,2,8,9]{4,3,2,1,0:T(8,128)}) custom-call(f32[16,128]{1,0:T(8,128)S(1)} %add.23.mine_ref, f32[1,32]{1,0:T(1,128)S(1)} %get-tuple-element.13.shift_row_ref, f32[16,32]{1,0:T(8,128)S(1)} %collective-permute-done.5.refs_0_, ...), custom_call_target="tpu_custom_call" | custom-call | tf_op jit(solution)/shard_map/write_outputs/pallas_call | solution.py:573
  (19 shorter events, 0.0 us)
Async XLA Ops:
  0.6 16.7 %copy-start.8 = (f32[3,128]{1,0:T(4,128)S(1)}, f32[3,128]{1,0:T(4,128)}, u32[]{:S(2)}) copy-start(f32[3,128]{1,0:T(4,128)} %refs_6_.1) | copy-start | bytes 4612
  0.6 0.7 %copy-start.10 = (s32[32]{0:T(128)S(1)}, s32[32]{0:T(128)}, u32[]{:S(2)}) copy-start(s32[32]{0:T(128)} %param.18) | copy-start | bytes 388
  0.7 0.7 %copy-start.11 = (f32[5]{0:T(128)S(1)}, f32[5]{0:T(128)}, u32[]{:S(2)}) copy-start(f32[5]{0:T(128)} %scale_ref.1) | copy-start | bytes 64
  0.7 0.7 %copy-start.12 = (f32[5]{0:T(128)S(1)}, f32[5]{0:T(128)}, u32[]{:S(2)}) copy-start(f32[5]{0:T(128)} %shift_ref.1) | copy-start | bytes 64
  1.3 0.7 %copy-start.4 = (f32[2,1,2,8,128]{4,3,2,1,0:T(8,128)S(1)}, f32[2,1,2,8,128]{4,3,2,1,0:T(8,128)}, u32[]{:S(2)}) copy-start(f32[2,1,2,8,128]{4,3,2,1,0:T(8,128)} %param.16) | copy-start | bytes 49156
  2.1 0.7 %copy-start.5 = (s32[32,32]{1,0:T(8,128)S(1)}, s32[32,32]{1,0:T(8,128)}, u32[]{:S(2)}) copy-start(s32[32,32]{1,0:T(8,128)} %neighbours_ref.1) | copy-start | bytes 12292
  2.8 0.7 %copy-start.6 = (f32[3,2,1,2,8]{4,3,2,1,0:T(2,128)S(1)}, f32[3,2,1,2,8]{4,3,2,1,0:T(2,128)}, u32[]{:S(2)}) copy-start(f32[3,2,1,2,8]{4,3,2,1,0:T(2,128)} %positions_ref.1) | copy-start | bytes 1156
  3.5 0.7 %copy-start.9 = (s32[2,1,2,8]{3,2,1,0:T(2,128)S(1)}, s32[2,1,2,8]{3,2,1,0:T(2,128)}, u32[]{:S(2)}) copy-start(s32[2,1,2,8]{3,2,1,0:T(2,128)} %species_ref.1) | copy-start | bytes 388
  4.1 13.2 %copy-start = (f32[128,256]{1,0:T(8,128)S(1)}, f32[128,256]{1,0:T(8,128)}, u32[]{:S(2)}) copy-start(f32[128,256]{1,0:T(8,128)} %refs_7_.1) | copy-start | bytes 393220
  4.2 13.2 %copy-start.1 = (f32[256,128]{1,0:T(8,128)S(1)}, f32[256,128]{1,0:T(8,128)}, u32[]{:S(2)}) copy-start(f32[256,128]{1,0:T(8,128)} %refs_8_.1) | copy-start | bytes 393220
  4.9 10.2 %collective-permute-start = (f32[48,128]{1,0:T(8,128)S(1)}, f32[48,128]{1,0:T(8,128)S(1)}, u32[]{:S(2)}, u32[]{:S(2)}) collective-permute-start(f32[48,128]{1,0:T(8,128)S(1)} %get-tuple-element.10.here_ref), channel_id=1, source_target_pairs={{0,24},{8,0},{16,8},{24,16},{1,25},{9,1},{17,9},{25,17},{2,26},{10... | collective-permute-start | bytes 73736 | tf_op jit(solution)/shard_map/ppermute | solution.py:509
  10.0 4.7 %collective-permute-start.2 = (f32[40,128]{1,0:T(8,128)S(1)}, f32[40,128]{1,0:T(8,128)S(1)}, u32[]{:S(2)}, u32[]{:S(2)}) collective-permute-start(f32[40,128]{1,0:T(8,128)S(1)} %slice.12), channel_id=1, source_target_pairs={{0,28},{4,24},{8,4},{12,0},{16,12},{20,8},{24,20},{28,16},{1,29},{... | collective-permute-start | bytes 61448 | tf_op jit(solution)/shard_map/ppermute | solution.py:509
  11.4 3.8 %collective-permute-start.1 = (f32[40,128]{1,0:T(8,128)S(1)}, f32[40,128]{1,0:T(8,128)S(1)}, u32[]{:S(2)}, u32[]{:S(2)}) collective-permute-start(f32[40,128]{1,0:T(8,128)S(1)} %slice.12), channel_id=1, source_target_pairs={{0,4},{4,0},{1,5},{5,1},{2,6},{6,2},{3,7},{7,3},{8,12},{12,8},{9,1... | collective-permute-start | bytes 61448 | tf_op jit(solution)/shard_map/ppermute | solution.py:509
  15.2 2.2 %copy-start.7 = (f32[8,128]{1,0:T(8,128)S(1)}, f32[8,128]{1,0:T(8,128)}, u32[]{:S(2)}) copy-start(f32[8,128]{1,0:T(8,128)} %refs_5_.1) | copy-start | bytes 12292
  15.2 2.2 %copy-start.13 = (f32[128]{0:T(128)S(1)}, f32[128]{0:T(128)}, u32[]{:S(2)}) copy-start(f32[128]{0:T(128)} %param.28) | copy-start | bytes 1540
  15.2 2.2 %collective-permute-start.3 = (f32[176,128]{1,0:T(8,128)S(1)}, f32[176,128]{1,0:T(8,128)S(1)}, u32[]{:S(2)}, u32[]{:S(2)}) collective-permute-start(f32[176,128]{1,0:T(8,128)S(1)} %pad_add_fusion), channel_id=1, source_target_pairs={{0,3},{1,0},{2,1},{3,2},{4,7},{5,4},{6,5},{7,6},{8,11},{9,8},{10,9... | collective-permute-start | bytes 270344 | tf_op jit(solution)/shard_map/ppermute | solution.py:509
  17.4 0.8 %copy-start.2 = (f32[128,128]{1,0:T(8,128)S(1)}, f32[128,128]{1,0:T(8,128)}, u32[]{:S(2)}) copy-start(f32[128,128]{1,0:T(8,128)} %refs_3_.1) | copy-start | bytes 196612
  18.2 0.8 %copy-start.3 = (f32[128,128]{1,0:T(8,128)S(1)}, f32[128,128]{1,0:T(8,128)}, u32[]{:S(2)}) copy-start(f32[128,128]{1,0:T(8,128)} %refs_4_.1) | copy-start | bytes 196612
  23.2 3.2 %collective-permute-start.4 = (f32[16,128]{1,0:T(8,128)S(1)}, f32[16,128]{1,0:T(8,128)S(1)}, u32[]{:S(2)}, u32[]{:S(2)}) collective-permute-start(f32[16,128]{1,0:T(8,128)S(1)} %get-tuple-element.12), channel_id=1, source_target_pairs={{0,1},{1,2},{2,3},{3,0},{4,5},{5,6},{6,7},{7,4},{8,9},{9,10},{10,1... | collective-permute-start | bytes 24584 | tf_op jit(solution)/shard_map/ppermute | solution.py:509
  26.5 3.7 %collective-permute-start.7 = (f32[16,32]{1,0:T(8,128)S(1)}, f32[16,32]{1,0:T(8,128)S(1)}, u32[]{:S(2)}, u32[]{:S(2)}) collective-permute-start(f32[16,32]{1,0:T(8,128)S(1)} %get-tuple-element.17), channel_id=1, source_target_pairs={{0,4},{4,0},{1,5},{5,1},{2,6},{6,2},{3,7},{7,3},{8,12},{12,8},{9,1... | collective-permute-start | bytes 6152 | tf_op jit(solution)/shard_map/ppermute | solution.py:509
  27.5 6.3 %collective-permute-start.6 = (f32[16,32]{1,0:T(8,128)S(1)}, f32[16,32]{1,0:T(8,128)S(1)}, u32[]{:S(2)}, u32[]{:S(2)}) collective-permute-start(f32[16,32]{1,0:T(8,128)S(1)} %get-tuple-element.18), channel_id=1, source_target_pairs={{0,12},{4,8},{8,20},{12,16},{16,28},{20,24},{24,4},{28,0},{1,13},{... | collective-permute-start | bytes 6152 | tf_op jit(solution)/shard_map/ppermute | solution.py:509
  29.5 5.4 %collective-permute-start.5 = (f32[16,32]{1,0:T(8,128)S(1)}, f32[16,32]{1,0:T(8,128)S(1)}, u32[]{:S(2)}, u32[]{:S(2)}) collective-permute-start(f32[16,32]{1,0:T(8,128)S(1)} %get-tuple-element.19), channel_id=1, source_target_pairs={{0,8},{8,16},{16,24},{24,0},{1,9},{9,17},{17,25},{25,1},{2,10},{10... | collective-permute-start | bytes 6152 | tf_op jit(solution)/shard_map/ppermute | solution.py:509

commit v8 on v7

--- a/solution.py
+++ b/solution.py
@@ -91,20 +91,43 @@
 
 def pack_kernel(
     kind,
+    positions_hbm,
+    features_hbm,
+    species_hbm,
+    centers_hbm,
+    neighbours_hbm,
+    scale_hbm,
+    shift_hbm,
+    payload_ref,
+    shift_row_ref,
+    wide_ref,
     positions_ref,
-    features_ref,
     species_ref,
     centers_ref,
     neighbours_ref,
     scale_ref,
     shift_ref,
-    payload_ref,
-    shift_row_ref,
-    wide_ref,
+    sems,
 ):
     owned, nbr = neighbours_ref.shape
     per_row = 128 // nbr
-    payload_ref[:owned] = features_ref[...]
+    pairs_in = (
+        (features_hbm, payload_ref.at[pl.ds(0, owned), :]),
+        (neighbours_hbm, neighbours_ref),
+        (centers_hbm, centers_ref),
+        (positions_hbm, positions_ref),
+        (species_hbm, species_ref),
+        (scale_hbm, scale_ref),
+        (shift_hbm, shift_ref),
+    )
+    copies = [
+        pltpu.make_async_copy(source, target, sems.at[i])
+        for i, (source, target) in enumerate(pairs_in)
+    ]
+    for copy in copies:
+        copy.start()
+    for copy in copies:
+        copy.wait()
     payload_ref[owned : owned + 8] = jnp.zeros((8, 128), F32)
     shift_row = jnp.zeros((1, 128), F32)
     for cell in range(OWN_CELLS):
@@ -142,7 +165,7 @@
     frame_y = column - 3 * frame_x
     near_x = frame_x + 1 - 2 * (cell >> 1)
     side = jnp.where(frame_y == 1, 0, jnp.where(frame_y == 2, 1, kind - 1))
-    block = (near_z >> 1) * 2 + (near_x >> 1)
+    block = (near_z >> 1) * 2 + 1 - (near_x >> 1)
     where = (block * kind + side) * owned + (near_x & 1) * 16 + (near_z & 1) * 8 + site
     code = jnp.where(live, 1 + where + (frame_y << 10), 0).astype(F32)
     wide_ref[...] = jnp.concatenate([code, jnp.zeros((owned, 128 - nbr), F32)], axis=1)
@@ -151,6 +174,18 @@
         more = wide_ref[pl.ds(j, owned // per_row, stride=per_row), :]
         codes = codes + pltpu.roll(more, j * nbr, 1)
     payload_ref[owned + 8 :] = codes
+
+
+def fetch_kernel(*refs):
+    count = len(refs) // 2
+    sems = refs[-1]
+    copies = [
+        pltpu.make_async_copy(refs[i], refs[count + i], sems.at[i]) for i in range(count)
+    ]
+    for copy in copies:
+        copy.start()
+    for copy in copies:
+        copy.wait()
 
 
 def finish_kernel(mine_ref, shift_row_ref, *refs):
@@ -170,7 +205,7 @@
         virial_ref[x, 0, z] = columns[lanes, 3:12]
 
 
-def force_kernel(kind, nbr, here_ref, next_x_ref, *refs):
+def force_kernel(kind, nbr, here_ref, last_x_ref, *refs):
     near_side_refs = refs[: 2 * kind - 2]
     (
         next_z_ref,
@@ -198,7 +233,7 @@
     root_fifteen = math.sqrt(15.0)
     root_five = math.sqrt(5.0)
     far = next_z_ref[...]
-    mains = [here_ref[...], next_x_ref[...], far[:height], far[height : 2 * height]]
+    mains = [here_ref[...], last_x_ref[...], far[:height], far[height : 2 * height]]
     near_sides = [ref[...] for ref in near_side_refs]
     far_sides = far[2 * height :]
     far_sides = [far_sides[i * short : (i + 1) * short] for i in range(2 * kind - 2)]
@@ -217,12 +252,12 @@
     cell_row = lax.broadcasted_iota(jnp.int32, (kind * OWN_CELLS, 128), 0) % OWN_CELLS
     tile_lane = lax.broadcasted_iota(jnp.int32, (kind * OWN_CELLS, 128), 1)
     for g, block in enumerate(blocks_in):
-        ahead_x, ahead_z = g % 2, g // 2
-        cell = (1 - ahead_x) * 2 + 1 - ahead_z
+        behind_x, ahead_z = g % 2, g // 2
+        cell = behind_x * 2 + 1 - ahead_z
         center_feats.append(block[0][cell * sites : (cell + 1) * sites])
         rows = jnp.concatenate([side[owned : owned + OWN_CELLS] for side in block], axis=0)
         scales.append(rows[cell : cell + 1])
-        corner_x = (cell_row // 2 + 2 * ahead_x).astype(F32) * CELL_SIDE
+        corner_x = (cell_row // 2 + 2 - 2 * behind_x).astype(F32) * CELL_SIDE
         corner_z = (cell_row % 2 + 2 * ahead_z).astype(F32) * CELL_SIDE
         corner = jnp.where(
             tile_lane < sites, corner_x, jnp.where(tile_lane < 2 * sites, 0.0, corner_z)
@@ -294,7 +329,7 @@
     slot_ids = lax.broadcasted_iota(jnp.int32, (owned, pairs), 0)
     slot_row = lax.broadcasted_iota(jnp.int32, (1, pairs), 1) // nbr
     group_row = slot_row // GROUP
-    center_cell = (1 - group_row % 2) * 2 + 1 - group_row // 2
+    center_cell = group_row % 2 * 2 + 1 - group_row // 2
     center_row = group_row * (kind * owned) + center_cell * sites + slot_row % GROUP
     block_row = lax.broadcasted_iota(jnp.int32, (wide, span), 0) // ORDERS
     block_lane = lax.broadcasted_iota(jnp.int32, (wide, span), 1) // nbr
@@ -459,6 +494,10 @@
     totals = folded(near_sums + center_sums)
     keep_ref[...] = totals[:, : known // 2]
     send_ref[...] = totals[:, known // 2 :]
+
+
+def in_hbm(*arrays):
+    return [pltpu.with_memory_space_constraint(array, pltpu.HBM) for array in arrays]
 
 
 def joined(parts):
@@ -509,34 +548,63 @@
         return lax.ppermute(array, names, route)
 
     vmem = pl.BlockSpec(memory_space=pltpu.VMEM)
-    smem = pl.BlockSpec(memory_space=pltpu.SMEM)
+    hbm = pl.BlockSpec(memory_space=pltpu.HBM)
     here, shift_row = pl.pallas_call(
         functools.partial(pack_kernel, kind),
         out_shape=(
             jax.ShapeDtypeStruct((owned + 8 + pairs // 128, width), F32),
             jax.ShapeDtypeStruct((1, owned), F32),
         ),
-        in_specs=[vmem] * 5 + [smem] * 2,
+        in_specs=[hbm] * 7,
         out_specs=(vmem, vmem),
-        scratch_shapes=[pltpu.VMEM((owned, 128), F32)],
+        scratch_shapes=[
+            pltpu.VMEM((owned, 128), F32),
+            pltpu.VMEM(positions.shape, F32),
+            pltpu.VMEM(species.shape, jnp.int32),
+            pltpu.VMEM((1, owned), jnp.int32),
+            pltpu.VMEM(neighbours.shape, jnp.int32),
+            pltpu.SMEM(species_scale.shape, F32),
+            pltpu.SMEM(species_shift.shape, F32),
+            pltpu.SemaphoreType.DMA((7,)),
+        ],
         compiler_params=pltpu.CompilerParams(vmem_limit_bytes=8 * 1024 * 1024),
         name="pack_payload",
     )(
-        positions,
-        features.reshape(owned, width),
-        species,
-        centers.reshape(1, owned),
-        neighbours,
-        species_scale,
-        species_shift,
-    )
+        *in_hbm(
+            positions,
+            features.reshape(owned, width),
+            species,
+            centers.reshape(1, owned),
+            neighbours,
+            species_scale,
+            species_shift,
+        )
+    )
+    weights = (
+        center_weight,
+        near_weight,
+        basis_weight,
+        path_weight,
+        value_weight,
+        latent_weight,
+        out_weight.reshape(1, width),
+    )
+    weights = pl.pallas_call(
+        fetch_kernel,
+        out_shape=tuple(jax.ShapeDtypeStruct(w.shape, F32) for w in weights),
+        in_specs=[hbm] * len(weights),
+        out_specs=(vmem,) * len(weights),
+        scratch_shapes=[pltpu.SemaphoreType.DMA((len(weights),))],
+        compiler_params=pltpu.CompilerParams(vmem_limit_bytes=8 * 1024 * 1024),
+        name="fetch_weights",
+    )(*in_hbm(*weights))
     short = here[: owned + 8]
-    next_x = moved(here, {"gx": -1})
+    last_x = moved(here, {"gx": 1})
     sides = []
     for step in (-1, 1)[: kind - 1]:
-        sides.append(moved(short, {"gx": -1, "gy": step}))
+        sides.append(moved(short, {"gx": 1, "gy": step}))
         sides.insert(-1, moved(short, {"gy": step}))
-    next_z = moved(joined([here, next_x, *sides]), {"gz": -1})
+    next_z = moved(joined([here, last_x, *sides]), {"gz": -1})
     half = 2 * kind * owned
     keep, send = pl.pallas_call(
         functools.partial(force_kernel, kind, nbr),
@@ -550,25 +618,19 @@
         name="pair_forces",
     )(
         here,
-        next_x,
+        last_x,
         *sides,
         next_z,
-        center_weight,
-        near_weight,
-        basis_weight,
-        path_weight,
-        value_weight,
-        latent_weight,
-        out_weight.reshape(1, width),
+        *weights,
     )
     totals = keep + moved(send, {"gz": 1})
 
     def part(index):
         return totals[:, index * owned : (index + 1) * owned]
 
-    back = [moved(part(kind), {"gx": 1})]
+    back = [moved(part(kind), {"gx": -1})]
     for i, step in enumerate((1, -1)[: kind - 1]):
-        back.append(moved(part(kind + 1 + i), {"gx": 1, "gy": step}))
+        back.append(moved(part(kind + 1 + i), {"gx": -1, "gy": step}))
         back.append(moved(part(1 + i), {"gy": step}))
     site_energy, forces, virial = pl.pallas_call(
         finish_kernel,

time: 36.1 us -> 29.1 us (0.81)
  local copies, waits for them, and re-layouts: 5.25 us -> 0.08 us
  waiting for transfers between devices: 12.3 us -> 9.09 us
  Pallas kernels: 5.61 us -> 7.1 us
    unnamed x28 -> x0, local copies, waits for them, and re-layouts: 5.17 us -> none
    ppermute x8, waiting for transfers between devices: 12.3 us -> 9.09 us  [moved(): return lax.ppermute(array, names, route)]
    pallas_call x0 -> x1, Pallas kernels: none -> 1.14 us  [local(): pl.pallas_call(fetch_kernel, out_shape=tuple((jax.ShapeDtypeStruct(w.shap...]
  transfers between devices with their start and end apart: 8 -> 8, of which waited for: 7 -> 5; matrix products, arithmetic and copies ran while one was open for 0% -> 0% of each run, Pallas kernels for 0% -> 4%
where the time goes in v8:
time: 29.1 us; the launch traced here: 28.8 us
  starting transfers between devices  11.9 us (41%)
  waiting for transfers between devices  9.09 us (31%)
  Pallas kernels  7.1 us (24%)
  between operations  0.67 us (2%)
    ppermute x8, starting transfers between devices, moved(): return lax.ppermute(array, names, route)  11.9 us
    ppermute x8, waiting for transfers between devices, moved(): return lax.ppermute(array, names, route)  9.09 us
    pallas_call x1, Pallas kernels, local(): pl.pallas_call(functools.partial(force_kernel, kind, nbr), out_shape=(jax...  4.1 us
    pallas_call x1, Pallas kernels, local(): pl.pallas_call(fetch_kernel, out_shape=tuple((jax.ShapeDtypeStruct(w.shap...  1.14 us
    pallas_call x1, Pallas kernels, local(): pl.pallas_call(functools.partial(pack_kernel, kind), out_shape=(jax.Shape...  1.11 us
    pallas_call x1, Pallas kernels, local(): pl.pallas_call(finish_kernel, out_shape=(jax.ShapeDtypeStruct(species.sha...  0.75 us
  transfers between devices with their start and end apart: 8, of which 5 were waited for; matrix products, arithmetic and copies ran while one was open for 0% of the time, Pallas kernels for 4%

profile of v8, /device:TPU:0, one launch (start us, length us, event | category | flops | bytes accessed | tf_op | source)
XLA Modules:
  0.0 28.8 jit_solution(8883729229810560488)
XLA Ops:
  0.6 1.1 %pack_payload.1 = (f32[48,128]{1,0:T(8,128)S(1)}, f32[1,32]{1,0:T(1,128)S(1)}) custom-call(f32[3,2,1,2,8]{4,3,2,1,0:T(2,128)} %positions_hbm.1, f32[32,128]{1,0:T(8,128)} %bitcast.4, s32[2,1,2,8]{3,2,1,0:T(2,128)} %species_hbm.1, s32[1,32]{1,0:T(1,128)} %bitcast.5, s32[32,32]{1,0:T(8,128)} %neighbours_hbm.1, f32[5]{0:T(128)} %scale_hbm.1, f32[5]{0:T(128)} %shift_hbm.1), custom_call_target="tpu_custom_call" | custom-call | tf_op jit(solution)/shard_map/pack_payload/pallas_call | solution.py:552
  1.8 3.1 %collective-permute-start = (f32[48,128]{1,0:T(8,128)S(1)}, f32[48,128]{1,0:T(8,128)S(1)}, u32[]{:S(2)}, u32[]{:S(2)}) collective-permute-start(f32[48,128]{1,0:T(8,128)S(1)} %get-tuple-element.17.here_ref), channel_id=1, source_target_pairs={{0,8},{8,16},{16,24},{24,0},{1,9},{9,17},{17,25},{25,1},{2,10},{10... | collective-permute-start | bytes 73736 | tf_op jit(solution)/shard_map/ppermute | solution.py:548
  4.8 2.5 %collective-permute-start.2 = (f32[40,128]{1,0:T(8,128)S(1)}, f32[40,128]{1,0:T(8,128)S(1)}, u32[]{:S(2)}, u32[]{:S(2)}) collective-permute-start(f32[40,128]{1,0:T(8,128)S(1)} %slice.12), channel_id=1, source_target_pairs={{0,12},{4,8},{8,20},{12,16},{16,28},{20,24},{24,4},{28,0},{1,13},{... | collective-permute-start | bytes 61448 | tf_op jit(solution)/shard_map/ppermute | solution.py:548
  7.3 0.5 %collective-permute-start.1 = (f32[40,128]{1,0:T(8,128)S(1)}, f32[40,128]{1,0:T(8,128)S(1)}, u32[]{:S(2)}, u32[]{:S(2)}) collective-permute-start(f32[40,128]{1,0:T(8,128)S(1)} %slice.12), channel_id=1, source_target_pairs={{0,4},{4,0},{1,5},{5,1},{2,6},{6,2},{3,7},{7,3},{8,12},{12,8},{9,1... | collective-permute-start | bytes 61448 | tf_op jit(solution)/shard_map/ppermute | solution.py:548
  7.9 3.5 %collective-permute-done.2.refs_1_ = f32[40,128]{1,0:T(8,128)S(1)} collective-permute-done((f32[40,128]{1,0:T(8,128)S(1)}, f32[40,128]{1,0:T(8,128)S(1)}, u32[]{:S(2)}, u32[]{:S(2)}) %collective-permute-start.2) | collective-permute-done | bytes 20512 | tf_op jit(solution)/shard_map/ppermute | solution.py:548
  11.3 0.0 collective-permute-done.1.refs_0_
  11.3 0.0 collective-permute-done.last_x_ref
  11.4 0.1 collective-permute-start.3
  11.4 1.1 %fetch_weights.1 = (f32[128,128]{1,0:T(8,128)S(1)}, f32[128,128]{1,0:T(8,128)S(1)}, f32[8,128]{1,0:T(8,128)S(1)}, f32[3,128]{1,0:T(4,128)S(1)}, f32[128,256]{1,0...) custom-call(f32[128,128]{1,0:T(8,128)} %refs_0_.1, f32[128,128]{1,0:T(8,128)} %refs_1_.1, f32[8,128]{1,0:T(8,128)} %refs_2_.1, ...), custom_call_target="tpu_custom_call" | custom-call | tf_op jit(solution)/shard_map/fetch_weights/pallas_call | solution.py:592
  12.6 1.0 %collective-permute-done.3.refs_2_ = f32[176,128]{1,0:T(8,128)S(1)} collective-permute-done((f32[176,128]{1,0:T(8,128)S(1)}, f32[176,128]{1,0:T(8,128)S(1)}, u32[]{:S(2)}, u32[]{:S(2)}) %collective-permute-start.3) | collective-permute-done | bytes 90144 | tf_op jit(solution)/shard_map/ppermute | solution.py:548
  13.6 4.1 %pair_forces.1 = (f32[16,128]{1,0:T(8,128)S(1)}, f32[16,128]{1,0:T(8,128)S(1)}) custom-call(f32[48,128]{1,0:T(8,128)S(1)} %get-tuple-element.17.here_ref, f32[48,128]{1,0:T(8,128)S(1)} %collective-permute-done.last_x_ref, f32[40,128]{1,0:T(8,128)S(1)} %collective-permute-done.1.refs_0_, f32[40,128]{1,0:T(8,128)S(1)} %collective-permute-done.2.refs_1_, ...), custom_call_target="tpu_custom_call" | custom-call | tf_op jit(solution)/shard_map/pair_forces/pallas_call | solution.py:609
  17.6 1.7 %collective-permute-start.4 = (f32[16,128]{1,0:T(8,128)S(1)}, f32[16,128]{1,0:T(8,128)S(1)}, u32[]{:S(2)}, u32[]{:S(2)}) collective-permute-start(f32[16,128]{1,0:T(8,128)S(1)} %get-tuple-element.26), channel_id=1, source_target_pairs={{0,1},{1,2},{2,3},{3,0},{4,5},{5,6},{6,7},{7,4},{8,9},{9,10},{10,1... | collective-permute-start | bytes 24584 | tf_op jit(solution)/shard_map/ppermute | solution.py:548
  19.4 1.4 %collective-permute-done.4 = f32[16,128]{1,0:T(8,128)S(1)} collective-permute-done((f32[16,128]{1,0:T(8,128)S(1)}, f32[16,128]{1,0:T(8,128)S(1)}, u32[]{:S(2)}, u32[]{:S(2)}) %collective-permute-start.4) | collective-permute-done | bytes 8224 | tf_op jit(solution)/shard_map/ppermute | solution.py:548
  20.8 0.1 fusion
  20.9 1.5 %collective-permute-start.7 = (f32[16,32]{1,0:T(8,128)S(1)}, f32[16,32]{1,0:T(8,128)S(1)}, u32[]{:S(2)}, u32[]{:S(2)}) collective-permute-start(f32[16,32]{1,0:T(8,128)S(1)} %get-tuple-element.31), channel_id=1, source_target_pairs={{0,4},{4,0},{1,5},{5,1},{2,6},{6,2},{3,7},{7,3},{8,12},{12,8},{9,1... | collective-permute-start | bytes 6152 | tf_op jit(solution)/shard_map/ppermute | solution.py:548
  22.4 2.0 %collective-permute-start.6 = (f32[16,32]{1,0:T(8,128)S(1)}, f32[16,32]{1,0:T(8,128)S(1)}, u32[]{:S(2)}, u32[]{:S(2)}) collective-permute-start(f32[16,32]{1,0:T(8,128)S(1)} %get-tuple-element.32), channel_id=1, source_target_pairs={{0,28},{4,24},{8,4},{12,0},{16,12},{20,8},{24,20},{28,16},{1,29},{... | collective-permute-start | bytes 6152 | tf_op jit(solution)/shard_map/ppermute | solution.py:548
  24.4 0.4 %collective-permute-start.5 = (f32[16,32]{1,0:T(8,128)S(1)}, f32[16,32]{1,0:T(8,128)S(1)}, u32[]{:S(2)}, u32[]{:S(2)}) collective-permute-start(f32[16,32]{1,0:T(8,128)S(1)} %get-tuple-element.33), channel_id=1, source_target_pairs={{0,24},{8,0},{16,8},{24,16},{1,25},{9,1},{17,9},{25,17},{2,26},{10... | collective-permute-start | bytes 6152 | tf_op jit(solution)/shard_map/ppermute | solution.py:548
  24.9 0.0 collective-permute-done.7.refs_2_
  24.9 2.1 %collective-permute-done.6.refs_1_ = f32[16,32]{1,0:T(8,128)S(1)} collective-permute-done((f32[16,32]{1,0:T(8,128)S(1)}, f32[16,32]{1,0:T(8,128)S(1)}, u32[]{:S(2)}, u32[]{:S(2)}) %collective-permute-start.6) | collective-permute-done | bytes 2080 | tf_op jit(solution)/shard_map/ppermute | solution.py:548
  26.9 1.1 %collective-permute-done.5.refs_0_ = f32[16,32]{1,0:T(8,128)S(1)} collective-permute-done((f32[16,32]{1,0:T(8,128)S(1)}, f32[16,32]{1,0:T(8,128)S(1)}, u32[]{:S(2)}, u32[]{:S(2)}) %collective-permute-start.5) | collective-permute-done | bytes 2080 | tf_op jit(solution)/shard_map/ppermute | solution.py:548
  28.1 0.8 %write_outputs.1 = (f32[2,1,2,8]{3,2,1,0:T(2,128)}, f32[3,2,1,2,8]{4,3,2,1,0:T(2,128)}, f32[2,1,2,8,9]{4,3,2,1,0:T(8,128)}) custom-call(f32[16,128]{1,0:T(8,128)S(1)} %add.23.mine_ref, f32[1,32]{1,0:T(1,128)S(1)} %get-tuple-element.27.shift_row_ref, f32[16,32]{1,0:T(8,128)S(1)} %collective-permute-done.5.refs_0_, ...), custom_call_target="tpu_custom_call" | custom-call | tf_op jit(solution)/shard_map/write_outputs/pallas_call | solution.py:635
  (3 shorter events, 0.0 us)
Async XLA Ops:
  1.8 9.6 %collective-permute-start = (f32[48,128]{1,0:T(8,128)S(1)}, f32[48,128]{1,0:T(8,128)S(1)}, u32[]{:S(2)}, u32[]{:S(2)}) collective-permute-start(f32[48,128]{1,0:T(8,128)S(1)} %get-tuple-element.17.here_ref), channel_id=1, source_target_pairs={{0,8},{8,16},{16,24},{24,0},{1,9},{9,17},{17,25},{25,1},{2,10},{10... | collective-permute-start | bytes 73736 | tf_op jit(solution)/shard_map/ppermute | solution.py:548
  4.8 6.5 %collective-permute-start.2 = (f32[40,128]{1,0:T(8,128)S(1)}, f32[40,128]{1,0:T(8,128)S(1)}, u32[]{:S(2)}, u32[]{:S(2)}) collective-permute-start(f32[40,128]{1,0:T(8,128)S(1)} %slice.12), channel_id=1, source_target_pairs={{0,12},{4,8},{8,20},{12,16},{16,28},{20,24},{24,4},{28,0},{1,13},{... | collective-permute-start | bytes 61448 | tf_op jit(solution)/shard_map/ppermute | solution.py:548
  7.3 4.0 %collective-permute-start.1 = (f32[40,128]{1,0:T(8,128)S(1)}, f32[40,128]{1,0:T(8,128)S(1)}, u32[]{:S(2)}, u32[]{:S(2)}) collective-permute-start(f32[40,128]{1,0:T(8,128)S(1)} %slice.12), channel_id=1, source_target_pairs={{0,4},{4,0},{1,5},{5,1},{2,6},{6,2},{3,7},{7,3},{8,12},{12,8},{9,1... | collective-permute-start | bytes 61448 | tf_op jit(solution)/shard_map/ppermute | solution.py:548
  11.4 2.2 %collective-permute-start.3 = (f32[176,128]{1,0:T(8,128)S(1)}, f32[176,128]{1,0:T(8,128)S(1)}, u32[]{:S(2)}, u32[]{:S(2)}) collective-permute-start(f32[176,128]{1,0:T(8,128)S(1)} %pad_add_fusion), channel_id=1, source_target_pairs={{0,3},{1,0},{2,1},{3,2},{4,7},{5,4},{6,5},{7,6},{8,11},{9,8},{10,9... | collective-permute-start | bytes 270344 | tf_op jit(solution)/shard_map/ppermute | solution.py:548
  17.6 3.2 %collective-permute-start.4 = (f32[16,128]{1,0:T(8,128)S(1)}, f32[16,128]{1,0:T(8,128)S(1)}, u32[]{:S(2)}, u32[]{:S(2)}) collective-permute-start(f32[16,128]{1,0:T(8,128)S(1)} %get-tuple-element.26), channel_id=1, source_target_pairs={{0,1},{1,2},{2,3},{3,0},{4,5},{5,6},{6,7},{7,4},{8,9},{9,10},{10,1... | collective-permute-start | bytes 24584 | tf_op jit(solution)/shard_map/ppermute | solution.py:548
  20.9 3.9 %collective-permute-start.7 = (f32[16,32]{1,0:T(8,128)S(1)}, f32[16,32]{1,0:T(8,128)S(1)}, u32[]{:S(2)}, u32[]{:S(2)}) collective-permute-start(f32[16,32]{1,0:T(8,128)S(1)} %get-tuple-element.31), channel_id=1, source_target_pairs={{0,4},{4,0},{1,5},{5,1},{2,6},{6,2},{3,7},{7,3},{8,12},{12,8},{9,1... | collective-permute-start | bytes 6152 | tf_op jit(solution)/shard_map/ppermute | solution.py:548
  22.4 4.5 %collective-permute-start.6 = (f32[16,32]{1,0:T(8,128)S(1)}, f32[16,32]{1,0:T(8,128)S(1)}, u32[]{:S(2)}, u32[]{:S(2)}) collective-permute-start(f32[16,32]{1,0:T(8,128)S(1)} %get-tuple-element.32), channel_id=1, source_target_pairs={{0,28},{4,24},{8,4},{12,0},{16,12},{20,8},{24,20},{28,16},{1,29},{... | collective-permute-start | bytes 6152 | tf_op jit(solution)/shard_map/ppermute | solution.py:548
  24.4 3.7 %collective-permute-start.5 = (f32[16,32]{1,0:T(8,128)S(1)}, f32[16,32]{1,0:T(8,128)S(1)}, u32[]{:S(2)}, u32[]{:S(2)}) collective-permute-start(f32[16,32]{1,0:T(8,128)S(1)} %get-tuple-element.33), channel_id=1, source_target_pairs={{0,24},{8,0},{16,8},{24,16},{1,25},{9,1},{17,9},{25,17},{2,26},{10... | collective-permute-start | bytes 6152 | tf_op jit(solution)/shard_map/ppermute | solution.py:548

commit v9 on v8

--- a/solution.py
+++ b/solution.py
@@ -97,16 +97,13 @@
     centers_hbm,
     neighbours_hbm,
     scale_hbm,
-    shift_hbm,
     payload_ref,
-    shift_row_ref,
     wide_ref,
     positions_ref,
     species_ref,
     centers_ref,
     neighbours_ref,
     scale_ref,
-    shift_ref,
     sems,
 ):
     owned, nbr = neighbours_ref.shape
@@ -118,7 +115,6 @@
         (positions_hbm, positions_ref),
         (species_hbm, species_ref),
         (scale_hbm, scale_ref),
-        (shift_hbm, shift_ref),
     )
     copies = [
         pltpu.make_async_copy(source, target, sems.at[i])
@@ -129,26 +125,20 @@
     for copy in copies:
         copy.wait()
     payload_ref[owned : owned + 8] = jnp.zeros((8, 128), F32)
-    shift_row = jnp.zeros((1, 128), F32)
     for cell in range(OWN_CELLS):
         x, z = cell // 2, cell % 2
         species = species_ref[x, 0, z : z + 1, :]
         scale = jnp.zeros(species.shape, F32)
-        shift = jnp.zeros(species.shape, F32)
         for s in range(scale_ref.shape[0]):
             scale = jnp.where(species == s, scale_ref[s], scale)
-            shift = jnp.where(species == s, shift_ref[s], shift)
         row = lane_row(scale, 3 * SITES)
         for c in range(3):
             row = row + lane_row(positions_ref[c, x, 0, z : z + 1, :], c * SITES)
         payload_ref[owned + cell : owned + cell + 1] = row
-        shift_row = shift_row + lane_row(shift, cell * SITES)
 
     chosen = lax.broadcasted_iota(jnp.int32, (owned, owned), 0) == centers_ref[...]
     chosen = jnp.where(chosen, 1.0, 0.0)
     occupied = jnp.sum(chosen, axis=1, keepdims=True) > 0.5
-    column = jnp.where(occupied, jnp.ones((owned, 128), F32), 0.0)
-    shift_row_ref[...] = shift_row[:, :owned] * jnp.transpose(column)[0:1]
     chosen = chosen.astype(BF16)
     rows = neighbours_ref[...]
     upper = mm(chosen, (rows >> 4).astype(F32).astype(BF16))
@@ -176,16 +166,35 @@
     payload_ref[owned + 8 :] = codes
 
 
-def fetch_kernel(*refs):
+def fetch_kernel(species_hbm, centers_hbm, shift_hbm, *refs):
+    *refs, shift_row_ref, species_ref, centers_ref, shift_ref, sems = refs
     count = len(refs) // 2
-    sems = refs[-1]
+    pairs_in = [
+        (species_hbm, species_ref),
+        (centers_hbm, centers_ref),
+        (shift_hbm, shift_ref),
+        *zip(refs[:count], refs[count:]),
+    ]
     copies = [
-        pltpu.make_async_copy(refs[i], refs[count + i], sems.at[i]) for i in range(count)
+        pltpu.make_async_copy(source, target, sems.at[i])
+        for i, (source, target) in enumerate(pairs_in)
     ]
     for copy in copies:
         copy.start()
     for copy in copies:
         copy.wait()
+    owned = centers_ref.shape[1]
+    shift_row = jnp.zeros((1, 128), F32)
+    for cell in range(OWN_CELLS):
+        species = species_ref[cell // 2, 0, cell % 2 : cell % 2 + 1, :]
+        shift = jnp.zeros(species.shape, F32)
+        for s in range(shift_ref.shape[0]):
+            shift = jnp.where(species == s, shift_ref[s], shift)
+        shift_row = shift_row + lane_row(shift, cell * SITES)
+    chosen = lax.broadcasted_iota(jnp.int32, (owned, owned), 0) == centers_ref[...]
+    occupied = jnp.sum(jnp.where(chosen, 1.0, 0.0), axis=1, keepdims=True) > 0.5
+    column = jnp.where(occupied, jnp.ones((owned, 128), F32), 0.0)
+    shift_row_ref[...] = shift_row[:, :owned] * jnp.transpose(column)[0:1]
 
 
 def finish_kernel(mine_ref, shift_row_ref, *refs):
@@ -209,6 +218,7 @@
     near_side_refs = refs[: 2 * kind - 2]
     (
         next_z_ref,
+        next_xz_ref,
         center_weight_ref,
         near_weight_ref,
         basis_weight_ref,
@@ -232,17 +242,17 @@
     root_three = math.sqrt(3.0)
     root_fifteen = math.sqrt(15.0)
     root_five = math.sqrt(5.0)
-    far = next_z_ref[...]
-    mains = [here_ref[...], last_x_ref[...], far[:height], far[height : 2 * height]]
     near_sides = [ref[...] for ref in near_side_refs]
-    far_sides = far[2 * height :]
-    far_sides = [far_sides[i * short : (i + 1) * short] for i in range(2 * kind - 2)]
     blocks_in = [
-        [mains[0], *near_sides[0::2]],
-        [mains[1], *near_sides[1::2]],
-        [mains[2], *far_sides[0::2]],
-        [mains[3], *far_sides[1::2]],
+        [here_ref[...], *near_sides[0::2]],
+        [last_x_ref[...], *near_sides[1::2]],
     ]
+    for far_ref in (next_z_ref, next_xz_ref):
+        far = far_ref[...]
+        sides = [
+            far[height + i * short : height + (i + 1) * short] for i in range(kind - 1)
+        ]
+        blocks_in.append([far[:height], *sides])
     feats = jnp.concatenate([side[:owned] for block in blocks_in for side in block], axis=0)
     known = feats.shape[0]
     center_feats = []
@@ -549,23 +559,20 @@
 
     vmem = pl.BlockSpec(memory_space=pltpu.VMEM)
     hbm = pl.BlockSpec(memory_space=pltpu.HBM)
-    here, shift_row = pl.pallas_call(
+    listed = centers.reshape(1, owned)
+    here = pl.pallas_call(
         functools.partial(pack_kernel, kind),
-        out_shape=(
-            jax.ShapeDtypeStruct((owned + 8 + pairs // 128, width), F32),
-            jax.ShapeDtypeStruct((1, owned), F32),
-        ),
-        in_specs=[hbm] * 7,
-        out_specs=(vmem, vmem),
+        out_shape=jax.ShapeDtypeStruct((owned + 8 + pairs // 128, width), F32),
+        in_specs=[hbm] * 6,
+        out_specs=vmem,
         scratch_shapes=[
             pltpu.VMEM((owned, 128), F32),
             pltpu.VMEM(positions.shape, F32),
             pltpu.VMEM(species.shape, jnp.int32),
-            pltpu.VMEM((1, owned), jnp.int32),
+            pltpu.VMEM(listed.shape, jnp.int32),
             pltpu.VMEM(neighbours.shape, jnp.int32),
             pltpu.SMEM(species_scale.shape, F32),
-            pltpu.SMEM(species_shift.shape, F32),
-            pltpu.SemaphoreType.DMA((7,)),
+            pltpu.SemaphoreType.DMA((6,)),
         ],
         compiler_params=pltpu.CompilerParams(vmem_limit_bytes=8 * 1024 * 1024),
         name="pack_payload",
@@ -574,10 +581,9 @@
             positions,
             features.reshape(owned, width),
             species,
-            centers.reshape(1, owned),
+            listed,
             neighbours,
             species_scale,
-            species_shift,
         )
     )
     weights = (
@@ -589,22 +595,31 @@
         latent_weight,
         out_weight.reshape(1, width),
     )
-    weights = pl.pallas_call(
+    *weights, shift_row = pl.pallas_call(
         fetch_kernel,
-        out_shape=tuple(jax.ShapeDtypeStruct(w.shape, F32) for w in weights),
-        in_specs=[hbm] * len(weights),
-        out_specs=(vmem,) * len(weights),
-        scratch_shapes=[pltpu.SemaphoreType.DMA((len(weights),))],
+        out_shape=(
+            *(jax.ShapeDtypeStruct(w.shape, F32) for w in weights),
+            jax.ShapeDtypeStruct((1, owned), F32),
+        ),
+        in_specs=[hbm] * (3 + len(weights)),
+        out_specs=(vmem,) * (1 + len(weights)),
+        scratch_shapes=[
+            pltpu.VMEM(species.shape, jnp.int32),
+            pltpu.VMEM(listed.shape, jnp.int32),
+            pltpu.SMEM(species_shift.shape, F32),
+            pltpu.SemaphoreType.DMA((3 + len(weights),)),
+        ],
         compiler_params=pltpu.CompilerParams(vmem_limit_bytes=8 * 1024 * 1024),
         name="fetch_weights",
-    )(*in_hbm(*weights))
+    )(*in_hbm(species, listed, species_shift, *weights))
     short = here[: owned + 8]
     last_x = moved(here, {"gx": 1})
     sides = []
     for step in (-1, 1)[: kind - 1]:
         sides.append(moved(short, {"gx": 1, "gy": step}))
         sides.insert(-1, moved(short, {"gy": step}))
-    next_z = moved(joined([here, last_x, *sides]), {"gz": -1})
+    next_z = moved(joined([here, *sides[0::2]]), {"gz": -1})
+    next_xz = moved(joined([last_x, *sides[1::2]]), {"gz": -1})
     half = 2 * kind * owned
     keep, send = pl.pallas_call(
         functools.partial(force_kernel, kind, nbr),
@@ -612,7 +627,7 @@
             jax.ShapeDtypeStruct((ORDERS, half), F32),
             jax.ShapeDtypeStruct((ORDERS, half), F32),
         ),
-        in_specs=[vmem] * (8 + 2 * kind),
+        in_specs=[vmem] * (9 + 2 * kind),
         out_specs=(vmem, vmem),
         compiler_params=pltpu.CompilerParams(vmem_limit_bytes=32 * 1024 * 1024),
         name="pair_forces",
@@ -621,17 +636,17 @@
         last_x,
         *sides,
         next_z,
+        next_xz,
         *weights,
     )
     totals = keep + moved(send, {"gz": 1})
 
-    def part(index):
-        return totals[:, index * owned : (index + 1) * owned]
-
-    back = [moved(part(kind), {"gx": -1})]
+    half = kind * owned
+    totals = totals[:, :half] + moved(totals[:, half:], {"gx": -1})
+    back = []
     for i, step in enumerate((1, -1)[: kind - 1]):
-        back.append(moved(part(kind + 1 + i), {"gx": -1, "gy": step}))
-        back.append(moved(part(1 + i), {"gy": step}))
+        part = totals[:, (1 + i) * owned : (2 + i) * owned]
+        back.append(moved(part, {"gy": step}))
     site_energy, forces, virial = pl.pallas_call(
         finish_kernel,
         out_shape=(

time: 29.1 us -> 29.4 us (1.010)
  waiting for transfers between devices: 9.09 us -> 10.3 us
  starting transfers between devices: 11.9 us -> 10.7 us
    ppermute x8, waiting for transfers between devices: 9.09 us -> 10.3 us  [moved(): return lax.ppermute(array, names, route)]
    ppermute x8, starting transfers between devices: 11.9 us -> 10.7 us  [moved(): return lax.ppermute(array, names, route)]
  transfers between devices with their start and end apart: 8 -> 8, of which waited for: 5 -> 6; matrix products, arithmetic and copies ran while one was open for 0% -> 0% of each run, Pallas kernels for 4% -> 5%
where the time goes in v9:
time: 29.4 us; the launch traced here: 29.1 us
  starting transfers between devices  10.7 us (36%)
  waiting for transfers between devices  10.3 us (35%)
  Pallas kernels  7.28 us (25%)
  between operations  0.68 us (2%)
    ppermute x8, starting transfers between devices, moved(): return lax.ppermute(array, names, route)  10.7 us
    ppermute x8, waiting for transfers between devices, moved(): return lax.ppermute(array, names, route)  10.3 us
    pallas_call x1, Pallas kernels, local(): pl.pallas_call(functools.partial(force_kernel, kind, nbr), out_shape=(jax...  4.1 us
    pallas_call x1, Pallas kernels, local(): pl.pallas_call(fetch_kernel, out_shape=(*(jax.ShapeDtypeStruct(w.shape, F...  1.35 us
    pallas_call x1, Pallas kernels, local(): pl.pallas_call(functools.partial(pack_kernel, kind), out_shape=jax.ShapeD...  1.08 us
    pallas_call x1, Pallas kernels, local(): pl.pallas_call(finish_kernel, out_shape=(jax.ShapeDtypeStruct(species.sha...  0.75 us
  transfers between devices with their start and end apart: 8, of which 6 were waited for; matrix products, arithmetic and copies ran while one was open for 0% of the time, Pallas kernels for 5%

profile of v9, /device:TPU:0, one launch (start us, length us, event | category | flops | bytes accessed | tf_op | source)
XLA Modules:
  0.0 29.1 jit_solution(8658020377963912663)
XLA Ops:
  0.6 1.1 %pack_payload.1.here_ref = f32[48,128]{1,0:T(8,128)S(1)} custom-call(f32[3,2,1,2,8]{4,3,2,1,0:T(2,128)} %positions_hbm.1, f32[32,128]{1,0:T(8,128)} %bitcast.4, s32[2,1,2,8]{3,2,1,0:T(2,128)} %species_hbm.3, s32[1,32]{1,0:T(1,128)} %bitcast.5, s32[32,32]{1,0:T(8,128)} %neighbours_hbm.1, f32[5]{0:T(128)} %scale_hbm.1), custom_call_target="tpu_custom_call" | custom-call | tf_op jit(solution)/shard_map/pack_payload/pallas_call | solution.py:563
  1.7 3.0 %collective-permute-start.1 = (f32[40,128]{1,0:T(8,128)S(1)}, f32[40,128]{1,0:T(8,128)S(1)}, u32[]{:S(2)}, u32[]{:S(2)}) collective-permute-start(f32[40,128]{1,0:T(8,128)S(1)} %slice.16), channel_id=1, source_target_pairs={{0,4},{4,0},{1,5},{5,1},{2,6},{6,2},{3,7},{7,3},{8,12},{12,8},{9,1... | collective-permute-start | bytes 61448 | tf_op jit(solution)/shard_map/ppermute | solution.py:558
  4.7 1.5 %collective-permute-start.2 = (f32[40,128]{1,0:T(8,128)S(1)}, f32[40,128]{1,0:T(8,128)S(1)}, u32[]{:S(2)}, u32[]{:S(2)}) collective-permute-start(f32[40,128]{1,0:T(8,128)S(1)} %slice.16), channel_id=1, source_target_pairs={{0,12},{4,8},{8,20},{12,16},{16,28},{20,24},{24,4},{28,0},{1,13},{... | collective-permute-start | bytes 61448 | tf_op jit(solution)/shard_map/ppermute | solution.py:558
  6.3 1.6 %collective-permute-start = (f32[48,128]{1,0:T(8,128)S(1)}, f32[48,128]{1,0:T(8,128)S(1)}, u32[]{:S(2)}, u32[]{:S(2)}) collective-permute-start(f32[48,128]{1,0:T(8,128)S(1)} %pack_payload.1.here_ref), channel_id=1, source_target_pairs={{0,8},{8,16},{16,24},{24,0},{1,9},{9,17},{17,25},{25,1},{2,10},{10... | collective-permute-start | bytes 73736 | tf_op jit(solution)/shard_map/ppermute | solution.py:558
  7.9 0.0 collective-permute-done.1.refs_0_
  7.9 0.2 collective-permute-start.3
  8.0 3.3 %collective-permute-done.2.refs_1_ = f32[40,128]{1,0:T(8,128)S(1)} collective-permute-done((f32[40,128]{1,0:T(8,128)S(1)}, f32[40,128]{1,0:T(8,128)S(1)}, u32[]{:S(2)}, u32[]{:S(2)}) %collective-permute-start.2) | collective-permute-done | bytes 20512 | tf_op jit(solution)/shard_map/ppermute | solution.py:558
  11.4 0.5 %collective-permute-done.last_x_ref = f32[48,128]{1,0:T(8,128)S(1)} collective-permute-done((f32[48,128]{1,0:T(8,128)S(1)}, f32[48,128]{1,0:T(8,128)S(1)}, u32[]{:S(2)}, u32[]{:S(2)}) %collective-permute-start) | collective-permute-done | bytes 24608 | tf_op jit(solution)/shard_map/ppermute | solution.py:558
  11.9 0.0 collective-permute-start.4
  11.9 1.3 %fetch_weights.1 = (f32[128,128]{1,0:T(8,128)S(1)}, f32[128,128]{1,0:T(8,128)S(1)}, f32[8,128]{1,0:T(8,128)S(1)}, f32[3,128]{1,0:T(4,128)S(1)}, f32[128,256]{1,0...) custom-call(s32[2,1,2,8]{3,2,1,0:T(2,128)} %species_hbm.3, s32[1,32]{1,0:T(1,128)} %bitcast.6, ...), custom_call_target="tpu_custom_call" | custom-call | tf_op jit(solution)/shard_map/fetch_weights/pallas_call | solution.py:598
  13.3 0.0 collective-permute-done.3.refs_2_
  13.3 0.3 %collective-permute-done.4.refs_3_ = f32[88,128]{1,0:T(8,128)S(1)} collective-permute-done((f32[88,128]{1,0:T(8,128)S(1)}, f32[88,128]{1,0:T(8,128)S(1)}, u32[]{:S(2)}, u32[]{:S(2)}) %collective-permute-start.4) | collective-permute-done | bytes 45088 | tf_op jit(solution)/shard_map/ppermute | solution.py:558
  13.6 4.1 %pair_forces.1 = (f32[16,128]{1,0:T(8,128)S(1)}, f32[16,128]{1,0:T(8,128)S(1)}) custom-call(f32[48,128]{1,0:T(8,128)S(1)} %pack_payload.1.here_ref, f32[48,128]{1,0:T(8,128)S(1)} %collective-permute-done.last_x_ref, f32[40,128]{1,0:T(8,128)S(1)} %collective-permute-done.1.refs_0_, f32[40,128]{1,0:T(8,128)S(1)} %collective-permute-done.2.refs_1_, ...), custom_call_target="tpu_custom_call" | custom-call | tf_op jit(solution)/shard_map/pair_forces/pallas_call | solution.py:624
  17.7 1.7 %collective-permute-start.5 = (f32[16,128]{1,0:T(8,128)S(1)}, f32[16,128]{1,0:T(8,128)S(1)}, u32[]{:S(2)}, u32[]{:S(2)}) collective-permute-start(f32[16,128]{1,0:T(8,128)S(1)} %get-tuple-element.24), channel_id=1, source_target_pairs={{0,1},{1,2},{2,3},{3,0},{4,5},{5,6},{6,7},{7,4},{8,9},{9,10},{10,1... | collective-permute-start | bytes 24584 | tf_op jit(solution)/shard_map/ppermute | solution.py:558
  19.4 1.4 %collective-permute-done.5 = f32[16,128]{1,0:T(8,128)S(1)} collective-permute-done((f32[16,128]{1,0:T(8,128)S(1)}, f32[16,128]{1,0:T(8,128)S(1)}, u32[]{:S(2)}, u32[]{:S(2)}) %collective-permute-start.5) | collective-permute-done | bytes 8224 | tf_op jit(solution)/shard_map/ppermute | solution.py:558
  20.9 0.1 slice.18
  20.9 1.2 %collective-permute-start.6 = (f32[16,64]{1,0:T(8,128)S(1)}, f32[16,64]{1,0:T(8,128)S(1)}, u32[]{:S(2)}, u32[]{:S(2)}) collective-permute-start(f32[16,64]{1,0:T(8,128)S(1)} %slice.18), channel_id=1, source_target_pairs={{0,24},{8,0},{16,8},{24,16},{1,25},{9,1},{17,9},{25,17},{2,26},{10... | collective-permute-start | bytes 12296 | tf_op jit(solution)/shard_map/ppermute | solution.py:558
  22.1 2.5 %collective-permute-done.6 = f32[16,64]{1,0:T(8,128)S(1)} collective-permute-done((f32[16,64]{1,0:T(8,128)S(1)}, f32[16,64]{1,0:T(8,128)S(1)}, u32[]{:S(2)}, u32[]{:S(2)}) %collective-permute-start.6) | collective-permute-done | bytes 4128 | tf_op jit(solution)/shard_map/ppermute | solution.py:558
  24.6 0.1 slice.19
  24.7 1.5 %collective-permute-start.7 = (f32[16,32]{1,0:T(8,128)S(1)}, f32[16,32]{1,0:T(8,128)S(1)}, u32[]{:S(2)}, u32[]{:S(2)}) collective-permute-start(f32[16,32]{1,0:T(8,128)S(1)} %slice.19), channel_id=1, source_target_pairs={{0,4},{4,0},{1,5},{5,1},{2,6},{6,2},{3,7},{7,3},{8,12},{12,8},{9,1... | collective-permute-start | bytes 6152 | tf_op jit(solution)/shard_map/ppermute | solution.py:558
  26.2 2.2 %collective-permute-done.7.refs_0_ = f32[16,32]{1,0:T(8,128)S(1)} collective-permute-done((f32[16,32]{1,0:T(8,128)S(1)}, f32[16,32]{1,0:T(8,128)S(1)}, u32[]{:S(2)}, u32[]{:S(2)}) %collective-permute-start.7) | collective-permute-done | bytes 2080 | tf_op jit(solution)/shard_map/ppermute | solution.py:558
  28.3 0.8 %write_outputs.1 = (f32[2,1,2,8]{3,2,1,0:T(2,128)}, f32[3,2,1,2,8]{4,3,2,1,0:T(2,128)}, f32[2,1,2,8,9]{4,3,2,1,0:T(8,128)}) custom-call(f32[16,64]{1,0:T(8,128)S(1)} %slice_add_fusion.mine_ref, f32[1,32]{1,0:T(1,128)S(1)} %get-tuple-element.25.shift_row_ref, f32[16,32]{1,0:T(8,128)S(1)} %collective-permute-done.7.refs_0_), custom_call_target="tpu_custom_call" | custom-call | tf_op jit(solution)/shard_map/write_outputs/pallas_call | solution.py:650
  (5 shorter events, 0.0 us)
Async XLA Ops:
  1.7 6.1 %collective-permute-start.1 = (f32[40,128]{1,0:T(8,128)S(1)}, f32[40,128]{1,0:T(8,128)S(1)}, u32[]{:S(2)}, u32[]{:S(2)}) collective-permute-start(f32[40,128]{1,0:T(8,128)S(1)} %slice.16), channel_id=1, source_target_pairs={{0,4},{4,0},{1,5},{5,1},{2,6},{6,2},{3,7},{7,3},{8,12},{12,8},{9,1... | collective-permute-start | bytes 61448 | tf_op jit(solution)/shard_map/ppermute | solution.py:558
  4.7 6.6 %collective-permute-start.2 = (f32[40,128]{1,0:T(8,128)S(1)}, f32[40,128]{1,0:T(8,128)S(1)}, u32[]{:S(2)}, u32[]{:S(2)}) collective-permute-start(f32[40,128]{1,0:T(8,128)S(1)} %slice.16), channel_id=1, source_target_pairs={{0,12},{4,8},{8,20},{12,16},{16,28},{20,24},{24,4},{28,0},{1,13},{... | collective-permute-start | bytes 61448 | tf_op jit(solution)/shard_map/ppermute | solution.py:558
  6.3 5.6 %collective-permute-start = (f32[48,128]{1,0:T(8,128)S(1)}, f32[48,128]{1,0:T(8,128)S(1)}, u32[]{:S(2)}, u32[]{:S(2)}) collective-permute-start(f32[48,128]{1,0:T(8,128)S(1)} %pack_payload.1.here_ref), channel_id=1, source_target_pairs={{0,8},{8,16},{16,24},{24,0},{1,9},{9,17},{17,25},{25,1},{2,10},{10... | collective-permute-start | bytes 73736 | tf_op jit(solution)/shard_map/ppermute | solution.py:558
  7.9 5.4 %collective-permute-start.3 = (f32[88,128]{1,0:T(8,128)S(1)}, f32[88,128]{1,0:T(8,128)S(1)}, u32[]{:S(2)}, u32[]{:S(2)}) collective-permute-start(f32[88,128]{1,0:T(8,128)S(1)} %pad_add_fusion.1), channel_id=1, source_target_pairs={{0,3},{1,0},{2,1},{3,2},{4,7},{5,4},{6,5},{7,6},{8,11},{9,8},{10,9... | collective-permute-start | bytes 135176 | tf_op jit(solution)/shard_map/ppermute | solution.py:558
  11.9 1.7 %collective-permute-start.4 = (f32[88,128]{1,0:T(8,128)S(1)}, f32[88,128]{1,0:T(8,128)S(1)}, u32[]{:S(2)}, u32[]{:S(2)}) collective-permute-start(f32[88,128]{1,0:T(8,128)S(1)} %pad_add_fusion), channel_id=1, source_target_pairs={{0,3},{1,0},{2,1},{3,2},{4,7},{5,4},{6,5},{7,6},{8,11},{9,8},{10,9... | collective-permute-start | bytes 135176 | tf_op jit(solution)/shard_map/ppermute | solution.py:558
  17.7 3.1 %collective-permute-start.5 = (f32[16,128]{1,0:T(8,128)S(1)}, f32[16,128]{1,0:T(8,128)S(1)}, u32[]{:S(2)}, u32[]{:S(2)}) collective-permute-start(f32[16,128]{1,0:T(8,128)S(1)} %get-tuple-element.24), channel_id=1, source_target_pairs={{0,1},{1,2},{2,3},{3,0},{4,5},{5,6},{6,7},{7,4},{8,9},{9,10},{10,1... | collective-permute-start | bytes 24584 | tf_op jit(solution)/shard_map/ppermute | solution.py:558
  20.9 3.7 %collective-permute-start.6 = (f32[16,64]{1,0:T(8,128)S(1)}, f32[16,64]{1,0:T(8,128)S(1)}, u32[]{:S(2)}, u32[]{:S(2)}) collective-permute-start(f32[16,64]{1,0:T(8,128)S(1)} %slice.18), channel_id=1, source_target_pairs={{0,24},{8,0},{16,8},{24,16},{1,25},{9,1},{17,9},{25,17},{2,26},{10... | collective-permute-start | bytes 12296 | tf_op jit(solution)/shard_map/ppermute | solution.py:558
  24.7 3.7 %collective-permute-start.7 = (f32[16,32]{1,0:T(8,128)S(1)}, f32[16,32]{1,0:T(8,128)S(1)}, u32[]{:S(2)}, u32[]{:S(2)}) collective-permute-start(f32[16,32]{1,0:T(8,128)S(1)} %slice.19), channel_id=1, source_target_pairs={{0,4},{4,0},{1,5},{5,1},{2,6},{6,2},{3,7},{7,3},{8,12},{12,8},{9,1... | collective-permute-start | bytes 6152 | tf_op jit(solution)/shard_map/ppermute | solution.py:558

commit v10 on v9

--- a/solution.py
+++ b/solution.py
@@ -155,8 +155,8 @@
     frame_y = column - 3 * frame_x
     near_x = frame_x + 1 - 2 * (cell >> 1)
     side = jnp.where(frame_y == 1, 0, jnp.where(frame_y == 2, 1, kind - 1))
-    block = (near_z >> 1) * 2 + 1 - (near_x >> 1)
-    where = (block * kind + side) * owned + (near_x & 1) * 16 + (near_z & 1) * 8 + site
+    block = ((1 - (near_z >> 1)) * kind + side) * 2 + 1 - (near_x >> 1)
+    where = block * owned + (near_x & 1) * 16 + (near_z & 1) * 8 + site
     code = jnp.where(live, 1 + where + (frame_y << 10), 0).astype(F32)
     wide_ref[...] = jnp.concatenate([code, jnp.zeros((owned, 128 - nbr), F32)], axis=1)
     codes = wide_ref[pl.ds(0, owned // per_row, stride=per_row), :]
@@ -197,12 +197,9 @@
     shift_row_ref[...] = shift_row[:, :owned] * jnp.transpose(column)[0:1]
 
 
-def finish_kernel(mine_ref, shift_row_ref, *refs):
-    *near_refs, energy_ref, forces_ref, virial_ref = refs
-    owned = near_refs[0].shape[1]
-    total = mine_ref[:, :owned]
-    for near_ref in near_refs:
-        total = total + near_ref[...]
+def finish_kernel(mine_ref, shift_row_ref, back_ref, energy_ref, forces_ref, virial_ref):
+    owned = back_ref.shape[1]
+    total = mine_ref[:, :owned] + back_ref[...]
     energy = total[12:13] + shift_row_ref[...]
     columns = jnp.transpose(jnp.concatenate([total, jnp.zeros((ORDERS, 128 - owned), F32)], axis=1))
     for cell in range(OWN_CELLS):
@@ -217,8 +214,7 @@
 def force_kernel(kind, nbr, here_ref, last_x_ref, *refs):
     near_side_refs = refs[: 2 * kind - 2]
     (
-        next_z_ref,
-        next_xz_ref,
+        last_z_ref,
         center_weight_ref,
         near_weight_ref,
         basis_weight_ref,
@@ -226,8 +222,7 @@
         value_weight_ref,
         latent_weight_ref,
         out_weight_ref,
-        keep_ref,
-        send_ref,
+        *totals_refs,
     ) = refs[2 * kind - 2 :]
     height, width = here_ref.shape
     owned = OWN_CELLS * SITES
@@ -243,38 +238,38 @@
     root_fifteen = math.sqrt(15.0)
     root_five = math.sqrt(5.0)
     near_sides = [ref[...] for ref in near_side_refs]
+    far = last_z_ref[...]
+    far_sides = [
+        far[2 * height + i * short : 2 * height + (i + 1) * short] for i in range(2 * kind - 2)
+    ]
     blocks_in = [
         [here_ref[...], *near_sides[0::2]],
         [last_x_ref[...], *near_sides[1::2]],
+        [far[:height], *far_sides[0::2]],
+        [far[height : 2 * height], *far_sides[1::2]],
     ]
-    for far_ref in (next_z_ref, next_xz_ref):
-        far = far_ref[...]
-        sides = [
-            far[height + i * short : height + (i + 1) * short] for i in range(kind - 1)
-        ]
-        blocks_in.append([far[:height], *sides])
-    feats = jnp.concatenate([side[:owned] for block in blocks_in for side in block], axis=0)
+    order_in = [(z, side, x) for z in range(2) for side in range(kind) for x in range(2)]
+    feats = jnp.concatenate([blocks_in[2 * z + x][side][:owned] for z, side, x in order_in], axis=0)
     known = feats.shape[0]
     center_feats = []
     coords = []
     scales = []
     codes = []
-    cell_row = lax.broadcasted_iota(jnp.int32, (kind * OWN_CELLS, 128), 0) % OWN_CELLS
-    tile_lane = lax.broadcasted_iota(jnp.int32, (kind * OWN_CELLS, 128), 1)
     for g, block in enumerate(blocks_in):
-        behind_x, ahead_z = g % 2, g // 2
-        cell = behind_x * 2 + 1 - ahead_z
+        cell = g % 2 * 2 + g // 2
         center_feats.append(block[0][cell * sites : (cell + 1) * sites])
-        rows = jnp.concatenate([side[owned : owned + OWN_CELLS] for side in block], axis=0)
-        scales.append(rows[cell : cell + 1])
-        corner_x = (cell_row // 2 + 2 - 2 * behind_x).astype(F32) * CELL_SIDE
-        corner_z = (cell_row % 2 + 2 * ahead_z).astype(F32) * CELL_SIDE
+        scales.append(block[0][owned + cell : owned + cell + 1])
+        start = short + cell * span // 128
+        codes.extend(block[0][start + r : start + r + 1] for r in range(span // 128))
+    cell_row = lax.broadcasted_iota(jnp.int32, (OWN_CELLS, 128), 0)
+    tile_lane = lax.broadcasted_iota(jnp.int32, (OWN_CELLS, 128), 1)
+    for z, side, x in order_in:
+        corner_x = (cell_row // 2 + 2 - 2 * x).astype(F32) * CELL_SIDE
+        corner_z = (cell_row % 2 + 2 - 2 * z).astype(F32) * CELL_SIDE
         corner = jnp.where(
             tile_lane < sites, corner_x, jnp.where(tile_lane < 2 * sites, 0.0, corner_z)
         )
-        coords.append(rows + corner)
-        start = short + cell * span // 128
-        codes.extend(block[0][start + r : start + r + 1] for r in range(span // 128))
+        coords.append(blocks_in[2 * z + x][side][owned : owned + OWN_CELLS] + corner)
     center_feats = jnp.concatenate(center_feats, axis=0)
     coords = jnp.concatenate(coords, axis=0)
     code = jnp.concatenate(codes, axis=1).astype(jnp.int32)
@@ -339,8 +334,9 @@
     slot_ids = lax.broadcasted_iota(jnp.int32, (owned, pairs), 0)
     slot_row = lax.broadcasted_iota(jnp.int32, (1, pairs), 1) // nbr
     group_row = slot_row // GROUP
-    center_cell = group_row % 2 * 2 + 1 - group_row // 2
-    center_row = group_row * (kind * owned) + center_cell * sites + slot_row % GROUP
+    center_cell = group_row % 2 * 2 + group_row // 2
+    center_block = group_row // 2 * kind * 2 + group_row % 2
+    center_row = center_block * owned + center_cell * sites + slot_row % GROUP
     block_row = lax.broadcasted_iota(jnp.int32, (wide, span), 0) // ORDERS
     block_lane = lax.broadcasted_iota(jnp.int32, (wide, span), 1) // nbr
     block_mask = (block_row == block_lane).astype(F32)
@@ -502,8 +498,8 @@
     near_sums = mm_nt(jnp.concatenate(split(near_terms), axis=0), pick_half)
     center_sums = mm_nt(jnp.concatenate(split(center_terms), axis=0), center_half)
     totals = folded(near_sums + center_sums)
-    keep_ref[...] = totals[:, : known // 2]
-    send_ref[...] = totals[:, known // 2 :]
+    for i, ref in enumerate(totals_refs):
+        ref[...] = totals[:, 2 * i * owned : 2 * (i + 1) * owned]
 
 
 def in_hbm(*arrays):
@@ -618,35 +614,26 @@
     for step in (-1, 1)[: kind - 1]:
         sides.append(moved(short, {"gx": 1, "gy": step}))
         sides.insert(-1, moved(short, {"gy": step}))
-    next_z = moved(joined([here, *sides[0::2]]), {"gz": -1})
-    next_xz = moved(joined([last_x, *sides[1::2]]), {"gz": -1})
-    half = 2 * kind * owned
-    keep, send = pl.pallas_call(
+    last_z = moved(joined([here, last_x, *sides]), {"gz": 1})
+    totals = pl.pallas_call(
         functools.partial(force_kernel, kind, nbr),
-        out_shape=(
-            jax.ShapeDtypeStruct((ORDERS, half), F32),
-            jax.ShapeDtypeStruct((ORDERS, half), F32),
-        ),
-        in_specs=[vmem] * (9 + 2 * kind),
-        out_specs=(vmem, vmem),
+        out_shape=[jax.ShapeDtypeStruct((ORDERS, 2 * owned), F32)] * (2 * kind),
+        in_specs=[vmem] * (8 + 2 * kind),
+        out_specs=[vmem] * (2 * kind),
         compiler_params=pltpu.CompilerParams(vmem_limit_bytes=32 * 1024 * 1024),
         name="pair_forces",
     )(
         here,
         last_x,
         *sides,
-        next_z,
-        next_xz,
+        last_z,
         *weights,
     )
-    totals = keep + moved(send, {"gz": 1})
-
-    half = kind * owned
-    totals = totals[:, :half] + moved(totals[:, half:], {"gx": -1})
-    back = []
+    total = totals[0] + moved(totals[kind], {"gz": -1})
     for i, step in enumerate((1, -1)[: kind - 1]):
-        part = totals[:, (1 + i) * owned : (2 + i) * owned]
-        back.append(moved(part, {"gy": step}))
+        total = total + moved(totals[kind + 1 + i], {"gy": step, "gz": -1})
+        total = total + moved(totals[1 + i], {"gy": step})
+    back = moved(total[:, owned:], {"gx": -1})
     site_energy, forces, virial = pl.pallas_call(
         finish_kernel,
         out_shape=(
@@ -654,11 +641,11 @@
             jax.ShapeDtypeStruct(positions.shape, F32),
             jax.ShapeDtypeStruct((*species.shape, 9), F32),
         ),
-        in_specs=[vmem] * (2 + len(back)),
+        in_specs=[vmem] * 3,
         out_specs=(vmem, vmem, vmem),
         compiler_params=pltpu.CompilerParams(vmem_limit_bytes=8 * 1024 * 1024),
         name="write_outputs",
-    )(totals, shift_row, *back)
+    )(total, shift_row, back)
     return (site_energy, forces, jnp.transpose(virial, (4, 0, 1, 2, 3)))
 
 

time: 29.4 us -> 30.5 us (1.037)
  waiting for transfers between devices: 10.3 us -> 11.7 us
    ppermute x8, waiting for transfers between devices: 10.3 us -> 11.7 us  [moved(): return lax.ppermute(array, names, route)]
  transfers between devices with their start and end apart: 8 -> 8, of which waited for: 6 -> 5; matrix products, arithmetic and copies ran while one was open for 0% -> 0% of each run, Pallas kernels for 5% -> 4%
where the time goes in v10:
time: 30.5 us; the launch traced here: 30.2 us
  waiting for transfers between devices  11.7 us (38%)
  starting transfers between devices  10.4 us (34%)
  Pallas kernels  7.36 us (24%)
  between operations  0.67 us (2%)
    ppermute x8, waiting for transfers between devices, moved(): return lax.ppermute(array, names, route)  11.7 us
    ppermute x8, starting transfers between devices, moved(): return lax.ppermute(array, names, route)  10.4 us
    pallas_call x1, Pallas kernels, local(): pl.pallas_call(functools.partial(force_kernel, kind, nbr), out_shape=[jax...  4.18 us
    pallas_call x1, Pallas kernels, local(): pl.pallas_call(fetch_kernel, out_shape=(*(jax.ShapeDtypeStruct(w.shape, F...  1.35 us
    pallas_call x1, Pallas kernels, local(): pl.pallas_call(functools.partial(pack_kernel, kind), out_shape=jax.ShapeD...  1.08 us
    pallas_call x1, Pallas kernels, local(): pl.pallas_call(finish_kernel, out_shape=(jax.ShapeDtypeStruct(species.sha...  0.75 us
  transfers between devices with their start and end apart: 8, of which 5 were waited for; matrix products, arithmetic and copies ran while one was open for 0% of the time, Pallas kernels for 4%

profile of v10, /device:TPU:0, one launch (start us, length us, event | category | flops | bytes accessed | tf_op | source)
XLA Modules:
  0.0 30.2 jit_solution(9693785532935971305)
XLA Ops:
  0.6 1.1 %pack_payload.1.here_ref = f32[48,128]{1,0:T(8,128)S(1)} custom-call(f32[3,2,1,2,8]{4,3,2,1,0:T(2,128)} %positions_hbm.1, f32[32,128]{1,0:T(8,128)} %bitcast.4, s32[2,1,2,8]{3,2,1,0:T(2,128)} %species_hbm.3, s32[1,32]{1,0:T(1,128)} %bitcast.5, s32[32,32]{1,0:T(8,128)} %neighbours_hbm.1, f32[5]{0:T(128)} %scale_hbm.1), custom_call_target="tpu_custom_call" | custom-call | tf_op jit(solution)/shard_map/pack_payload/pallas_call | solution.py:559
  1.7 3.1 %collective-permute-start = (f32[48,128]{1,0:T(8,128)S(1)}, f32[48,128]{1,0:T(8,128)S(1)}, u32[]{:S(2)}, u32[]{:S(2)}) collective-permute-start(f32[48,128]{1,0:T(8,128)S(1)} %pack_payload.1.here_ref), channel_id=1, source_target_pairs={{0,8},{8,16},{16,24},{24,0},{1,9},{9,17},{17,25},{25,1},{2,10},{10... | collective-permute-start | bytes 73736 | tf_op jit(solution)/shard_map/ppermute | solution.py:554
  4.8 2.5 %collective-permute-start.2 = (f32[40,128]{1,0:T(8,128)S(1)}, f32[40,128]{1,0:T(8,128)S(1)}, u32[]{:S(2)}, u32[]{:S(2)}) collective-permute-start(f32[40,128]{1,0:T(8,128)S(1)} %slice.8), channel_id=1, source_target_pairs={{0,12},{4,8},{8,20},{12,16},{16,28},{20,24},{24,4},{28,0},{1,13},{... | collective-permute-start | bytes 61448 | tf_op jit(solution)/shard_map/ppermute | solution.py:554
  7.3 0.5 %collective-permute-start.1 = (f32[40,128]{1,0:T(8,128)S(1)}, f32[40,128]{1,0:T(8,128)S(1)}, u32[]{:S(2)}, u32[]{:S(2)}) collective-permute-start(f32[40,128]{1,0:T(8,128)S(1)} %slice.8), channel_id=1, source_target_pairs={{0,4},{4,0},{1,5},{5,1},{2,6},{6,2},{3,7},{7,3},{8,12},{12,8},{9,1... | collective-permute-start | bytes 61448 | tf_op jit(solution)/shard_map/ppermute | solution.py:554
  7.8 3.5 %collective-permute-done.2.refs_1_ = f32[40,128]{1,0:T(8,128)S(1)} collective-permute-done((f32[40,128]{1,0:T(8,128)S(1)}, f32[40,128]{1,0:T(8,128)S(1)}, u32[]{:S(2)}, u32[]{:S(2)}) %collective-permute-start.2) | collective-permute-done | bytes 20512 | tf_op jit(solution)/shard_map/ppermute | solution.py:554
  11.3 0.0 collective-permute-done.1.refs_0_
  11.3 0.0 collective-permute-done.last_x_ref
  11.3 0.1 collective-permute-start.3
  11.4 1.3 %fetch_weights.1 = (f32[128,128]{1,0:T(8,128)S(1)}, f32[128,128]{1,0:T(8,128)S(1)}, f32[8,128]{1,0:T(8,128)S(1)}, f32[3,128]{1,0:T(4,128)S(1)}, f32[128,256]{1,0...) custom-call(s32[2,1,2,8]{3,2,1,0:T(2,128)} %species_hbm.3, s32[1,32]{1,0:T(1,128)} %bitcast.6, ...), custom_call_target="tpu_custom_call" | custom-call | tf_op jit(solution)/shard_map/fetch_weights/pallas_call | solution.py:594
  12.7 2.6 %collective-permute-done.3.refs_2_ = f32[176,128]{1,0:T(8,128)S(1)} collective-permute-done((f32[176,128]{1,0:T(8,128)S(1)}, f32[176,128]{1,0:T(8,128)S(1)}, u32[]{:S(2)}, u32[]{:S(2)}) %collective-permute-start.3) | collective-permute-done | bytes 90144 | tf_op jit(solution)/shard_map/ppermute | solution.py:554
  15.3 4.2 %pair_forces.1 = (f32[16,64]{1,0:T(8,128)S(1)}, f32[16,64]{1,0:T(8,128)S(1)}, f32[16,64]{1,0:T(8,128)S(1)}, f32[16,64]{1,0:T(8,128)S(1)}) custom-call(f32[48,128]{1,0:T(8,128)S(1)} %pack_payload.1.here_ref, f32[48,128]{1,0:T(8,128)S(1)} %collective-permute-done.last_x_ref, f32[40,128]{1,0:T(8,128)S(1)} %collective-permute-done.1.refs_0_, ...), custom_call_target="tpu_custom_call" | custom-call | tf_op jit(solution)/shard_map/pair_forces/pallas_call | solution.py:618
  19.5 0.0 collective-permute-start.4
  19.5 2.6 %collective-permute-start.5 = (f32[16,64]{1,0:T(8,128)S(1)}, f32[16,64]{1,0:T(8,128)S(1)}, u32[]{:S(2)}, u32[]{:S(2)}) collective-permute-start(f32[16,64]{1,0:T(8,128)S(1)} %get-tuple-element.27), channel_id=1, source_target_pairs={{0,7},{1,4},{2,5},{3,6},{4,3},{5,0},{6,1},{7,2},{8,15},{9,12},{10,... | collective-permute-start | bytes 12296 | tf_op jit(solution)/shard_map/ppermute | solution.py:554
  22.1 0.6 %collective-permute-start.6 = (f32[16,64]{1,0:T(8,128)S(1)}, f32[16,64]{1,0:T(8,128)S(1)}, u32[]{:S(2)}, u32[]{:S(2)}) collective-permute-start(f32[16,64]{1,0:T(8,128)S(1)} %get-tuple-element.28), channel_id=1, source_target_pairs={{0,4},{4,0},{1,5},{5,1},{2,6},{6,2},{3,7},{7,3},{8,12},{12,8},{9,1... | collective-permute-start | bytes 12296 | tf_op jit(solution)/shard_map/ppermute | solution.py:554
  22.6 0.0 collective-permute-done.4
  22.6 0.8 %collective-permute-done.5 = f32[16,64]{1,0:T(8,128)S(1)} collective-permute-done((f32[16,64]{1,0:T(8,128)S(1)}, f32[16,64]{1,0:T(8,128)S(1)}, u32[]{:S(2)}, u32[]{:S(2)}) %collective-permute-start.5) | collective-permute-done | bytes 4128 | tf_op jit(solution)/shard_map/ppermute | solution.py:554
  23.4 2.3 %collective-permute-done.6 = f32[16,64]{1,0:T(8,128)S(1)} collective-permute-done((f32[16,64]{1,0:T(8,128)S(1)}, f32[16,64]{1,0:T(8,128)S(1)}, u32[]{:S(2)}, u32[]{:S(2)}) %collective-permute-start.6) | collective-permute-done | bytes 4128 | tf_op jit(solution)/shard_map/ppermute | solution.py:554
  25.7 0.1 slice.9
  25.8 1.1 %collective-permute-start.7 = (f32[16,32]{1,0:T(8,128)S(1)}, f32[16,32]{1,0:T(8,128)S(1)}, u32[]{:S(2)}, u32[]{:S(2)}) collective-permute-start(f32[16,32]{1,0:T(8,128)S(1)} %slice.9), channel_id=1, source_target_pairs={{0,24},{8,0},{16,8},{24,16},{1,25},{9,1},{17,9},{25,17},{2,26},{10... | collective-permute-start | bytes 6152 | tf_op jit(solution)/shard_map/ppermute | solution.py:554
  26.9 2.6 %collective-permute-done.7.back_ref = f32[16,32]{1,0:T(8,128)S(1)} collective-permute-done((f32[16,32]{1,0:T(8,128)S(1)}, f32[16,32]{1,0:T(8,128)S(1)}, u32[]{:S(2)}, u32[]{:S(2)}) %collective-permute-start.7) | collective-permute-done | bytes 2080 | tf_op jit(solution)/shard_map/ppermute | solution.py:554
  29.5 0.8 %write_outputs.1 = (f32[2,1,2,8]{3,2,1,0:T(2,128)}, f32[3,2,1,2,8]{4,3,2,1,0:T(2,128)}, f32[2,1,2,8,9]{4,3,2,1,0:T(8,128)}) custom-call(f32[16,64]{1,0:T(8,128)S(1)} %add_add_fusion.mine_ref, f32[1,32]{1,0:T(1,128)S(1)} %get-tuple-element.29.shift_row_ref, f32[16,32]{1,0:T(8,128)S(1)} %collective-permute-done.7.back_ref), custom_call_target="tpu_custom_call" | custom-call | tf_op jit(solution)/shard_map/write_outputs/pallas_call | solution.py:637
  (3 shorter events, 0.0 us)
Async XLA Ops:
  1.7 9.6 %collective-permute-start = (f32[48,128]{1,0:T(8,128)S(1)}, f32[48,128]{1,0:T(8,128)S(1)}, u32[]{:S(2)}, u32[]{:S(2)}) collective-permute-start(f32[48,128]{1,0:T(8,128)S(1)} %pack_payload.1.here_ref), channel_id=1, source_target_pairs={{0,8},{8,16},{16,24},{24,0},{1,9},{9,17},{17,25},{25,1},{2,10},{10... | collective-permute-start | bytes 73736 | tf_op jit(solution)/shard_map/ppermute | solution.py:554
  4.8 6.5 %collective-permute-start.2 = (f32[40,128]{1,0:T(8,128)S(1)}, f32[40,128]{1,0:T(8,128)S(1)}, u32[]{:S(2)}, u32[]{:S(2)}) collective-permute-start(f32[40,128]{1,0:T(8,128)S(1)} %slice.8), channel_id=1, source_target_pairs={{0,12},{4,8},{8,20},{12,16},{16,28},{20,24},{24,4},{28,0},{1,13},{... | collective-permute-start | bytes 61448 | tf_op jit(solution)/shard_map/ppermute | solution.py:554
  7.3 4.0 %collective-permute-start.1 = (f32[40,128]{1,0:T(8,128)S(1)}, f32[40,128]{1,0:T(8,128)S(1)}, u32[]{:S(2)}, u32[]{:S(2)}) collective-permute-start(f32[40,128]{1,0:T(8,128)S(1)} %slice.8), channel_id=1, source_target_pairs={{0,4},{4,0},{1,5},{5,1},{2,6},{6,2},{3,7},{7,3},{8,12},{12,8},{9,1... | collective-permute-start | bytes 61448 | tf_op jit(solution)/shard_map/ppermute | solution.py:554
  11.3 4.0 %collective-permute-start.3 = (f32[176,128]{1,0:T(8,128)S(1)}, f32[176,128]{1,0:T(8,128)S(1)}, u32[]{:S(2)}, u32[]{:S(2)}) collective-permute-start(f32[176,128]{1,0:T(8,128)S(1)} %pad_add_fusion), channel_id=1, source_target_pairs={{0,1},{1,2},{2,3},{3,0},{4,5},{5,6},{6,7},{7,4},{8,9},{9,10},{10,1... | collective-permute-start | bytes 270344 | tf_op jit(solution)/shard_map/ppermute | solution.py:554
  19.5 3.1 %collective-permute-start.4 = (f32[16,64]{1,0:T(8,128)S(1)}, f32[16,64]{1,0:T(8,128)S(1)}, u32[]{:S(2)}, u32[]{:S(2)}) collective-permute-start(f32[16,64]{1,0:T(8,128)S(1)} %get-tuple-element.26), channel_id=1, source_target_pairs={{0,3},{1,0},{2,1},{3,2},{4,7},{5,4},{6,5},{7,6},{8,11},{9,8},{10,9... | collective-permute-start | bytes 12296 | tf_op jit(solution)/shard_map/ppermute | solution.py:554
  19.5 3.9 %collective-permute-start.5 = (f32[16,64]{1,0:T(8,128)S(1)}, f32[16,64]{1,0:T(8,128)S(1)}, u32[]{:S(2)}, u32[]{:S(2)}) collective-permute-start(f32[16,64]{1,0:T(8,128)S(1)} %get-tuple-element.27), channel_id=1, source_target_pairs={{0,7},{1,4},{2,5},{3,6},{4,3},{5,0},{6,1},{7,2},{8,15},{9,12},{10,... | collective-permute-start | bytes 12296 | tf_op jit(solution)/shard_map/ppermute | solution.py:554
  22.1 3.7 %collective-permute-start.6 = (f32[16,64]{1,0:T(8,128)S(1)}, f32[16,64]{1,0:T(8,128)S(1)}, u32[]{:S(2)}, u32[]{:S(2)}) collective-permute-start(f32[16,64]{1,0:T(8,128)S(1)} %get-tuple-element.28), channel_id=1, source_target_pairs={{0,4},{4,0},{1,5},{5,1},{2,6},{6,2},{3,7},{7,3},{8,12},{12,8},{9,1... | collective-permute-start | bytes 12296 | tf_op jit(solution)/shard_map/ppermute | solution.py:554
  25.8 3.7 %collective-permute-start.7 = (f32[16,32]{1,0:T(8,128)S(1)}, f32[16,32]{1,0:T(8,128)S(1)}, u32[]{:S(2)}, u32[]{:S(2)}) collective-permute-start(f32[16,32]{1,0:T(8,128)S(1)} %slice.9), channel_id=1, source_target_pairs={{0,24},{8,0},{16,8},{24,16},{1,25},{9,1},{17,9},{25,17},{2,26},{10... | collective-permute-start | bytes 6152 | tf_op jit(solution)/shard_map/ppermute | solution.py:554

commit v11 on v9

--- a/solution.py
+++ b/solution.py
@@ -98,6 +98,7 @@
     neighbours_hbm,
     scale_hbm,
     payload_ref,
+    again_ref,
     wide_ref,
     positions_ref,
     species_ref,
@@ -164,6 +165,7 @@
         more = wide_ref[pl.ds(j, owned // per_row, stride=per_row), :]
         codes = codes + pltpu.roll(more, j * nbr, 1)
     payload_ref[owned + 8 :] = codes
+    again_ref[...] = payload_ref[...]
 
 
 def fetch_kernel(species_hbm, centers_hbm, shift_hbm, *refs):
@@ -218,7 +220,6 @@
     near_side_refs = refs[: 2 * kind - 2]
     (
         next_z_ref,
-        next_xz_ref,
         center_weight_ref,
         near_weight_ref,
         basis_weight_ref,
@@ -242,17 +243,17 @@
     root_three = math.sqrt(3.0)
     root_fifteen = math.sqrt(15.0)
     root_five = math.sqrt(5.0)
+    far = next_z_ref[...]
+    mains = [here_ref[...], last_x_ref[...], far[:height], far[height : 2 * height]]
     near_sides = [ref[...] for ref in near_side_refs]
+    far_sides = far[2 * height :]
+    far_sides = [far_sides[i * short : (i + 1) * short] for i in range(2 * kind - 2)]
     blocks_in = [
-        [here_ref[...], *near_sides[0::2]],
-        [last_x_ref[...], *near_sides[1::2]],
+        [mains[0], *near_sides[0::2]],
+        [mains[1], *near_sides[1::2]],
+        [mains[2], *far_sides[0::2]],
+        [mains[3], *far_sides[1::2]],
     ]
-    for far_ref in (next_z_ref, next_xz_ref):
-        far = far_ref[...]
-        sides = [
-            far[height + i * short : height + (i + 1) * short] for i in range(kind - 1)
-        ]
-        blocks_in.append([far[:height], *sides])
     feats = jnp.concatenate([side[:owned] for block in blocks_in for side in block], axis=0)
     known = feats.shape[0]
     center_feats = []
@@ -546,12 +547,14 @@
     nbr = pairs // owned
     kind = min(3, lax.axis_size("gy"))
 
-    def moved(array, steps):
+    def moved(array, steps, wrap=None):
         names = tuple(steps)
         sizes = [lax.axis_size(name) for name in names]
         route = []
         for at in np.ndindex(*sizes):
             to = [(p + steps[name]) % size for p, name, size in zip(at, names, sizes)]
+            if wrap is not None and wrap != (to[0] != at[0] + steps[names[0]]):
+                continue
             route.append(
                 (int(np.ravel_multi_index(at, sizes)), int(np.ravel_multi_index(to, sizes)))
             )
@@ -560,11 +563,12 @@
     vmem = pl.BlockSpec(memory_space=pltpu.VMEM)
     hbm = pl.BlockSpec(memory_space=pltpu.HBM)
     listed = centers.reshape(1, owned)
-    here = pl.pallas_call(
+    payload = jax.ShapeDtypeStruct((owned + 8 + pairs // 128, width), F32)
+    here, again = pl.pallas_call(
         functools.partial(pack_kernel, kind),
-        out_shape=jax.ShapeDtypeStruct((owned + 8 + pairs // 128, width), F32),
+        out_shape=(payload, payload),
         in_specs=[hbm] * 6,
-        out_specs=vmem,
+        out_specs=(vmem, vmem),
         scratch_shapes=[
             pltpu.VMEM((owned, 128), F32),
             pltpu.VMEM(positions.shape, F32),
@@ -613,13 +617,18 @@
         name="fetch_weights",
     )(*in_hbm(species, listed, species_shift, *weights))
     short = here[: owned + 8]
-    last_x = moved(here, {"gx": 1})
+    steps = (-1, 1)[: kind - 1]
+    last_y = [moved(again, {"gy": step})[: owned + 8] for step in steps]
+    last_xy = [moved(again, {"gx": 1, "gy": step}, False)[: owned + 8] for step in steps]
+    last_x = moved(again, {"gx": 1}, False)
+    wrap_xy = [moved(here, {"gx": 1, "gy": step}, True) for step in steps]
+    wrap_x = moved(here, {"gx": 1}, True)
+    wrap_x, *wrap_xy = lax.optimization_barrier((wrap_x, *wrap_xy))
+    last_x = wrap_x + last_x
     sides = []
-    for step in (-1, 1)[: kind - 1]:
-        sides.append(moved(short, {"gx": 1, "gy": step}))
-        sides.insert(-1, moved(short, {"gy": step}))
-    next_z = moved(joined([here, *sides[0::2]]), {"gz": -1})
-    next_xz = moved(joined([last_x, *sides[1::2]]), {"gz": -1})
+    for y, xy, wrapped in zip(last_y, last_xy, wrap_xy):
+        sides.extend((y, wrapped[: owned + 8] + xy))
+    next_z = moved(joined([here, last_x, *sides]), {"gz": -1})
     half = 2 * kind * owned
     keep, send = pl.pallas_call(
         functools.partial(force_kernel, kind, nbr),
@@ -627,7 +636,7 @@
             jax.ShapeDtypeStruct((ORDERS, half), F32),
             jax.ShapeDtypeStruct((ORDERS, half), F32),
         ),
-        in_specs=[vmem] * (9 + 2 * kind),
+        in_specs=[vmem] * (8 + 2 * kind),
         out_specs=(vmem, vmem),
         compiler_params=pltpu.CompilerParams(vmem_limit_bytes=32 * 1024 * 1024),
         name="pair_forces",
@@ -636,17 +645,23 @@
         last_x,
         *sides,
         next_z,
-        next_xz,
         *weights,
     )
     totals = keep + moved(send, {"gz": 1})
 
-    half = kind * owned
-    totals = totals[:, :half] + moved(totals[:, half:], {"gx": -1})
-    back = []
-    for i, step in enumerate((1, -1)[: kind - 1]):
-        part = totals[:, (1 + i) * owned : (2 + i) * owned]
-        back.append(moved(part, {"gy": step}))
+    def part(index):
+        return totals[:, index * owned : (index + 1) * owned]
+
+    steps = tuple(enumerate((1, -1)[: kind - 1]))
+    far = totals[:, kind * owned :]
+    back = [moved(far, {"gx": -1}, False)[:, :owned]]
+    for i, step in steps:
+        wrapped = moved(far, {"gx": -1, "gy": step}, False)
+        back.append(wrapped[:, (1 + i) * owned : (2 + i) * owned])
+    for i, step in steps:
+        back.append(moved(totals, {"gy": step})[:, (1 + i) * owned : (2 + i) * owned])
+    back.extend(moved(part(kind + 1 + i), {"gx": -1, "gy": step}, True) for i, step in steps)
+    back.append(moved(part(kind), {"gx": -1}, True))
     site_energy, forces, virial = pl.pallas_call(
         finish_kernel,
         out_shape=(

time: 29.4 us -> 43 us (1.46)
  starting transfers between devices: 10.7 us -> 29.4 us
  waiting for transfers between devices: 10.3 us -> 4.86 us
    ppermute x8 -> x12, starting transfers between devices: 10.7 us -> 29.4 us  [moved(): return lax.ppermute(array, names, route)]
    ppermute x8 -> x12, waiting for transfers between devices: 10.3 us -> 4.86 us  [moved(): return lax.ppermute(array, names, route)]
  transfers between devices with their start and end apart: 8 -> 12, of which waited for: 6 -> 4; matrix products, arithmetic and copies ran while one was open for 0% -> 1% of each run, Pallas kernels for 5% -> 3%
where the time goes in v11:
time: 43 us; the launch traced here: 42.6 us
  starting transfers between devices  29.4 us (68%)
  Pallas kernels  7.29 us (17%)
  waiting for transfers between devices  4.86 us (11%)
  between operations  0.78 us (2%)
    ppermute x12, starting transfers between devices, moved(): return lax.ppermute(array, names, route)  29.4 us
    ppermute x12, waiting for transfers between devices, moved(): return lax.ppermute(array, names, route)  4.86 us
    pallas_call x1, Pallas kernels, local(): pl.pallas_call(functools.partial(force_kernel, kind, nbr), out_shape=(jax...  4.1 us
    pallas_call x1, Pallas kernels, local(): pl.pallas_call(fetch_kernel, out_shape=(*(jax.ShapeDtypeStruct(w.shape, F...  1.35 us
    pallas_call x1, Pallas kernels, local(): pl.pallas_call(functools.partial(pack_kernel, kind), out_shape=(payload,...  1.09 us
  transfers between devices with their start and end apart: 12, of which 4 were waited for; matrix products, arithmetic and copies ran while one was open for 1% of the time, Pallas kernels for 3%

profile of v11, /device:TPU:0, one launch (start us, length us, event | category | flops | bytes accessed | tf_op | source)
XLA Modules:
  0.0 42.6 jit_solution(9711208581234203225)
XLA Ops:
  0.6 1.1 %pack_payload.1 = (f32[48,128]{1,0:T(8,128)S(1)}, f32[48,128]{1,0:T(8,128)S(1)}) custom-call(f32[3,2,1,2,8]{4,3,2,1,0:T(2,128)} %positions_hbm.1, f32[32,128]{1,0:T(8,128)} %bitcast.6, s32[2,1,2,8]{3,2,1,0:T(2,128)} %species_hbm.3, s32[1,32]{1,0:T(1,128)} %bitcast.7, s32[32,32]{1,0:T(8,128)} %neighbours_hbm.1, f32[5]{0:T(128)} %scale_hbm.1), custom_call_target="tpu_custom_call" | custom-call | tf_op jit(solution)/shard_map/pack_payload/pallas_call | solution.py:567
  1.7 1.3 %collective-permute-start.1 = (f32[48,128]{1,0:T(8,128)S(1)}, f32[48,128]{1,0:T(8,128)S(1)}, u32[]{:S(2)}, u32[]{:S(2)}) collective-permute-start(f32[48,128]{1,0:T(8,128)S(1)} %get-tuple-element.20.here_ref), channel_id=1, source_target_pairs={{24,4},{28,0},{25,5},{29,1},{26,6},{30,2},{27,7},{31,3}} | collective-permute-start | bytes 73736 | tf_op jit(solution)/shard_map/ppermute | solution.py:561
  3.0 1.3 %collective-permute-start = (f32[48,128]{1,0:T(8,128)S(1)}, f32[48,128]{1,0:T(8,128)S(1)}, u32[]{:S(2)}, u32[]{:S(2)}) collective-permute-start(f32[48,128]{1,0:T(8,128)S(1)} %get-tuple-element.20.here_ref), channel_id=1, source_target_pairs={{24,0},{25,1},{26,2},{27,3},{28,4},{29,5},{30,6},{31,7}} | collective-permute-start | bytes 73736 | tf_op jit(solution)/shard_map/ppermute | solution.py:561
  4.3 4.6 %collective-permute-start.4 = (f32[48,128]{1,0:T(8,128)S(1)}, f32[48,128]{1,0:T(8,128)S(1)}, u32[]{:S(2)}, u32[]{:S(2)}) collective-permute-start(f32[48,128]{1,0:T(8,128)S(1)} %get-tuple-element.22), channel_id=1, source_target_pairs={{0,12},{4,8},{8,20},{12,16},{16,28},{20,24},{1,13},{5,9},{9,21},{1... | collective-permute-start | bytes 73736 | tf_op jit(solution)/shard_map/ppermute | solution.py:561
  8.9 0.6 %collective-permute-start.3 = (f32[48,128]{1,0:T(8,128)S(1)}, f32[48,128]{1,0:T(8,128)S(1)}, u32[]{:S(2)}, u32[]{:S(2)}) collective-permute-start(f32[48,128]{1,0:T(8,128)S(1)} %get-tuple-element.22), channel_id=1, source_target_pairs={{0,4},{4,0},{1,5},{5,1},{2,6},{6,2},{3,7},{7,3},{8,12},{12,8},{9,1... | collective-permute-start | bytes 73736 | tf_op jit(solution)/shard_map/ppermute | solution.py:561
  9.5 3.5 %collective-permute-start.2 = (f32[48,128]{1,0:T(8,128)S(1)}, f32[48,128]{1,0:T(8,128)S(1)}, u32[]{:S(2)}, u32[]{:S(2)}) collective-permute-start(f32[48,128]{1,0:T(8,128)S(1)} %get-tuple-element.22), channel_id=1, source_target_pairs={{0,8},{8,16},{16,24},{1,9},{9,17},{17,25},{2,10},{10,18},{18,26},{... | collective-permute-start | bytes 73736 | tf_op jit(solution)/shard_map/ppermute | solution.py:561
  13.0 0.0 collective-permute-done.1
  13.0 0.0 collective-permute-done
  13.0 0.0 collective-permute-done.4
  13.1 0.0 collective-permute-done.3
  13.1 1.4 %collective-permute-done.2 = f32[48,128]{1,0:T(8,128)S(1)} collective-permute-done((f32[48,128]{1,0:T(8,128)S(1)}, f32[48,128]{1,0:T(8,128)S(1)}, u32[]{:S(2)}, u32[]{:S(2)}) %collective-permute-start.2) | collective-permute-done | bytes 24608 | tf_op jit(solution)/shard_map/ppermute | solution.py:561
  14.5 0.1 collective-permute-start.5
  14.6 1.3 %fetch_weights.1 = (f32[128,128]{1,0:T(8,128)S(1)}, f32[128,128]{1,0:T(8,128)S(1)}, f32[8,128]{1,0:T(8,128)S(1)}, f32[3,128]{1,0:T(4,128)S(1)}, f32[128,256]{1,0...) custom-call(s32[2,1,2,8]{3,2,1,0:T(2,128)} %species_hbm.3, s32[1,32]{1,0:T(1,128)} %bitcast.8, ...), custom_call_target="tpu_custom_call" | custom-call | tf_op jit(solution)/shard_map/fetch_weights/pallas_call | solution.py:602
  15.9 0.8 %collective-permute-done.5.refs_2_ = f32[176,128]{1,0:T(8,128)S(1)} collective-permute-done((f32[176,128]{1,0:T(8,128)S(1)}, f32[176,128]{1,0:T(8,128)S(1)}, u32[]{:S(2)}, u32[]{:S(2)}) %collective-permute-start.5) | collective-permute-done | bytes 90144 | tf_op jit(solution)/shard_map/ppermute | solution.py:561
  16.7 4.1 %pair_forces.1 = (f32[16,128]{1,0:T(8,128)S(1)}, f32[16,128]{1,0:T(8,128)S(1)}) custom-call(f32[48,128]{1,0:T(8,128)S(1)} %get-tuple-element.20.here_ref, f32[48,128]{1,0:T(8,128)S(1)} %add.26.last_x_ref, f32[40,128]{1,0:T(8,128)S(1)} %slice.36.refs_0_, f32[40,128]{1,0:T(8,128)S(1)} %slice_add_fusion.refs_1_, f32[176,128]{1,0:T(8,128)S(1)} %collective-permute-done.5.refs_2_, ...), custom_call_target="tpu_custom_call" | custom-call | tf_op jit(solution)/shard_map/pair_forces/pallas_call | solution.py:633
  20.8 1.7 %collective-permute-start.6 = (f32[16,128]{1,0:T(8,128)S(1)}, f32[16,128]{1,0:T(8,128)S(1)}, u32[]{:S(2)}, u32[]{:S(2)}) collective-permute-start(f32[16,128]{1,0:T(8,128)S(1)} %get-tuple-element.32), channel_id=1, source_target_pairs={{0,1},{1,2},{2,3},{3,0},{4,5},{5,6},{6,7},{7,4},{8,9},{9,10},{10,1... | collective-permute-start | bytes 24584 | tf_op jit(solution)/shard_map/ppermute | solution.py:561
  22.6 1.4 %collective-permute-done.6 = f32[16,128]{1,0:T(8,128)S(1)} collective-permute-done((f32[16,128]{1,0:T(8,128)S(1)}, f32[16,128]{1,0:T(8,128)S(1)}, u32[]{:S(2)}, u32[]{:S(2)}) %collective-permute-start.6) | collective-permute-done | bytes 8224 | tf_op jit(solution)/shard_map/ppermute | solution.py:561
  24.0 0.1 slice.38
  24.1 1.3 %collective-permute-start.8 = (f32[16,64]{1,0:T(8,128)S(1)}, f32[16,64]{1,0:T(8,128)S(1)}, u32[]{:S(2)}, u32[]{:S(2)}) collective-permute-start(f32[16,64]{1,0:T(8,128)S(1)} %slice.38), channel_id=1, source_target_pairs={{8,4},{12,0},{16,12},{20,8},{24,20},{28,16},{9,5},{13,1},{17,13},{... | collective-permute-start | bytes 12296 | tf_op jit(solution)/shard_map/ppermute | solution.py:561
  25.4 1.3 %collective-permute-start.7 = (f32[16,64]{1,0:T(8,128)S(1)}, f32[16,64]{1,0:T(8,128)S(1)}, u32[]{:S(2)}, u32[]{:S(2)}) collective-permute-start(f32[16,64]{1,0:T(8,128)S(1)} %slice.38), channel_id=1, source_target_pairs={{8,0},{16,8},{24,16},{9,1},{17,9},{25,17},{10,2},{18,10},{26,18},{... | collective-permute-start | bytes 12296 | tf_op jit(solution)/shard_map/ppermute | solution.py:561
  26.7 1.6 %collective-permute-start.9 = (f32[16,128]{1,0:T(8,128)S(1)}, f32[16,128]{1,0:T(8,128)S(1)}, u32[]{:S(2)}, u32[]{:S(2)}) collective-permute-start(f32[16,128]{1,0:T(8,128)S(1)} %add.31.mine_ref), channel_id=1, source_target_pairs={{0,4},{4,0},{1,5},{5,1},{2,6},{6,2},{3,7},{7,3},{8,12},{12,8},{9,1... | collective-permute-start | bytes 24584 | tf_op jit(solution)/shard_map/ppermute | solution.py:561
  28.2 0.1 fusion
  28.3 10.6 %collective-permute-start.11 = (f32[16,32]{1,0:T(8,128)S(1)}, f32[16,32]{1,0:T(8,128)S(1)}, u32[]{:S(2)}, u32[]{:S(2)}) collective-permute-start(f32[16,32]{1,0:T(8,128)S(1)} %get-tuple-element.37), channel_id=1, source_target_pairs={{0,24},{1,25},{2,26},{3,27},{4,28},{5,29},{6,30},{7,31}} | collective-permute-start | bytes 6152 | tf_op jit(solution)/shard_map/ppermute | solution.py:561
  38.9 1.6 %collective-permute-start.10 = (f32[16,32]{1,0:T(8,128)S(1)}, f32[16,32]{1,0:T(8,128)S(1)}, u32[]{:S(2)}, u32[]{:S(2)}) collective-permute-start(f32[16,32]{1,0:T(8,128)S(1)} %get-tuple-element.38), channel_id=1, source_target_pairs={{0,28},{4,24},{1,29},{5,25},{2,30},{6,26},{3,31},{7,27}} | collective-permute-start | bytes 6152 | tf_op jit(solution)/shard_map/ppermute | solution.py:561
  40.5 0.0 collective-permute-done.8
  40.5 0.1 slice.40.refs_1_
  40.6 0.0 collective-permute-done.9
  40.6 0.1 slice.41.refs_2_
  40.7 0.0 collective-permute-done.11.refs_4_
  40.7 1.2 %collective-permute-done.10.refs_3_ = f32[16,32]{1,0:T(8,128)S(1)} collective-permute-done((f32[16,32]{1,0:T(8,128)S(1)}, f32[16,32]{1,0:T(8,128)S(1)}, u32[]{:S(2)}, u32[]{:S(2)}) %collective-permute-start.10) | collective-permute-done | bytes 2080 | tf_op jit(solution)/shard_map/ppermute | solution.py:561
  41.9 0.0 collective-permute-done.7
  41.9 0.8 %write_outputs.1 = (f32[2,1,2,8]{3,2,1,0:T(2,128)}, f32[3,2,1,2,8]{4,3,2,1,0:T(2,128)}, f32[2,1,2,8,9]{4,3,2,1,0:T(8,128)}) custom-call(f32[16,128]{1,0:T(8,128)S(1)} %add.31.mine_ref, f32[1,32]{1,0:T(1,128)S(1)} %get-tuple-element.33.shift_row_ref, f32[16,32]{1,0:T(8,128)S(1)} %bitcast.5, f32[16,32]{1,0:T(8,128)S(1)} %slice.40.refs_1_, ...), custom_call_target="tpu_custom_call" | custom-call | tf_op jit(solution)/shard_map/write_outputs/pallas_call | solution.py:665
  (5 shorter events, 0.0 us)
Async XLA Ops:
  1.7 11.3 %collective-permute-start.1 = (f32[48,128]{1,0:T(8,128)S(1)}, f32[48,128]{1,0:T(8,128)S(1)}, u32[]{:S(2)}, u32[]{:S(2)}) collective-permute-start(f32[48,128]{1,0:T(8,128)S(1)} %get-tuple-element.20.here_ref), channel_id=1, source_target_pairs={{24,4},{28,0},{25,5},{29,1},{26,6},{30,2},{27,7},{31,3}} | collective-permute-start | bytes 73736 | tf_op jit(solution)/shard_map/ppermute | solution.py:561
  3.0 10.0 %collective-permute-start = (f32[48,128]{1,0:T(8,128)S(1)}, f32[48,128]{1,0:T(8,128)S(1)}, u32[]{:S(2)}, u32[]{:S(2)}) collective-permute-start(f32[48,128]{1,0:T(8,128)S(1)} %get-tuple-element.20.here_ref), channel_id=1, source_target_pairs={{24,0},{25,1},{26,2},{27,3},{28,4},{29,5},{30,6},{31,7}} | collective-permute-start | bytes 73736 | tf_op jit(solution)/shard_map/ppermute | solution.py:561
  4.3 8.7 %collective-permute-start.4 = (f32[48,128]{1,0:T(8,128)S(1)}, f32[48,128]{1,0:T(8,128)S(1)}, u32[]{:S(2)}, u32[]{:S(2)}) collective-permute-start(f32[48,128]{1,0:T(8,128)S(1)} %get-tuple-element.22), channel_id=1, source_target_pairs={{0,12},{4,8},{8,20},{12,16},{16,28},{20,24},{1,13},{5,9},{9,21},{1... | collective-permute-start | bytes 73736 | tf_op jit(solution)/shard_map/ppermute | solution.py:561
  8.9 4.1 %collective-permute-start.3 = (f32[48,128]{1,0:T(8,128)S(1)}, f32[48,128]{1,0:T(8,128)S(1)}, u32[]{:S(2)}, u32[]{:S(2)}) collective-permute-start(f32[48,128]{1,0:T(8,128)S(1)} %get-tuple-element.22), channel_id=1, source_target_pairs={{0,4},{4,0},{1,5},{5,1},{2,6},{6,2},{3,7},{7,3},{8,12},{12,8},{9,1... | collective-permute-start | bytes 73736 | tf_op jit(solution)/shard_map/ppermute | solution.py:561
  9.5 5.0 %collective-permute-start.2 = (f32[48,128]{1,0:T(8,128)S(1)}, f32[48,128]{1,0:T(8,128)S(1)}, u32[]{:S(2)}, u32[]{:S(2)}) collective-permute-start(f32[48,128]{1,0:T(8,128)S(1)} %get-tuple-element.22), channel_id=1, source_target_pairs={{0,8},{8,16},{16,24},{1,9},{9,17},{17,25},{2,10},{10,18},{18,26},{... | collective-permute-start | bytes 73736 | tf_op jit(solution)/shard_map/ppermute | solution.py:561
  14.5 2.2 %collective-permute-start.5 = (f32[176,128]{1,0:T(8,128)S(1)}, f32[176,128]{1,0:T(8,128)S(1)}, u32[]{:S(2)}, u32[]{:S(2)}) collective-permute-start(f32[176,128]{1,0:T(8,128)S(1)} %pad_add_fusion), channel_id=1, source_target_pairs={{0,3},{1,0},{2,1},{3,2},{4,7},{5,4},{6,5},{7,6},{8,11},{9,8},{10,9... | collective-permute-start | bytes 270344 | tf_op jit(solution)/shard_map/ppermute | solution.py:561
  20.8 3.2 %collective-permute-start.6 = (f32[16,128]{1,0:T(8,128)S(1)}, f32[16,128]{1,0:T(8,128)S(1)}, u32[]{:S(2)}, u32[]{:S(2)}) collective-permute-start(f32[16,128]{1,0:T(8,128)S(1)} %get-tuple-element.32), channel_id=1, source_target_pairs={{0,1},{1,2},{2,3},{3,0},{4,5},{5,6},{6,7},{7,4},{8,9},{9,10},{10,1... | collective-permute-start | bytes 24584 | tf_op jit(solution)/shard_map/ppermute | solution.py:561
  24.1 16.4 %collective-permute-start.8 = (f32[16,64]{1,0:T(8,128)S(1)}, f32[16,64]{1,0:T(8,128)S(1)}, u32[]{:S(2)}, u32[]{:S(2)}) collective-permute-start(f32[16,64]{1,0:T(8,128)S(1)} %slice.38), channel_id=1, source_target_pairs={{8,4},{12,0},{16,12},{20,8},{24,20},{28,16},{9,5},{13,1},{17,13},{... | collective-permute-start | bytes 12296 | tf_op jit(solution)/shard_map/ppermute | solution.py:561
  25.4 16.5 %collective-permute-start.7 = (f32[16,64]{1,0:T(8,128)S(1)}, f32[16,64]{1,0:T(8,128)S(1)}, u32[]{:S(2)}, u32[]{:S(2)}) collective-permute-start(f32[16,64]{1,0:T(8,128)S(1)} %slice.38), channel_id=1, source_target_pairs={{8,0},{16,8},{24,16},{9,1},{17,9},{25,17},{10,2},{18,10},{26,18},{... | collective-permute-start | bytes 12296 | tf_op jit(solution)/shard_map/ppermute | solution.py:561
  26.7 13.9 %collective-permute-start.9 = (f32[16,128]{1,0:T(8,128)S(1)}, f32[16,128]{1,0:T(8,128)S(1)}, u32[]{:S(2)}, u32[]{:S(2)}) collective-permute-start(f32[16,128]{1,0:T(8,128)S(1)} %add.31.mine_ref), channel_id=1, source_target_pairs={{0,4},{4,0},{1,5},{5,1},{2,6},{6,2},{3,7},{7,3},{8,12},{12,8},{9,1... | collective-permute-start | bytes 24584 | tf_op jit(solution)/shard_map/ppermute | solution.py:561
  28.3 12.4 %collective-permute-start.11 = (f32[16,32]{1,0:T(8,128)S(1)}, f32[16,32]{1,0:T(8,128)S(1)}, u32[]{:S(2)}, u32[]{:S(2)}) collective-permute-start(f32[16,32]{1,0:T(8,128)S(1)} %get-tuple-element.37), channel_id=1, source_target_pairs={{0,24},{1,25},{2,26},{3,27},{4,28},{5,29},{6,30},{7,31}} | collective-permute-start | bytes 6152 | tf_op jit(solution)/shard_map/ppermute | solution.py:561
  38.9 2.9 %collective-permute-start.10 = (f32[16,32]{1,0:T(8,128)S(1)}, f32[16,32]{1,0:T(8,128)S(1)}, u32[]{:S(2)}, u32[]{:S(2)}) collective-permute-start(f32[16,32]{1,0:T(8,128)S(1)} %get-tuple-element.38), channel_id=1, source_target_pairs={{0,28},{4,24},{1,29},{5,25},{2,30},{6,26},{3,31},{7,27}} | collective-permute-start | bytes 6152 | tf_op jit(solution)/shard_map/ppermute | solution.py:561

commit v12 on v9

--- a/solution.py
+++ b/solution.py
@@ -218,7 +218,6 @@
     near_side_refs = refs[: 2 * kind - 2]
     (
         next_z_ref,
-        next_xz_ref,
         center_weight_ref,
         near_weight_ref,
         basis_weight_ref,
@@ -242,20 +241,21 @@
     root_three = math.sqrt(3.0)
     root_fifteen = math.sqrt(15.0)
     root_five = math.sqrt(5.0)
+    far = next_z_ref[...]
+    mains = [here_ref[...], last_x_ref[...], far[:height], far[height : 2 * height]]
     near_sides = [ref[...] for ref in near_side_refs]
+    far_sides = far[2 * height :]
+    far_sides = [far_sides[i * short : (i + 1) * short] for i in range(2 * kind - 2)]
     blocks_in = [
-        [here_ref[...], *near_sides[0::2]],
-        [last_x_ref[...], *near_sides[1::2]],
+        [mains[0], *near_sides[0::2]],
+        [mains[1], *near_sides[1::2]],
+        [mains[2], *far_sides[0::2]],
+        [mains[3], *far_sides[1::2]],
     ]
-    for far_ref in (next_z_ref, next_xz_ref):
-        far = far_ref[...]
-        sides = [
-            far[height + i * short : height + (i + 1) * short] for i in range(kind - 1)
-        ]
-        blocks_in.append([far[:height], *sides])
     feats = jnp.concatenate([side[:owned] for block in blocks_in for side in block], axis=0)
     known = feats.shape[0]
     center_feats = []
+    center_coords = []
     coords = []
     scales = []
     codes = []
@@ -272,7 +272,9 @@
         corner = jnp.where(
             tile_lane < sites, corner_x, jnp.where(tile_lane < 2 * sites, 0.0, corner_z)
         )
-        coords.append(rows + corner)
+        rows = rows + corner
+        coords.append(rows)
+        center_coords.append(rows[cell : cell + 1])
         start = short + cell * span // 128
         codes.extend(block[0][start + r : start + r + 1] for r in range(span // 128))
     center_feats = jnp.concatenate(center_feats, axis=0)
@@ -283,13 +285,18 @@
     side_y = ((code >> 10) - 1).astype(F32)
     near_row = jnp.where(live, code & 1023, known)
 
-    spread = jnp.broadcast_to(coords[:, None, :], (coords.shape[0], sites, 128))
-    spread = spread.reshape(known, 128)
-    keep_lane = lax.broadcasted_iota(jnp.int32, (known, 128), 1)
-    keep_row = lax.broadcasted_iota(jnp.int32, (known, 128), 0)
-    keep = (keep_lane % sites == keep_row % sites) & (keep_lane < 3 * sites)
-    spread = jnp.where(keep, spread, 0.0)
-    place_parts = jnp.concatenate(split3(jnp.transpose(spread)[: 3 * sites]), axis=0)
+    def place_rows(cell_rows):
+        count = cell_rows.shape[0] * sites
+        spread = jnp.broadcast_to(cell_rows[:, None, :], (cell_rows.shape[0], sites, 128))
+        spread = spread.reshape(count, 128)
+        lane = lax.broadcasted_iota(jnp.int32, (count, 128), 1)
+        row = lax.broadcasted_iota(jnp.int32, (count, 128), 0)
+        keep = (lane % sites == row % sites) & (lane < 3 * sites)
+        spread = jnp.transpose(jnp.where(keep, spread, 0.0))
+        return jnp.concatenate(split3(spread[: 3 * sites]), axis=0)
+
+    place_parts = place_rows(coords)
+    center_parts = place_rows(jnp.concatenate(center_coords, axis=0))
 
     value_rows = stacked(*split(jnp.transpose(value_weight_ref[...])))
     latent_high_t, latent_low_t = split(jnp.transpose(latent_weight_ref[...]))
@@ -338,9 +345,6 @@
     site_ids = lax.broadcasted_iota(jnp.int32, (known, pairs), 0)
     slot_ids = lax.broadcasted_iota(jnp.int32, (owned, pairs), 0)
     slot_row = lax.broadcasted_iota(jnp.int32, (1, pairs), 1) // nbr
-    group_row = slot_row // GROUP
-    center_cell = group_row % 2 * 2 + 1 - group_row // 2
-    center_row = group_row * (kind * owned) + center_cell * sites + slot_row % GROUP
     block_row = lax.broadcasted_iota(jnp.int32, (wide, span), 0) // ORDERS
     block_lane = lax.broadcasted_iota(jnp.int32, (wide, span), 1) // nbr
     block_mask = (block_row == block_lane).astype(F32)
@@ -349,12 +353,10 @@
     lanes = [slice(g * span, (g + 1) * span) for g in range(groups)]
 
     pick = jnp.where(site_ids == near_row, 1.0, 0.0)
-    from_center = jnp.where(site_ids == center_row, 1.0, 0.0)
     pick_half = pick.astype(BF16)
-    center_half = from_center.astype(BF16)
     slot_half = jnp.where(slot_ids == slot_row, 1.0, 0.0).astype(BF16)
 
-    moved = mm(place_parts, (pick - from_center).astype(BF16))
+    moved = mm(place_parts, pick_half) - mm(center_parts, slot_half)
     moved = moved[: 3 * sites] + moved[3 * sites : 6 * sites] + moved[6 * sites :]
     dx = jnp.where(live, jnp.sum(moved[:sites], axis=0, keepdims=True), 6.0)
     dy = jnp.sum(moved[sites : 2 * sites], axis=0, keepdims=True) + CELL_SIDE * side_y
@@ -418,7 +420,8 @@
     gate = 0.5 * jnp.tanh(0.5 * before) + 0.5
     active = before * gate
     latent = weight * active
-    mixed = half_depth(value_rows, latent)
+    latent_high, latent_low = split(latent)
+    mixed = folded(mm(value_rows, jnp.concatenate([latent_high, latent_low], axis=0)))
     values = mixed[:width]
     env_high, env_low = split(mixed[width:])
 
@@ -436,8 +439,13 @@
     weighted = over_pairs(env_high, env_low)
     inner = over_orders(weighted)
     scalars = values * inner
-    joined_high, joined_low = split(jnp.concatenate([latent, scalars], axis=0))
-    z = full_depth(latent_both_t, latent_high_t, joined_high, joined_low)
+    scalars_high, scalars_low = split(scalars)
+    z = full_depth(
+        latent_both_t,
+        latent_high_t,
+        jnp.concatenate([latent_high, scalars_high], axis=0),
+        jnp.concatenate([latent_low, scalars_low], axis=0),
+    )
     z_gate = 0.5 * jnp.tanh(0.5 * z) + 0.5
     update = z * z_gate
     update_out = update * out_column
@@ -500,8 +508,22 @@
     )
     center_terms = jnp.concatenate([gx, gy, gz, *virial, pair_energy, *rest], axis=0)
     near_sums = mm_nt(jnp.concatenate(split(near_terms), axis=0), pick_half)
-    center_sums = mm_nt(jnp.concatenate(split(center_terms), axis=0), center_half)
-    totals = folded(near_sums + center_sums)
+    center_sums = mm_nt(jnp.concatenate(split(center_terms), axis=0), slot_half)
+    center_sums = jnp.concatenate(
+        [folded(center_sums), jnp.zeros((ORDERS, 128 - owned), F32)], axis=1
+    )
+    totals = folded(near_sums)
+    lane = lax.broadcasted_iota(jnp.int32, (ORDERS, 128), 1)
+    tiles = [totals[:, 128 * i : 128 * (i + 1)] for i in range(known // 128)]
+    for g in range(groups):
+        cell = g % 2 * 2 + 1 - g // 2
+        target = g * kind * owned + cell * sites
+        turn = (target - g * GROUP) % 128
+        piece = pltpu.roll(center_sums, turn, 1) if turn else center_sums
+        begin = target % 128
+        piece = jnp.where((lane >= begin) & (lane < begin + GROUP), piece, 0.0)
+        tiles[target // 128] = tiles[target // 128] + piece
+    totals = jnp.concatenate(tiles, axis=1)
     keep_ref[...] = totals[:, : known // 2]
     send_ref[...] = totals[:, known // 2 :]
 
@@ -618,8 +640,7 @@
     for step in (-1, 1)[: kind - 1]:
         sides.append(moved(short, {"gx": 1, "gy": step}))
         sides.insert(-1, moved(short, {"gy": step}))
-    next_z = moved(joined([here, *sides[0::2]]), {"gz": -1})
-    next_xz = moved(joined([last_x, *sides[1::2]]), {"gz": -1})
+    next_z = moved(joined([here, last_x, *sides]), {"gz": -1})
     half = 2 * kind * owned
     keep, send = pl.pallas_call(
         functools.partial(force_kernel, kind, nbr),
@@ -627,7 +648,7 @@
             jax.ShapeDtypeStruct((ORDERS, half), F32),
             jax.ShapeDtypeStruct((ORDERS, half), F32),
         ),
-        in_specs=[vmem] * (9 + 2 * kind),
+        in_specs=[vmem] * (8 + 2 * kind),
         out_specs=(vmem, vmem),
         compiler_params=pltpu.CompilerParams(vmem_limit_bytes=32 * 1024 * 1024),
         name="pair_forces",
@@ -636,17 +657,17 @@
         last_x,
         *sides,
         next_z,
-        next_xz,
         *weights,
     )
     totals = keep + moved(send, {"gz": 1})
 
-    half = kind * owned
-    totals = totals[:, :half] + moved(totals[:, half:], {"gx": -1})
-    back = []
+    def part(index):
+        return totals[:, index * owned : (index + 1) * owned]
+
+    back = [moved(part(kind), {"gx": -1})]
     for i, step in enumerate((1, -1)[: kind - 1]):
-        part = totals[:, (1 + i) * owned : (2 + i) * owned]
-        back.append(moved(part, {"gy": step}))
+        back.append(moved(part(kind + 1 + i), {"gx": -1, "gy": step}))
+        back.append(moved(part(1 + i), {"gy": step}))
     site_energy, forces, virial = pl.pallas_call(
         finish_kernel,
         out_shape=(

time: 29.4 us -> 28.6 us (0.973)
  waiting for transfers between devices: 10.3 us -> 8.89 us
  starting transfers between devices: 10.7 us -> 11.9 us
  Pallas kernels: 7.28 us -> 6.76 us
    ppermute x8, waiting for transfers between devices: 10.3 us -> 8.89 us  [moved(): return lax.ppermute(array, names, route)]
    ppermute x8, starting transfers between devices: 10.7 us -> 11.9 us  [moved(): return lax.ppermute(array, names, route)]
    pallas_call x1, Pallas kernels: 4.1 us -> 3.58 us  [local(): pl.pallas_call(functools.partial(force_kernel, kind, nbr), out_shape=(jax...]
  transfers between devices with their start and end apart: 8 -> 8, of which waited for: 6 -> 5; matrix products, arithmetic and copies ran while one was open for 0% -> 0% of each run, Pallas kernels for 5% -> 5%
where the time goes in v12:
time: 28.6 us; the launch traced here: 28.3 us
  starting transfers between devices  11.9 us (42%)
  waiting for transfers between devices  8.89 us (31%)
  Pallas kernels  6.76 us (24%)
  between operations  0.68 us (2%)
    ppermute x8, starting transfers between devices, moved(): return lax.ppermute(array, names, route)  11.9 us
    ppermute x8, waiting for transfers between devices, moved(): return lax.ppermute(array, names, route)  8.89 us
    pallas_call x1, Pallas kernels, local(): pl.pallas_call(functools.partial(force_kernel, kind, nbr), out_shape=(jax...  3.58 us
    pallas_call x1, Pallas kernels, local(): pl.pallas_call(fetch_kernel, out_shape=(*(jax.ShapeDtypeStruct(w.shape, F...  1.35 us
    pallas_call x1, Pallas kernels, local(): pl.pallas_call(functools.partial(pack_kernel, kind), out_shape=jax.ShapeD...  1.08 us
    pallas_call x1, Pallas kernels, local(): pl.pallas_call(finish_kernel, out_shape=(jax.ShapeDtypeStruct(species.sha...  0.75 us
  transfers between devices with their start and end apart: 8, of which 5 were waited for; matrix products, arithmetic and copies ran while one was open for 0% of the time, Pallas kernels for 5%

profile of v12, /device:TPU:0, one launch (start us, length us, event | category | flops | bytes accessed | tf_op | source)
XLA Modules:
  0.0 28.3 jit_solution(4262199822302578372)
XLA Ops:
  0.6 1.1 %pack_payload.1.here_ref = f32[48,128]{1,0:T(8,128)S(1)} custom-call(f32[3,2,1,2,8]{4,3,2,1,0:T(2,128)} %positions_hbm.1, f32[32,128]{1,0:T(8,128)} %bitcast.4, s32[2,1,2,8]{3,2,1,0:T(2,128)} %species_hbm.3, s32[1,32]{1,0:T(1,128)} %bitcast.5, s32[32,32]{1,0:T(8,128)} %neighbours_hbm.1, f32[5]{0:T(128)} %scale_hbm.1), custom_call_target="tpu_custom_call" | custom-call | tf_op jit(solution)/shard_map/pack_payload/pallas_call | solution.py:585
  1.7 3.1 %collective-permute-start = (f32[48,128]{1,0:T(8,128)S(1)}, f32[48,128]{1,0:T(8,128)S(1)}, u32[]{:S(2)}, u32[]{:S(2)}) collective-permute-start(f32[48,128]{1,0:T(8,128)S(1)} %pack_payload.1.here_ref), channel_id=1, source_target_pairs={{0,8},{8,16},{16,24},{24,0},{1,9},{9,17},{17,25},{25,1},{2,10},{10... | collective-permute-start | bytes 73736 | tf_op jit(solution)/shard_map/ppermute | solution.py:580
  4.8 2.5 %collective-permute-start.2 = (f32[40,128]{1,0:T(8,128)S(1)}, f32[40,128]{1,0:T(8,128)S(1)}, u32[]{:S(2)}, u32[]{:S(2)}) collective-permute-start(f32[40,128]{1,0:T(8,128)S(1)} %slice.16), channel_id=1, source_target_pairs={{0,12},{4,8},{8,20},{12,16},{16,28},{20,24},{24,4},{28,0},{1,13},{... | collective-permute-start | bytes 61448 | tf_op jit(solution)/shard_map/ppermute | solution.py:580
  7.3 0.5 %collective-permute-start.1 = (f32[40,128]{1,0:T(8,128)S(1)}, f32[40,128]{1,0:T(8,128)S(1)}, u32[]{:S(2)}, u32[]{:S(2)}) collective-permute-start(f32[40,128]{1,0:T(8,128)S(1)} %slice.16), channel_id=1, source_target_pairs={{0,4},{4,0},{1,5},{5,1},{2,6},{6,2},{3,7},{7,3},{8,12},{12,8},{9,1... | collective-permute-start | bytes 61448 | tf_op jit(solution)/shard_map/ppermute | solution.py:580
  7.8 3.5 %collective-permute-done.2.refs_1_ = f32[40,128]{1,0:T(8,128)S(1)} collective-permute-done((f32[40,128]{1,0:T(8,128)S(1)}, f32[40,128]{1,0:T(8,128)S(1)}, u32[]{:S(2)}, u32[]{:S(2)}) %collective-permute-start.2) | collective-permute-done | bytes 20512 | tf_op jit(solution)/shard_map/ppermute | solution.py:580
  11.3 0.0 collective-permute-done.1.refs_0_
  11.3 0.0 collective-permute-done.last_x_ref
  11.3 0.1 collective-permute-start.3
  11.4 1.3 %fetch_weights.1 = (f32[128,128]{1,0:T(8,128)S(1)}, f32[128,128]{1,0:T(8,128)S(1)}, f32[8,128]{1,0:T(8,128)S(1)}, f32[3,128]{1,0:T(4,128)S(1)}, f32[128,256]{1,0...) custom-call(s32[2,1,2,8]{3,2,1,0:T(2,128)} %species_hbm.3, s32[1,32]{1,0:T(1,128)} %bitcast.6, ...), custom_call_target="tpu_custom_call" | custom-call | tf_op jit(solution)/shard_map/fetch_weights/pallas_call | solution.py:620
  12.7 0.8 %collective-permute-done.3.refs_2_ = f32[176,128]{1,0:T(8,128)S(1)} collective-permute-done((f32[176,128]{1,0:T(8,128)S(1)}, f32[176,128]{1,0:T(8,128)S(1)}, u32[]{:S(2)}, u32[]{:S(2)}) %collective-permute-start.3) | collective-permute-done | bytes 90144 | tf_op jit(solution)/shard_map/ppermute | solution.py:580
  13.5 3.6 %pair_forces.1 = (f32[16,128]{1,0:T(8,128)S(1)}, f32[16,128]{1,0:T(8,128)S(1)}) custom-call(f32[48,128]{1,0:T(8,128)S(1)} %pack_payload.1.here_ref, f32[48,128]{1,0:T(8,128)S(1)} %collective-permute-done.last_x_ref, f32[40,128]{1,0:T(8,128)S(1)} %collective-permute-done.1.refs_0_, f32[40,128]{1,0:T(8,128)S(1)} %collective-permute-done.2.refs_1_, ...), custom_call_target="tpu_custom_call" | custom-call | tf_op jit(solution)/shard_map/pair_forces/pallas_call | solution.py:645
  17.1 1.8 %collective-permute-start.4 = (f32[16,128]{1,0:T(8,128)S(1)}, f32[16,128]{1,0:T(8,128)S(1)}, u32[]{:S(2)}, u32[]{:S(2)}) collective-permute-start(f32[16,128]{1,0:T(8,128)S(1)} %get-tuple-element.24), channel_id=1, source_target_pairs={{0,1},{1,2},{2,3},{3,0},{4,5},{5,6},{6,7},{7,4},{8,9},{9,10},{10,1... | collective-permute-start | bytes 24584 | tf_op jit(solution)/shard_map/ppermute | solution.py:580
  18.9 1.4 %collective-permute-done.4 = f32[16,128]{1,0:T(8,128)S(1)} collective-permute-done((f32[16,128]{1,0:T(8,128)S(1)}, f32[16,128]{1,0:T(8,128)S(1)}, u32[]{:S(2)}, u32[]{:S(2)}) %collective-permute-start.4) | collective-permute-done | bytes 8224 | tf_op jit(solution)/shard_map/ppermute | solution.py:580
  20.3 0.1 fusion
  20.4 1.5 %collective-permute-start.7 = (f32[16,32]{1,0:T(8,128)S(1)}, f32[16,32]{1,0:T(8,128)S(1)}, u32[]{:S(2)}, u32[]{:S(2)}) collective-permute-start(f32[16,32]{1,0:T(8,128)S(1)} %get-tuple-element.29), channel_id=1, source_target_pairs={{0,4},{4,0},{1,5},{5,1},{2,6},{6,2},{3,7},{7,3},{8,12},{12,8},{9,1... | collective-permute-start | bytes 6152 | tf_op jit(solution)/shard_map/ppermute | solution.py:580
  21.9 2.0 %collective-permute-start.6 = (f32[16,32]{1,0:T(8,128)S(1)}, f32[16,32]{1,0:T(8,128)S(1)}, u32[]{:S(2)}, u32[]{:S(2)}) collective-permute-start(f32[16,32]{1,0:T(8,128)S(1)} %get-tuple-element.30), channel_id=1, source_target_pairs={{0,28},{4,24},{8,4},{12,0},{16,12},{20,8},{24,20},{28,16},{1,29},{... | collective-permute-start | bytes 6152 | tf_op jit(solution)/shard_map/ppermute | solution.py:580
  23.9 0.5 %collective-permute-start.5 = (f32[16,32]{1,0:T(8,128)S(1)}, f32[16,32]{1,0:T(8,128)S(1)}, u32[]{:S(2)}, u32[]{:S(2)}) collective-permute-start(f32[16,32]{1,0:T(8,128)S(1)} %get-tuple-element.31), channel_id=1, source_target_pairs={{0,24},{8,0},{16,8},{24,16},{1,25},{9,1},{17,9},{25,17},{2,26},{10... | collective-permute-start | bytes 6152 | tf_op jit(solution)/shard_map/ppermute | solution.py:580
  24.3 0.0 collective-permute-done.7.refs_2_
  24.3 2.1 %collective-permute-done.6.refs_1_ = f32[16,32]{1,0:T(8,128)S(1)} collective-permute-done((f32[16,32]{1,0:T(8,128)S(1)}, f32[16,32]{1,0:T(8,128)S(1)}, u32[]{:S(2)}, u32[]{:S(2)}) %collective-permute-start.6) | collective-permute-done | bytes 2080 | tf_op jit(solution)/shard_map/ppermute | solution.py:580
  26.4 1.1 %collective-permute-done.5.refs_0_ = f32[16,32]{1,0:T(8,128)S(1)} collective-permute-done((f32[16,32]{1,0:T(8,128)S(1)}, f32[16,32]{1,0:T(8,128)S(1)}, u32[]{:S(2)}, u32[]{:S(2)}) %collective-permute-start.5) | collective-permute-done | bytes 2080 | tf_op jit(solution)/shard_map/ppermute | solution.py:580
  27.5 0.8 %write_outputs.1 = (f32[2,1,2,8]{3,2,1,0:T(2,128)}, f32[3,2,1,2,8]{4,3,2,1,0:T(2,128)}, f32[2,1,2,8,9]{4,3,2,1,0:T(8,128)}) custom-call(f32[16,128]{1,0:T(8,128)S(1)} %add.23.mine_ref, f32[1,32]{1,0:T(1,128)S(1)} %get-tuple-element.25.shift_row_ref, f32[16,32]{1,0:T(8,128)S(1)} %collective-permute-done.5.refs_0_, ...), custom_call_target="tpu_custom_call" | custom-call | tf_op jit(solution)/shard_map/write_outputs/pallas_call | solution.py:671
  (3 shorter events, 0.0 us)
Async XLA Ops:
  1.7 9.6 %collective-permute-start = (f32[48,128]{1,0:T(8,128)S(1)}, f32[48,128]{1,0:T(8,128)S(1)}, u32[]{:S(2)}, u32[]{:S(2)}) collective-permute-start(f32[48,128]{1,0:T(8,128)S(1)} %pack_payload.1.here_ref), channel_id=1, source_target_pairs={{0,8},{8,16},{16,24},{24,0},{1,9},{9,17},{17,25},{25,1},{2,10},{10... | collective-permute-start | bytes 73736 | tf_op jit(solution)/shard_map/ppermute | solution.py:580
  4.8 6.5 %collective-permute-start.2 = (f32[40,128]{1,0:T(8,128)S(1)}, f32[40,128]{1,0:T(8,128)S(1)}, u32[]{:S(2)}, u32[]{:S(2)}) collective-permute-start(f32[40,128]{1,0:T(8,128)S(1)} %slice.16), channel_id=1, source_target_pairs={{0,12},{4,8},{8,20},{12,16},{16,28},{20,24},{24,4},{28,0},{1,13},{... | collective-permute-start | bytes 61448 | tf_op jit(solution)/shard_map/ppermute | solution.py:580
  7.3 4.0 %collective-permute-start.1 = (f32[40,128]{1,0:T(8,128)S(1)}, f32[40,128]{1,0:T(8,128)S(1)}, u32[]{:S(2)}, u32[]{:S(2)}) collective-permute-start(f32[40,128]{1,0:T(8,128)S(1)} %slice.16), channel_id=1, source_target_pairs={{0,4},{4,0},{1,5},{5,1},{2,6},{6,2},{3,7},{7,3},{8,12},{12,8},{9,1... | collective-permute-start | bytes 61448 | tf_op jit(solution)/shard_map/ppermute | solution.py:580
  11.3 2.2 %collective-permute-start.3 = (f32[176,128]{1,0:T(8,128)S(1)}, f32[176,128]{1,0:T(8,128)S(1)}, u32[]{:S(2)}, u32[]{:S(2)}) collective-permute-start(f32[176,128]{1,0:T(8,128)S(1)} %pad_add_fusion), channel_id=1, source_target_pairs={{0,3},{1,0},{2,1},{3,2},{4,7},{5,4},{6,5},{7,6},{8,11},{9,8},{10,9... | collective-permute-start | bytes 270344 | tf_op jit(solution)/shard_map/ppermute | solution.py:580
  17.1 3.2 %collective-permute-start.4 = (f32[16,128]{1,0:T(8,128)S(1)}, f32[16,128]{1,0:T(8,128)S(1)}, u32[]{:S(2)}, u32[]{:S(2)}) collective-permute-start(f32[16,128]{1,0:T(8,128)S(1)} %get-tuple-element.24), channel_id=1, source_target_pairs={{0,1},{1,2},{2,3},{3,0},{4,5},{5,6},{6,7},{7,4},{8,9},{9,10},{10,1... | collective-permute-start | bytes 24584 | tf_op jit(solution)/shard_map/ppermute | solution.py:580
  20.4 3.9 %collective-permute-start.7 = (f32[16,32]{1,0:T(8,128)S(1)}, f32[16,32]{1,0:T(8,128)S(1)}, u32[]{:S(2)}, u32[]{:S(2)}) collective-permute-start(f32[16,32]{1,0:T(8,128)S(1)} %get-tuple-element.29), channel_id=1, source_target_pairs={{0,4},{4,0},{1,5},{5,1},{2,6},{6,2},{3,7},{7,3},{8,12},{12,8},{9,1... | collective-permute-start | bytes 6152 | tf_op jit(solution)/shard_map/ppermute | solution.py:580
  21.9 4.5 %collective-permute-start.6 = (f32[16,32]{1,0:T(8,128)S(1)}, f32[16,32]{1,0:T(8,128)S(1)}, u32[]{:S(2)}, u32[]{:S(2)}) collective-permute-start(f32[16,32]{1,0:T(8,128)S(1)} %get-tuple-element.30), channel_id=1, source_target_pairs={{0,28},{4,24},{8,4},{12,0},{16,12},{20,8},{24,20},{28,16},{1,29},{... | collective-permute-start | bytes 6152 | tf_op jit(solution)/shard_map/ppermute | solution.py:580
  23.9 3.7 %collective-permute-start.5 = (f32[16,32]{1,0:T(8,128)S(1)}, f32[16,32]{1,0:T(8,128)S(1)}, u32[]{:S(2)}, u32[]{:S(2)}) collective-permute-start(f32[16,32]{1,0:T(8,128)S(1)} %get-tuple-element.31), channel_id=1, source_target_pairs={{0,24},{8,0},{16,8},{24,16},{1,25},{9,1},{17,9},{25,17},{2,26},{10... | collective-permute-start | bytes 6152 | tf_op jit(solution)/shard_map/ppermute | solution.py:580

commit v13 on v12

--- a/solution.py
+++ b/solution.py
@@ -231,10 +231,14 @@
     height, width = here_ref.shape
     owned = OWN_CELLS * SITES
     short = owned + 8
-    pairs = owned * nbr
+    center_sides = 2 if kind == 2 else 1
+    kept_sides = 1 if kind == 2 else kind
+    own_pairs = owned * nbr
+    pairs = center_sides * own_pairs
+    centers = center_sides * owned
     radial = basis_weight_ref.shape[0]
     span = GROUP * nbr
-    groups = owned // GROUP
+    groups = centers // GROUP
     wide = GROUP * ORDERS
     sites = SITES
     root_count = math.sqrt(nbr)
@@ -245,7 +249,8 @@
     mains = [here_ref[...], last_x_ref[...], far[:height], far[height : 2 * height]]
     near_sides = [ref[...] for ref in near_side_refs]
     far_sides = far[2 * height :]
-    far_sides = [far_sides[i * short : (i + 1) * short] for i in range(2 * kind - 2)]
+    tall = far_sides.shape[0] // (2 * kind - 2)
+    far_sides = [far_sides[i * tall : (i + 1) * tall] for i in range(2 * kind - 2)]
     blocks_in = [
         [mains[0], *near_sides[0::2]],
         [mains[1], *near_sides[1::2]],
@@ -263,27 +268,33 @@
     tile_lane = lax.broadcasted_iota(jnp.int32, (kind * OWN_CELLS, 128), 1)
     for g, block in enumerate(blocks_in):
         behind_x, ahead_z = g % 2, g // 2
-        cell = behind_x * 2 + 1 - ahead_z
-        center_feats.append(block[0][cell * sites : (cell + 1) * sites])
         rows = jnp.concatenate([side[owned : owned + OWN_CELLS] for side in block], axis=0)
-        scales.append(rows[cell : cell + 1])
         corner_x = (cell_row // 2 + 2 - 2 * behind_x).astype(F32) * CELL_SIDE
         corner_z = (cell_row % 2 + 2 * ahead_z).astype(F32) * CELL_SIDE
         corner = jnp.where(
             tile_lane < sites, corner_x, jnp.where(tile_lane < 2 * sites, 0.0, corner_z)
         )
-        rows = rows + corner
-        coords.append(rows)
-        center_coords.append(rows[cell : cell + 1])
-        start = short + cell * span // 128
-        codes.extend(block[0][start + r : start + r + 1] for r in range(span // 128))
+        coords.append(rows + corner)
+    for c in range(center_sides):
+        for g, block in enumerate(blocks_in):
+            cell = g % 2 * 2 + 1 - g // 2
+            row = c * OWN_CELLS + cell
+            center_feats.append(block[c][cell * sites : (cell + 1) * sites])
+            scales.append(block[c][owned + cell : owned + cell + 1])
+            center_coords.append(coords[g][row : row + 1])
+            start = short + cell * span // 128
+            codes.extend(block[c][start + r : start + r + 1] for r in range(span // 128))
     center_feats = jnp.concatenate(center_feats, axis=0)
     coords = jnp.concatenate(coords, axis=0)
     code = jnp.concatenate(codes, axis=1).astype(jnp.int32)
     live = code > 0
     code = jnp.maximum(code - 1, 0)
     side_y = ((code >> 10) - 1).astype(F32)
-    near_row = jnp.where(live, code & 1023, known)
+    near_row = code & 1023
+    if center_sides == 2:
+        pair_lane = lax.broadcasted_iota(jnp.int32, (1, pairs), 1)
+        near_row = jnp.where(pair_lane < own_pairs, near_row, near_row ^ owned)
+    near_row = jnp.where(live, near_row, known)
 
     def place_rows(cell_rows):
         count = cell_rows.shape[0] * sites
@@ -301,7 +312,7 @@
     value_rows = stacked(*split(jnp.transpose(value_weight_ref[...])))
     latent_high_t, latent_low_t = split(jnp.transpose(latent_weight_ref[...]))
     latent_both_t = jnp.concatenate([latent_high_t, latent_low_t], axis=0)
-    latent_rows = stacked(*split(latent_weight_ref[...]))
+    latent_rows = stacked(*split(latent_weight_ref[...] * out_weight_ref[...]))
     value_high, value_low = split(value_weight_ref[...])
     value_both = jnp.concatenate([value_high, value_low], axis=0)
     basis_t = jnp.transpose(basis_weight_ref[...])
@@ -325,7 +336,7 @@
     )
     scale_rows = jnp.concatenate(scales, axis=0)
     scale_parts = jnp.concatenate(
-        [*split3(scale_rows), jnp.zeros((16 - 3 * groups, 128), BF16)], axis=0
+        [*split3(scale_rows), jnp.zeros((-3 * groups % 16, 128), BF16)], axis=0
     )
 
     level = lax.broadcasted_iota(jnp.int32, (ORDERS, width), 0)
@@ -343,7 +354,7 @@
     out_column = jnp.concatenate([out_column] * (pairs // width), axis=1)
 
     site_ids = lax.broadcasted_iota(jnp.int32, (known, pairs), 0)
-    slot_ids = lax.broadcasted_iota(jnp.int32, (owned, pairs), 0)
+    slot_ids = lax.broadcasted_iota(jnp.int32, (centers, pairs), 0)
     slot_row = lax.broadcasted_iota(jnp.int32, (1, pairs), 1) // nbr
     block_row = lax.broadcasted_iota(jnp.int32, (wide, span), 0) // ORDERS
     block_lane = lax.broadcasted_iota(jnp.int32, (wide, span), 1) // nbr
@@ -448,10 +459,12 @@
     )
     z_gate = 0.5 * jnp.tanh(0.5 * z) + 0.5
     update = z * z_gate
-    update_out = update * out_column
-    pair_energy = jnp.sum(latent * out_column + weight * update_out, axis=0, keepdims=True)
-    pair_energy = pair_energy * pull
-    d_z = (pull * weight) * out_column * (z_gate + update * (1.0 - z_gate))
+    update_sum = jnp.sum(update * out_column, axis=0, keepdims=True)
+    active_sum = jnp.sum(
+        active[:, :own_pairs] * out_column[:, :own_pairs], axis=0, keepdims=True
+    )
+    pair_energy = (active_sum + update_sum[:, :own_pairs]) * (pull * weight)[:, :own_pairs]
+    d_z = (pull * weight) * (z_gate + update * (1.0 - z_gate))
     spread_back = half_depth(latent_rows, d_z)
     d_scalars = spread_back[width:]
     d_values = d_scalars * inner
@@ -482,7 +495,7 @@
         + spread_back[:width]
         + pull * out_column
     )
-    d_weight = jnp.sum(d_latent * active + pull * update_out, axis=0, keepdims=True)
+    d_weight = jnp.sum(d_latent * active, axis=0, keepdims=True) + pull * update_sum
     d_before = d_latent * weight * (gate + active * (1.0 - gate))
     d_basis = half_depth(basis_rows, d_before)
 
@@ -506,18 +519,28 @@
     near_terms = jnp.concatenate(
         [-gx, -gy, -gz, *virial, jnp.zeros_like(gx), *rest], axis=0
     )
-    center_terms = jnp.concatenate([gx, gy, gz, *virial, pair_energy, *rest], axis=0)
-    near_sums = mm_nt(jnp.concatenate(split(near_terms), axis=0), pick_half)
-    center_sums = mm_nt(jnp.concatenate(split(center_terms), axis=0), slot_half)
+    center_rows = [gx, gy, gz, *virial]
+    center_rows = [r[:, :own_pairs] for r in center_rows] + [pair_energy]
+    center_rows.append(jnp.zeros((ORDERS - 13, own_pairs), F32))
+    center_terms = jnp.concatenate(center_rows, axis=0)
+    reach = pick_half
+    if kept_sides < kind:
+        step = kind * owned
+        reach = jnp.concatenate([pick_half[i : i + owned] for i in range(0, known, step)], axis=0)
+    near_sums = mm_nt(jnp.concatenate(split(near_terms), axis=0), reach)
+    center_sums = mm_nt(
+        jnp.concatenate(split(center_terms), axis=0), slot_half[:owned, :own_pairs]
+    )
     center_sums = jnp.concatenate(
         [folded(center_sums), jnp.zeros((ORDERS, 128 - owned), F32)], axis=1
     )
     totals = folded(near_sums)
     lane = lax.broadcasted_iota(jnp.int32, (ORDERS, 128), 1)
+    known = totals.shape[1]
     tiles = [totals[:, 128 * i : 128 * (i + 1)] for i in range(known // 128)]
-    for g in range(groups):
+    for g in range(owned // GROUP):
         cell = g % 2 * 2 + 1 - g // 2
-        target = g * kind * owned + cell * sites
+        target = g * kept_sides * owned + cell * sites
         turn = (target - g * GROUP) % 128
         piece = pltpu.roll(center_sums, turn, 1) if turn else center_sums
         begin = target % 128
@@ -634,14 +657,15 @@
         compiler_params=pltpu.CompilerParams(vmem_limit_bytes=8 * 1024 * 1024),
         name="fetch_weights",
     )(*in_hbm(species, listed, species_shift, *weights))
-    short = here[: owned + 8]
+    short = here if kind == 2 else here[: owned + 8]
     last_x = moved(here, {"gx": 1})
     sides = []
     for step in (-1, 1)[: kind - 1]:
         sides.append(moved(short, {"gx": 1, "gy": step}))
         sides.insert(-1, moved(short, {"gy": step}))
     next_z = moved(joined([here, last_x, *sides]), {"gz": -1})
-    half = 2 * kind * owned
+    kept = 1 if kind == 2 else kind
+    half = 2 * kept * owned
     keep, send = pl.pallas_call(
         functools.partial(force_kernel, kind, nbr),
         out_shape=(
@@ -650,7 +674,7 @@
         ),
         in_specs=[vmem] * (8 + 2 * kind),
         out_specs=(vmem, vmem),
-        compiler_params=pltpu.CompilerParams(vmem_limit_bytes=32 * 1024 * 1024),
+        compiler_params=pltpu.CompilerParams(vmem_limit_bytes=44 * 1024 * 1024),
         name="pair_forces",
     )(
         here,
@@ -664,9 +688,9 @@
     def part(index):
         return totals[:, index * owned : (index + 1) * owned]
 
-    back = [moved(part(kind), {"gx": -1})]
-    for i, step in enumerate((1, -1)[: kind - 1]):
-        back.append(moved(part(kind + 1 + i), {"gx": -1, "gy": step}))
+    back = [moved(part(kept), {"gx": -1})]
+    for i, step in enumerate((1, -1)[: kept - 1]):
+        back.append(moved(part(kept + 1 + i), {"gx": -1, "gy": step}))
         back.append(moved(part(1 + i), {"gy": step}))
     site_energy, forces, virial = pl.pallas_call(
         finish_kernel,

time: 28.6 us -> 27.7 us (0.969)
  starting transfers between devices: 11.9 us -> 8.24 us
  Pallas kernels: 6.76 us -> 8.8 us
  waiting for transfers between devices: 8.89 us -> 9.66 us
    ppermute x8 -> x6, starting transfers between devices: 11.9 us -> 8.24 us  [moved(): return lax.ppermute(array, names, route)]
    pallas_call x1, Pallas kernels: 3.58 us -> 5.62 us  [local(): pl.pallas_call(functools.partial(force_kernel, kind, nbr), out_shape=(jax...]
    ppermute x8 -> x6, waiting for transfers between devices: 8.89 us -> 9.66 us  [moved(): return lax.ppermute(array, names, route)]
  transfers between devices with their start and end apart: 8 -> 6, of which waited for: 5 -> 6; matrix products, arithmetic and copies ran while one was open for 0% -> 0% of each run, Pallas kernels for 5% -> 5%
where the time goes in v13:
time: 27.7 us; the launch traced here: 27.4 us
  waiting for transfers between devices  9.66 us (35%)
  Pallas kernels  8.8 us (32%)
  starting transfers between devices  8.24 us (30%)
  between operations  0.67 us (2%)
    ppermute x6, waiting for transfers between devices, moved(): return lax.ppermute(array, names, route)  9.66 us
    ppermute x6, starting transfers between devices, moved(): return lax.ppermute(array, names, route)  8.24 us
    pallas_call x1, Pallas kernels, local(): pl.pallas_call(functools.partial(force_kernel, kind, nbr), out_shape=(jax...  5.62 us
    pallas_call x1, Pallas kernels, local(): pl.pallas_call(fetch_kernel, out_shape=(*(jax.ShapeDtypeStruct(w.shape, F...  1.35 us
    pallas_call x1, Pallas kernels, local(): pl.pallas_call(functools.partial(pack_kernel, kind), out_shape=jax.ShapeD...  1.08 us
    pallas_call x1, Pallas kernels, local(): pl.pallas_call(finish_kernel, out_shape=(jax.ShapeDtypeStruct(species.sha...  0.75 us
  transfers between devices with their start and end apart: 6, of which 6 were waited for; matrix products, arithmetic and copies ran while one was open for 0% of the time, Pallas kernels for 5%

profile of v13, /device:TPU:0, one launch (start us, length us, event | category | flops | bytes accessed | tf_op | source)
XLA Modules:
  0.0 27.4 jit_solution(15448751707438719627)
XLA Ops:
  0.6 1.1 %pack_payload.1.here_ref = f32[48,128]{1,0:T(8,128)S(1)} custom-call(f32[3,2,1,2,8]{4,3,2,1,0:T(2,128)} %positions_hbm.1, f32[32,128]{1,0:T(8,128)} %bitcast.4, s32[2,1,2,8]{3,2,1,0:T(2,128)} %species_hbm.3, s32[1,32]{1,0:T(1,128)} %bitcast.5, s32[32,32]{1,0:T(8,128)} %neighbours_hbm.1, f32[5]{0:T(128)} %scale_hbm.1), custom_call_target="tpu_custom_call" | custom-call | tf_op jit(solution)/shard_map/pack_payload/pallas_call | solution.py:608
  1.7 4.0 %collective-permute-start.2 = (f32[48,128]{1,0:T(8,128)S(1)}, f32[48,128]{1,0:T(8,128)S(1)}, u32[]{:S(2)}, u32[]{:S(2)}) collective-permute-start(f32[48,128]{1,0:T(8,128)S(1)} %pack_payload.1.here_ref), channel_id=1, source_target_pairs={{0,12},{4,8},{8,20},{12,16},{16,28},{20,24},{24,4},{28,0},{1,13},{... | collective-permute-start | bytes 73736 | tf_op jit(solution)/shard_map/ppermute | solution.py:603
  5.7 0.5 %collective-permute-start.1 = (f32[48,128]{1,0:T(8,128)S(1)}, f32[48,128]{1,0:T(8,128)S(1)}, u32[]{:S(2)}, u32[]{:S(2)}) collective-permute-start(f32[48,128]{1,0:T(8,128)S(1)} %pack_payload.1.here_ref), channel_id=1, source_target_pairs={{0,4},{4,0},{1,5},{5,1},{2,6},{6,2},{3,7},{7,3},{8,12},{12,8},{9,1... | collective-permute-start | bytes 73736 | tf_op jit(solution)/shard_map/ppermute | solution.py:603
  6.3 1.6 %collective-permute-start = (f32[48,128]{1,0:T(8,128)S(1)}, f32[48,128]{1,0:T(8,128)S(1)}, u32[]{:S(2)}, u32[]{:S(2)}) collective-permute-start(f32[48,128]{1,0:T(8,128)S(1)} %pack_payload.1.here_ref), channel_id=1, source_target_pairs={{0,8},{8,16},{16,24},{24,0},{1,9},{9,17},{17,25},{25,1},{2,10},{10... | collective-permute-start | bytes 73736 | tf_op jit(solution)/shard_map/ppermute | solution.py:603
  7.8 1.8 %collective-permute-done.2.refs_1_ = f32[48,128]{1,0:T(8,128)S(1)} collective-permute-done((f32[48,128]{1,0:T(8,128)S(1)}, f32[48,128]{1,0:T(8,128)S(1)}, u32[]{:S(2)}, u32[]{:S(2)}) %collective-permute-start.2) | collective-permute-done | bytes 24608 | tf_op jit(solution)/shard_map/ppermute | solution.py:603
  9.7 0.2 collective-permute-done.1.refs_0_
  9.8 2.1 %collective-permute-done.last_x_ref = f32[48,128]{1,0:T(8,128)S(1)} collective-permute-done((f32[48,128]{1,0:T(8,128)S(1)}, f32[48,128]{1,0:T(8,128)S(1)}, u32[]{:S(2)}, u32[]{:S(2)}) %collective-permute-start) | collective-permute-done | bytes 24608 | tf_op jit(solution)/shard_map/ppermute | solution.py:603
  11.9 0.1 collective-permute-start.3
  12.0 1.3 %fetch_weights.1 = (f32[128,128]{1,0:T(8,128)S(1)}, f32[128,128]{1,0:T(8,128)S(1)}, f32[8,128]{1,0:T(8,128)S(1)}, f32[3,128]{1,0:T(4,128)S(1)}, f32[128,256]{1,0...) custom-call(s32[2,1,2,8]{3,2,1,0:T(2,128)} %species_hbm.3, s32[1,32]{1,0:T(1,128)} %bitcast.6, ...), custom_call_target="tpu_custom_call" | custom-call | tf_op jit(solution)/shard_map/fetch_weights/pallas_call | solution.py:643
  13.3 0.9 %collective-permute-done.3.refs_2_ = f32[192,128]{1,0:T(8,128)S(1)} collective-permute-done((f32[192,128]{1,0:T(8,128)S(1)}, f32[192,128]{1,0:T(8,128)S(1)}, u32[]{:S(2)}, u32[]{:S(2)}) %collective-permute-start.3) | collective-permute-done | bytes 98336 | tf_op jit(solution)/shard_map/ppermute | solution.py:603
  14.2 5.6 %pair_forces.1 = (f32[16,64]{1,0:T(8,128)S(1)}, f32[16,64]{1,0:T(8,128)S(1)}) custom-call(f32[48,128]{1,0:T(8,128)S(1)} %pack_payload.1.here_ref, f32[48,128]{1,0:T(8,128)S(1)} %collective-permute-done.last_x_ref, f32[48,128]{1,0:T(8,128)S(1)} %collective-permute-done.1.refs_0_, f32[48,128]{1,0:T(8,128)S(1)} %collective-permute-done.2.refs_1_, ...), custom_call_target="tpu_custom_call" | custom-call | tf_op jit(solution)/shard_map/pair_forces/pallas_call | solution.py:669
  19.8 1.7 %collective-permute-start.4 = (f32[16,64]{1,0:T(8,128)S(1)}, f32[16,64]{1,0:T(8,128)S(1)}, u32[]{:S(2)}, u32[]{:S(2)}) collective-permute-start(f32[16,64]{1,0:T(8,128)S(1)} %get-tuple-element.24), channel_id=1, source_target_pairs={{0,1},{1,2},{2,3},{3,0},{4,5},{5,6},{6,7},{7,4},{8,9},{9,10},{10,1... | collective-permute-start | bytes 12296 | tf_op jit(solution)/shard_map/ppermute | solution.py:603
  21.5 1.4 %collective-permute-done.4 = f32[16,64]{1,0:T(8,128)S(1)} collective-permute-done((f32[16,64]{1,0:T(8,128)S(1)}, f32[16,64]{1,0:T(8,128)S(1)}, u32[]{:S(2)}, u32[]{:S(2)}) %collective-permute-start.4) | collective-permute-done | bytes 4128 | tf_op jit(solution)/shard_map/ppermute | solution.py:603
  23.0 0.1 slice.4
  23.0 0.3 %collective-permute-start.5 = (f32[16,32]{1,0:T(8,128)S(1)}, f32[16,32]{1,0:T(8,128)S(1)}, u32[]{:S(2)}, u32[]{:S(2)}) collective-permute-start(f32[16,32]{1,0:T(8,128)S(1)} %slice.4), channel_id=1, source_target_pairs={{0,24},{8,0},{16,8},{24,16},{1,25},{9,1},{17,9},{25,17},{2,26},{10... | collective-permute-start | bytes 6152 | tf_op jit(solution)/shard_map/ppermute | solution.py:603
  23.4 3.3 %collective-permute-done.5.refs_0_ = f32[16,32]{1,0:T(8,128)S(1)} collective-permute-done((f32[16,32]{1,0:T(8,128)S(1)}, f32[16,32]{1,0:T(8,128)S(1)}, u32[]{:S(2)}, u32[]{:S(2)}) %collective-permute-start.5) | collective-permute-done | bytes 2080 | tf_op jit(solution)/shard_map/ppermute | solution.py:603
  26.7 0.8 %write_outputs.1 = (f32[2,1,2,8]{3,2,1,0:T(2,128)}, f32[3,2,1,2,8]{4,3,2,1,0:T(2,128)}, f32[2,1,2,8,9]{4,3,2,1,0:T(8,128)}) custom-call(f32[16,64]{1,0:T(8,128)S(1)} %add.23.mine_ref, f32[1,32]{1,0:T(1,128)S(1)} %get-tuple-element.25.shift_row_ref, f32[16,32]{1,0:T(8,128)S(1)} %collective-permute-done.5.refs_0_), custom_call_target="tpu_custom_call" | custom-call | tf_op jit(solution)/shard_map/write_outputs/pallas_call | solution.py:695
  (2 shorter events, 0.0 us)
Async XLA Ops:
  1.7 7.9 %collective-permute-start.2 = (f32[48,128]{1,0:T(8,128)S(1)}, f32[48,128]{1,0:T(8,128)S(1)}, u32[]{:S(2)}, u32[]{:S(2)}) collective-permute-start(f32[48,128]{1,0:T(8,128)S(1)} %pack_payload.1.here_ref), channel_id=1, source_target_pairs={{0,12},{4,8},{8,20},{12,16},{16,28},{20,24},{24,4},{28,0},{1,13},{... | collective-permute-start | bytes 73736 | tf_op jit(solution)/shard_map/ppermute | solution.py:603
  5.7 4.1 %collective-permute-start.1 = (f32[48,128]{1,0:T(8,128)S(1)}, f32[48,128]{1,0:T(8,128)S(1)}, u32[]{:S(2)}, u32[]{:S(2)}) collective-permute-start(f32[48,128]{1,0:T(8,128)S(1)} %pack_payload.1.here_ref), channel_id=1, source_target_pairs={{0,4},{4,0},{1,5},{5,1},{2,6},{6,2},{3,7},{7,3},{8,12},{12,8},{9,1... | collective-permute-start | bytes 73736 | tf_op jit(solution)/shard_map/ppermute | solution.py:603
  6.3 5.6 %collective-permute-start = (f32[48,128]{1,0:T(8,128)S(1)}, f32[48,128]{1,0:T(8,128)S(1)}, u32[]{:S(2)}, u32[]{:S(2)}) collective-permute-start(f32[48,128]{1,0:T(8,128)S(1)} %pack_payload.1.here_ref), channel_id=1, source_target_pairs={{0,8},{8,16},{16,24},{24,0},{1,9},{9,17},{17,25},{25,1},{2,10},{10... | collective-permute-start | bytes 73736 | tf_op jit(solution)/shard_map/ppermute | solution.py:603
  11.9 2.3 %collective-permute-start.3 = (f32[192,128]{1,0:T(8,128)S(1)}, f32[192,128]{1,0:T(8,128)S(1)}, u32[]{:S(2)}, u32[]{:S(2)}) collective-permute-start(f32[192,128]{1,0:T(8,128)S(1)} %pad_add_fusion), channel_id=1, source_target_pairs={{0,3},{1,0},{2,1},{3,2},{4,7},{5,4},{6,5},{7,6},{8,11},{9,8},{10,9... | collective-permute-start | bytes 294920 | tf_op jit(solution)/shard_map/ppermute | solution.py:603
  19.8 3.2 %collective-permute-start.4 = (f32[16,64]{1,0:T(8,128)S(1)}, f32[16,64]{1,0:T(8,128)S(1)}, u32[]{:S(2)}, u32[]{:S(2)}) collective-permute-start(f32[16,64]{1,0:T(8,128)S(1)} %get-tuple-element.24), channel_id=1, source_target_pairs={{0,1},{1,2},{2,3},{3,0},{4,5},{5,6},{6,7},{7,4},{8,9},{9,10},{10,1... | collective-permute-start | bytes 12296 | tf_op jit(solution)/shard_map/ppermute | solution.py:603
  23.0 3.7 %collective-permute-start.5 = (f32[16,32]{1,0:T(8,128)S(1)}, f32[16,32]{1,0:T(8,128)S(1)}, u32[]{:S(2)}, u32[]{:S(2)}) collective-permute-start(f32[16,32]{1,0:T(8,128)S(1)} %slice.4), channel_id=1, source_target_pairs={{0,24},{8,0},{16,8},{24,16},{1,25},{9,1},{17,9},{25,17},{2,26},{10... | collective-permute-start | bytes 6152 | tf_op jit(solution)/shard_map/ppermute | solution.py:603

commit v14 on v13

--- a/solution.py
+++ b/solution.py
@@ -97,7 +97,8 @@
     centers_hbm,
     neighbours_hbm,
     scale_hbm,
-    payload_ref,
+    low_ref,
+    high_ref,
     wide_ref,
     positions_ref,
     species_ref,
@@ -109,7 +110,7 @@
     owned, nbr = neighbours_ref.shape
     per_row = 128 // nbr
     pairs_in = (
-        (features_hbm, payload_ref.at[pl.ds(0, owned), :]),
+        (features_hbm, low_ref.at[pl.ds(0, owned), :]),
         (neighbours_hbm, neighbours_ref),
         (centers_hbm, centers_ref),
         (positions_hbm, positions_ref),
@@ -124,7 +125,6 @@
         copy.start()
     for copy in copies:
         copy.wait()
-    payload_ref[owned : owned + 8] = jnp.zeros((8, 128), F32)
     for cell in range(OWN_CELLS):
         x, z = cell // 2, cell % 2
         species = species_ref[x, 0, z : z + 1, :]
@@ -134,7 +134,7 @@
         row = lane_row(scale, 3 * SITES)
         for c in range(3):
             row = row + lane_row(positions_ref[c, x, 0, z : z + 1, :], c * SITES)
-        payload_ref[owned + cell : owned + cell + 1] = row
+        low_ref[owned + cell : owned + cell + 1] = row
 
     chosen = lax.broadcasted_iota(jnp.int32, (owned, owned), 0) == centers_ref[...]
     chosen = jnp.where(chosen, 1.0, 0.0)
@@ -163,7 +163,10 @@
     for j in range(1, per_row):
         more = wide_ref[pl.ds(j, owned // per_row, stride=per_row), :]
         codes = codes + pltpu.roll(more, j * nbr, 1)
-    payload_ref[owned + 8 :] = codes
+    tile = owned + OWN_CELLS
+    low_ref[tile:] = codes[: codes.shape[0] // 2]
+    high_ref[:tile] = low_ref[:tile]
+    high_ref[tile:] = codes[codes.shape[0] // 2 :]
 
 
 def fetch_kernel(species_hbm, centers_hbm, shift_hbm, *refs):
@@ -230,7 +233,6 @@
     ) = refs[2 * kind - 2 :]
     height, width = here_ref.shape
     owned = OWN_CELLS * SITES
-    short = owned + 8
     center_sides = 2 if kind == 2 else 1
     kept_sides = 1 if kind == 2 else kind
     own_pairs = owned * nbr
@@ -249,8 +251,7 @@
     mains = [here_ref[...], last_x_ref[...], far[:height], far[height : 2 * height]]
     near_sides = [ref[...] for ref in near_side_refs]
     far_sides = far[2 * height :]
-    tall = far_sides.shape[0] // (2 * kind - 2)
-    far_sides = [far_sides[i * tall : (i + 1) * tall] for i in range(2 * kind - 2)]
+    far_sides = [far_sides[i * height : (i + 1) * height] for i in range(2 * kind - 2)]
     blocks_in = [
         [mains[0], *near_sides[0::2]],
         [mains[1], *near_sides[1::2]],
@@ -282,7 +283,7 @@
             center_feats.append(block[c][cell * sites : (cell + 1) * sites])
             scales.append(block[c][owned + cell : owned + cell + 1])
             center_coords.append(coords[g][row : row + 1])
-            start = short + cell * span // 128
+            start = owned + OWN_CELLS + (1 - g // 2) * span // 128
             codes.extend(block[c][start + r : start + r + 1] for r in range(span // 128))
     center_feats = jnp.concatenate(center_feats, axis=0)
     coords = jnp.concatenate(coords, axis=0)
@@ -310,13 +311,13 @@
     center_parts = place_rows(jnp.concatenate(center_coords, axis=0))
 
     value_rows = stacked(*split(jnp.transpose(value_weight_ref[...])))
-    latent_high_t, latent_low_t = split(jnp.transpose(latent_weight_ref[...]))
+    latent_high_t, latent_low_t = split(0.5 * jnp.transpose(latent_weight_ref[...]))
     latent_both_t = jnp.concatenate([latent_high_t, latent_low_t], axis=0)
     latent_rows = stacked(*split(latent_weight_ref[...] * out_weight_ref[...]))
     value_high, value_low = split(value_weight_ref[...])
     value_both = jnp.concatenate([value_high, value_low], axis=0)
     basis_t = jnp.transpose(basis_weight_ref[...])
-    basis_high_t, basis_low_t = split(basis_t)
+    basis_high_t, basis_low_t = split(0.5 * basis_t)
     basis_rows = stacked(*split(basis_weight_ref[...]))
 
     def project(weight, rows):
@@ -325,8 +326,8 @@
 
     near_t = project(near_weight_ref[...], feats)
     own_t = project(center_weight_ref[...], center_feats)
-    near_high, near_low = split(near_t)
-    own_high, own_low = split(own_t)
+    near_high, near_low = split(0.5 * near_t)
+    own_high, own_low = split(0.5 * own_t)
     lookup = jnp.concatenate(
         [
             jnp.concatenate([near_high, own_high, basis_high_t, basis_high_t], axis=1),
@@ -428,7 +429,7 @@
     before = folded(
         mm(lookup, jnp.concatenate([pick_half, slot_half, basis_high, basis_low], axis=0))
     )
-    gate = 0.5 * jnp.tanh(0.5 * before) + 0.5
+    gate = 1.0 + jnp.tanh(before)
     active = before * gate
     latent = weight * active
     latent_high, latent_low = split(latent)
@@ -457,14 +458,14 @@
         jnp.concatenate([latent_high, scalars_high], axis=0),
         jnp.concatenate([latent_low, scalars_low], axis=0),
     )
-    z_gate = 0.5 * jnp.tanh(0.5 * z) + 0.5
+    z_gate = 1.0 + jnp.tanh(z)
     update = z * z_gate
     update_sum = jnp.sum(update * out_column, axis=0, keepdims=True)
     active_sum = jnp.sum(
         active[:, :own_pairs] * out_column[:, :own_pairs], axis=0, keepdims=True
     )
     pair_energy = (active_sum + update_sum[:, :own_pairs]) * (pull * weight)[:, :own_pairs]
-    d_z = (pull * weight) * (z_gate + update * (1.0 - z_gate))
+    d_z = (0.5 * pull * weight) * (z_gate + update * (2.0 - z_gate))
     spread_back = half_depth(latent_rows, d_z)
     d_scalars = spread_back[width:]
     d_values = d_scalars * inner
@@ -496,8 +497,8 @@
         + pull * out_column
     )
     d_weight = jnp.sum(d_latent * active, axis=0, keepdims=True) + pull * update_sum
-    d_before = d_latent * weight * (gate + active * (1.0 - gate))
-    d_basis = half_depth(basis_rows, d_before)
+    d_before = d_latent * (gate + active * (2.0 - gate))
+    d_basis = half_depth(basis_rows, d_before) * (0.5 * weight)
 
     d_length = jnp.sum(d_basis * basis_slope, axis=0, keepdims=True) + d_weight * slope * (
         1.0 / CUTOFF
@@ -605,11 +606,12 @@
     vmem = pl.BlockSpec(memory_space=pltpu.VMEM)
     hbm = pl.BlockSpec(memory_space=pltpu.HBM)
     listed = centers.reshape(1, owned)
-    here = pl.pallas_call(
+    payload = jax.ShapeDtypeStruct((owned + OWN_CELLS + pairs // 256, width), F32)
+    low, high = pl.pallas_call(
         functools.partial(pack_kernel, kind),
-        out_shape=jax.ShapeDtypeStruct((owned + 8 + pairs // 128, width), F32),
+        out_shape=(payload, payload),
         in_specs=[hbm] * 6,
-        out_specs=vmem,
+        out_specs=(vmem, vmem),
         scratch_shapes=[
             pltpu.VMEM((owned, 128), F32),
             pltpu.VMEM(positions.shape, F32),
@@ -657,13 +659,12 @@
         compiler_params=pltpu.CompilerParams(vmem_limit_bytes=8 * 1024 * 1024),
         name="fetch_weights",
     )(*in_hbm(species, listed, species_shift, *weights))
-    short = here if kind == 2 else here[: owned + 8]
-    last_x = moved(here, {"gx": 1})
+    last_x = moved(high, {"gx": 1})
     sides = []
     for step in (-1, 1)[: kind - 1]:
-        sides.append(moved(short, {"gx": 1, "gy": step}))
-        sides.insert(-1, moved(short, {"gy": step}))
-    next_z = moved(joined([here, last_x, *sides]), {"gz": -1})
+        sides.append(moved(high, {"gx": 1, "gy": step}))
+        sides.insert(-1, moved(low, {"gy": step}))
+    next_z = moved(joined([low, last_x, *sides]), {"gz": -1})
     kept = 1 if kind == 2 else kind
     half = 2 * kept * owned
     keep, send = pl.pallas_call(
@@ -677,7 +678,7 @@
         compiler_params=pltpu.CompilerParams(vmem_limit_bytes=44 * 1024 * 1024),
         name="pair_forces",
     )(
-        here,
+        low,
         last_x,
         *sides,
         next_z,

time: 27.7 us -> 27 us (0.975)
  waiting for transfers between devices: 9.66 us -> 7.3 us
  starting transfers between devices: 8.24 us -> 9.85 us
    ppermute x6, waiting for transfers between devices: 9.66 us -> 7.3 us  [moved(): return lax.ppermute(array, names, route)]
    ppermute x6, starting transfers between devices: 8.24 us -> 9.85 us  [moved(): return lax.ppermute(array, names, route)]
  transfers between devices with their start and end apart: 6 -> 6, of which waited for: 6 -> 5; matrix products, arithmetic and copies ran while one was open for 0% -> 0% of each run, Pallas kernels for 5% -> 5%
where the time goes in v14:
time: 27 us; the launch traced here: 26.7 us
  starting transfers between devices  9.85 us (36%)
  Pallas kernels  8.84 us (33%)
  waiting for transfers between devices  7.3 us (27%)
  between operations  0.67 us (2%)
    ppermute x6, starting transfers between devices, moved(): return lax.ppermute(array, names, route)  9.85 us
    ppermute x6, waiting for transfers between devices, moved(): return lax.ppermute(array, names, route)  7.3 us
    pallas_call x1, Pallas kernels, local(): pl.pallas_call(functools.partial(force_kernel, kind, nbr), out_shape=(jax...  5.66 us
    pallas_call x1, Pallas kernels, local(): pl.pallas_call(fetch_kernel, out_shape=(*(jax.ShapeDtypeStruct(w.shape, F...  1.35 us
    pallas_call x1, Pallas kernels, local(): pl.pallas_call(functools.partial(pack_kernel, kind), out_shape=(payload,...  1.08 us
    pallas_call x1, Pallas kernels, local(): pl.pallas_call(finish_kernel, out_shape=(jax.ShapeDtypeStruct(species.sha...  0.75 us
  transfers between devices with their start and end apart: 6, of which 5 were waited for; matrix products, arithmetic and copies ran while one was open for 0% of the time, Pallas kernels for 5%

profile of v14, /device:TPU:0, one launch (start us, length us, event | category | flops | bytes accessed | tf_op | source)
XLA Modules:
  0.0 26.7 jit_solution(12111123931906634065)
XLA Ops:
  0.6 1.1 %pack_payload.1 = (f32[40,128]{1,0:T(8,128)S(1)}, f32[40,128]{1,0:T(8,128)S(1)}) custom-call(f32[3,2,1,2,8]{4,3,2,1,0:T(2,128)} %positions_hbm.1, f32[32,128]{1,0:T(8,128)} %bitcast.4, s32[2,1,2,8]{3,2,1,0:T(2,128)} %species_hbm.3, s32[1,32]{1,0:T(1,128)} %bitcast.5, s32[32,32]{1,0:T(8,128)} %neighbours_hbm.1, f32[5]{0:T(128)} %scale_hbm.1), custom_call_target="tpu_custom_call" | custom-call | tf_op jit(solution)/shard_map/pack_payload/pallas_call | solution.py:610
  1.7 4.0 %collective-permute-start.2 = (f32[40,128]{1,0:T(8,128)S(1)}, f32[40,128]{1,0:T(8,128)S(1)}, u32[]{:S(2)}, u32[]{:S(2)}) collective-permute-start(f32[40,128]{1,0:T(8,128)S(1)} %get-tuple-element.19), channel_id=1, source_target_pairs={{0,12},{4,8},{8,20},{12,16},{16,28},{20,24},{24,4},{28,0},{1,13},{... | collective-permute-start | bytes 61448 | tf_op jit(solution)/shard_map/ppermute | solution.py:604
  5.7 1.6 %collective-permute-start = (f32[40,128]{1,0:T(8,128)S(1)}, f32[40,128]{1,0:T(8,128)S(1)}, u32[]{:S(2)}, u32[]{:S(2)}) collective-permute-start(f32[40,128]{1,0:T(8,128)S(1)} %get-tuple-element.19), channel_id=1, source_target_pairs={{0,8},{8,16},{16,24},{24,0},{1,9},{9,17},{17,25},{25,1},{2,10},{10... | collective-permute-start | bytes 61448 | tf_op jit(solution)/shard_map/ppermute | solution.py:604
  7.3 0.5 %collective-permute-start.1 = (f32[40,128]{1,0:T(8,128)S(1)}, f32[40,128]{1,0:T(8,128)S(1)}, u32[]{:S(2)}, u32[]{:S(2)}) collective-permute-start(f32[40,128]{1,0:T(8,128)S(1)} %get-tuple-element.18.here_ref), channel_id=1, source_target_pairs={{0,4},{4,0},{1,5},{5,1},{2,6},{6,2},{3,7},{7,3},{8,12},{12,8},{9,1... | collective-permute-start | bytes 61448 | tf_op jit(solution)/shard_map/ppermute | solution.py:604
  7.8 1.8 %collective-permute-done.2.refs_1_ = f32[40,128]{1,0:T(8,128)S(1)} collective-permute-done((f32[40,128]{1,0:T(8,128)S(1)}, f32[40,128]{1,0:T(8,128)S(1)}, u32[]{:S(2)}, u32[]{:S(2)}) %collective-permute-start.2) | collective-permute-done | bytes 20512 | tf_op jit(solution)/shard_map/ppermute | solution.py:604
  9.6 1.7 %collective-permute-done.last_x_ref = f32[40,128]{1,0:T(8,128)S(1)} collective-permute-done((f32[40,128]{1,0:T(8,128)S(1)}, f32[40,128]{1,0:T(8,128)S(1)}, u32[]{:S(2)}, u32[]{:S(2)}) %collective-permute-start) | collective-permute-done | bytes 20512 | tf_op jit(solution)/shard_map/ppermute | solution.py:604
  11.3 0.0 collective-permute-done.1.refs_0_
  11.3 0.1 collective-permute-start.3
  11.4 1.3 %fetch_weights.1 = (f32[128,128]{1,0:T(8,128)S(1)}, f32[128,128]{1,0:T(8,128)S(1)}, f32[8,128]{1,0:T(8,128)S(1)}, f32[3,128]{1,0:T(4,128)S(1)}, f32[128,256]{1,0...) custom-call(s32[2,1,2,8]{3,2,1,0:T(2,128)} %species_hbm.3, s32[1,32]{1,0:T(1,128)} %bitcast.6, ...), custom_call_target="tpu_custom_call" | custom-call | tf_op jit(solution)/shard_map/fetch_weights/pallas_call | solution.py:645
  12.7 0.7 %collective-permute-done.3.refs_2_ = f32[160,128]{1,0:T(8,128)S(1)} collective-permute-done((f32[160,128]{1,0:T(8,128)S(1)}, f32[160,128]{1,0:T(8,128)S(1)}, u32[]{:S(2)}, u32[]{:S(2)}) %collective-permute-start.3) | collective-permute-done | bytes 81952 | tf_op jit(solution)/shard_map/ppermute | solution.py:604
  13.4 5.7 %pair_forces.1 = (f32[16,64]{1,0:T(8,128)S(1)}, f32[16,64]{1,0:T(8,128)S(1)}) custom-call(f32[40,128]{1,0:T(8,128)S(1)} %get-tuple-element.18.here_ref, f32[40,128]{1,0:T(8,128)S(1)} %collective-permute-done.last_x_ref, f32[40,128]{1,0:T(8,128)S(1)} %collective-permute-done.1.refs_0_, f32[40,128]{1,0:T(8,128)S(1)} %collective-permute-done.2.refs_1_, ...), custom_call_target="tpu_custom_call" | custom-call | tf_op jit(solution)/shard_map/pair_forces/pallas_call | solution.py:670
  19.1 1.7 %collective-permute-start.4 = (f32[16,64]{1,0:T(8,128)S(1)}, f32[16,64]{1,0:T(8,128)S(1)}, u32[]{:S(2)}, u32[]{:S(2)}) collective-permute-start(f32[16,64]{1,0:T(8,128)S(1)} %get-tuple-element.28), channel_id=1, source_target_pairs={{0,1},{1,2},{2,3},{3,0},{4,5},{5,6},{6,7},{7,4},{8,9},{9,10},{10,1... | collective-permute-start | bytes 12296 | tf_op jit(solution)/shard_map/ppermute | solution.py:604
  20.8 1.4 %collective-permute-done.4 = f32[16,64]{1,0:T(8,128)S(1)} collective-permute-done((f32[16,64]{1,0:T(8,128)S(1)}, f32[16,64]{1,0:T(8,128)S(1)}, u32[]{:S(2)}, u32[]{:S(2)}) %collective-permute-start.4) | collective-permute-done | bytes 4128 | tf_op jit(solution)/shard_map/ppermute | solution.py:604
  22.3 0.1 slice.4
  22.3 2.0 %collective-permute-start.5 = (f32[16,32]{1,0:T(8,128)S(1)}, f32[16,32]{1,0:T(8,128)S(1)}, u32[]{:S(2)}, u32[]{:S(2)}) collective-permute-start(f32[16,32]{1,0:T(8,128)S(1)} %slice.4), channel_id=1, source_target_pairs={{0,24},{8,0},{16,8},{24,16},{1,25},{9,1},{17,9},{25,17},{2,26},{10... | collective-permute-start | bytes 6152 | tf_op jit(solution)/shard_map/ppermute | solution.py:604
  24.3 1.7 %collective-permute-done.5.refs_0_ = f32[16,32]{1,0:T(8,128)S(1)} collective-permute-done((f32[16,32]{1,0:T(8,128)S(1)}, f32[16,32]{1,0:T(8,128)S(1)}, u32[]{:S(2)}, u32[]{:S(2)}) %collective-permute-start.5) | collective-permute-done | bytes 2080 | tf_op jit(solution)/shard_map/ppermute | solution.py:604
  26.0 0.8 %write_outputs.1 = (f32[2,1,2,8]{3,2,1,0:T(2,128)}, f32[3,2,1,2,8]{4,3,2,1,0:T(2,128)}, f32[2,1,2,8,9]{4,3,2,1,0:T(8,128)}) custom-call(f32[16,64]{1,0:T(8,128)S(1)} %add.23.mine_ref, f32[1,32]{1,0:T(1,128)S(1)} %get-tuple-element.29.shift_row_ref, f32[16,32]{1,0:T(8,128)S(1)} %collective-permute-done.5.refs_0_), custom_call_target="tpu_custom_call" | custom-call | tf_op jit(solution)/shard_map/write_outputs/pallas_call | solution.py:696
  (2 shorter events, 0.0 us)
Async XLA Ops:
  1.7 7.9 %collective-permute-start.2 = (f32[40,128]{1,0:T(8,128)S(1)}, f32[40,128]{1,0:T(8,128)S(1)}, u32[]{:S(2)}, u32[]{:S(2)}) collective-permute-start(f32[40,128]{1,0:T(8,128)S(1)} %get-tuple-element.19), channel_id=1, source_target_pairs={{0,12},{4,8},{8,20},{12,16},{16,28},{20,24},{24,4},{28,0},{1,13},{... | collective-permute-start | bytes 61448 | tf_op jit(solution)/shard_map/ppermute | solution.py:604
  5.7 5.6 %collective-permute-start = (f32[40,128]{1,0:T(8,128)S(1)}, f32[40,128]{1,0:T(8,128)S(1)}, u32[]{:S(2)}, u32[]{:S(2)}) collective-permute-start(f32[40,128]{1,0:T(8,128)S(1)} %get-tuple-element.19), channel_id=1, source_target_pairs={{0,8},{8,16},{16,24},{24,0},{1,9},{9,17},{17,25},{25,1},{2,10},{10... | collective-permute-start | bytes 61448 | tf_op jit(solution)/shard_map/ppermute | solution.py:604
  7.3 4.0 %collective-permute-start.1 = (f32[40,128]{1,0:T(8,128)S(1)}, f32[40,128]{1,0:T(8,128)S(1)}, u32[]{:S(2)}, u32[]{:S(2)}) collective-permute-start(f32[40,128]{1,0:T(8,128)S(1)} %get-tuple-element.18.here_ref), channel_id=1, source_target_pairs={{0,4},{4,0},{1,5},{5,1},{2,6},{6,2},{3,7},{7,3},{8,12},{12,8},{9,1... | collective-permute-start | bytes 61448 | tf_op jit(solution)/shard_map/ppermute | solution.py:604
  11.3 2.1 %collective-permute-start.3 = (f32[160,128]{1,0:T(8,128)S(1)}, f32[160,128]{1,0:T(8,128)S(1)}, u32[]{:S(2)}, u32[]{:S(2)}) collective-permute-start(f32[160,128]{1,0:T(8,128)S(1)} %pad_add_fusion), channel_id=1, source_target_pairs={{0,3},{1,0},{2,1},{3,2},{4,7},{5,4},{6,5},{7,6},{8,11},{9,8},{10,9... | collective-permute-start | bytes 245768 | tf_op jit(solution)/shard_map/ppermute | solution.py:604
  19.1 3.2 %collective-permute-start.4 = (f32[16,64]{1,0:T(8,128)S(1)}, f32[16,64]{1,0:T(8,128)S(1)}, u32[]{:S(2)}, u32[]{:S(2)}) collective-permute-start(f32[16,64]{1,0:T(8,128)S(1)} %get-tuple-element.28), channel_id=1, source_target_pairs={{0,1},{1,2},{2,3},{3,0},{4,5},{5,6},{6,7},{7,4},{8,9},{9,10},{10,1... | collective-permute-start | bytes 12296 | tf_op jit(solution)/shard_map/ppermute | solution.py:604
  22.3 3.7 %collective-permute-start.5 = (f32[16,32]{1,0:T(8,128)S(1)}, f32[16,32]{1,0:T(8,128)S(1)}, u32[]{:S(2)}, u32[]{:S(2)}) collective-permute-start(f32[16,32]{1,0:T(8,128)S(1)} %slice.4), channel_id=1, source_target_pairs={{0,24},{8,0},{16,8},{24,16},{1,25},{9,1},{17,9},{25,17},{2,26},{10... | collective-permute-start | bytes 6152 | tf_op jit(solution)/shard_map/ppermute | solution.py:604

commit v15 on v14

--- a/solution.py
+++ b/solution.py
@@ -524,10 +524,11 @@
     center_rows = [r[:, :own_pairs] for r in center_rows] + [pair_energy]
     center_rows.append(jnp.zeros((ORDERS - 13, own_pairs), F32))
     center_terms = jnp.concatenate(center_rows, axis=0)
-    reach = pick_half
-    if kept_sides < kind:
-        step = kind * owned
-        reach = jnp.concatenate([pick_half[i : i + owned] for i in range(0, known, step)], axis=0)
+    reach = []
+    for x, z, side in np.ndindex(2, 2, kept_sides):
+        start = ((2 * z + x) * kind + side) * owned
+        reach.append(pick_half[start : start + owned])
+    reach = jnp.concatenate(reach, axis=0)
     near_sums = mm_nt(jnp.concatenate(split(near_terms), axis=0), reach)
     center_sums = mm_nt(
         jnp.concatenate(split(center_terms), axis=0), slot_half[:owned, :own_pairs]
@@ -541,7 +542,7 @@
     tiles = [totals[:, 128 * i : 128 * (i + 1)] for i in range(known // 128)]
     for g in range(owned // GROUP):
         cell = g % 2 * 2 + 1 - g // 2
-        target = g * kept_sides * owned + cell * sites
+        target = (g % 2 * 2 + g // 2) * kept_sides * owned + cell * sites
         turn = (target - g * GROUP) % 128
         piece = pltpu.roll(center_sums, turn, 1) if turn else center_sums
         begin = target % 128
@@ -684,14 +685,14 @@
         next_z,
         *weights,
     )
-    totals = keep + moved(send, {"gz": 1})
+    totals = keep + moved(send, {"gx": -1})
 
     def part(index):
         return totals[:, index * owned : (index + 1) * owned]
 
-    back = [moved(part(kept), {"gx": -1})]
+    back = [moved(part(kept), {"gz": 1})]
     for i, step in enumerate((1, -1)[: kept - 1]):
-        back.append(moved(part(kept + 1 + i), {"gx": -1, "gy": step}))
+        back.append(moved(part(kept + 1 + i), {"gy": step, "gz": 1}))
         back.append(moved(part(1 + i), {"gy": step}))
     site_energy, forces, virial = pl.pallas_call(
         finish_kernel,

time: 27 us -> 26.9 us (level)
  starting transfers between devices: 9.85 us -> 8.72 us
  waiting for transfers between devices: 7.3 us -> 8.36 us
    ppermute x6, starting transfers between devices: 9.85 us -> 8.72 us  [moved(): return lax.ppermute(array, names, route)]
    ppermute x6, waiting for transfers between devices: 7.3 us -> 8.36 us  [moved(): return lax.ppermute(array, names, route)]
where the time goes in v15:
time: 26.9 us; the launch traced here: 26.7 us
  Pallas kernels  8.84 us (33%)
  starting transfers between devices  8.72 us (32%)
  waiting for transfers between devices  8.36 us (31%)
  between operations  0.67 us (2%)
    ppermute x6, starting transfers between devices, moved(): return lax.ppermute(array, names, route)  8.72 us
    ppermute x6, waiting for transfers between devices, moved(): return lax.ppermute(array, names, route)  8.36 us
    pallas_call x1, Pallas kernels, local(): pl.pallas_call(functools.partial(force_kernel, kind, nbr), out_shape=(jax...  5.66 us
    pallas_call x1, Pallas kernels, local(): pl.pallas_call(fetch_kernel, out_shape=(*(jax.ShapeDtypeStruct(w.shape, F...  1.35 us
    pallas_call x1, Pallas kernels, local(): pl.pallas_call(functools.partial(pack_kernel, kind), out_shape=(payload,...  1.08 us
    pallas_call x1, Pallas kernels, local(): pl.pallas_call(finish_kernel, out_shape=(jax.ShapeDtypeStruct(species.sha...  0.75 us
  transfers between devices with their start and end apart: 6, of which 5 were waited for; matrix products, arithmetic and copies ran while one was open for 0% of the time, Pallas kernels for 5%

profile of v15, /device:TPU:0, one launch (start us, length us, event | category | flops | bytes accessed | tf_op | source)
XLA Modules:
  0.0 26.7 jit_solution(7263887808097990855)
XLA Ops:
  0.6 1.1 %pack_payload.1 = (f32[40,128]{1,0:T(8,128)S(1)}, f32[40,128]{1,0:T(8,128)S(1)}) custom-call(f32[3,2,1,2,8]{4,3,2,1,0:T(2,128)} %positions_hbm.1, f32[32,128]{1,0:T(8,128)} %bitcast.4, s32[2,1,2,8]{3,2,1,0:T(2,128)} %species_hbm.3, s32[1,32]{1,0:T(1,128)} %bitcast.5, s32[32,32]{1,0:T(8,128)} %neighbours_hbm.1, f32[5]{0:T(128)} %scale_hbm.1), custom_call_target="tpu_custom_call" | custom-call | tf_op jit(solution)/shard_map/pack_payload/pallas_call | solution.py:611
  1.7 4.0 %collective-permute-start.2 = (f32[40,128]{1,0:T(8,128)S(1)}, f32[40,128]{1,0:T(8,128)S(1)}, u32[]{:S(2)}, u32[]{:S(2)}) collective-permute-start(f32[40,128]{1,0:T(8,128)S(1)} %get-tuple-element.19), channel_id=1, source_target_pairs={{0,12},{4,8},{8,20},{12,16},{16,28},{20,24},{24,4},{28,0},{1,13},{... | collective-permute-start | bytes 61448 | tf_op jit(solution)/shard_map/ppermute | solution.py:605
  5.7 1.6 %collective-permute-start = (f32[40,128]{1,0:T(8,128)S(1)}, f32[40,128]{1,0:T(8,128)S(1)}, u32[]{:S(2)}, u32[]{:S(2)}) collective-permute-start(f32[40,128]{1,0:T(8,128)S(1)} %get-tuple-element.19), channel_id=1, source_target_pairs={{0,8},{8,16},{16,24},{24,0},{1,9},{9,17},{17,25},{25,1},{2,10},{10... | collective-permute-start | bytes 61448 | tf_op jit(solution)/shard_map/ppermute | solution.py:605
  7.3 0.5 %collective-permute-start.1 = (f32[40,128]{1,0:T(8,128)S(1)}, f32[40,128]{1,0:T(8,128)S(1)}, u32[]{:S(2)}, u32[]{:S(2)}) collective-permute-start(f32[40,128]{1,0:T(8,128)S(1)} %get-tuple-element.18.here_ref), channel_id=1, source_target_pairs={{0,4},{4,0},{1,5},{5,1},{2,6},{6,2},{3,7},{7,3},{8,12},{12,8},{9,1... | collective-permute-start | bytes 61448 | tf_op jit(solution)/shard_map/ppermute | solution.py:605
  7.8 1.8 %collective-permute-done.2.refs_1_ = f32[40,128]{1,0:T(8,128)S(1)} collective-permute-done((f32[40,128]{1,0:T(8,128)S(1)}, f32[40,128]{1,0:T(8,128)S(1)}, u32[]{:S(2)}, u32[]{:S(2)}) %collective-permute-start.2) | collective-permute-done | bytes 20512 | tf_op jit(solution)/shard_map/ppermute | solution.py:605
  9.6 1.7 %collective-permute-done.last_x_ref = f32[40,128]{1,0:T(8,128)S(1)} collective-permute-done((f32[40,128]{1,0:T(8,128)S(1)}, f32[40,128]{1,0:T(8,128)S(1)}, u32[]{:S(2)}, u32[]{:S(2)}) %collective-permute-start) | collective-permute-done | bytes 20512 | tf_op jit(solution)/shard_map/ppermute | solution.py:605
  11.3 0.0 collective-permute-done.1.refs_0_
  11.3 0.1 collective-permute-start.3
  11.4 1.3 %fetch_weights.1 = (f32[128,128]{1,0:T(8,128)S(1)}, f32[128,128]{1,0:T(8,128)S(1)}, f32[8,128]{1,0:T(8,128)S(1)}, f32[3,128]{1,0:T(4,128)S(1)}, f32[128,256]{1,0...) custom-call(s32[2,1,2,8]{3,2,1,0:T(2,128)} %species_hbm.3, s32[1,32]{1,0:T(1,128)} %bitcast.6, ...), custom_call_target="tpu_custom_call" | custom-call | tf_op jit(solution)/shard_map/fetch_weights/pallas_call | solution.py:646
  12.7 0.7 %collective-permute-done.3.refs_2_ = f32[160,128]{1,0:T(8,128)S(1)} collective-permute-done((f32[160,128]{1,0:T(8,128)S(1)}, f32[160,128]{1,0:T(8,128)S(1)}, u32[]{:S(2)}, u32[]{:S(2)}) %collective-permute-start.3) | collective-permute-done | bytes 81952 | tf_op jit(solution)/shard_map/ppermute | solution.py:605
  13.4 5.7 %pair_forces.1 = (f32[16,64]{1,0:T(8,128)S(1)}, f32[16,64]{1,0:T(8,128)S(1)}) custom-call(f32[40,128]{1,0:T(8,128)S(1)} %get-tuple-element.18.here_ref, f32[40,128]{1,0:T(8,128)S(1)} %collective-permute-done.last_x_ref, f32[40,128]{1,0:T(8,128)S(1)} %collective-permute-done.1.refs_0_, f32[40,128]{1,0:T(8,128)S(1)} %collective-permute-done.2.refs_1_, ...), custom_call_target="tpu_custom_call" | custom-call | tf_op jit(solution)/shard_map/pair_forces/pallas_call | solution.py:671
  19.1 2.0 %collective-permute-start.4 = (f32[16,64]{1,0:T(8,128)S(1)}, f32[16,64]{1,0:T(8,128)S(1)}, u32[]{:S(2)}, u32[]{:S(2)}) collective-permute-start(f32[16,64]{1,0:T(8,128)S(1)} %get-tuple-element.28), channel_id=1, source_target_pairs={{0,24},{8,0},{16,8},{24,16},{1,25},{9,1},{17,9},{25,17},{2,26},{10... | collective-permute-start | bytes 12296 | tf_op jit(solution)/shard_map/ppermute | solution.py:605
  21.1 1.7 %collective-permute-done.4 = f32[16,64]{1,0:T(8,128)S(1)} collective-permute-done((f32[16,64]{1,0:T(8,128)S(1)}, f32[16,64]{1,0:T(8,128)S(1)}, u32[]{:S(2)}, u32[]{:S(2)}) %collective-permute-start.4) | collective-permute-done | bytes 4128 | tf_op jit(solution)/shard_map/ppermute | solution.py:605
  22.8 0.1 slice.4
  22.8 0.6 %collective-permute-start.5 = (f32[16,32]{1,0:T(8,128)S(1)}, f32[16,32]{1,0:T(8,128)S(1)}, u32[]{:S(2)}, u32[]{:S(2)}) collective-permute-start(f32[16,32]{1,0:T(8,128)S(1)} %slice.4), channel_id=1, source_target_pairs={{0,1},{1,2},{2,3},{3,0},{4,5},{5,6},{6,7},{7,4},{8,9},{9,10},{10,1... | collective-permute-start | bytes 6152 | tf_op jit(solution)/shard_map/ppermute | solution.py:605
  23.4 2.5 %collective-permute-done.5.refs_0_ = f32[16,32]{1,0:T(8,128)S(1)} collective-permute-done((f32[16,32]{1,0:T(8,128)S(1)}, f32[16,32]{1,0:T(8,128)S(1)}, u32[]{:S(2)}, u32[]{:S(2)}) %collective-permute-start.5) | collective-permute-done | bytes 2080 | tf_op jit(solution)/shard_map/ppermute | solution.py:605
  25.9 0.8 %write_outputs.1 = (f32[2,1,2,8]{3,2,1,0:T(2,128)}, f32[3,2,1,2,8]{4,3,2,1,0:T(2,128)}, f32[2,1,2,8,9]{4,3,2,1,0:T(8,128)}) custom-call(f32[16,64]{1,0:T(8,128)S(1)} %add.23.mine_ref, f32[1,32]{1,0:T(1,128)S(1)} %get-tuple-element.29.shift_row_ref, f32[16,32]{1,0:T(8,128)S(1)} %collective-permute-done.5.refs_0_), custom_call_target="tpu_custom_call" | custom-call | tf_op jit(solution)/shard_map/write_outputs/pallas_call | solution.py:697
  (2 shorter events, 0.0 us)
Async XLA Ops:
  1.7 7.9 %collective-permute-start.2 = (f32[40,128]{1,0:T(8,128)S(1)}, f32[40,128]{1,0:T(8,128)S(1)}, u32[]{:S(2)}, u32[]{:S(2)}) collective-permute-start(f32[40,128]{1,0:T(8,128)S(1)} %get-tuple-element.19), channel_id=1, source_target_pairs={{0,12},{4,8},{8,20},{12,16},{16,28},{20,24},{24,4},{28,0},{1,13},{... | collective-permute-start | bytes 61448 | tf_op jit(solution)/shard_map/ppermute | solution.py:605
  5.7 5.6 %collective-permute-start = (f32[40,128]{1,0:T(8,128)S(1)}, f32[40,128]{1,0:T(8,128)S(1)}, u32[]{:S(2)}, u32[]{:S(2)}) collective-permute-start(f32[40,128]{1,0:T(8,128)S(1)} %get-tuple-element.19), channel_id=1, source_target_pairs={{0,8},{8,16},{16,24},{24,0},{1,9},{9,17},{17,25},{25,1},{2,10},{10... | collective-permute-start | bytes 61448 | tf_op jit(solution)/shard_map/ppermute | solution.py:605
  7.3 4.0 %collective-permute-start.1 = (f32[40,128]{1,0:T(8,128)S(1)}, f32[40,128]{1,0:T(8,128)S(1)}, u32[]{:S(2)}, u32[]{:S(2)}) collective-permute-start(f32[40,128]{1,0:T(8,128)S(1)} %get-tuple-element.18.here_ref), channel_id=1, source_target_pairs={{0,4},{4,0},{1,5},{5,1},{2,6},{6,2},{3,7},{7,3},{8,12},{12,8},{9,1... | collective-permute-start | bytes 61448 | tf_op jit(solution)/shard_map/ppermute | solution.py:605
  11.3 2.1 %collective-permute-start.3 = (f32[160,128]{1,0:T(8,128)S(1)}, f32[160,128]{1,0:T(8,128)S(1)}, u32[]{:S(2)}, u32[]{:S(2)}) collective-permute-start(f32[160,128]{1,0:T(8,128)S(1)} %pad_add_fusion), channel_id=1, source_target_pairs={{0,3},{1,0},{2,1},{3,2},{4,7},{5,4},{6,5},{7,6},{8,11},{9,8},{10,9... | collective-permute-start | bytes 245768 | tf_op jit(solution)/shard_map/ppermute | solution.py:605
  19.1 3.7 %collective-permute-start.4 = (f32[16,64]{1,0:T(8,128)S(1)}, f32[16,64]{1,0:T(8,128)S(1)}, u32[]{:S(2)}, u32[]{:S(2)}) collective-permute-start(f32[16,64]{1,0:T(8,128)S(1)} %get-tuple-element.28), channel_id=1, source_target_pairs={{0,24},{8,0},{16,8},{24,16},{1,25},{9,1},{17,9},{25,17},{2,26},{10... | collective-permute-start | bytes 12296 | tf_op jit(solution)/shard_map/ppermute | solution.py:605
  22.8 3.1 %collective-permute-start.5 = (f32[16,32]{1,0:T(8,128)S(1)}, f32[16,32]{1,0:T(8,128)S(1)}, u32[]{:S(2)}, u32[]{:S(2)}) collective-permute-start(f32[16,32]{1,0:T(8,128)S(1)} %slice.4), channel_id=1, source_target_pairs={{0,1},{1,2},{2,3},{3,0},{4,5},{5,6},{6,7},{7,4},{8,9},{9,10},{10,1... | collective-permute-start | bytes 6152 | tf_op jit(solution)/shard_map/ppermute | solution.py:605

commit v16 on v15

--- a/solution.py
+++ b/solution.py
@@ -15,6 +15,7 @@
 ROOT_HALF = 0.7071067811865476
 GROUP = 8
 ORDERS = 16
+LEVELS = (0, 1, 1, 1, 2, 2, 2, 2, 2)
 SITES = 8
 OWN_CELLS = 4
 FRAME_CELLS = 48
@@ -34,6 +35,11 @@
     middle = rest.astype(BF16)
     low = (rest - middle.astype(F32)).astype(BF16)
     return high, middle, low
+
+
+def halves(value):
+    high = value.astype(BF16).astype(F32)
+    return high, value - high
 
 
 def mm(a, b):
@@ -241,7 +247,6 @@
     radial = basis_weight_ref.shape[0]
     span = GROUP * nbr
     groups = centers // GROUP
-    wide = GROUP * ORDERS
     sites = SITES
     root_count = math.sqrt(nbr)
     root_three = math.sqrt(3.0)
@@ -328,39 +333,28 @@
     own_t = project(center_weight_ref[...], center_feats)
     near_high, near_low = split(0.5 * near_t)
     own_high, own_low = split(0.5 * own_t)
-    lookup = jnp.concatenate(
-        [
-            jnp.concatenate([near_high, own_high, basis_high_t, basis_high_t], axis=1),
-            jnp.concatenate([near_low, own_low, basis_low_t, jnp.zeros_like(basis_low_t)], axis=1),
-        ],
-        axis=0,
+    near_lookup = jnp.concatenate([near_high, near_low], axis=0)
+    rest_lookup = jnp.concatenate(
+        [own_high, own_low, basis_high_t, basis_high_t, basis_low_t], axis=1
     )
     scale_rows = jnp.concatenate(scales, axis=0)
     scale_parts = jnp.concatenate(
         [*split3(scale_rows), jnp.zeros((-3 * groups % 16, 128), BF16)], axis=0
     )
 
-    level = lax.broadcasted_iota(jnp.int32, (ORDERS, width), 0)
-    path_rows = jnp.where(
-        level == 0,
-        path_weight_ref[0:1, :],
-        jnp.where(
-            level < 4,
-            path_weight_ref[1:2, :],
-            jnp.where(level < 9, path_weight_ref[2:3, :], 0.0),
-        ),
-    )
-    paths_t = jnp.transpose(jnp.concatenate([path_rows] * GROUP, axis=0)) * (1.0 / root_count)
+    path_rows = jnp.concatenate(
+        [jnp.broadcast_to(path_weight_ref[l : l + 1, :], (GROUP, width)) for l in LEVELS], axis=0
+    ) * (1.0 / root_count)
     out_column = jnp.transpose(jnp.broadcast_to(out_weight_ref[...], (width, width)))
     out_column = jnp.concatenate([out_column] * (pairs // width), axis=1)
 
     site_ids = lax.broadcasted_iota(jnp.int32, (known, pairs), 0)
     slot_ids = lax.broadcasted_iota(jnp.int32, (centers, pairs), 0)
     slot_row = lax.broadcasted_iota(jnp.int32, (1, pairs), 1) // nbr
-    block_row = lax.broadcasted_iota(jnp.int32, (wide, span), 0) // ORDERS
-    block_lane = lax.broadcasted_iota(jnp.int32, (wide, span), 1) // nbr
-    block_mask = (block_row == block_lane).astype(F32)
-    block_half = block_mask.astype(BF16)
+    group_lane = lax.broadcasted_iota(jnp.int32, (GROUP, pairs), 1) // nbr % GROUP
+    group_mask = group_lane == lax.broadcasted_iota(jnp.int32, (GROUP, pairs), 0)
+    group_mask = jnp.where(group_mask, 1.0, 0.0)
+    tall = len(LEVELS) * GROUP
     order = lax.broadcasted_iota(jnp.int32, (radial, pairs), 0).astype(F32) + 1.0
     lanes = [slice(g * span, (g + 1) * span) for g in range(groups)]
 
@@ -402,21 +396,14 @@
             0.5 * root_five * (3.0 * ez * ez - 1.0),
             root_fifteen * ex * ez,
             0.5 * root_fifteen * (ex * ex - ey * ey),
-            jnp.zeros((ORDERS - 9, pairs), F32),
         ],
         axis=0,
     )
-    angular_high, angular_low = split(angular)
-    blocks = [
-        jnp.concatenate(
-            [
-                jnp.concatenate([angular_high[:, cut]] * GROUP, axis=0) * block_half,
-                jnp.concatenate([angular_low[:, cut]] * GROUP, axis=0) * block_half,
-            ],
-            axis=0,
-        )
-        for cut in lanes
-    ]
+    angular_high, angular_low = halves(angular)
+    angular_low = angular_low.astype(BF16).astype(F32)
+    block_high = [angular_high[m : m + 1] * group_mask for m in range(len(LEVELS))]
+    block_low = [angular_low[m : m + 1] * group_mask for m in range(len(LEVELS))]
+    blocks = jnp.concatenate(block_high + block_low + block_high, axis=0).astype(BF16)
     lane_ids = lax.broadcasted_iota(jnp.int32, (128, span), 0)
     lane_slot = lax.broadcasted_iota(jnp.int32, (128, span), 1) // nbr + 3 * sites
     scale = mm(scale_parts, jnp.where(lane_ids == lane_slot, 1.0, 0.0).astype(BF16))
@@ -425,9 +412,10 @@
     scale = scale * (1.0 / root_count)
     pull = ROOT_HALF * scale
 
-    basis_high, basis_low = split(basis)
-    before = folded(
-        mm(lookup, jnp.concatenate([pick_half, slot_half, basis_high, basis_low], axis=0))
+    basis_high, basis_low = halves(basis)
+    basis_rest = jnp.concatenate([basis_high, basis_low, basis_high], axis=0).astype(BF16)
+    before = folded(mm(near_lookup, pick_half)) + mm(
+        rest_lookup, jnp.concatenate([slot_half, slot_half, basis_rest], axis=0)
     )
     gate = 1.0 + jnp.tanh(before)
     active = before * gate
@@ -439,13 +427,19 @@
 
     def over_pairs(high, low):
         sums = []
-        for cut, block in zip(lanes, blocks):
-            quad = mm_nt(jnp.concatenate([high[:, cut], low[:, cut]], axis=0), block)
-            sums.append((quad[:width, :wide] + quad[:width, wide:] + quad[width:, :wide]) * paths_t)
+        for cut in lanes:
+            both = jnp.concatenate([high[:, cut], low[:, cut]], axis=0)
+            quad = mm_nt(blocks[: 2 * tall, cut], both)
+            quad = quad[:tall, :width] + quad[tall:, :width] + quad[:tall, width:]
+            sums.append(quad * path_rows)
         return sums
 
     def over_orders(tables):
-        parts = [folded(mm(stacked(*split(t)), block)) for t, block in zip(tables, blocks)]
+        parts = []
+        for table, cut in zip(tables, lanes):
+            high, low = halves(table)
+            table = jnp.transpose(jnp.concatenate([high, high, low], axis=0)).astype(BF16)
+            parts.append(mm(table, blocks[:, cut]))
         return jnp.concatenate(parts, axis=1)
 
     weighted = over_pairs(env_high, env_low)
@@ -475,19 +469,15 @@
 
     d_angular = []
     for g, cut in enumerate(lanes):
-        sides = jnp.transpose(jnp.concatenate([weighted[g], d_embed[g]], axis=0))
-        sides_high, sides_low = split(sides)
+        sides_high, sides_low = halves(jnp.concatenate([weighted[g], d_embed[g]], axis=1))
         d_block = full_depth(
-            jnp.concatenate([sides_high, sides_low], axis=0),
-            sides_high,
+            jnp.concatenate([sides_high, sides_low], axis=0).astype(BF16),
+            sides_high.astype(BF16),
             jnp.concatenate([dinner_high[:, cut], env_high[:, cut]], axis=0),
             jnp.concatenate([dinner_low[:, cut], env_low[:, cut]], axis=0),
         )
-        d_block = d_block * block_mask
-        total = d_block[:ORDERS]
-        for k in range(1, GROUP):
-            total = total + d_block[k * ORDERS : (k + 1) * ORDERS]
-        d_angular.append(total)
+        d_block = d_block.reshape(len(LEVELS), GROUP, span) * group_mask[None, :, cut]
+        d_angular.append(jnp.sum(d_block, axis=1))
     d_angular = jnp.concatenate(d_angular, axis=1)
 
     mixed_high, mixed_low = split(jnp.concatenate([d_values, d_env], axis=0))

time: 26.9 us -> 26.9 us (level)
  no operation moved by 1% of the time
where the time goes in v16:
time: 26.9 us; the launch traced here: 26.6 us
  Pallas kernels  8.81 us (33%)
  starting transfers between devices  8.69 us (32%)
  waiting for transfers between devices  8.38 us (31%)
  between operations  0.67 us (2%)
    ppermute x6, starting transfers between devices, moved(): return lax.ppermute(array, names, route)  8.69 us
    ppermute x6, waiting for transfers between devices, moved(): return lax.ppermute(array, names, route)  8.38 us
    pallas_call x1, Pallas kernels, local(): pl.pallas_call(functools.partial(force_kernel, kind, nbr), out_shape=(jax...  5.63 us
    pallas_call x1, Pallas kernels, local(): pl.pallas_call(fetch_kernel, out_shape=(*(jax.ShapeDtypeStruct(w.shape, F...  1.35 us
    pallas_call x1, Pallas kernels, local(): pl.pallas_call(functools.partial(pack_kernel, kind), out_shape=(payload,...  1.08 us
    pallas_call x1, Pallas kernels, local(): pl.pallas_call(finish_kernel, out_shape=(jax.ShapeDtypeStruct(species.sha...  0.75 us
  transfers between devices with their start and end apart: 6, of which 5 were waited for; matrix products, arithmetic and copies ran while one was open for 0% of the time, Pallas kernels for 5%

profile of v16, /device:TPU:0, one launch (start us, length us, event | category | flops | bytes accessed | tf_op | source)
XLA Modules:
  0.0 26.6 jit_solution(4655147110089687287)
XLA Ops:
  0.6 1.1 %pack_payload.1 = (f32[40,128]{1,0:T(8,128)S(1)}, f32[40,128]{1,0:T(8,128)S(1)}) custom-call(f32[3,2,1,2,8]{4,3,2,1,0:T(2,128)} %positions_hbm.1, f32[32,128]{1,0:T(8,128)} %bitcast.4, s32[2,1,2,8]{3,2,1,0:T(2,128)} %species_hbm.3, s32[1,32]{1,0:T(1,128)} %bitcast.5, s32[32,32]{1,0:T(8,128)} %neighbours_hbm.1, f32[5]{0:T(128)} %scale_hbm.1), custom_call_target="tpu_custom_call" | custom-call | tf_op jit(solution)/shard_map/pack_payload/pallas_call | solution.py:601
  1.7 4.0 %collective-permute-start.2 = (f32[40,128]{1,0:T(8,128)S(1)}, f32[40,128]{1,0:T(8,128)S(1)}, u32[]{:S(2)}, u32[]{:S(2)}) collective-permute-start(f32[40,128]{1,0:T(8,128)S(1)} %get-tuple-element.19), channel_id=1, source_target_pairs={{0,12},{4,8},{8,20},{12,16},{16,28},{20,24},{24,4},{28,0},{1,13},{... | collective-permute-start | bytes 61448 | tf_op jit(solution)/shard_map/ppermute | solution.py:595
  5.7 1.6 %collective-permute-start = (f32[40,128]{1,0:T(8,128)S(1)}, f32[40,128]{1,0:T(8,128)S(1)}, u32[]{:S(2)}, u32[]{:S(2)}) collective-permute-start(f32[40,128]{1,0:T(8,128)S(1)} %get-tuple-element.19), channel_id=1, source_target_pairs={{0,8},{8,16},{16,24},{24,0},{1,9},{9,17},{17,25},{25,1},{2,10},{10... | collective-permute-start | bytes 61448 | tf_op jit(solution)/shard_map/ppermute | solution.py:595
  7.3 0.5 %collective-permute-start.1 = (f32[40,128]{1,0:T(8,128)S(1)}, f32[40,128]{1,0:T(8,128)S(1)}, u32[]{:S(2)}, u32[]{:S(2)}) collective-permute-start(f32[40,128]{1,0:T(8,128)S(1)} %get-tuple-element.18.here_ref), channel_id=1, source_target_pairs={{0,4},{4,0},{1,5},{5,1},{2,6},{6,2},{3,7},{7,3},{8,12},{12,8},{9,1... | collective-permute-start | bytes 61448 | tf_op jit(solution)/shard_map/ppermute | solution.py:595
  7.8 1.8 %collective-permute-done.2.refs_1_ = f32[40,128]{1,0:T(8,128)S(1)} collective-permute-done((f32[40,128]{1,0:T(8,128)S(1)}, f32[40,128]{1,0:T(8,128)S(1)}, u32[]{:S(2)}, u32[]{:S(2)}) %collective-permute-start.2) | collective-permute-done | bytes 20512 | tf_op jit(solution)/shard_map/ppermute | solution.py:595
  9.6 1.7 %collective-permute-done.last_x_ref = f32[40,128]{1,0:T(8,128)S(1)} collective-permute-done((f32[40,128]{1,0:T(8,128)S(1)}, f32[40,128]{1,0:T(8,128)S(1)}, u32[]{:S(2)}, u32[]{:S(2)}) %collective-permute-start) | collective-permute-done | bytes 20512 | tf_op jit(solution)/shard_map/ppermute | solution.py:595
  11.3 0.0 collective-permute-done.1.refs_0_
  11.3 0.1 collective-permute-start.3
  11.4 1.3 %fetch_weights.1 = (f32[128,128]{1,0:T(8,128)S(1)}, f32[128,128]{1,0:T(8,128)S(1)}, f32[8,128]{1,0:T(8,128)S(1)}, f32[3,128]{1,0:T(4,128)S(1)}, f32[128,256]{1,0...) custom-call(s32[2,1,2,8]{3,2,1,0:T(2,128)} %species_hbm.3, s32[1,32]{1,0:T(1,128)} %bitcast.6, ...), custom_call_target="tpu_custom_call" | custom-call | tf_op jit(solution)/shard_map/fetch_weights/pallas_call | solution.py:636
  12.7 0.7 %collective-permute-done.3.refs_2_ = f32[160,128]{1,0:T(8,128)S(1)} collective-permute-done((f32[160,128]{1,0:T(8,128)S(1)}, f32[160,128]{1,0:T(8,128)S(1)}, u32[]{:S(2)}, u32[]{:S(2)}) %collective-permute-start.3) | collective-permute-done | bytes 81952 | tf_op jit(solution)/shard_map/ppermute | solution.py:595
  13.4 5.6 %pair_forces.1 = (f32[16,64]{1,0:T(8,128)S(1)}, f32[16,64]{1,0:T(8,128)S(1)}) custom-call(f32[40,128]{1,0:T(8,128)S(1)} %get-tuple-element.18.here_ref, f32[40,128]{1,0:T(8,128)S(1)} %collective-permute-done.last_x_ref, f32[40,128]{1,0:T(8,128)S(1)} %collective-permute-done.1.refs_0_, f32[40,128]{1,0:T(8,128)S(1)} %collective-permute-done.2.refs_1_, ...), custom_call_target="tpu_custom_call" | custom-call | tf_op jit(solution)/shard_map/pair_forces/pallas_call | solution.py:661
  19.1 2.0 %collective-permute-start.4 = (f32[16,64]{1,0:T(8,128)S(1)}, f32[16,64]{1,0:T(8,128)S(1)}, u32[]{:S(2)}, u32[]{:S(2)}) collective-permute-start(f32[16,64]{1,0:T(8,128)S(1)} %get-tuple-element.28), channel_id=1, source_target_pairs={{0,24},{8,0},{16,8},{24,16},{1,25},{9,1},{17,9},{25,17},{2,26},{10... | collective-permute-start | bytes 12296 | tf_op jit(solution)/shard_map/ppermute | solution.py:595
  21.0 1.7 %collective-permute-done.4 = f32[16,64]{1,0:T(8,128)S(1)} collective-permute-done((f32[16,64]{1,0:T(8,128)S(1)}, f32[16,64]{1,0:T(8,128)S(1)}, u32[]{:S(2)}, u32[]{:S(2)}) %collective-permute-start.4) | collective-permute-done | bytes 4128 | tf_op jit(solution)/shard_map/ppermute | solution.py:595
  22.7 0.1 slice.4
  22.8 0.5 %collective-permute-start.5 = (f32[16,32]{1,0:T(8,128)S(1)}, f32[16,32]{1,0:T(8,128)S(1)}, u32[]{:S(2)}, u32[]{:S(2)}) collective-permute-start(f32[16,32]{1,0:T(8,128)S(1)} %slice.4), channel_id=1, source_target_pairs={{0,1},{1,2},{2,3},{3,0},{4,5},{5,6},{6,7},{7,4},{8,9},{9,10},{10,1... | collective-permute-start | bytes 6152 | tf_op jit(solution)/shard_map/ppermute | solution.py:595
  23.4 2.5 %collective-permute-done.5.refs_0_ = f32[16,32]{1,0:T(8,128)S(1)} collective-permute-done((f32[16,32]{1,0:T(8,128)S(1)}, f32[16,32]{1,0:T(8,128)S(1)}, u32[]{:S(2)}, u32[]{:S(2)}) %collective-permute-start.5) | collective-permute-done | bytes 2080 | tf_op jit(solution)/shard_map/ppermute | solution.py:595
  25.9 0.8 %write_outputs.1 = (f32[2,1,2,8]{3,2,1,0:T(2,128)}, f32[3,2,1,2,8]{4,3,2,1,0:T(2,128)}, f32[2,1,2,8,9]{4,3,2,1,0:T(8,128)}) custom-call(f32[16,64]{1,0:T(8,128)S(1)} %add.23.mine_ref, f32[1,32]{1,0:T(1,128)S(1)} %get-tuple-element.29.shift_row_ref, f32[16,32]{1,0:T(8,128)S(1)} %collective-permute-done.5.refs_0_), custom_call_target="tpu_custom_call" | custom-call | tf_op jit(solution)/shard_map/write_outputs/pallas_call | solution.py:687
  (2 shorter events, 0.0 us)
Async XLA Ops:
  1.7 7.9 %collective-permute-start.2 = (f32[40,128]{1,0:T(8,128)S(1)}, f32[40,128]{1,0:T(8,128)S(1)}, u32[]{:S(2)}, u32[]{:S(2)}) collective-permute-start(f32[40,128]{1,0:T(8,128)S(1)} %get-tuple-element.19), channel_id=1, source_target_pairs={{0,12},{4,8},{8,20},{12,16},{16,28},{20,24},{24,4},{28,0},{1,13},{... | collective-permute-start | bytes 61448 | tf_op jit(solution)/shard_map/ppermute | solution.py:595
  5.7 5.6 %collective-permute-start = (f32[40,128]{1,0:T(8,128)S(1)}, f32[40,128]{1,0:T(8,128)S(1)}, u32[]{:S(2)}, u32[]{:S(2)}) collective-permute-start(f32[40,128]{1,0:T(8,128)S(1)} %get-tuple-element.19), channel_id=1, source_target_pairs={{0,8},{8,16},{16,24},{24,0},{1,9},{9,17},{17,25},{25,1},{2,10},{10... | collective-permute-start | bytes 61448 | tf_op jit(solution)/shard_map/ppermute | solution.py:595
  7.3 4.0 %collective-permute-start.1 = (f32[40,128]{1,0:T(8,128)S(1)}, f32[40,128]{1,0:T(8,128)S(1)}, u32[]{:S(2)}, u32[]{:S(2)}) collective-permute-start(f32[40,128]{1,0:T(8,128)S(1)} %get-tuple-element.18.here_ref), channel_id=1, source_target_pairs={{0,4},{4,0},{1,5},{5,1},{2,6},{6,2},{3,7},{7,3},{8,12},{12,8},{9,1... | collective-permute-start | bytes 61448 | tf_op jit(solution)/shard_map/ppermute | solution.py:595
  11.3 2.1 %collective-permute-start.3 = (f32[160,128]{1,0:T(8,128)S(1)}, f32[160,128]{1,0:T(8,128)S(1)}, u32[]{:S(2)}, u32[]{:S(2)}) collective-permute-start(f32[160,128]{1,0:T(8,128)S(1)} %pad_add_fusion), channel_id=1, source_target_pairs={{0,3},{1,0},{2,1},{3,2},{4,7},{5,4},{6,5},{7,6},{8,11},{9,8},{10,9... | collective-permute-start | bytes 245768 | tf_op jit(solution)/shard_map/ppermute | solution.py:595
  19.1 3.7 %collective-permute-start.4 = (f32[16,64]{1,0:T(8,128)S(1)}, f32[16,64]{1,0:T(8,128)S(1)}, u32[]{:S(2)}, u32[]{:S(2)}) collective-permute-start(f32[16,64]{1,0:T(8,128)S(1)} %get-tuple-element.28), channel_id=1, source_target_pairs={{0,24},{8,0},{16,8},{24,16},{1,25},{9,1},{17,9},{25,17},{2,26},{10... | collective-permute-start | bytes 12296 | tf_op jit(solution)/shard_map/ppermute | solution.py:595
  22.8 3.1 %collective-permute-start.5 = (f32[16,32]{1,0:T(8,128)S(1)}, f32[16,32]{1,0:T(8,128)S(1)}, u32[]{:S(2)}, u32[]{:S(2)}) collective-permute-start(f32[16,32]{1,0:T(8,128)S(1)} %slice.4), channel_id=1, source_target_pairs={{0,1},{1,2},{2,3},{3,0},{4,5},{5,6},{6,7},{7,4},{8,9},{9,10},{10,1... | collective-permute-start | bytes 6152 | tf_op jit(solution)/shard_map/ppermute | solution.py:595

commit v17 on v16

--- a/solution.py
+++ b/solution.py
@@ -346,9 +346,9 @@
         [jnp.broadcast_to(path_weight_ref[l : l + 1, :], (GROUP, width)) for l in LEVELS], axis=0
     ) * (1.0 / root_count)
     out_column = jnp.transpose(jnp.broadcast_to(out_weight_ref[...], (width, width)))
-    out_column = jnp.concatenate([out_column] * (pairs // width), axis=1)
-
-    site_ids = lax.broadcasted_iota(jnp.int32, (known, pairs), 0)
+    out_column = jnp.concatenate([out_column] * (span // width), axis=1)
+
+    site_ids = lax.broadcasted_iota(jnp.int32, (known, span), 0)
     slot_ids = lax.broadcasted_iota(jnp.int32, (centers, pairs), 0)
     slot_row = lax.broadcasted_iota(jnp.int32, (1, pairs), 1) // nbr
     group_lane = lax.broadcasted_iota(jnp.int32, (GROUP, pairs), 1) // nbr % GROUP
@@ -356,13 +356,15 @@
     group_mask = jnp.where(group_mask, 1.0, 0.0)
     tall = len(LEVELS) * GROUP
     order = lax.broadcasted_iota(jnp.int32, (radial, pairs), 0).astype(F32) + 1.0
+
     lanes = [slice(g * span, (g + 1) * span) for g in range(groups)]
-
-    pick = jnp.where(site_ids == near_row, 1.0, 0.0)
-    pick_half = pick.astype(BF16)
+    picks = [
+        jnp.where(site_ids == near_row[:, cut], 1.0, 0.0).astype(BF16) for cut in lanes
+    ]
     slot_half = jnp.where(slot_ids == slot_row, 1.0, 0.0).astype(BF16)
 
-    moved = mm(place_parts, pick_half) - mm(center_parts, slot_half)
+    moved = [mm(place_parts, pick) for pick in picks]
+    moved = jnp.concatenate(moved, axis=1) - mm(center_parts, slot_half)
     moved = moved[: 3 * sites] + moved[3 * sites : 6 * sites] + moved[6 * sites :]
     dx = jnp.where(live, jnp.sum(moved[:sites], axis=0, keepdims=True), 6.0)
     dy = jnp.sum(moved[sites : 2 * sites], axis=0, keepdims=True) + CELL_SIDE * side_y
@@ -414,81 +416,98 @@
 
     basis_high, basis_low = halves(basis)
     basis_rest = jnp.concatenate([basis_high, basis_low, basis_high], axis=0).astype(BF16)
-    before = folded(mm(near_lookup, pick_half)) + mm(
-        rest_lookup, jnp.concatenate([slot_half, slot_half, basis_rest], axis=0)
-    )
-    gate = 1.0 + jnp.tanh(before)
-    active = before * gate
-    latent = weight * active
-    latent_high, latent_low = split(latent)
-    mixed = folded(mm(value_rows, jnp.concatenate([latent_high, latent_low], axis=0)))
-    values = mixed[:width]
-    env_high, env_low = split(mixed[width:])
-
-    def over_pairs(high, low):
-        sums = []
-        for cut in lanes:
-            both = jnp.concatenate([high[:, cut], low[:, cut]], axis=0)
-            quad = mm_nt(blocks[: 2 * tall, cut], both)
-            quad = quad[:tall, :width] + quad[tall:, :width] + quad[:tall, width:]
-            sums.append(quad * path_rows)
-        return sums
-
-    def over_orders(tables):
-        parts = []
-        for table, cut in zip(tables, lanes):
-            high, low = halves(table)
-            table = jnp.transpose(jnp.concatenate([high, high, low], axis=0)).astype(BF16)
-            parts.append(mm(table, blocks[:, cut]))
-        return jnp.concatenate(parts, axis=1)
-
-    weighted = over_pairs(env_high, env_low)
-    inner = over_orders(weighted)
-    scalars = values * inner
-    scalars_high, scalars_low = split(scalars)
-    z = full_depth(
-        latent_both_t,
-        latent_high_t,
-        jnp.concatenate([latent_high, scalars_high], axis=0),
-        jnp.concatenate([latent_low, scalars_low], axis=0),
-    )
-    z_gate = 1.0 + jnp.tanh(z)
-    update = z * z_gate
-    update_sum = jnp.sum(update * out_column, axis=0, keepdims=True)
-    active_sum = jnp.sum(
-        active[:, :own_pairs] * out_column[:, :own_pairs], axis=0, keepdims=True
-    )
-    pair_energy = (active_sum + update_sum[:, :own_pairs]) * (pull * weight)[:, :own_pairs]
-    d_z = (0.5 * pull * weight) * (z_gate + update * (2.0 - z_gate))
-    spread_back = half_depth(latent_rows, d_z)
-    d_scalars = spread_back[width:]
-    d_values = d_scalars * inner
-    dinner_high, dinner_low = split(d_scalars * values)
-    d_embed = over_pairs(dinner_high, dinner_low)
-    d_env = over_orders(d_embed)
+    rest = jnp.concatenate([slot_half, slot_half, basis_rest], axis=0)
+    fall = 0.5 * pull * weight
+    each = range(groups)
+
+    gate, active, latent = [], [], []
+    for g in each:
+        cut = lanes[g]
+        before = folded(mm(near_lookup, picks[g])) + mm(rest_lookup, rest[:, cut])
+        gate.append(1.0 + jnp.tanh(before))
+        active.append(before * gate[g])
+        latent.append(split(weight[:, cut] * active[g]))
+
+    values, env = [], []
+    for g in each:
+        mixed = folded(mm(value_rows, jnp.concatenate(latent[g], axis=0)))
+        values.append(mixed[:width])
+        env.append(split(mixed[width:]))
+
+    def over_pairs(g, parts):
+        quad = mm_nt(blocks[: 2 * tall, lanes[g]], jnp.concatenate(parts, axis=0))
+        quad = quad[:tall, :width] + quad[tall:, :width] + quad[:tall, width:]
+        return quad * path_rows
+
+    def over_orders(g, table):
+        high, low = halves(table)
+        table = jnp.transpose(jnp.concatenate([high, high, low], axis=0)).astype(BF16)
+        return mm(table, blocks[:, lanes[g]])
+
+    weighted = [over_pairs(g, env[g]) for g in each]
+    inner, scalars = [], []
+    for g in each:
+        inner.append(over_orders(g, weighted[g]))
+        scalars.append(split(values[g] * inner[g]))
+
+    update_sum, slope_z = [], []
+    for g in each:
+        z = full_depth(
+            latent_both_t,
+            latent_high_t,
+            jnp.concatenate([latent[g][0], scalars[g][0]], axis=0),
+            jnp.concatenate([latent[g][1], scalars[g][1]], axis=0),
+        )
+        z_gate = 1.0 + jnp.tanh(z)
+        update = z * z_gate
+        update_sum.append(jnp.sum(update * out_column, axis=0, keepdims=True))
+        slope_z.append(split(fall[:, lanes[g]] * (z_gate + update * (2.0 - z_gate))))
+
+    d_direct, d_values, d_inner = [], [], []
+    for g in each:
+        spread_back = folded(mm(latent_rows, jnp.concatenate(slope_z[g], axis=0)))
+        d_direct.append(spread_back[:width] + pull[:, lanes[g]] * out_column)
+        d_scalars = spread_back[width:]
+        d_values.append(split(d_scalars * inner[g]))
+        d_inner.append(split(d_scalars * values[g]))
+
+    d_embed = [over_pairs(g, d_inner[g]) for g in each]
+    d_env = [split(over_orders(g, d_embed[g])) for g in each]
 
     d_angular = []
-    for g, cut in enumerate(lanes):
+    for g in each:
         sides_high, sides_low = halves(jnp.concatenate([weighted[g], d_embed[g]], axis=1))
         d_block = full_depth(
             jnp.concatenate([sides_high, sides_low], axis=0).astype(BF16),
             sides_high.astype(BF16),
-            jnp.concatenate([dinner_high[:, cut], env_high[:, cut]], axis=0),
-            jnp.concatenate([dinner_low[:, cut], env_low[:, cut]], axis=0),
+            jnp.concatenate([d_inner[g][0], env[g][0]], axis=0),
+            jnp.concatenate([d_inner[g][1], env[g][1]], axis=0),
         )
-        d_block = d_block.reshape(len(LEVELS), GROUP, span) * group_mask[None, :, cut]
+        d_block = d_block.reshape(len(LEVELS), GROUP, span) * group_mask[None, :, lanes[g]]
         d_angular.append(jnp.sum(d_block, axis=1))
+
+    d_weight, d_basis = [], []
+    for g in each:
+        d_latent = d_direct[g] + full_depth(
+            value_both,
+            value_high,
+            jnp.concatenate([d_values[g][0], d_env[g][0]], axis=0),
+            jnp.concatenate([d_values[g][1], d_env[g][1]], axis=0),
+        )
+        d_weight.append(jnp.sum(d_latent * active[g], axis=0, keepdims=True))
+        d_before = d_latent * (gate[g] + active[g] * (2.0 - gate[g]))
+        d_basis.append(half_depth(basis_rows, d_before))
+
+    active_sum = [
+        jnp.sum(active[g] * out_column, axis=0, keepdims=True) for g in range(own_pairs // span)
+    ]
+    update_sum = jnp.concatenate(update_sum, axis=1)
+    pair_energy = (jnp.concatenate(active_sum, axis=1) + update_sum[:, :own_pairs]) * (
+        pull * weight
+    )[:, :own_pairs]
     d_angular = jnp.concatenate(d_angular, axis=1)
-
-    mixed_high, mixed_low = split(jnp.concatenate([d_values, d_env], axis=0))
-    d_latent = (
-        full_depth(value_both, value_high, mixed_high, mixed_low)
-        + spread_back[:width]
-        + pull * out_column
-    )
-    d_weight = jnp.sum(d_latent * active, axis=0, keepdims=True) + pull * update_sum
-    d_before = d_latent * (gate + active * (2.0 - gate))
-    d_basis = half_depth(basis_rows, d_before) * (0.5 * weight)
+    d_weight = jnp.concatenate(d_weight, axis=1) + pull * update_sum
+    d_basis = jnp.concatenate(d_basis, axis=1) * (0.5 * weight)
 
     d_length = jnp.sum(d_basis * basis_slope, axis=0, keepdims=True) + d_weight * slope * (
         1.0 / CUTOFF
@@ -514,12 +533,15 @@
     center_rows = [r[:, :own_pairs] for r in center_rows] + [pair_energy]
     center_rows.append(jnp.zeros((ORDERS - 13, own_pairs), F32))
     center_terms = jnp.concatenate(center_rows, axis=0)
-    reach = []
-    for x, z, side in np.ndindex(2, 2, kept_sides):
-        start = ((2 * z + x) * kind + side) * owned
-        reach.append(pick_half[start : start + owned])
-    reach = jnp.concatenate(reach, axis=0)
-    near_sums = mm_nt(jnp.concatenate(split(near_terms), axis=0), reach)
+    terms_high, terms_low = split(near_terms)
+    near_parts = jnp.concatenate([terms_high, terms_low], axis=0)
+    near_sums = 0.0
+    for g in each:
+        reach = []
+        for x, z, side in np.ndindex(2, 2, kept_sides):
+            start = ((2 * z + x) * kind + side) * owned
+            reach.append(picks[g][start : start + owned])
+        near_sums = near_sums + mm_nt(near_parts[:, lanes[g]], jnp.concatenate(reach, axis=0))
     center_sums = mm_nt(
         jnp.concatenate(split(center_terms), axis=0), slot_half[:owned, :own_pairs]
     )

time: 26.9 us -> 28 us (1.041)
  Pallas kernels: 8.81 us -> 9.9 us
    pallas_call x1, Pallas kernels: 5.63 us -> 6.72 us  [local(): pl.pallas_call(functools.partial(force_kernel, kind, nbr), out_shape=(jax...]
where the time goes in v17:
time: 28 us; the launch traced here: 27.7 us
  Pallas kernels  9.9 us (35%)
  starting transfers between devices  8.69 us (31%)
  waiting for transfers between devices  8.38 us (30%)
  between operations  0.67 us (2%)
    ppermute x6, starting transfers between devices, moved(): return lax.ppermute(array, names, route)  8.69 us
    ppermute x6, waiting for transfers between devices, moved(): return lax.ppermute(array, names, route)  8.38 us
    pallas_call x1, Pallas kernels, local(): pl.pallas_call(functools.partial(force_kernel, kind, nbr), out_shape=(jax...  6.72 us
    pallas_call x1, Pallas kernels, local(): pl.pallas_call(fetch_kernel, out_shape=(*(jax.ShapeDtypeStruct(w.shape, F...  1.35 us
    pallas_call x1, Pallas kernels, local(): pl.pallas_call(functools.partial(pack_kernel, kind), out_shape=(payload,...  1.08 us
    pallas_call x1, Pallas kernels, local(): pl.pallas_call(finish_kernel, out_shape=(jax.ShapeDtypeStruct(species.sha...  0.75 us
  transfers between devices with their start and end apart: 6, of which 5 were waited for; matrix products, arithmetic and copies ran while one was open for 0% of the time, Pallas kernels for 5%

profile of v17, /device:TPU:0, one launch (start us, length us, event | category | flops | bytes accessed | tf_op | source)
XLA Modules:
  0.0 27.7 jit_solution(15679493197416365957)
XLA Ops:
  0.6 1.1 %pack_payload.1 = (f32[40,128]{1,0:T(8,128)S(1)}, f32[40,128]{1,0:T(8,128)S(1)}) custom-call(f32[3,2,1,2,8]{4,3,2,1,0:T(2,128)} %positions_hbm.1, f32[32,128]{1,0:T(8,128)} %bitcast.4, s32[2,1,2,8]{3,2,1,0:T(2,128)} %species_hbm.3, s32[1,32]{1,0:T(1,128)} %bitcast.5, s32[32,32]{1,0:T(8,128)} %neighbours_hbm.1, f32[5]{0:T(128)} %scale_hbm.1), custom_call_target="tpu_custom_call" | custom-call | tf_op jit(solution)/shard_map/pack_payload/pallas_call | solution.py:623
  1.7 4.0 %collective-permute-start.2 = (f32[40,128]{1,0:T(8,128)S(1)}, f32[40,128]{1,0:T(8,128)S(1)}, u32[]{:S(2)}, u32[]{:S(2)}) collective-permute-start(f32[40,128]{1,0:T(8,128)S(1)} %get-tuple-element.19), channel_id=1, source_target_pairs={{0,12},{4,8},{8,20},{12,16},{16,28},{20,24},{24,4},{28,0},{1,13},{... | collective-permute-start | bytes 61448 | tf_op jit(solution)/shard_map/ppermute | solution.py:617
  5.7 1.6 %collective-permute-start = (f32[40,128]{1,0:T(8,128)S(1)}, f32[40,128]{1,0:T(8,128)S(1)}, u32[]{:S(2)}, u32[]{:S(2)}) collective-permute-start(f32[40,128]{1,0:T(8,128)S(1)} %get-tuple-element.19), channel_id=1, source_target_pairs={{0,8},{8,16},{16,24},{24,0},{1,9},{9,17},{17,25},{25,1},{2,10},{10... | collective-permute-start | bytes 61448 | tf_op jit(solution)/shard_map/ppermute | solution.py:617
  7.3 0.5 %collective-permute-start.1 = (f32[40,128]{1,0:T(8,128)S(1)}, f32[40,128]{1,0:T(8,128)S(1)}, u32[]{:S(2)}, u32[]{:S(2)}) collective-permute-start(f32[40,128]{1,0:T(8,128)S(1)} %get-tuple-element.18.here_ref), channel_id=1, source_target_pairs={{0,4},{4,0},{1,5},{5,1},{2,6},{6,2},{3,7},{7,3},{8,12},{12,8},{9,1... | collective-permute-start | bytes 61448 | tf_op jit(solution)/shard_map/ppermute | solution.py:617
  7.8 1.8 %collective-permute-done.2.refs_1_ = f32[40,128]{1,0:T(8,128)S(1)} collective-permute-done((f32[40,128]{1,0:T(8,128)S(1)}, f32[40,128]{1,0:T(8,128)S(1)}, u32[]{:S(2)}, u32[]{:S(2)}) %collective-permute-start.2) | collective-permute-done | bytes 20512 | tf_op jit(solution)/shard_map/ppermute | solution.py:617
  9.6 1.7 %collective-permute-done.last_x_ref = f32[40,128]{1,0:T(8,128)S(1)} collective-permute-done((f32[40,128]{1,0:T(8,128)S(1)}, f32[40,128]{1,0:T(8,128)S(1)}, u32[]{:S(2)}, u32[]{:S(2)}) %collective-permute-start) | collective-permute-done | bytes 20512 | tf_op jit(solution)/shard_map/ppermute | solution.py:617
  11.3 0.0 collective-permute-done.1.refs_0_
  11.3 0.1 collective-permute-start.3
  11.4 1.3 %fetch_weights.1 = (f32[128,128]{1,0:T(8,128)S(1)}, f32[128,128]{1,0:T(8,128)S(1)}, f32[8,128]{1,0:T(8,128)S(1)}, f32[3,128]{1,0:T(4,128)S(1)}, f32[128,256]{1,0...) custom-call(s32[2,1,2,8]{3,2,1,0:T(2,128)} %species_hbm.3, s32[1,32]{1,0:T(1,128)} %bitcast.6, ...), custom_call_target="tpu_custom_call" | custom-call | tf_op jit(solution)/shard_map/fetch_weights/pallas_call | solution.py:658
  12.7 0.7 %collective-permute-done.3.refs_2_ = f32[160,128]{1,0:T(8,128)S(1)} collective-permute-done((f32[160,128]{1,0:T(8,128)S(1)}, f32[160,128]{1,0:T(8,128)S(1)}, u32[]{:S(2)}, u32[]{:S(2)}) %collective-permute-start.3) | collective-permute-done | bytes 81952 | tf_op jit(solution)/shard_map/ppermute | solution.py:617
  13.4 6.7 %pair_forces.1 = (f32[16,64]{1,0:T(8,128)S(1)}, f32[16,64]{1,0:T(8,128)S(1)}) custom-call(f32[40,128]{1,0:T(8,128)S(1)} %get-tuple-element.18.here_ref, f32[40,128]{1,0:T(8,128)S(1)} %collective-permute-done.last_x_ref, f32[40,128]{1,0:T(8,128)S(1)} %collective-permute-done.1.refs_0_, f32[40,128]{1,0:T(8,128)S(1)} %collective-permute-done.2.refs_1_, ...), custom_call_target="tpu_custom_call" | custom-call | tf_op jit(solution)/shard_map/pair_forces/pallas_call | solution.py:683
  20.2 2.0 %collective-permute-start.4 = (f32[16,64]{1,0:T(8,128)S(1)}, f32[16,64]{1,0:T(8,128)S(1)}, u32[]{:S(2)}, u32[]{:S(2)}) collective-permute-start(f32[16,64]{1,0:T(8,128)S(1)} %get-tuple-element.28), channel_id=1, source_target_pairs={{0,24},{8,0},{16,8},{24,16},{1,25},{9,1},{17,9},{25,17},{2,26},{10... | collective-permute-start | bytes 12296 | tf_op jit(solution)/shard_map/ppermute | solution.py:617
  22.1 1.7 %collective-permute-done.4 = f32[16,64]{1,0:T(8,128)S(1)} collective-permute-done((f32[16,64]{1,0:T(8,128)S(1)}, f32[16,64]{1,0:T(8,128)S(1)}, u32[]{:S(2)}, u32[]{:S(2)}) %collective-permute-start.4) | collective-permute-done | bytes 4128 | tf_op jit(solution)/shard_map/ppermute | solution.py:617
  23.8 0.1 slice.4
  23.9 0.5 %collective-permute-start.5 = (f32[16,32]{1,0:T(8,128)S(1)}, f32[16,32]{1,0:T(8,128)S(1)}, u32[]{:S(2)}, u32[]{:S(2)}) collective-permute-start(f32[16,32]{1,0:T(8,128)S(1)} %slice.4), channel_id=1, source_target_pairs={{0,1},{1,2},{2,3},{3,0},{4,5},{5,6},{6,7},{7,4},{8,9},{9,10},{10,1... | collective-permute-start | bytes 6152 | tf_op jit(solution)/shard_map/ppermute | solution.py:617
  24.4 2.5 %collective-permute-done.5.refs_0_ = f32[16,32]{1,0:T(8,128)S(1)} collective-permute-done((f32[16,32]{1,0:T(8,128)S(1)}, f32[16,32]{1,0:T(8,128)S(1)}, u32[]{:S(2)}, u32[]{:S(2)}) %collective-permute-start.5) | collective-permute-done | bytes 2080 | tf_op jit(solution)/shard_map/ppermute | solution.py:617
  27.0 0.8 %write_outputs.1 = (f32[2,1,2,8]{3,2,1,0:T(2,128)}, f32[3,2,1,2,8]{4,3,2,1,0:T(2,128)}, f32[2,1,2,8,9]{4,3,2,1,0:T(8,128)}) custom-call(f32[16,64]{1,0:T(8,128)S(1)} %add.23.mine_ref, f32[1,32]{1,0:T(1,128)S(1)} %get-tuple-element.29.shift_row_ref, f32[16,32]{1,0:T(8,128)S(1)} %collective-permute-done.5.refs_0_), custom_call_target="tpu_custom_call" | custom-call | tf_op jit(solution)/shard_map/write_outputs/pallas_call | solution.py:709
  (2 shorter events, 0.0 us)
Async XLA Ops:
  1.7 7.9 %collective-permute-start.2 = (f32[40,128]{1,0:T(8,128)S(1)}, f32[40,128]{1,0:T(8,128)S(1)}, u32[]{:S(2)}, u32[]{:S(2)}) collective-permute-start(f32[40,128]{1,0:T(8,128)S(1)} %get-tuple-element.19), channel_id=1, source_target_pairs={{0,12},{4,8},{8,20},{12,16},{16,28},{20,24},{24,4},{28,0},{1,13},{... | collective-permute-start | bytes 61448 | tf_op jit(solution)/shard_map/ppermute | solution.py:617
  5.7 5.6 %collective-permute-start = (f32[40,128]{1,0:T(8,128)S(1)}, f32[40,128]{1,0:T(8,128)S(1)}, u32[]{:S(2)}, u32[]{:S(2)}) collective-permute-start(f32[40,128]{1,0:T(8,128)S(1)} %get-tuple-element.19), channel_id=1, source_target_pairs={{0,8},{8,16},{16,24},{24,0},{1,9},{9,17},{17,25},{25,1},{2,10},{10... | collective-permute-start | bytes 61448 | tf_op jit(solution)/shard_map/ppermute | solution.py:617
  7.3 4.0 %collective-permute-start.1 = (f32[40,128]{1,0:T(8,128)S(1)}, f32[40,128]{1,0:T(8,128)S(1)}, u32[]{:S(2)}, u32[]{:S(2)}) collective-permute-start(f32[40,128]{1,0:T(8,128)S(1)} %get-tuple-element.18.here_ref), channel_id=1, source_target_pairs={{0,4},{4,0},{1,5},{5,1},{2,6},{6,2},{3,7},{7,3},{8,12},{12,8},{9,1... | collective-permute-start | bytes 61448 | tf_op jit(solution)/shard_map/ppermute | solution.py:617
  11.3 2.1 %collective-permute-start.3 = (f32[160,128]{1,0:T(8,128)S(1)}, f32[160,128]{1,0:T(8,128)S(1)}, u32[]{:S(2)}, u32[]{:S(2)}) collective-permute-start(f32[160,128]{1,0:T(8,128)S(1)} %pad_add_fusion), channel_id=1, source_target_pairs={{0,3},{1,0},{2,1},{3,2},{4,7},{5,4},{6,5},{7,6},{8,11},{9,8},{10,9... | collective-permute-start | bytes 245768 | tf_op jit(solution)/shard_map/ppermute | solution.py:617
  20.2 3.7 %collective-permute-start.4 = (f32[16,64]{1,0:T(8,128)S(1)}, f32[16,64]{1,0:T(8,128)S(1)}, u32[]{:S(2)}, u32[]{:S(2)}) collective-permute-start(f32[16,64]{1,0:T(8,128)S(1)} %get-tuple-element.28), channel_id=1, source_target_pairs={{0,24},{8,0},{16,8},{24,16},{1,25},{9,1},{17,9},{25,17},{2,26},{10... | collective-permute-start | bytes 12296 | tf_op jit(solution)/shard_map/ppermute | solution.py:617
  23.9 3.1 %collective-permute-start.5 = (f32[16,32]{1,0:T(8,128)S(1)}, f32[16,32]{1,0:T(8,128)S(1)}, u32[]{:S(2)}, u32[]{:S(2)}) collective-permute-start(f32[16,32]{1,0:T(8,128)S(1)} %slice.4), channel_id=1, source_target_pairs={{0,1},{1,2},{2,3},{3,0},{4,5},{5,6},{6,7},{7,4},{8,9},{9,10},{10,1... | collective-permute-start | bytes 6152 | tf_op jit(solution)/shard_map/ppermute | solution.py:617

commit v18 on v16

--- a/solution.py
+++ b/solution.py
@@ -14,6 +14,7 @@
 CELL_SIDE = 4.6
 ROOT_HALF = 0.7071067811865476
 GROUP = 8
+TEAM = 16
 ORDERS = 16
 LEVELS = (0, 1, 1, 1, 2, 2, 2, 2, 2)
 SITES = 8
@@ -343,7 +344,7 @@
     )
 
     path_rows = jnp.concatenate(
-        [jnp.broadcast_to(path_weight_ref[l : l + 1, :], (GROUP, width)) for l in LEVELS], axis=0
+        [jnp.broadcast_to(path_weight_ref[l : l + 1, :], (TEAM, width)) for l in LEVELS], axis=0
     ) * (1.0 / root_count)
     out_column = jnp.transpose(jnp.broadcast_to(out_weight_ref[...], (width, width)))
     out_column = jnp.concatenate([out_column] * (pairs // width), axis=1)
@@ -351,12 +352,13 @@
     site_ids = lax.broadcasted_iota(jnp.int32, (known, pairs), 0)
     slot_ids = lax.broadcasted_iota(jnp.int32, (centers, pairs), 0)
     slot_row = lax.broadcasted_iota(jnp.int32, (1, pairs), 1) // nbr
-    group_lane = lax.broadcasted_iota(jnp.int32, (GROUP, pairs), 1) // nbr % GROUP
-    group_mask = group_lane == lax.broadcasted_iota(jnp.int32, (GROUP, pairs), 0)
+    group_lane = lax.broadcasted_iota(jnp.int32, (TEAM, pairs), 1) // nbr % TEAM
+    group_mask = group_lane == lax.broadcasted_iota(jnp.int32, (TEAM, pairs), 0)
     group_mask = jnp.where(group_mask, 1.0, 0.0)
-    tall = len(LEVELS) * GROUP
+    tall = len(LEVELS) * TEAM
+    reach = TEAM * nbr
     order = lax.broadcasted_iota(jnp.int32, (radial, pairs), 0).astype(F32) + 1.0
-    lanes = [slice(g * span, (g + 1) * span) for g in range(groups)]
+    lanes = [slice(i, i + reach) for i in range(0, pairs, reach)]
 
     pick = jnp.where(site_ids == near_row, 1.0, 0.0)
     pick_half = pick.astype(BF16)
@@ -476,7 +478,7 @@
             jnp.concatenate([dinner_high[:, cut], env_high[:, cut]], axis=0),
             jnp.concatenate([dinner_low[:, cut], env_low[:, cut]], axis=0),
         )
-        d_block = d_block.reshape(len(LEVELS), GROUP, span) * group_mask[None, :, cut]
+        d_block = d_block.reshape(len(LEVELS), TEAM, reach) * group_mask[None, :, cut]
         d_angular.append(jnp.sum(d_block, axis=1))
     d_angular = jnp.concatenate(d_angular, axis=1)
 
@@ -514,12 +516,12 @@
     center_rows = [r[:, :own_pairs] for r in center_rows] + [pair_energy]
     center_rows.append(jnp.zeros((ORDERS - 13, own_pairs), F32))
     center_terms = jnp.concatenate(center_rows, axis=0)
-    reach = []
+    rows = []
     for x, z, side in np.ndindex(2, 2, kept_sides):
         start = ((2 * z + x) * kind + side) * owned
-        reach.append(pick_half[start : start + owned])
-    reach = jnp.concatenate(reach, axis=0)
-    near_sums = mm_nt(jnp.concatenate(split(near_terms), axis=0), reach)
+        rows.append(pick_half[start : start + owned])
+    rows = jnp.concatenate(rows, axis=0)
+    near_sums = mm_nt(jnp.concatenate(split(near_terms), axis=0), rows)
     center_sums = mm_nt(
         jnp.concatenate(split(center_terms), axis=0), slot_half[:owned, :own_pairs]
     )

time: 26.9 us -> 27.4 us (1.019)
  Pallas kernels: 8.81 us -> 9.32 us
    pallas_call x1, Pallas kernels: 5.63 us -> 6.14 us  [local(): pl.pallas_call(functools.partial(force_kernel, kind, nbr), out_shape=(jax...]
where the time goes in v18:
time: 27.4 us; the launch traced here: 27.1 us
  Pallas kernels  9.32 us (34%)
  starting transfers between devices  8.7 us (32%)
  waiting for transfers between devices  8.38 us (31%)
  between operations  0.67 us (2%)
    ppermute x6, starting transfers between devices, moved(): return lax.ppermute(array, names, route)  8.7 us
    ppermute x6, waiting for transfers between devices, moved(): return lax.ppermute(array, names, route)  8.38 us
    pallas_call x1, Pallas kernels, local(): pl.pallas_call(functools.partial(force_kernel, kind, nbr), out_shape=(jax...  6.14 us
    pallas_call x1, Pallas kernels, local(): pl.pallas_call(fetch_kernel, out_shape=(*(jax.ShapeDtypeStruct(w.shape, F...  1.35 us
    pallas_call x1, Pallas kernels, local(): pl.pallas_call(functools.partial(pack_kernel, kind), out_shape=(payload,...  1.08 us
    pallas_call x1, Pallas kernels, local(): pl.pallas_call(finish_kernel, out_shape=(jax.ShapeDtypeStruct(species.sha...  0.75 us
  transfers between devices with their start and end apart: 6, of which 5 were waited for; matrix products, arithmetic and copies ran while one was open for 0% of the time, Pallas kernels for 5%

profile of v18, /device:TPU:0, one launch (start us, length us, event | category | flops | bytes accessed | tf_op | source)
XLA Modules:
  0.0 27.1 jit_solution(6358303544483957778)
XLA Ops:
  0.6 1.1 %pack_payload.1 = (f32[40,128]{1,0:T(8,128)S(1)}, f32[40,128]{1,0:T(8,128)S(1)}) custom-call(f32[3,2,1,2,8]{4,3,2,1,0:T(2,128)} %positions_hbm.1, f32[32,128]{1,0:T(8,128)} %bitcast.4, s32[2,1,2,8]{3,2,1,0:T(2,128)} %species_hbm.3, s32[1,32]{1,0:T(1,128)} %bitcast.5, s32[32,32]{1,0:T(8,128)} %neighbours_hbm.1, f32[5]{0:T(128)} %scale_hbm.1), custom_call_target="tpu_custom_call" | custom-call | tf_op jit(solution)/shard_map/pack_payload/pallas_call | solution.py:603
  1.7 4.0 %collective-permute-start.2 = (f32[40,128]{1,0:T(8,128)S(1)}, f32[40,128]{1,0:T(8,128)S(1)}, u32[]{:S(2)}, u32[]{:S(2)}) collective-permute-start(f32[40,128]{1,0:T(8,128)S(1)} %get-tuple-element.19), channel_id=1, source_target_pairs={{0,12},{4,8},{8,20},{12,16},{16,28},{20,24},{24,4},{28,0},{1,13},{... | collective-permute-start | bytes 61448 | tf_op jit(solution)/shard_map/ppermute | solution.py:597
  5.7 1.6 %collective-permute-start = (f32[40,128]{1,0:T(8,128)S(1)}, f32[40,128]{1,0:T(8,128)S(1)}, u32[]{:S(2)}, u32[]{:S(2)}) collective-permute-start(f32[40,128]{1,0:T(8,128)S(1)} %get-tuple-element.19), channel_id=1, source_target_pairs={{0,8},{8,16},{16,24},{24,0},{1,9},{9,17},{17,25},{25,1},{2,10},{10... | collective-permute-start | bytes 61448 | tf_op jit(solution)/shard_map/ppermute | solution.py:597
  7.3 0.5 %collective-permute-start.1 = (f32[40,128]{1,0:T(8,128)S(1)}, f32[40,128]{1,0:T(8,128)S(1)}, u32[]{:S(2)}, u32[]{:S(2)}) collective-permute-start(f32[40,128]{1,0:T(8,128)S(1)} %get-tuple-element.18.here_ref), channel_id=1, source_target_pairs={{0,4},{4,0},{1,5},{5,1},{2,6},{6,2},{3,7},{7,3},{8,12},{12,8},{9,1... | collective-permute-start | bytes 61448 | tf_op jit(solution)/shard_map/ppermute | solution.py:597
  7.8 1.8 %collective-permute-done.2.refs_1_ = f32[40,128]{1,0:T(8,128)S(1)} collective-permute-done((f32[40,128]{1,0:T(8,128)S(1)}, f32[40,128]{1,0:T(8,128)S(1)}, u32[]{:S(2)}, u32[]{:S(2)}) %collective-permute-start.2) | collective-permute-done | bytes 20512 | tf_op jit(solution)/shard_map/ppermute | solution.py:597
  9.6 1.7 %collective-permute-done.last_x_ref = f32[40,128]{1,0:T(8,128)S(1)} collective-permute-done((f32[40,128]{1,0:T(8,128)S(1)}, f32[40,128]{1,0:T(8,128)S(1)}, u32[]{:S(2)}, u32[]{:S(2)}) %collective-permute-start) | collective-permute-done | bytes 20512 | tf_op jit(solution)/shard_map/ppermute | solution.py:597
  11.3 0.0 collective-permute-done.1.refs_0_
  11.3 0.1 collective-permute-start.3
  11.4 1.3 %fetch_weights.1 = (f32[128,128]{1,0:T(8,128)S(1)}, f32[128,128]{1,0:T(8,128)S(1)}, f32[8,128]{1,0:T(8,128)S(1)}, f32[3,128]{1,0:T(4,128)S(1)}, f32[128,256]{1,0...) custom-call(s32[2,1,2,8]{3,2,1,0:T(2,128)} %species_hbm.3, s32[1,32]{1,0:T(1,128)} %bitcast.6, ...), custom_call_target="tpu_custom_call" | custom-call | tf_op jit(solution)/shard_map/fetch_weights/pallas_call | solution.py:638
  12.7 0.7 %collective-permute-done.3.refs_2_ = f32[160,128]{1,0:T(8,128)S(1)} collective-permute-done((f32[160,128]{1,0:T(8,128)S(1)}, f32[160,128]{1,0:T(8,128)S(1)}, u32[]{:S(2)}, u32[]{:S(2)}) %collective-permute-start.3) | collective-permute-done | bytes 81952 | tf_op jit(solution)/shard_map/ppermute | solution.py:597
  13.4 6.1 %pair_forces.1 = (f32[16,64]{1,0:T(8,128)S(1)}, f32[16,64]{1,0:T(8,128)S(1)}) custom-call(f32[40,128]{1,0:T(8,128)S(1)} %get-tuple-element.18.here_ref, f32[40,128]{1,0:T(8,128)S(1)} %collective-permute-done.last_x_ref, f32[40,128]{1,0:T(8,128)S(1)} %collective-permute-done.1.refs_0_, f32[40,128]{1,0:T(8,128)S(1)} %collective-permute-done.2.refs_1_, ...), custom_call_target="tpu_custom_call" | custom-call | tf_op jit(solution)/shard_map/pair_forces/pallas_call | solution.py:663
  19.6 2.0 %collective-permute-start.4 = (f32[16,64]{1,0:T(8,128)S(1)}, f32[16,64]{1,0:T(8,128)S(1)}, u32[]{:S(2)}, u32[]{:S(2)}) collective-permute-start(f32[16,64]{1,0:T(8,128)S(1)} %get-tuple-element.28), channel_id=1, source_target_pairs={{0,24},{8,0},{16,8},{24,16},{1,25},{9,1},{17,9},{25,17},{2,26},{10... | collective-permute-start | bytes 12296 | tf_op jit(solution)/shard_map/ppermute | solution.py:597
  21.6 1.7 %collective-permute-done.4 = f32[16,64]{1,0:T(8,128)S(1)} collective-permute-done((f32[16,64]{1,0:T(8,128)S(1)}, f32[16,64]{1,0:T(8,128)S(1)}, u32[]{:S(2)}, u32[]{:S(2)}) %collective-permute-start.4) | collective-permute-done | bytes 4128 | tf_op jit(solution)/shard_map/ppermute | solution.py:597
  23.2 0.1 slice.4
  23.3 0.5 %collective-permute-start.5 = (f32[16,32]{1,0:T(8,128)S(1)}, f32[16,32]{1,0:T(8,128)S(1)}, u32[]{:S(2)}, u32[]{:S(2)}) collective-permute-start(f32[16,32]{1,0:T(8,128)S(1)} %slice.4), channel_id=1, source_target_pairs={{0,1},{1,2},{2,3},{3,0},{4,5},{5,6},{6,7},{7,4},{8,9},{9,10},{10,1... | collective-permute-start | bytes 6152 | tf_op jit(solution)/shard_map/ppermute | solution.py:597
  23.9 2.5 %collective-permute-done.5.refs_0_ = f32[16,32]{1,0:T(8,128)S(1)} collective-permute-done((f32[16,32]{1,0:T(8,128)S(1)}, f32[16,32]{1,0:T(8,128)S(1)}, u32[]{:S(2)}, u32[]{:S(2)}) %collective-permute-start.5) | collective-permute-done | bytes 2080 | tf_op jit(solution)/shard_map/ppermute | solution.py:597
  26.4 0.8 %write_outputs.1 = (f32[2,1,2,8]{3,2,1,0:T(2,128)}, f32[3,2,1,2,8]{4,3,2,1,0:T(2,128)}, f32[2,1,2,8,9]{4,3,2,1,0:T(8,128)}) custom-call(f32[16,64]{1,0:T(8,128)S(1)} %add.23.mine_ref, f32[1,32]{1,0:T(1,128)S(1)} %get-tuple-element.29.shift_row_ref, f32[16,32]{1,0:T(8,128)S(1)} %collective-permute-done.5.refs_0_), custom_call_target="tpu_custom_call" | custom-call | tf_op jit(solution)/shard_map/write_outputs/pallas_call | solution.py:689
  (2 shorter events, 0.0 us)
Async XLA Ops:
  1.7 7.9 %collective-permute-start.2 = (f32[40,128]{1,0:T(8,128)S(1)}, f32[40,128]{1,0:T(8,128)S(1)}, u32[]{:S(2)}, u32[]{:S(2)}) collective-permute-start(f32[40,128]{1,0:T(8,128)S(1)} %get-tuple-element.19), channel_id=1, source_target_pairs={{0,12},{4,8},{8,20},{12,16},{16,28},{20,24},{24,4},{28,0},{1,13},{... | collective-permute-start | bytes 61448 | tf_op jit(solution)/shard_map/ppermute | solution.py:597
  5.7 5.6 %collective-permute-start = (f32[40,128]{1,0:T(8,128)S(1)}, f32[40,128]{1,0:T(8,128)S(1)}, u32[]{:S(2)}, u32[]{:S(2)}) collective-permute-start(f32[40,128]{1,0:T(8,128)S(1)} %get-tuple-element.19), channel_id=1, source_target_pairs={{0,8},{8,16},{16,24},{24,0},{1,9},{9,17},{17,25},{25,1},{2,10},{10... | collective-permute-start | bytes 61448 | tf_op jit(solution)/shard_map/ppermute | solution.py:597
  7.3 4.0 %collective-permute-start.1 = (f32[40,128]{1,0:T(8,128)S(1)}, f32[40,128]{1,0:T(8,128)S(1)}, u32[]{:S(2)}, u32[]{:S(2)}) collective-permute-start(f32[40,128]{1,0:T(8,128)S(1)} %get-tuple-element.18.here_ref), channel_id=1, source_target_pairs={{0,4},{4,0},{1,5},{5,1},{2,6},{6,2},{3,7},{7,3},{8,12},{12,8},{9,1... | collective-permute-start | bytes 61448 | tf_op jit(solution)/shard_map/ppermute | solution.py:597
  11.3 2.1 %collective-permute-start.3 = (f32[160,128]{1,0:T(8,128)S(1)}, f32[160,128]{1,0:T(8,128)S(1)}, u32[]{:S(2)}, u32[]{:S(2)}) collective-permute-start(f32[160,128]{1,0:T(8,128)S(1)} %pad_add_fusion), channel_id=1, source_target_pairs={{0,3},{1,0},{2,1},{3,2},{4,7},{5,4},{6,5},{7,6},{8,11},{9,8},{10,9... | collective-permute-start | bytes 245768 | tf_op jit(solution)/shard_map/ppermute | solution.py:597
  19.6 3.7 %collective-permute-start.4 = (f32[16,64]{1,0:T(8,128)S(1)}, f32[16,64]{1,0:T(8,128)S(1)}, u32[]{:S(2)}, u32[]{:S(2)}) collective-permute-start(f32[16,64]{1,0:T(8,128)S(1)} %get-tuple-element.28), channel_id=1, source_target_pairs={{0,24},{8,0},{16,8},{24,16},{1,25},{9,1},{17,9},{25,17},{2,26},{10... | collective-permute-start | bytes 12296 | tf_op jit(solution)/shard_map/ppermute | solution.py:597
  23.3 3.1 %collective-permute-start.5 = (f32[16,32]{1,0:T(8,128)S(1)}, f32[16,32]{1,0:T(8,128)S(1)}, u32[]{:S(2)}, u32[]{:S(2)}) collective-permute-start(f32[16,32]{1,0:T(8,128)S(1)} %slice.4), channel_id=1, source_target_pairs={{0,1},{1,2},{2,3},{3,0},{4,5},{5,6},{6,7},{7,4},{8,9},{9,10},{10,1... | collective-permute-start | bytes 6152 | tf_op jit(solution)/shard_map/ppermute | solution.py:597

commit v19 on v16

--- a/solution.py
+++ b/solution.py
@@ -61,12 +61,12 @@
     return product[:half] + product[half:]
 
 
-def half_depth(weights, value):
-    return folded(mm(weights, jnp.concatenate(split(value), axis=0)))
-
-
-def full_depth(both, high, value_high, value_low):
-    return folded(mm(both, value_high)) + mm(high, value_low)
+def three(high, low):
+    return jnp.concatenate([high, low, high], axis=1)
+
+
+def deep(weights, value_high, value_low):
+    return mm(weights, jnp.concatenate([value_high, value_high, value_low], axis=0))
 
 
 def sin_cos_pi(turns):
@@ -315,15 +315,13 @@
     place_parts = place_rows(coords)
     center_parts = place_rows(jnp.concatenate(center_coords, axis=0))
 
-    value_rows = stacked(*split(jnp.transpose(value_weight_ref[...])))
-    latent_high_t, latent_low_t = split(0.5 * jnp.transpose(latent_weight_ref[...]))
-    latent_both_t = jnp.concatenate([latent_high_t, latent_low_t], axis=0)
-    latent_rows = stacked(*split(latent_weight_ref[...] * out_weight_ref[...]))
-    value_high, value_low = split(value_weight_ref[...])
-    value_both = jnp.concatenate([value_high, value_low], axis=0)
+    value_rows = three(*split(jnp.transpose(value_weight_ref[...])))
+    latent_t = three(*split(0.5 * jnp.transpose(latent_weight_ref[...])))
+    latent_rows = three(*split(latent_weight_ref[...] * out_weight_ref[...]))
+    value_plain = three(*split(value_weight_ref[...]))
     basis_t = jnp.transpose(basis_weight_ref[...])
     basis_high_t, basis_low_t = split(0.5 * basis_t)
-    basis_rows = stacked(*split(basis_weight_ref[...]))
+    basis_rows = three(*split(basis_weight_ref[...]))
 
     def project(weight, rows):
         weight = stacked(*split(jnp.transpose(weight)))
@@ -333,9 +331,8 @@
     own_t = project(center_weight_ref[...], center_feats)
     near_high, near_low = split(0.5 * near_t)
     own_high, own_low = split(0.5 * own_t)
-    near_lookup = jnp.concatenate([near_high, near_low], axis=0)
-    rest_lookup = jnp.concatenate(
-        [own_high, own_low, basis_high_t, basis_high_t, basis_low_t], axis=1
+    lookup = jnp.concatenate(
+        [near_high, near_low, own_high, own_low, basis_high_t, basis_high_t, basis_low_t], axis=1
     )
     scale_rows = jnp.concatenate(scales, axis=0)
     scale_parts = jnp.concatenate(
@@ -362,7 +359,10 @@
     pick_half = pick.astype(BF16)
     slot_half = jnp.where(slot_ids == slot_row, 1.0, 0.0).astype(BF16)
 
-    moved = mm(place_parts, pick_half) - mm(center_parts, slot_half)
+    moved = mm(
+        jnp.concatenate([place_parts, -center_parts], axis=1),
+        jnp.concatenate([pick_half, slot_half], axis=0),
+    )
     moved = moved[: 3 * sites] + moved[3 * sites : 6 * sites] + moved[6 * sites :]
     dx = jnp.where(live, jnp.sum(moved[:sites], axis=0, keepdims=True), 6.0)
     dy = jnp.sum(moved[sites : 2 * sites], axis=0, keepdims=True) + CELL_SIDE * side_y
@@ -414,14 +414,15 @@
 
     basis_high, basis_low = halves(basis)
     basis_rest = jnp.concatenate([basis_high, basis_low, basis_high], axis=0).astype(BF16)
-    before = folded(mm(near_lookup, pick_half)) + mm(
-        rest_lookup, jnp.concatenate([slot_half, slot_half, basis_rest], axis=0)
+    before = mm(
+        lookup,
+        jnp.concatenate([pick_half, pick_half, slot_half, slot_half, basis_rest], axis=0),
     )
     gate = 1.0 + jnp.tanh(before)
     active = before * gate
     latent = weight * active
     latent_high, latent_low = split(latent)
-    mixed = folded(mm(value_rows, jnp.concatenate([latent_high, latent_low], axis=0)))
+    mixed = deep(value_rows, latent_high, latent_low)
     values = mixed[:width]
     env_high, env_low = split(mixed[width:])
 
@@ -446,9 +447,8 @@
     inner = over_orders(weighted)
     scalars = values * inner
     scalars_high, scalars_low = split(scalars)
-    z = full_depth(
-        latent_both_t,
-        latent_high_t,
+    z = deep(
+        latent_t,
         jnp.concatenate([latent_high, scalars_high], axis=0),
         jnp.concatenate([latent_low, scalars_low], axis=0),
     )
@@ -460,7 +460,7 @@
     )
     pair_energy = (active_sum + update_sum[:, :own_pairs]) * (pull * weight)[:, :own_pairs]
     d_z = (0.5 * pull * weight) * (z_gate + update * (2.0 - z_gate))
-    spread_back = half_depth(latent_rows, d_z)
+    spread_back = deep(latent_rows, *split(d_z))
     d_scalars = spread_back[width:]
     d_values = d_scalars * inner
     dinner_high, dinner_low = split(d_scalars * values)
@@ -470,9 +470,8 @@
     d_angular = []
     for g, cut in enumerate(lanes):
         sides_high, sides_low = halves(jnp.concatenate([weighted[g], d_embed[g]], axis=1))
-        d_block = full_depth(
-            jnp.concatenate([sides_high, sides_low], axis=0).astype(BF16),
-            sides_high.astype(BF16),
+        d_block = deep(
+            three(sides_high.astype(BF16), sides_low.astype(BF16)),
             jnp.concatenate([dinner_high[:, cut], env_high[:, cut]], axis=0),
             jnp.concatenate([dinner_low[:, cut], env_low[:, cut]], axis=0),
         )
@@ -482,13 +481,13 @@
 
     mixed_high, mixed_low = split(jnp.concatenate([d_values, d_env], axis=0))
     d_latent = (
-        full_depth(value_both, value_high, mixed_high, mixed_low)
+        deep(value_plain, mixed_high, mixed_low)
         + spread_back[:width]
         + pull * out_column
     )
     d_weight = jnp.sum(d_latent * active, axis=0, keepdims=True) + pull * update_sum
     d_before = d_latent * (gate + active * (2.0 - gate))
-    d_basis = half_depth(basis_rows, d_before) * (0.5 * weight)
+    d_basis = deep(basis_rows, *split(d_before)) * (0.5 * weight)
 
     d_length = jnp.sum(d_basis * basis_slope, axis=0, keepdims=True) + d_weight * slope * (
         1.0 / CUTOFF

time: 26.9 us -> 26.9 us (level)
  no operation moved by 1% of the time
where the time goes in v19:
time: 26.9 us; the launch traced here: 26.6 us
  Pallas kernels  8.77 us (33%)
  starting transfers between devices  8.69 us (32%)
  waiting for transfers between devices  8.38 us (31%)
  between operations  0.67 us (2%)
    ppermute x6, starting transfers between devices, moved(): return lax.ppermute(array, names, route)  8.69 us
    ppermute x6, waiting for transfers between devices, moved(): return lax.ppermute(array, names, route)  8.38 us
    pallas_call x1, Pallas kernels, local(): pl.pallas_call(functools.partial(force_kernel, kind, nbr), out_shape=(jax...  5.59 us
    pallas_call x1, Pallas kernels, local(): pl.pallas_call(fetch_kernel, out_shape=(*(jax.ShapeDtypeStruct(w.shape, F...  1.35 us
    pallas_call x1, Pallas kernels, local(): pl.pallas_call(functools.partial(pack_kernel, kind), out_shape=(payload,...  1.08 us
    pallas_call x1, Pallas kernels, local(): pl.pallas_call(finish_kernel, out_shape=(jax.ShapeDtypeStruct(species.sha...  0.75 us
  transfers between devices with their start and end apart: 6, of which 5 were waited for; matrix products, arithmetic and copies ran while one was open for 0% of the time, Pallas kernels for 5%

profile of v19, /device:TPU:0, one launch (start us, length us, event | category | flops | bytes accessed | tf_op | source)
XLA Modules:
  0.0 26.6 jit_solution(13999821667314057005)
XLA Ops:
  0.6 1.1 %pack_payload.1 = (f32[40,128]{1,0:T(8,128)S(1)}, f32[40,128]{1,0:T(8,128)S(1)}) custom-call(f32[3,2,1,2,8]{4,3,2,1,0:T(2,128)} %positions_hbm.1, f32[32,128]{1,0:T(8,128)} %bitcast.4, s32[2,1,2,8]{3,2,1,0:T(2,128)} %species_hbm.3, s32[1,32]{1,0:T(1,128)} %bitcast.5, s32[32,32]{1,0:T(8,128)} %neighbours_hbm.1, f32[5]{0:T(128)} %scale_hbm.1), custom_call_target="tpu_custom_call" | custom-call | tf_op jit(solution)/shard_map/pack_payload/pallas_call | solution.py:600
  1.7 4.0 %collective-permute-start.2 = (f32[40,128]{1,0:T(8,128)S(1)}, f32[40,128]{1,0:T(8,128)S(1)}, u32[]{:S(2)}, u32[]{:S(2)}) collective-permute-start(f32[40,128]{1,0:T(8,128)S(1)} %get-tuple-element.19), channel_id=1, source_target_pairs={{0,12},{4,8},{8,20},{12,16},{16,28},{20,24},{24,4},{28,0},{1,13},{... | collective-permute-start | bytes 61448 | tf_op jit(solution)/shard_map/ppermute | solution.py:594
  5.7 1.6 %collective-permute-start = (f32[40,128]{1,0:T(8,128)S(1)}, f32[40,128]{1,0:T(8,128)S(1)}, u32[]{:S(2)}, u32[]{:S(2)}) collective-permute-start(f32[40,128]{1,0:T(8,128)S(1)} %get-tuple-element.19), channel_id=1, source_target_pairs={{0,8},{8,16},{16,24},{24,0},{1,9},{9,17},{17,25},{25,1},{2,10},{10... | collective-permute-start | bytes 61448 | tf_op jit(solution)/shard_map/ppermute | solution.py:594
  7.3 0.5 %collective-permute-start.1 = (f32[40,128]{1,0:T(8,128)S(1)}, f32[40,128]{1,0:T(8,128)S(1)}, u32[]{:S(2)}, u32[]{:S(2)}) collective-permute-start(f32[40,128]{1,0:T(8,128)S(1)} %get-tuple-element.18.here_ref), channel_id=1, source_target_pairs={{0,4},{4,0},{1,5},{5,1},{2,6},{6,2},{3,7},{7,3},{8,12},{12,8},{9,1... | collective-permute-start | bytes 61448 | tf_op jit(solution)/shard_map/ppermute | solution.py:594
  7.8 1.8 %collective-permute-done.2.refs_1_ = f32[40,128]{1,0:T(8,128)S(1)} collective-permute-done((f32[40,128]{1,0:T(8,128)S(1)}, f32[40,128]{1,0:T(8,128)S(1)}, u32[]{:S(2)}, u32[]{:S(2)}) %collective-permute-start.2) | collective-permute-done | bytes 20512 | tf_op jit(solution)/shard_map/ppermute | solution.py:594
  9.6 1.7 %collective-permute-done.last_x_ref = f32[40,128]{1,0:T(8,128)S(1)} collective-permute-done((f32[40,128]{1,0:T(8,128)S(1)}, f32[40,128]{1,0:T(8,128)S(1)}, u32[]{:S(2)}, u32[]{:S(2)}) %collective-permute-start) | collective-permute-done | bytes 20512 | tf_op jit(solution)/shard_map/ppermute | solution.py:594
  11.3 0.0 collective-permute-done.1.refs_0_
  11.3 0.1 collective-permute-start.3
  11.4 1.3 %fetch_weights.1 = (f32[128,128]{1,0:T(8,128)S(1)}, f32[128,128]{1,0:T(8,128)S(1)}, f32[8,128]{1,0:T(8,128)S(1)}, f32[3,128]{1,0:T(4,128)S(1)}, f32[128,256]{1,0...) custom-call(s32[2,1,2,8]{3,2,1,0:T(2,128)} %species_hbm.3, s32[1,32]{1,0:T(1,128)} %bitcast.6, ...), custom_call_target="tpu_custom_call" | custom-call | tf_op jit(solution)/shard_map/fetch_weights/pallas_call | solution.py:635
  12.7 0.7 %collective-permute-done.3.refs_2_ = f32[160,128]{1,0:T(8,128)S(1)} collective-permute-done((f32[160,128]{1,0:T(8,128)S(1)}, f32[160,128]{1,0:T(8,128)S(1)}, u32[]{:S(2)}, u32[]{:S(2)}) %collective-permute-start.3) | collective-permute-done | bytes 81952 | tf_op jit(solution)/shard_map/ppermute | solution.py:594
  13.4 5.6 %pair_forces.1 = (f32[16,64]{1,0:T(8,128)S(1)}, f32[16,64]{1,0:T(8,128)S(1)}) custom-call(f32[40,128]{1,0:T(8,128)S(1)} %get-tuple-element.18.here_ref, f32[40,128]{1,0:T(8,128)S(1)} %collective-permute-done.last_x_ref, f32[40,128]{1,0:T(8,128)S(1)} %collective-permute-done.1.refs_0_, f32[40,128]{1,0:T(8,128)S(1)} %collective-permute-done.2.refs_1_, ...), custom_call_target="tpu_custom_call" | custom-call | tf_op jit(solution)/shard_map/pair_forces/pallas_call | solution.py:660
  19.0 2.0 %collective-permute-start.4 = (f32[16,64]{1,0:T(8,128)S(1)}, f32[16,64]{1,0:T(8,128)S(1)}, u32[]{:S(2)}, u32[]{:S(2)}) collective-permute-start(f32[16,64]{1,0:T(8,128)S(1)} %get-tuple-element.28), channel_id=1, source_target_pairs={{0,24},{8,0},{16,8},{24,16},{1,25},{9,1},{17,9},{25,17},{2,26},{10... | collective-permute-start | bytes 12296 | tf_op jit(solution)/shard_map/ppermute | solution.py:594
  21.0 1.7 %collective-permute-done.4 = f32[16,64]{1,0:T(8,128)S(1)} collective-permute-done((f32[16,64]{1,0:T(8,128)S(1)}, f32[16,64]{1,0:T(8,128)S(1)}, u32[]{:S(2)}, u32[]{:S(2)}) %collective-permute-start.4) | collective-permute-done | bytes 4128 | tf_op jit(solution)/shard_map/ppermute | solution.py:594
  22.7 0.1 slice.4
  22.8 0.5 %collective-permute-start.5 = (f32[16,32]{1,0:T(8,128)S(1)}, f32[16,32]{1,0:T(8,128)S(1)}, u32[]{:S(2)}, u32[]{:S(2)}) collective-permute-start(f32[16,32]{1,0:T(8,128)S(1)} %slice.4), channel_id=1, source_target_pairs={{0,1},{1,2},{2,3},{3,0},{4,5},{5,6},{6,7},{7,4},{8,9},{9,10},{10,1... | collective-permute-start | bytes 6152 | tf_op jit(solution)/shard_map/ppermute | solution.py:594
  23.3 2.5 %collective-permute-done.5.refs_0_ = f32[16,32]{1,0:T(8,128)S(1)} collective-permute-done((f32[16,32]{1,0:T(8,128)S(1)}, f32[16,32]{1,0:T(8,128)S(1)}, u32[]{:S(2)}, u32[]{:S(2)}) %collective-permute-start.5) | collective-permute-done | bytes 2080 | tf_op jit(solution)/shard_map/ppermute | solution.py:594
  25.8 0.8 %write_outputs.1 = (f32[2,1,2,8]{3,2,1,0:T(2,128)}, f32[3,2,1,2,8]{4,3,2,1,0:T(2,128)}, f32[2,1,2,8,9]{4,3,2,1,0:T(8,128)}) custom-call(f32[16,64]{1,0:T(8,128)S(1)} %add.23.mine_ref, f32[1,32]{1,0:T(1,128)S(1)} %get-tuple-element.29.shift_row_ref, f32[16,32]{1,0:T(8,128)S(1)} %collective-permute-done.5.refs_0_), custom_call_target="tpu_custom_call" | custom-call | tf_op jit(solution)/shard_map/write_outputs/pallas_call | solution.py:686
  (2 shorter events, 0.0 us)
Async XLA Ops:
  1.7 7.9 %collective-permute-start.2 = (f32[40,128]{1,0:T(8,128)S(1)}, f32[40,128]{1,0:T(8,128)S(1)}, u32[]{:S(2)}, u32[]{:S(2)}) collective-permute-start(f32[40,128]{1,0:T(8,128)S(1)} %get-tuple-element.19), channel_id=1, source_target_pairs={{0,12},{4,8},{8,20},{12,16},{16,28},{20,24},{24,4},{28,0},{1,13},{... | collective-permute-start | bytes 61448 | tf_op jit(solution)/shard_map/ppermute | solution.py:594
  5.7 5.6 %collective-permute-start = (f32[40,128]{1,0:T(8,128)S(1)}, f32[40,128]{1,0:T(8,128)S(1)}, u32[]{:S(2)}, u32[]{:S(2)}) collective-permute-start(f32[40,128]{1,0:T(8,128)S(1)} %get-tuple-element.19), channel_id=1, source_target_pairs={{0,8},{8,16},{16,24},{24,0},{1,9},{9,17},{17,25},{25,1},{2,10},{10... | collective-permute-start | bytes 61448 | tf_op jit(solution)/shard_map/ppermute | solution.py:594
  7.3 4.0 %collective-permute-start.1 = (f32[40,128]{1,0:T(8,128)S(1)}, f32[40,128]{1,0:T(8,128)S(1)}, u32[]{:S(2)}, u32[]{:S(2)}) collective-permute-start(f32[40,128]{1,0:T(8,128)S(1)} %get-tuple-element.18.here_ref), channel_id=1, source_target_pairs={{0,4},{4,0},{1,5},{5,1},{2,6},{6,2},{3,7},{7,3},{8,12},{12,8},{9,1... | collective-permute-start | bytes 61448 | tf_op jit(solution)/shard_map/ppermute | solution.py:594
  11.3 2.1 %collective-permute-start.3 = (f32[160,128]{1,0:T(8,128)S(1)}, f32[160,128]{1,0:T(8,128)S(1)}, u32[]{:S(2)}, u32[]{:S(2)}) collective-permute-start(f32[160,128]{1,0:T(8,128)S(1)} %pad_add_fusion), channel_id=1, source_target_pairs={{0,3},{1,0},{2,1},{3,2},{4,7},{5,4},{6,5},{7,6},{8,11},{9,8},{10,9... | collective-permute-start | bytes 245768 | tf_op jit(solution)/shard_map/ppermute | solution.py:594
  19.0 3.7 %collective-permute-start.4 = (f32[16,64]{1,0:T(8,128)S(1)}, f32[16,64]{1,0:T(8,128)S(1)}, u32[]{:S(2)}, u32[]{:S(2)}) collective-permute-start(f32[16,64]{1,0:T(8,128)S(1)} %get-tuple-element.28), channel_id=1, source_target_pairs={{0,24},{8,0},{16,8},{24,16},{1,25},{9,1},{17,9},{25,17},{2,26},{10... | collective-permute-start | bytes 12296 | tf_op jit(solution)/shard_map/ppermute | solution.py:594
  22.8 3.1 %collective-permute-start.5 = (f32[16,32]{1,0:T(8,128)S(1)}, f32[16,32]{1,0:T(8,128)S(1)}, u32[]{:S(2)}, u32[]{:S(2)}) collective-permute-start(f32[16,32]{1,0:T(8,128)S(1)} %slice.4), channel_id=1, source_target_pairs={{0,1},{1,2},{2,3},{3,0},{4,5},{5,6},{6,7},{7,4},{8,9},{9,10},{10,1... | collective-permute-start | bytes 6152 | tf_op jit(solution)/shard_map/ppermute | solution.py:594

commit v20 on v19

--- a/solution.py
+++ b/solution.py
@@ -111,17 +111,18 @@
     centers_ref,
     neighbours_ref,
     scale_ref,
+    features_ref,
     sems,
 ):
     owned, nbr = neighbours_ref.shape
     per_row = 128 // nbr
     pairs_in = (
-        (features_hbm, low_ref.at[pl.ds(0, owned), :]),
+        (centers_hbm, centers_ref),
         (neighbours_hbm, neighbours_ref),
-        (centers_hbm, centers_ref),
         (positions_hbm, positions_ref),
         (species_hbm, species_ref),
         (scale_hbm, scale_ref),
+        (features_hbm, features_ref),
     )
     copies = [
         pltpu.make_async_copy(source, target, sems.at[i])
@@ -129,19 +130,8 @@
     ]
     for copy in copies:
         copy.start()
-    for copy in copies:
+    for copy in copies[:2]:
         copy.wait()
-    for cell in range(OWN_CELLS):
-        x, z = cell // 2, cell % 2
-        species = species_ref[x, 0, z : z + 1, :]
-        scale = jnp.zeros(species.shape, F32)
-        for s in range(scale_ref.shape[0]):
-            scale = jnp.where(species == s, scale_ref[s], scale)
-        row = lane_row(scale, 3 * SITES)
-        for c in range(3):
-            row = row + lane_row(positions_ref[c, x, 0, z : z + 1, :], c * SITES)
-        low_ref[owned + cell : owned + cell + 1] = row
-
     chosen = lax.broadcasted_iota(jnp.int32, (owned, owned), 0) == centers_ref[...]
     chosen = jnp.where(chosen, 1.0, 0.0)
     occupied = jnp.sum(chosen, axis=1, keepdims=True) > 0.5
@@ -171,27 +161,63 @@
         codes = codes + pltpu.roll(more, j * nbr, 1)
     tile = owned + OWN_CELLS
     low_ref[tile:] = codes[: codes.shape[0] // 2]
-    high_ref[:tile] = low_ref[:tile]
     high_ref[tile:] = codes[codes.shape[0] // 2 :]
-
-
-def fetch_kernel(species_hbm, centers_hbm, shift_hbm, *refs):
-    *refs, shift_row_ref, species_ref, centers_ref, shift_ref, sems = refs
-    count = len(refs) // 2
-    pairs_in = [
-        (species_hbm, species_ref),
-        (centers_hbm, centers_ref),
-        (shift_hbm, shift_ref),
-        *zip(refs[:count], refs[count:]),
-    ]
+    for copy in copies[2:]:
+        copy.wait()
+    for cell in range(OWN_CELLS):
+        x, z = cell // 2, cell % 2
+        species = species_ref[x, 0, z : z + 1, :]
+        scale = jnp.zeros(species.shape, F32)
+        for s in range(scale_ref.shape[0]):
+            scale = jnp.where(species == s, scale_ref[s], scale)
+        row = lane_row(scale, 3 * SITES)
+        for c in range(3):
+            row = row + lane_row(positions_ref[c, x, 0, z : z + 1, :], c * SITES)
+        low_ref[owned + cell : owned + cell + 1] = row
+        high_ref[owned + cell : owned + cell + 1] = row
+
+    low_ref[:owned] = features_ref[...]
+    high_ref[:owned] = features_ref[...]
+
+
+def fetch_kernel(nbr, *refs):
+    sources = refs[:9]
+    (
+        near_ref,
+        center_ref,
+        path_rows_ref,
+        value_rows_ref,
+        value_plain_ref,
+        latent_t_ref,
+        latent_rows_ref,
+        out_column_ref,
+        shift_row_ref,
+    ) = refs[9:18]
+    targets = refs[18:27]
+    sems = refs[27]
     copies = [
         pltpu.make_async_copy(source, target, sems.at[i])
-        for i, (source, target) in enumerate(pairs_in)
+        for i, (source, target) in enumerate(zip(sources, targets))
     ]
     for copy in copies:
         copy.start()
     for copy in copies:
         copy.wait()
+    species_ref, centers_ref, shift_ref, *weights = targets
+    center_weight, near_weight, path_weight, value_weight, latent_weight, out_weight = [
+        ref[...] for ref in weights
+    ]
+    width = near_weight.shape[0]
+    near_ref[...] = stacked(*split(jnp.transpose(near_weight)))
+    center_ref[...] = stacked(*split(jnp.transpose(center_weight)))
+    path_rows_ref[...] = jnp.concatenate(
+        [jnp.broadcast_to(path_weight[l : l + 1, :], (GROUP, width)) for l in LEVELS], axis=0
+    ) * (1.0 / math.sqrt(nbr))
+    value_rows_ref[...] = three(*split(jnp.transpose(value_weight)))
+    value_plain_ref[...] = three(*split(value_weight))
+    latent_t_ref[...] = three(*split(0.5 * jnp.transpose(latent_weight)))
+    latent_rows_ref[...] = three(*split(latent_weight * out_weight))
+    out_column_ref[...] = jnp.transpose(jnp.broadcast_to(out_weight, (width, width)))
     owned = centers_ref.shape[1]
     shift_row = jnp.zeros((1, 128), F32)
     for cell in range(OWN_CELLS):
@@ -208,10 +234,11 @@
 
 def finish_kernel(mine_ref, shift_row_ref, *refs):
     *near_refs, energy_ref, forces_ref, virial_ref = refs
-    owned = near_refs[0].shape[1]
+    owned = shift_row_ref.shape[1]
     total = mine_ref[:, :owned]
     for near_ref in near_refs:
-        total = total + near_ref[...]
+        start = near_ref.shape[1] - owned
+        total = total + near_ref[:, start : start + owned]
     energy = total[12:13] + shift_row_ref[...]
     columns = jnp.transpose(jnp.concatenate([total, jnp.zeros((ORDERS, 128 - owned), F32)], axis=1))
     for cell in range(OWN_CELLS):
@@ -227,13 +254,15 @@
     near_side_refs = refs[: 2 * kind - 2]
     (
         next_z_ref,
-        center_weight_ref,
-        near_weight_ref,
+        near_stack_ref,
+        center_stack_ref,
+        path_rows_ref,
+        value_rows_ref,
+        value_plain_ref,
+        latent_t_ref,
+        latent_rows_ref,
+        out_column_ref,
         basis_weight_ref,
-        path_weight_ref,
-        value_weight_ref,
-        latent_weight_ref,
-        out_weight_ref,
         keep_ref,
         send_ref,
     ) = refs[2 * kind - 2 :]
@@ -315,20 +344,20 @@
     place_parts = place_rows(coords)
     center_parts = place_rows(jnp.concatenate(center_coords, axis=0))
 
-    value_rows = three(*split(jnp.transpose(value_weight_ref[...])))
-    latent_t = three(*split(0.5 * jnp.transpose(latent_weight_ref[...])))
-    latent_rows = three(*split(latent_weight_ref[...] * out_weight_ref[...]))
-    value_plain = three(*split(value_weight_ref[...]))
+    value_rows = value_rows_ref[...]
+    value_plain = value_plain_ref[...]
+    latent_t = latent_t_ref[...]
+    latent_rows = latent_rows_ref[...]
+    path_rows = path_rows_ref[...]
     basis_t = jnp.transpose(basis_weight_ref[...])
     basis_high_t, basis_low_t = split(0.5 * basis_t)
     basis_rows = three(*split(basis_weight_ref[...]))
 
     def project(weight, rows):
-        weight = stacked(*split(jnp.transpose(weight)))
         return folded(mm_nt(weight, jnp.concatenate(split(rows), axis=1)))
 
-    near_t = project(near_weight_ref[...], feats)
-    own_t = project(center_weight_ref[...], center_feats)
+    near_t = project(near_stack_ref[...], feats)
+    own_t = project(center_stack_ref[...], center_feats)
     near_high, near_low = split(0.5 * near_t)
     own_high, own_low = split(0.5 * own_t)
     lookup = jnp.concatenate(
@@ -339,11 +368,7 @@
         [*split3(scale_rows), jnp.zeros((-3 * groups % 16, 128), BF16)], axis=0
     )
 
-    path_rows = jnp.concatenate(
-        [jnp.broadcast_to(path_weight_ref[l : l + 1, :], (GROUP, width)) for l in LEVELS], axis=0
-    ) * (1.0 / root_count)
-    out_column = jnp.transpose(jnp.broadcast_to(out_weight_ref[...], (width, width)))
-    out_column = jnp.concatenate([out_column] * (pairs // width), axis=1)
+    out_column = jnp.concatenate([out_column_ref[...]] * (pairs // width), axis=1)
 
     site_ids = lax.broadcasted_iota(jnp.int32, (known, pairs), 0)
     slot_ids = lax.broadcasted_iota(jnp.int32, (centers, pairs), 0)
@@ -609,6 +634,7 @@
             pltpu.VMEM(listed.shape, jnp.int32),
             pltpu.VMEM(neighbours.shape, jnp.int32),
             pltpu.SMEM(species_scale.shape, F32),
+            pltpu.VMEM((owned, width), F32),
             pltpu.SemaphoreType.DMA((6,)),
         ],
         compiler_params=pltpu.CompilerParams(vmem_limit_bytes=8 * 1024 * 1024),
@@ -623,32 +649,41 @@
             species_scale,
         )
     )
-    weights = (
+    fetched = (
+        species,
+        listed,
+        species_shift,
         center_weight,
         near_weight,
-        basis_weight,
         path_weight,
         value_weight,
         latent_weight,
         out_weight.reshape(1, width),
     )
+    smem_at = 2
     *weights, shift_row = pl.pallas_call(
-        fetch_kernel,
+        functools.partial(fetch_kernel, nbr),
         out_shape=(
-            *(jax.ShapeDtypeStruct(w.shape, F32) for w in weights),
+            jax.ShapeDtypeStruct((2 * width, 2 * width), BF16),
+            jax.ShapeDtypeStruct((2 * width, 2 * width), BF16),
+            jax.ShapeDtypeStruct((len(LEVELS) * GROUP, width), F32),
+            jax.ShapeDtypeStruct((2 * width, 3 * width), BF16),
+            jax.ShapeDtypeStruct((width, 6 * width), BF16),
+            jax.ShapeDtypeStruct((width, 6 * width), BF16),
+            jax.ShapeDtypeStruct((2 * width, 3 * width), BF16),
+            jax.ShapeDtypeStruct((width, width), F32),
             jax.ShapeDtypeStruct((1, owned), F32),
         ),
-        in_specs=[hbm] * (3 + len(weights)),
-        out_specs=(vmem,) * (1 + len(weights)),
+        in_specs=[hbm] * len(fetched),
+        out_specs=(vmem,) * 9,
         scratch_shapes=[
-            pltpu.VMEM(species.shape, jnp.int32),
-            pltpu.VMEM(listed.shape, jnp.int32),
-            pltpu.SMEM(species_shift.shape, F32),
-            pltpu.SemaphoreType.DMA((3 + len(weights),)),
-        ],
+            (pltpu.SMEM if i == smem_at else pltpu.VMEM)(a.shape, a.dtype)
+            for i, a in enumerate(fetched)
+        ]
+        + [pltpu.SemaphoreType.DMA((len(fetched),))],
         compiler_params=pltpu.CompilerParams(vmem_limit_bytes=8 * 1024 * 1024),
         name="fetch_weights",
-    )(*in_hbm(species, listed, species_shift, *weights))
+    )(*in_hbm(*fetched))
     last_x = moved(high, {"gx": 1})
     sides = []
     for step in (-1, 1)[: kind - 1]:
@@ -663,7 +698,7 @@
             jax.ShapeDtypeStruct((ORDERS, half), F32),
             jax.ShapeDtypeStruct((ORDERS, half), F32),
         ),
-        in_specs=[vmem] * (8 + 2 * kind),
+        in_specs=[vmem] * (10 + 2 * kind),
         out_specs=(vmem, vmem),
         compiler_params=pltpu.CompilerParams(vmem_limit_bytes=44 * 1024 * 1024),
         name="pair_forces",
@@ -673,13 +708,14 @@
         *sides,
         next_z,
         *weights,
+        basis_weight,
     )
     totals = keep + moved(send, {"gx": -1})
 
     def part(index):
         return totals[:, index * owned : (index + 1) * owned]
 
-    back = [moved(part(kept), {"gz": 1})]
+    back = [moved(totals, {"gz": 1}) if kept == 1 else moved(part(kept), {"gz": 1})]
     for i, step in enumerate((1, -1)[: kept - 1]):
         back.append(moved(part(kept + 1 + i), {"gy": step, "gz": 1}))
         back.append(moved(part(1 + i), {"gy": step}))

time: 26.9 us -> 27.8 us (1.033)
  local copies, waits for them, and re-layouts: 0.08 us -> 0.69 us
  Pallas kernels: 8.77 us -> 9.19 us
    unnamed x0 -> x2, local copies, waits for them, and re-layouts: none -> 0.69 us
where the time goes in v20:
time: 27.8 us; the launch traced here: 27.5 us
  Pallas kernels  9.19 us (33%)
  starting transfers between devices  8.7 us (31%)
  waiting for transfers between devices  8.28 us (30%)
  local copies, waits for them, and re-layouts  0.69 us (2%)
  between operations  0.67 us (2%)
    ppermute x6, starting transfers between devices, moved(): return lax.ppermute(array, names, route)  8.7 us
    ppermute x6, waiting for transfers between devices, moved(): return lax.ppermute(array, names, route)  8.28 us
    pallas_call x1, Pallas kernels, local(): pl.pallas_call(functools.partial(force_kernel, kind, nbr), out_shape=(jax...  5.83 us
    pallas_call x1, Pallas kernels, local(): pl.pallas_call(functools.partial(fetch_kernel, nbr), out_shape=(jax.Shape...  1.44 us
    pallas_call x1, Pallas kernels, local(): pl.pallas_call(functools.partial(pack_kernel, kind), out_shape=(payload,...  1.11 us
    pallas_call x1, Pallas kernels, local(): pl.pallas_call(finish_kernel, out_shape=(jax.ShapeDtypeStruct(species.sha...  0.82 us
    unnamed x2, local copies, waits for them, and re-layouts  0.69 us
  transfers between devices with their start and end apart: 6, of which 5 were waited for; matrix products, arithmetic and copies ran while one was open for 0% of the time, Pallas kernels for 5%

profile of v20, /device:TPU:0, one launch (start us, length us, event | category | flops | bytes accessed | tf_op | source)
XLA Modules:
  0.0 27.5 jit_solution(4509003217910441843)
XLA Ops:
  0.6 1.1 %pack_payload.1 = (f32[40,128]{1,0:T(8,128)S(1)}, f32[40,128]{1,0:T(8,128)S(1)}) custom-call(f32[3,2,1,2,8]{4,3,2,1,0:T(2,128)} %positions_hbm.1, f32[32,128]{1,0:T(8,128)} %bitcast.4, s32[2,1,2,8]{3,2,1,0:T(2,128)} %refs_0_.1, s32[1,32]{1,0:T(1,128)} %bitcast.5, s32[32,32]{1,0:T(8,128)} %neighbours_hbm.1, f32[5]{0:T(128)} %scale_hbm.1), custom_call_target="tpu_custom_call" | custom-call | tf_op jit(solution)/shard_map/pack_payload/pallas_call | solution.py:625
  1.8 4.0 %collective-permute-start.2 = (f32[40,128]{1,0:T(8,128)S(1)}, f32[40,128]{1,0:T(8,128)S(1)}, u32[]{:S(2)}, u32[]{:S(2)}) collective-permute-start(f32[40,128]{1,0:T(8,128)S(1)} %get-tuple-element.20), channel_id=1, source_target_pairs={{0,12},{4,8},{8,20},{12,16},{16,28},{20,24},{24,4},{28,0},{1,13},{... | collective-permute-start | bytes 61448 | tf_op jit(solution)/shard_map/ppermute | solution.py:619
  5.8 1.6 %collective-permute-start = (f32[40,128]{1,0:T(8,128)S(1)}, f32[40,128]{1,0:T(8,128)S(1)}, u32[]{:S(2)}, u32[]{:S(2)}) collective-permute-start(f32[40,128]{1,0:T(8,128)S(1)} %get-tuple-element.20), channel_id=1, source_target_pairs={{0,8},{8,16},{16,24},{24,0},{1,9},{9,17},{17,25},{25,1},{2,10},{10... | collective-permute-start | bytes 61448 | tf_op jit(solution)/shard_map/ppermute | solution.py:619
  7.3 0.5 %collective-permute-start.1 = (f32[40,128]{1,0:T(8,128)S(1)}, f32[40,128]{1,0:T(8,128)S(1)}, u32[]{:S(2)}, u32[]{:S(2)}) collective-permute-start(f32[40,128]{1,0:T(8,128)S(1)} %get-tuple-element.19.here_ref), channel_id=1, source_target_pairs={{0,4},{4,0},{1,5},{5,1},{2,6},{6,2},{3,7},{7,3},{8,12},{12,8},{9,1... | collective-permute-start | bytes 61448 | tf_op jit(solution)/shard_map/ppermute | solution.py:619
  7.9 1.8 %collective-permute-done.2.refs_1_ = f32[40,128]{1,0:T(8,128)S(1)} collective-permute-done((f32[40,128]{1,0:T(8,128)S(1)}, f32[40,128]{1,0:T(8,128)S(1)}, u32[]{:S(2)}, u32[]{:S(2)}) %collective-permute-start.2) | collective-permute-done | bytes 20512 | tf_op jit(solution)/shard_map/ppermute | solution.py:619
  9.6 1.7 %collective-permute-done.last_x_ref = f32[40,128]{1,0:T(8,128)S(1)} collective-permute-done((f32[40,128]{1,0:T(8,128)S(1)}, f32[40,128]{1,0:T(8,128)S(1)}, u32[]{:S(2)}, u32[]{:S(2)}) %collective-permute-start) | collective-permute-done | bytes 20512 | tf_op jit(solution)/shard_map/ppermute | solution.py:619
  11.3 0.0 collective-permute-done.1.refs_0_
  11.4 0.1 collective-permute-start.3
  11.4 1.4 %fetch_weights.1 = (bf16[256,256]{1,0:T(8,128)(2,1)S(1)}, bf16[256,256]{1,0:T(8,128)(2,1)S(1)}, f32[72,128]{1,0:T(8,128)S(1)}, bf16[256,384]{1,0:T(8,128)(2,1)S(...) custom-call(s32[2,1,2,8]{3,2,1,0:T(2,128)} %refs_0_.1, ...), custom_call_target="tpu_custom_call" | custom-call | tf_op jit(solution)/shard_map/fetch_weights/pallas_call | solution.py:664
  12.9 0.6 %collective-permute-done.3.refs_2_ = f32[160,128]{1,0:T(8,128)S(1)} collective-permute-done((f32[160,128]{1,0:T(8,128)S(1)}, f32[160,128]{1,0:T(8,128)S(1)}, u32[]{:S(2)}, u32[]{:S(2)}) %collective-permute-start.3) | collective-permute-done | bytes 81952 | tf_op jit(solution)/shard_map/ppermute | solution.py:619
  13.5 0.0 copy-start
  13.5 0.7 %copy-done = f32[8,128]{1,0:T(8,128)S(1)} copy-done((f32[8,128]{1,0:T(8,128)S(1)}, f32[8,128]{1,0:T(8,128)}, u32[]{:S(2)}) %copy-start) | copy-done | bytes 4120
  14.2 5.8 %pair_forces.1 = (f32[16,64]{1,0:T(8,128)S(1)}, f32[16,64]{1,0:T(8,128)S(1)}) custom-call(f32[40,128]{1,0:T(8,128)S(1)} %get-tuple-element.19.here_ref, f32[40,128]{1,0:T(8,128)S(1)} %collective-permute-done.last_x_ref, f32[40,128]{1,0:T(8,128)S(1)} %collective-permute-done.1.refs_0_, f32[40,128]{1,0:T(8,128)S(1)} %collective-permute-done.2.refs_1_, ...), custom_call_target="tpu_custom_call" | custom-call | tf_op jit(solution)/shard_map/pair_forces/pallas_call | solution.py:695
  20.0 2.0 %collective-permute-start.4 = (f32[16,64]{1,0:T(8,128)S(1)}, f32[16,64]{1,0:T(8,128)S(1)}, u32[]{:S(2)}, u32[]{:S(2)}) collective-permute-start(f32[16,64]{1,0:T(8,128)S(1)} %get-tuple-element.30), channel_id=1, source_target_pairs={{0,24},{8,0},{16,8},{24,16},{1,25},{9,1},{17,9},{25,17},{2,26},{10... | collective-permute-start | bytes 12296 | tf_op jit(solution)/shard_map/ppermute | solution.py:619
  22.0 1.7 %collective-permute-done.4 = f32[16,64]{1,0:T(8,128)S(1)} collective-permute-done((f32[16,64]{1,0:T(8,128)S(1)}, f32[16,64]{1,0:T(8,128)S(1)}, u32[]{:S(2)}, u32[]{:S(2)}) %collective-permute-start.4) | collective-permute-done | bytes 4128 | tf_op jit(solution)/shard_map/ppermute | solution.py:619
  23.6 0.5 %collective-permute-start.5 = (f32[16,64]{1,0:T(8,128)S(1)}, f32[16,64]{1,0:T(8,128)S(1)}, u32[]{:S(2)}, u32[]{:S(2)}) collective-permute-start(f32[16,64]{1,0:T(8,128)S(1)} %add.23.mine_ref), channel_id=1, source_target_pairs={{0,1},{1,2},{2,3},{3,0},{4,5},{5,6},{6,7},{7,4},{8,9},{9,10},{10,1... | collective-permute-start | bytes 12296 | tf_op jit(solution)/shard_map/ppermute | solution.py:619
  24.2 2.5 %collective-permute-done.5.refs_0_ = f32[16,64]{1,0:T(8,128)S(1)} collective-permute-done((f32[16,64]{1,0:T(8,128)S(1)}, f32[16,64]{1,0:T(8,128)S(1)}, u32[]{:S(2)}, u32[]{:S(2)}) %collective-permute-start.5) | collective-permute-done | bytes 4128 | tf_op jit(solution)/shard_map/ppermute | solution.py:619
  26.7 0.8 %write_outputs.1 = (f32[2,1,2,8]{3,2,1,0:T(2,128)}, f32[3,2,1,2,8]{4,3,2,1,0:T(2,128)}, f32[2,1,2,8,9]{4,3,2,1,0:T(8,128)}) custom-call(f32[16,64]{1,0:T(8,128)S(1)} %add.23.mine_ref, f32[1,32]{1,0:T(1,128)S(1)} %get-tuple-element.31.shift_row_ref, f32[16,64]{1,0:T(8,128)S(1)} %collective-permute-done.5.refs_0_), custom_call_target="tpu_custom_call" | custom-call | tf_op jit(solution)/shard_map/write_outputs/pallas_call | solution.py:722
  (2 shorter events, 0.0 us)
Async XLA Ops:
  1.8 7.9 %collective-permute-start.2 = (f32[40,128]{1,0:T(8,128)S(1)}, f32[40,128]{1,0:T(8,128)S(1)}, u32[]{:S(2)}, u32[]{:S(2)}) collective-permute-start(f32[40,128]{1,0:T(8,128)S(1)} %get-tuple-element.20), channel_id=1, source_target_pairs={{0,12},{4,8},{8,20},{12,16},{16,28},{20,24},{24,4},{28,0},{1,13},{... | collective-permute-start | bytes 61448 | tf_op jit(solution)/shard_map/ppermute | solution.py:619
  5.8 5.6 %collective-permute-start = (f32[40,128]{1,0:T(8,128)S(1)}, f32[40,128]{1,0:T(8,128)S(1)}, u32[]{:S(2)}, u32[]{:S(2)}) collective-permute-start(f32[40,128]{1,0:T(8,128)S(1)} %get-tuple-element.20), channel_id=1, source_target_pairs={{0,8},{8,16},{16,24},{24,0},{1,9},{9,17},{17,25},{25,1},{2,10},{10... | collective-permute-start | bytes 61448 | tf_op jit(solution)/shard_map/ppermute | solution.py:619
  7.3 4.0 %collective-permute-start.1 = (f32[40,128]{1,0:T(8,128)S(1)}, f32[40,128]{1,0:T(8,128)S(1)}, u32[]{:S(2)}, u32[]{:S(2)}) collective-permute-start(f32[40,128]{1,0:T(8,128)S(1)} %get-tuple-element.19.here_ref), channel_id=1, source_target_pairs={{0,4},{4,0},{1,5},{5,1},{2,6},{6,2},{3,7},{7,3},{8,12},{12,8},{9,1... | collective-permute-start | bytes 61448 | tf_op jit(solution)/shard_map/ppermute | solution.py:619
  11.4 2.1 %collective-permute-start.3 = (f32[160,128]{1,0:T(8,128)S(1)}, f32[160,128]{1,0:T(8,128)S(1)}, u32[]{:S(2)}, u32[]{:S(2)}) collective-permute-start(f32[160,128]{1,0:T(8,128)S(1)} %pad_add_fusion), channel_id=1, source_target_pairs={{0,3},{1,0},{2,1},{3,2},{4,7},{5,4},{6,5},{7,6},{8,11},{9,8},{10,9... | collective-permute-start | bytes 245768 | tf_op jit(solution)/shard_map/ppermute | solution.py:619
  13.5 0.7 %copy-start = (f32[8,128]{1,0:T(8,128)S(1)}, f32[8,128]{1,0:T(8,128)}, u32[]{:S(2)}) copy-start(f32[8,128]{1,0:T(8,128)} %refs_11_.1) | copy-start | bytes 12292
  20.0 3.7 %collective-permute-start.4 = (f32[16,64]{1,0:T(8,128)S(1)}, f32[16,64]{1,0:T(8,128)S(1)}, u32[]{:S(2)}, u32[]{:S(2)}) collective-permute-start(f32[16,64]{1,0:T(8,128)S(1)} %get-tuple-element.30), channel_id=1, source_target_pairs={{0,24},{8,0},{16,8},{24,16},{1,25},{9,1},{17,9},{25,17},{2,26},{10... | collective-permute-start | bytes 12296 | tf_op jit(solution)/shard_map/ppermute | solution.py:619
  23.6 3.1 %collective-permute-start.5 = (f32[16,64]{1,0:T(8,128)S(1)}, f32[16,64]{1,0:T(8,128)S(1)}, u32[]{:S(2)}, u32[]{:S(2)}) collective-permute-start(f32[16,64]{1,0:T(8,128)S(1)} %add.23.mine_ref), channel_id=1, source_target_pairs={{0,1},{1,2},{2,3},{3,0},{4,5},{5,6},{6,7},{7,4},{8,9},{9,10},{10,1... | collective-permute-start | bytes 12296 | tf_op jit(solution)/shard_map/ppermute | solution.py:619

commit v21 on v19

--- a/solution.py
+++ b/solution.py
@@ -208,10 +208,11 @@
 
 def finish_kernel(mine_ref, shift_row_ref, *refs):
     *near_refs, energy_ref, forces_ref, virial_ref = refs
-    owned = near_refs[0].shape[1]
+    owned = shift_row_ref.shape[1]
     total = mine_ref[:, :owned]
     for near_ref in near_refs:
-        total = total + near_ref[...]
+        start = near_ref.shape[1] - owned
+        total = total + near_ref[:, start : start + owned]
     energy = total[12:13] + shift_row_ref[...]
     columns = jnp.transpose(jnp.concatenate([total, jnp.zeros((ORDERS, 128 - owned), F32)], axis=1))
     for cell in range(OWN_CELLS):
@@ -345,7 +346,6 @@
     out_column = jnp.transpose(jnp.broadcast_to(out_weight_ref[...], (width, width)))
     out_column = jnp.concatenate([out_column] * (pairs // width), axis=1)
 
-    site_ids = lax.broadcasted_iota(jnp.int32, (known, pairs), 0)
     slot_ids = lax.broadcasted_iota(jnp.int32, (centers, pairs), 0)
     slot_row = lax.broadcasted_iota(jnp.int32, (1, pairs), 1) // nbr
     group_lane = lax.broadcasted_iota(jnp.int32, (GROUP, pairs), 1) // nbr % GROUP
@@ -355,8 +355,17 @@
     order = lax.broadcasted_iota(jnp.int32, (radial, pairs), 0).astype(F32) + 1.0
     lanes = [slice(g * span, (g + 1) * span) for g in range(groups)]
 
-    pick = jnp.where(site_ids == near_row, 1.0, 0.0)
-    pick_half = pick.astype(BF16)
+    site_ids = lax.broadcasted_iota(jnp.int32, (known, 128), 0)
+    if known <= 256:
+        site_ids = site_ids.astype(F32).astype(BF16)
+        wanted = jnp.broadcast_to(near_row.astype(F32), (16, pairs)).astype(BF16)
+        wanted = jnp.concatenate([wanted] * (known // 16), axis=0)
+        one, zero = jnp.ones((), BF16), jnp.zeros((), BF16)
+    else:
+        wanted = near_row
+        one, zero = 1.0, 0.0
+    site_ids = jnp.concatenate([site_ids] * (pairs // 128), axis=1)
+    pick_half = jnp.where(site_ids == wanted, one, zero).astype(BF16)
     slot_half = jnp.where(slot_ids == slot_row, 1.0, 0.0).astype(BF16)
 
     moved = mm(
@@ -679,7 +688,7 @@
     def part(index):
         return totals[:, index * owned : (index + 1) * owned]
 
-    back = [moved(part(kept), {"gz": 1})]
+    back = [moved(totals, {"gz": 1}) if kept == 1 else moved(part(kept), {"gz": 1})]
     for i, step in enumerate((1, -1)[: kept - 1]):
         back.append(moved(part(kept + 1 + i), {"gy": step, "gz": 1}))
         back.append(moved(part(1 + i), {"gy": step}))

time: 26.9 us -> 26.7 us (level)
  no operation moved by 1% of the time
where the time goes in v21:
time: 26.7 us; the launch traced here: 26.5 us
  Pallas kernels  8.72 us (33%)
  starting transfers between devices  8.69 us (33%)
  waiting for transfers between devices  8.38 us (31%)
  between operations  0.67 us (3%)
    ppermute x6, starting transfers between devices, moved(): return lax.ppermute(array, names, route)  8.69 us
    ppermute x6, waiting for transfers between devices, moved(): return lax.ppermute(array, names, route)  8.38 us
    pallas_call x1, Pallas kernels, local(): pl.pallas_call(functools.partial(force_kernel, kind, nbr), out_shape=(jax...  5.48 us
    pallas_call x1, Pallas kernels, local(): pl.pallas_call(fetch_kernel, out_shape=(*(jax.ShapeDtypeStruct(w.shape, F...  1.35 us
    pallas_call x1, Pallas kernels, local(): pl.pallas_call(functools.partial(pack_kernel, kind), out_shape=(payload,...  1.08 us
    pallas_call x1, Pallas kernels, local(): pl.pallas_call(finish_kernel, out_shape=(jax.ShapeDtypeStruct(species.sha...  0.82 us
  transfers between devices with their start and end apart: 6, of which 5 were waited for; matrix products, arithmetic and copies ran while one was open for 0% of the time, Pallas kernels for 5%

profile of v21, /device:TPU:0, one launch (start us, length us, event | category | flops | bytes accessed | tf_op | source)
XLA Modules:
  0.0 26.5 jit_solution(17152451065774216026)
XLA Ops:
  0.6 1.1 %pack_payload.1 = (f32[40,128]{1,0:T(8,128)S(1)}, f32[40,128]{1,0:T(8,128)S(1)}) custom-call(f32[3,2,1,2,8]{4,3,2,1,0:T(2,128)} %positions_hbm.1, f32[32,128]{1,0:T(8,128)} %bitcast.4, s32[2,1,2,8]{3,2,1,0:T(2,128)} %species_hbm.3, s32[1,32]{1,0:T(1,128)} %bitcast.5, s32[32,32]{1,0:T(8,128)} %neighbours_hbm.1, f32[5]{0:T(128)} %scale_hbm.1), custom_call_target="tpu_custom_call" | custom-call | tf_op jit(solution)/shard_map/pack_payload/pallas_call | solution.py:609
  1.7 4.0 %collective-permute-start.2 = (f32[40,128]{1,0:T(8,128)S(1)}, f32[40,128]{1,0:T(8,128)S(1)}, u32[]{:S(2)}, u32[]{:S(2)}) collective-permute-start(f32[40,128]{1,0:T(8,128)S(1)} %get-tuple-element.19), channel_id=1, source_target_pairs={{0,12},{4,8},{8,20},{12,16},{16,28},{20,24},{24,4},{28,0},{1,13},{... | collective-permute-start | bytes 61448 | tf_op jit(solution)/shard_map/ppermute | solution.py:603
  5.7 1.6 %collective-permute-start = (f32[40,128]{1,0:T(8,128)S(1)}, f32[40,128]{1,0:T(8,128)S(1)}, u32[]{:S(2)}, u32[]{:S(2)}) collective-permute-start(f32[40,128]{1,0:T(8,128)S(1)} %get-tuple-element.19), channel_id=1, source_target_pairs={{0,8},{8,16},{16,24},{24,0},{1,9},{9,17},{17,25},{25,1},{2,10},{10... | collective-permute-start | bytes 61448 | tf_op jit(solution)/shard_map/ppermute | solution.py:603
  7.3 0.5 %collective-permute-start.1 = (f32[40,128]{1,0:T(8,128)S(1)}, f32[40,128]{1,0:T(8,128)S(1)}, u32[]{:S(2)}, u32[]{:S(2)}) collective-permute-start(f32[40,128]{1,0:T(8,128)S(1)} %get-tuple-element.18.here_ref), channel_id=1, source_target_pairs={{0,4},{4,0},{1,5},{5,1},{2,6},{6,2},{3,7},{7,3},{8,12},{12,8},{9,1... | collective-permute-start | bytes 61448 | tf_op jit(solution)/shard_map/ppermute | solution.py:603
  7.8 1.8 %collective-permute-done.2.refs_1_ = f32[40,128]{1,0:T(8,128)S(1)} collective-permute-done((f32[40,128]{1,0:T(8,128)S(1)}, f32[40,128]{1,0:T(8,128)S(1)}, u32[]{:S(2)}, u32[]{:S(2)}) %collective-permute-start.2) | collective-permute-done | bytes 20512 | tf_op jit(solution)/shard_map/ppermute | solution.py:603
  9.6 1.7 %collective-permute-done.last_x_ref = f32[40,128]{1,0:T(8,128)S(1)} collective-permute-done((f32[40,128]{1,0:T(8,128)S(1)}, f32[40,128]{1,0:T(8,128)S(1)}, u32[]{:S(2)}, u32[]{:S(2)}) %collective-permute-start) | collective-permute-done | bytes 20512 | tf_op jit(solution)/shard_map/ppermute | solution.py:603
  11.3 0.0 collective-permute-done.1.refs_0_
  11.3 0.1 collective-permute-start.3
  11.4 1.3 %fetch_weights.1 = (f32[128,128]{1,0:T(8,128)S(1)}, f32[128,128]{1,0:T(8,128)S(1)}, f32[8,128]{1,0:T(8,128)S(1)}, f32[3,128]{1,0:T(4,128)S(1)}, f32[128,256]{1,0...) custom-call(s32[2,1,2,8]{3,2,1,0:T(2,128)} %species_hbm.3, s32[1,32]{1,0:T(1,128)} %bitcast.6, ...), custom_call_target="tpu_custom_call" | custom-call | tf_op jit(solution)/shard_map/fetch_weights/pallas_call | solution.py:644
  12.7 0.7 %collective-permute-done.3.refs_2_ = f32[160,128]{1,0:T(8,128)S(1)} collective-permute-done((f32[160,128]{1,0:T(8,128)S(1)}, f32[160,128]{1,0:T(8,128)S(1)}, u32[]{:S(2)}, u32[]{:S(2)}) %collective-permute-start.3) | collective-permute-done | bytes 81952 | tf_op jit(solution)/shard_map/ppermute | solution.py:603
  13.4 5.5 %pair_forces.1 = (f32[16,64]{1,0:T(8,128)S(1)}, f32[16,64]{1,0:T(8,128)S(1)}) custom-call(f32[40,128]{1,0:T(8,128)S(1)} %get-tuple-element.18.here_ref, f32[40,128]{1,0:T(8,128)S(1)} %collective-permute-done.last_x_ref, f32[40,128]{1,0:T(8,128)S(1)} %collective-permute-done.1.refs_0_, f32[40,128]{1,0:T(8,128)S(1)} %collective-permute-done.2.refs_1_, ...), custom_call_target="tpu_custom_call" | custom-call | tf_op jit(solution)/shard_map/pair_forces/pallas_call | solution.py:669
  18.9 2.0 %collective-permute-start.4 = (f32[16,64]{1,0:T(8,128)S(1)}, f32[16,64]{1,0:T(8,128)S(1)}, u32[]{:S(2)}, u32[]{:S(2)}) collective-permute-start(f32[16,64]{1,0:T(8,128)S(1)} %get-tuple-element.28), channel_id=1, source_target_pairs={{0,24},{8,0},{16,8},{24,16},{1,25},{9,1},{17,9},{25,17},{2,26},{10... | collective-permute-start | bytes 12296 | tf_op jit(solution)/shard_map/ppermute | solution.py:603
  20.9 1.7 %collective-permute-done.4 = f32[16,64]{1,0:T(8,128)S(1)} collective-permute-done((f32[16,64]{1,0:T(8,128)S(1)}, f32[16,64]{1,0:T(8,128)S(1)}, u32[]{:S(2)}, u32[]{:S(2)}) %collective-permute-start.4) | collective-permute-done | bytes 4128 | tf_op jit(solution)/shard_map/ppermute | solution.py:603
  22.6 0.5 %collective-permute-start.5 = (f32[16,64]{1,0:T(8,128)S(1)}, f32[16,64]{1,0:T(8,128)S(1)}, u32[]{:S(2)}, u32[]{:S(2)}) collective-permute-start(f32[16,64]{1,0:T(8,128)S(1)} %add.23.mine_ref), channel_id=1, source_target_pairs={{0,1},{1,2},{2,3},{3,0},{4,5},{5,6},{6,7},{7,4},{8,9},{9,10},{10,1... | collective-permute-start | bytes 12296 | tf_op jit(solution)/shard_map/ppermute | solution.py:603
  23.1 2.5 %collective-permute-done.5.refs_0_ = f32[16,64]{1,0:T(8,128)S(1)} collective-permute-done((f32[16,64]{1,0:T(8,128)S(1)}, f32[16,64]{1,0:T(8,128)S(1)}, u32[]{:S(2)}, u32[]{:S(2)}) %collective-permute-start.5) | collective-permute-done | bytes 4128 | tf_op jit(solution)/shard_map/ppermute | solution.py:603
  25.7 0.8 %write_outputs.1 = (f32[2,1,2,8]{3,2,1,0:T(2,128)}, f32[3,2,1,2,8]{4,3,2,1,0:T(2,128)}, f32[2,1,2,8,9]{4,3,2,1,0:T(8,128)}) custom-call(f32[16,64]{1,0:T(8,128)S(1)} %add.23.mine_ref, f32[1,32]{1,0:T(1,128)S(1)} %get-tuple-element.29.shift_row_ref, f32[16,64]{1,0:T(8,128)S(1)} %collective-permute-done.5.refs_0_), custom_call_target="tpu_custom_call" | custom-call | tf_op jit(solution)/shard_map/write_outputs/pallas_call | solution.py:695
  (2 shorter events, 0.0 us)
Async XLA Ops:
  1.7 7.9 %collective-permute-start.2 = (f32[40,128]{1,0:T(8,128)S(1)}, f32[40,128]{1,0:T(8,128)S(1)}, u32[]{:S(2)}, u32[]{:S(2)}) collective-permute-start(f32[40,128]{1,0:T(8,128)S(1)} %get-tuple-element.19), channel_id=1, source_target_pairs={{0,12},{4,8},{8,20},{12,16},{16,28},{20,24},{24,4},{28,0},{1,13},{... | collective-permute-start | bytes 61448 | tf_op jit(solution)/shard_map/ppermute | solution.py:603
  5.7 5.6 %collective-permute-start = (f32[40,128]{1,0:T(8,128)S(1)}, f32[40,128]{1,0:T(8,128)S(1)}, u32[]{:S(2)}, u32[]{:S(2)}) collective-permute-start(f32[40,128]{1,0:T(8,128)S(1)} %get-tuple-element.19), channel_id=1, source_target_pairs={{0,8},{8,16},{16,24},{24,0},{1,9},{9,17},{17,25},{25,1},{2,10},{10... | collective-permute-start | bytes 61448 | tf_op jit(solution)/shard_map/ppermute | solution.py:603
  7.3 4.0 %collective-permute-start.1 = (f32[40,128]{1,0:T(8,128)S(1)}, f32[40,128]{1,0:T(8,128)S(1)}, u32[]{:S(2)}, u32[]{:S(2)}) collective-permute-start(f32[40,128]{1,0:T(8,128)S(1)} %get-tuple-element.18.here_ref), channel_id=1, source_target_pairs={{0,4},{4,0},{1,5},{5,1},{2,6},{6,2},{3,7},{7,3},{8,12},{12,8},{9,1... | collective-permute-start | bytes 61448 | tf_op jit(solution)/shard_map/ppermute | solution.py:603
  11.3 2.1 %collective-permute-start.3 = (f32[160,128]{1,0:T(8,128)S(1)}, f32[160,128]{1,0:T(8,128)S(1)}, u32[]{:S(2)}, u32[]{:S(2)}) collective-permute-start(f32[160,128]{1,0:T(8,128)S(1)} %pad_add_fusion), channel_id=1, source_target_pairs={{0,3},{1,0},{2,1},{3,2},{4,7},{5,4},{6,5},{7,6},{8,11},{9,8},{10,9... | collective-permute-start | bytes 245768 | tf_op jit(solution)/shard_map/ppermute | solution.py:603
  18.9 3.7 %collective-permute-start.4 = (f32[16,64]{1,0:T(8,128)S(1)}, f32[16,64]{1,0:T(8,128)S(1)}, u32[]{:S(2)}, u32[]{:S(2)}) collective-permute-start(f32[16,64]{1,0:T(8,128)S(1)} %get-tuple-element.28), channel_id=1, source_target_pairs={{0,24},{8,0},{16,8},{24,16},{1,25},{9,1},{17,9},{25,17},{2,26},{10... | collective-permute-start | bytes 12296 | tf_op jit(solution)/shard_map/ppermute | solution.py:603
  22.6 3.1 %collective-permute-start.5 = (f32[16,64]{1,0:T(8,128)S(1)}, f32[16,64]{1,0:T(8,128)S(1)}, u32[]{:S(2)}, u32[]{:S(2)}) collective-permute-start(f32[16,64]{1,0:T(8,128)S(1)} %add.23.mine_ref), channel_id=1, source_target_pairs={{0,1},{1,2},{2,3},{3,0},{4,5},{5,6},{6,7},{7,4},{8,9},{9,10},{10,1... | collective-permute-start | bytes 12296 | tf_op jit(solution)/shard_map/ppermute | solution.py:603

commit v22 on v21

--- a/solution.py
+++ b/solution.py
@@ -448,7 +448,8 @@
         parts = []
         for table, cut in zip(tables, lanes):
             high, low = halves(table)
-            table = jnp.transpose(jnp.concatenate([high, high, low], axis=0)).astype(BF16)
+            table = jnp.concatenate([high, high, low], axis=0).astype(BF16)
+            table = jnp.transpose(table)
             parts.append(mm(table, blocks[:, cut]))
         return jnp.concatenate(parts, axis=1)
 

time: 26.7 us -> 26.7 us (level)
  no operation moved by 1% of the time
where the time goes in v22:
time: 26.7 us; the launch traced here: 26.4 us
  Pallas kernels  8.69 us (33%)
  starting transfers between devices  8.69 us (33%)
  waiting for transfers between devices  8.38 us (31%)
  between operations  0.67 us (3%)
    ppermute x6, starting transfers between devices, moved(): return lax.ppermute(array, names, route)  8.69 us
    ppermute x6, waiting for transfers between devices, moved(): return lax.ppermute(array, names, route)  8.38 us
    pallas_call x1, Pallas kernels, local(): pl.pallas_call(functools.partial(force_kernel, kind, nbr), out_shape=(jax...  5.44 us
    pallas_call x1, Pallas kernels, local(): pl.pallas_call(fetch_kernel, out_shape=(*(jax.ShapeDtypeStruct(w.shape, F...  1.35 us
    pallas_call x1, Pallas kernels, local(): pl.pallas_call(functools.partial(pack_kernel, kind), out_shape=(payload,...  1.08 us
    pallas_call x1, Pallas kernels, local(): pl.pallas_call(finish_kernel, out_shape=(jax.ShapeDtypeStruct(species.sha...  0.82 us
  transfers between devices with their start and end apart: 6, of which 5 were waited for; matrix products, arithmetic and copies ran while one was open for 0% of the time, Pallas kernels for 5%

profile of v22, /device:TPU:0, one launch (start us, length us, event | category | flops | bytes accessed | tf_op | source)
XLA Modules:
  0.0 26.4 jit_solution(11125236337473200150)
XLA Ops:
  0.6 1.1 %pack_payload.1 = (f32[40,128]{1,0:T(8,128)S(1)}, f32[40,128]{1,0:T(8,128)S(1)}) custom-call(f32[3,2,1,2,8]{4,3,2,1,0:T(2,128)} %positions_hbm.1, f32[32,128]{1,0:T(8,128)} %bitcast.4, s32[2,1,2,8]{3,2,1,0:T(2,128)} %species_hbm.3, s32[1,32]{1,0:T(1,128)} %bitcast.5, s32[32,32]{1,0:T(8,128)} %neighbours_hbm.1, f32[5]{0:T(128)} %scale_hbm.1), custom_call_target="tpu_custom_call" | custom-call | tf_op jit(solution)/shard_map/pack_payload/pallas_call | solution.py:610
  1.7 4.0 %collective-permute-start.2 = (f32[40,128]{1,0:T(8,128)S(1)}, f32[40,128]{1,0:T(8,128)S(1)}, u32[]{:S(2)}, u32[]{:S(2)}) collective-permute-start(f32[40,128]{1,0:T(8,128)S(1)} %get-tuple-element.19), channel_id=1, source_target_pairs={{0,12},{4,8},{8,20},{12,16},{16,28},{20,24},{24,4},{28,0},{1,13},{... | collective-permute-start | bytes 61448 | tf_op jit(solution)/shard_map/ppermute | solution.py:604
  5.7 1.6 %collective-permute-start = (f32[40,128]{1,0:T(8,128)S(1)}, f32[40,128]{1,0:T(8,128)S(1)}, u32[]{:S(2)}, u32[]{:S(2)}) collective-permute-start(f32[40,128]{1,0:T(8,128)S(1)} %get-tuple-element.19), channel_id=1, source_target_pairs={{0,8},{8,16},{16,24},{24,0},{1,9},{9,17},{17,25},{25,1},{2,10},{10... | collective-permute-start | bytes 61448 | tf_op jit(solution)/shard_map/ppermute | solution.py:604
  7.3 0.5 %collective-permute-start.1 = (f32[40,128]{1,0:T(8,128)S(1)}, f32[40,128]{1,0:T(8,128)S(1)}, u32[]{:S(2)}, u32[]{:S(2)}) collective-permute-start(f32[40,128]{1,0:T(8,128)S(1)} %get-tuple-element.18.here_ref), channel_id=1, source_target_pairs={{0,4},{4,0},{1,5},{5,1},{2,6},{6,2},{3,7},{7,3},{8,12},{12,8},{9,1... | collective-permute-start | bytes 61448 | tf_op jit(solution)/shard_map/ppermute | solution.py:604
  7.8 1.8 %collective-permute-done.2.refs_1_ = f32[40,128]{1,0:T(8,128)S(1)} collective-permute-done((f32[40,128]{1,0:T(8,128)S(1)}, f32[40,128]{1,0:T(8,128)S(1)}, u32[]{:S(2)}, u32[]{:S(2)}) %collective-permute-start.2) | collective-permute-done | bytes 20512 | tf_op jit(solution)/shard_map/ppermute | solution.py:604
  9.6 1.7 %collective-permute-done.last_x_ref = f32[40,128]{1,0:T(8,128)S(1)} collective-permute-done((f32[40,128]{1,0:T(8,128)S(1)}, f32[40,128]{1,0:T(8,128)S(1)}, u32[]{:S(2)}, u32[]{:S(2)}) %collective-permute-start) | collective-permute-done | bytes 20512 | tf_op jit(solution)/shard_map/ppermute | solution.py:604
  11.3 0.0 collective-permute-done.1.refs_0_
  11.3 0.1 collective-permute-start.3
  11.4 1.3 %fetch_weights.1 = (f32[128,128]{1,0:T(8,128)S(1)}, f32[128,128]{1,0:T(8,128)S(1)}, f32[8,128]{1,0:T(8,128)S(1)}, f32[3,128]{1,0:T(4,128)S(1)}, f32[128,256]{1,0...) custom-call(s32[2,1,2,8]{3,2,1,0:T(2,128)} %species_hbm.3, s32[1,32]{1,0:T(1,128)} %bitcast.6, ...), custom_call_target="tpu_custom_call" | custom-call | tf_op jit(solution)/shard_map/fetch_weights/pallas_call | solution.py:645
  12.7 0.7 %collective-permute-done.3.refs_2_ = f32[160,128]{1,0:T(8,128)S(1)} collective-permute-done((f32[160,128]{1,0:T(8,128)S(1)}, f32[160,128]{1,0:T(8,128)S(1)}, u32[]{:S(2)}, u32[]{:S(2)}) %collective-permute-start.3) | collective-permute-done | bytes 81952 | tf_op jit(solution)/shard_map/ppermute | solution.py:604
  13.4 5.4 %pair_forces.1 = (f32[16,64]{1,0:T(8,128)S(1)}, f32[16,64]{1,0:T(8,128)S(1)}) custom-call(f32[40,128]{1,0:T(8,128)S(1)} %get-tuple-element.18.here_ref, f32[40,128]{1,0:T(8,128)S(1)} %collective-permute-done.last_x_ref, f32[40,128]{1,0:T(8,128)S(1)} %collective-permute-done.1.refs_0_, f32[40,128]{1,0:T(8,128)S(1)} %collective-permute-done.2.refs_1_, ...), custom_call_target="tpu_custom_call" | custom-call | tf_op jit(solution)/shard_map/pair_forces/pallas_call | solution.py:670
  18.9 2.0 %collective-permute-start.4 = (f32[16,64]{1,0:T(8,128)S(1)}, f32[16,64]{1,0:T(8,128)S(1)}, u32[]{:S(2)}, u32[]{:S(2)}) collective-permute-start(f32[16,64]{1,0:T(8,128)S(1)} %get-tuple-element.28), channel_id=1, source_target_pairs={{0,24},{8,0},{16,8},{24,16},{1,25},{9,1},{17,9},{25,17},{2,26},{10... | collective-permute-start | bytes 12296 | tf_op jit(solution)/shard_map/ppermute | solution.py:604
  20.9 1.7 %collective-permute-done.4 = f32[16,64]{1,0:T(8,128)S(1)} collective-permute-done((f32[16,64]{1,0:T(8,128)S(1)}, f32[16,64]{1,0:T(8,128)S(1)}, u32[]{:S(2)}, u32[]{:S(2)}) %collective-permute-start.4) | collective-permute-done | bytes 4128 | tf_op jit(solution)/shard_map/ppermute | solution.py:604
  22.5 0.5 %collective-permute-start.5 = (f32[16,64]{1,0:T(8,128)S(1)}, f32[16,64]{1,0:T(8,128)S(1)}, u32[]{:S(2)}, u32[]{:S(2)}) collective-permute-start(f32[16,64]{1,0:T(8,128)S(1)} %add.23.mine_ref), channel_id=1, source_target_pairs={{0,1},{1,2},{2,3},{3,0},{4,5},{5,6},{6,7},{7,4},{8,9},{9,10},{10,1... | collective-permute-start | bytes 12296 | tf_op jit(solution)/shard_map/ppermute | solution.py:604
  23.1 2.5 %collective-permute-done.5.refs_0_ = f32[16,64]{1,0:T(8,128)S(1)} collective-permute-done((f32[16,64]{1,0:T(8,128)S(1)}, f32[16,64]{1,0:T(8,128)S(1)}, u32[]{:S(2)}, u32[]{:S(2)}) %collective-permute-start.5) | collective-permute-done | bytes 4128 | tf_op jit(solution)/shard_map/ppermute | solution.py:604
  25.6 0.8 %write_outputs.1 = (f32[2,1,2,8]{3,2,1,0:T(2,128)}, f32[3,2,1,2,8]{4,3,2,1,0:T(2,128)}, f32[2,1,2,8,9]{4,3,2,1,0:T(8,128)}) custom-call(f32[16,64]{1,0:T(8,128)S(1)} %add.23.mine_ref, f32[1,32]{1,0:T(1,128)S(1)} %get-tuple-element.29.shift_row_ref, f32[16,64]{1,0:T(8,128)S(1)} %collective-permute-done.5.refs_0_), custom_call_target="tpu_custom_call" | custom-call | tf_op jit(solution)/shard_map/write_outputs/pallas_call | solution.py:696
  (2 shorter events, 0.0 us)
Async XLA Ops:
  1.7 7.9 %collective-permute-start.2 = (f32[40,128]{1,0:T(8,128)S(1)}, f32[40,128]{1,0:T(8,128)S(1)}, u32[]{:S(2)}, u32[]{:S(2)}) collective-permute-start(f32[40,128]{1,0:T(8,128)S(1)} %get-tuple-element.19), channel_id=1, source_target_pairs={{0,12},{4,8},{8,20},{12,16},{16,28},{20,24},{24,4},{28,0},{1,13},{... | collective-permute-start | bytes 61448 | tf_op jit(solution)/shard_map/ppermute | solution.py:604
  5.7 5.6 %collective-permute-start = (f32[40,128]{1,0:T(8,128)S(1)}, f32[40,128]{1,0:T(8,128)S(1)}, u32[]{:S(2)}, u32[]{:S(2)}) collective-permute-start(f32[40,128]{1,0:T(8,128)S(1)} %get-tuple-element.19), channel_id=1, source_target_pairs={{0,8},{8,16},{16,24},{24,0},{1,9},{9,17},{17,25},{25,1},{2,10},{10... | collective-permute-start | bytes 61448 | tf_op jit(solution)/shard_map/ppermute | solution.py:604
  7.3 4.0 %collective-permute-start.1 = (f32[40,128]{1,0:T(8,128)S(1)}, f32[40,128]{1,0:T(8,128)S(1)}, u32[]{:S(2)}, u32[]{:S(2)}) collective-permute-start(f32[40,128]{1,0:T(8,128)S(1)} %get-tuple-element.18.here_ref), channel_id=1, source_target_pairs={{0,4},{4,0},{1,5},{5,1},{2,6},{6,2},{3,7},{7,3},{8,12},{12,8},{9,1... | collective-permute-start | bytes 61448 | tf_op jit(solution)/shard_map/ppermute | solution.py:604
  11.3 2.1 %collective-permute-start.3 = (f32[160,128]{1,0:T(8,128)S(1)}, f32[160,128]{1,0:T(8,128)S(1)}, u32[]{:S(2)}, u32[]{:S(2)}) collective-permute-start(f32[160,128]{1,0:T(8,128)S(1)} %pad_add_fusion), channel_id=1, source_target_pairs={{0,3},{1,0},{2,1},{3,2},{4,7},{5,4},{6,5},{7,6},{8,11},{9,8},{10,9... | collective-permute-start | bytes 245768 | tf_op jit(solution)/shard_map/ppermute | solution.py:604
  18.9 3.7 %collective-permute-start.4 = (f32[16,64]{1,0:T(8,128)S(1)}, f32[16,64]{1,0:T(8,128)S(1)}, u32[]{:S(2)}, u32[]{:S(2)}) collective-permute-start(f32[16,64]{1,0:T(8,128)S(1)} %get-tuple-element.28), channel_id=1, source_target_pairs={{0,24},{8,0},{16,8},{24,16},{1,25},{9,1},{17,9},{25,17},{2,26},{10... | collective-permute-start | bytes 12296 | tf_op jit(solution)/shard_map/ppermute | solution.py:604
  22.5 3.1 %collective-permute-start.5 = (f32[16,64]{1,0:T(8,128)S(1)}, f32[16,64]{1,0:T(8,128)S(1)}, u32[]{:S(2)}, u32[]{:S(2)}) collective-permute-start(f32[16,64]{1,0:T(8,128)S(1)} %add.23.mine_ref), channel_id=1, source_target_pairs={{0,1},{1,2},{2,3},{3,0},{4,5},{5,6},{6,7},{7,4},{8,9},{9,10},{10,1... | collective-permute-start | bytes 12296 | tf_op jit(solution)/shard_map/ppermute | solution.py:604

commit v23 on v22

--- a/solution.py
+++ b/solution.py
@@ -63,6 +63,10 @@
 
 def three(high, low):
     return jnp.concatenate([high, low, high], axis=1)
+
+
+def tall_product(weights, value_high, value_low):
+    return folded(mm(weights, jnp.concatenate([value_high, value_low], axis=0)))
 
 
 def deep(weights, value_high, value_low):
@@ -316,13 +320,13 @@
     place_parts = place_rows(coords)
     center_parts = place_rows(jnp.concatenate(center_coords, axis=0))
 
-    value_rows = three(*split(jnp.transpose(value_weight_ref[...])))
+    value_rows = stacked(*split(jnp.transpose(value_weight_ref[...])))
     latent_t = three(*split(0.5 * jnp.transpose(latent_weight_ref[...])))
-    latent_rows = three(*split(latent_weight_ref[...] * out_weight_ref[...]))
+    latent_rows = stacked(*split(latent_weight_ref[...] * out_weight_ref[...]))
     value_plain = three(*split(value_weight_ref[...]))
     basis_t = jnp.transpose(basis_weight_ref[...])
     basis_high_t, basis_low_t = split(0.5 * basis_t)
-    basis_rows = three(*split(basis_weight_ref[...]))
+    basis_rows = stacked(*split(basis_weight_ref[...]))
 
     def project(weight, rows):
         weight = stacked(*split(jnp.transpose(weight)))
@@ -431,7 +435,7 @@
     active = before * gate
     latent = weight * active
     latent_high, latent_low = split(latent)
-    mixed = deep(value_rows, latent_high, latent_low)
+    mixed = tall_product(value_rows, latent_high, latent_low)
     values = mixed[:width]
     env_high, env_low = split(mixed[width:])
 
@@ -470,7 +474,7 @@
     )
     pair_energy = (active_sum + update_sum[:, :own_pairs]) * (pull * weight)[:, :own_pairs]
     d_z = (0.5 * pull * weight) * (z_gate + update * (2.0 - z_gate))
-    spread_back = deep(latent_rows, *split(d_z))
+    spread_back = tall_product(latent_rows, *split(d_z))
     d_scalars = spread_back[width:]
     d_values = d_scalars * inner
     dinner_high, dinner_low = split(d_scalars * values)
@@ -497,7 +501,7 @@
     )
     d_weight = jnp.sum(d_latent * active, axis=0, keepdims=True) + pull * update_sum
     d_before = d_latent * (gate + active * (2.0 - gate))
-    d_basis = deep(basis_rows, *split(d_before)) * (0.5 * weight)
+    d_basis = tall_product(basis_rows, *split(d_before)) * (0.5 * weight)
 
     d_length = jnp.sum(d_basis * basis_slope, axis=0, keepdims=True) + d_weight * slope * (
         1.0 / CUTOFF

time: 26.7 us -> 26.7 us (level)
  no operation moved by 1% of the time
where the time goes in v23:
time: 26.7 us; the launch traced here: 26.5 us
  Pallas kernels  8.71 us (33%)
  starting transfers between devices  8.71 us (33%)
  waiting for transfers between devices  8.37 us (31%)
  between operations  0.67 us (3%)
    ppermute x6, starting transfers between devices, moved(): return lax.ppermute(array, names, route)  8.71 us
    ppermute x6, waiting for transfers between devices, moved(): return lax.ppermute(array, names, route)  8.37 us
    pallas_call x1, Pallas kernels, local(): pl.pallas_call(functools.partial(force_kernel, kind, nbr), out_shape=(jax...  5.46 us
    pallas_call x1, Pallas kernels, local(): pl.pallas_call(fetch_kernel, out_shape=(*(jax.ShapeDtypeStruct(w.shape, F...  1.35 us
    pallas_call x1, Pallas kernels, local(): pl.pallas_call(functools.partial(pack_kernel, kind), out_shape=(payload,...  1.08 us
    pallas_call x1, Pallas kernels, local(): pl.pallas_call(finish_kernel, out_shape=(jax.ShapeDtypeStruct(species.sha...  0.82 us
  transfers between devices with their start and end apart: 6, of which 5 were waited for; matrix products, arithmetic and copies ran while one was open for 0% of the time, Pallas kernels for 5%

profile of v23, /device:TPU:0, one launch (start us, length us, event | category | flops | bytes accessed | tf_op | source)
XLA Modules:
  0.0 26.5 jit_solution(4059258944958750796)
XLA Ops:
  0.6 1.1 %pack_payload.1 = (f32[40,128]{1,0:T(8,128)S(1)}, f32[40,128]{1,0:T(8,128)S(1)}) custom-call(f32[3,2,1,2,8]{4,3,2,1,0:T(2,128)} %positions_hbm.1, f32[32,128]{1,0:T(8,128)} %bitcast.4, s32[2,1,2,8]{3,2,1,0:T(2,128)} %species_hbm.3, s32[1,32]{1,0:T(1,128)} %bitcast.5, s32[32,32]{1,0:T(8,128)} %neighbours_hbm.1, f32[5]{0:T(128)} %scale_hbm.1), custom_call_target="tpu_custom_call" | custom-call | tf_op jit(solution)/shard_map/pack_payload/pallas_call | solution.py:614
  1.7 4.0 %collective-permute-start.2 = (f32[40,128]{1,0:T(8,128)S(1)}, f32[40,128]{1,0:T(8,128)S(1)}, u32[]{:S(2)}, u32[]{:S(2)}) collective-permute-start(f32[40,128]{1,0:T(8,128)S(1)} %get-tuple-element.19), channel_id=1, source_target_pairs={{0,12},{4,8},{8,20},{12,16},{16,28},{20,24},{24,4},{28,0},{1,13},{... | collective-permute-start | bytes 61448 | tf_op jit(solution)/shard_map/ppermute | solution.py:608
  5.7 1.6 %collective-permute-start = (f32[40,128]{1,0:T(8,128)S(1)}, f32[40,128]{1,0:T(8,128)S(1)}, u32[]{:S(2)}, u32[]{:S(2)}) collective-permute-start(f32[40,128]{1,0:T(8,128)S(1)} %get-tuple-element.19), channel_id=1, source_target_pairs={{0,8},{8,16},{16,24},{24,0},{1,9},{9,17},{17,25},{25,1},{2,10},{10... | collective-permute-start | bytes 61448 | tf_op jit(solution)/shard_map/ppermute | solution.py:608
  7.3 0.5 %collective-permute-start.1 = (f32[40,128]{1,0:T(8,128)S(1)}, f32[40,128]{1,0:T(8,128)S(1)}, u32[]{:S(2)}, u32[]{:S(2)}) collective-permute-start(f32[40,128]{1,0:T(8,128)S(1)} %get-tuple-element.18.here_ref), channel_id=1, source_target_pairs={{0,4},{4,0},{1,5},{5,1},{2,6},{6,2},{3,7},{7,3},{8,12},{12,8},{9,1... | collective-permute-start | bytes 61448 | tf_op jit(solution)/shard_map/ppermute | solution.py:608
  7.8 1.8 %collective-permute-done.2.refs_1_ = f32[40,128]{1,0:T(8,128)S(1)} collective-permute-done((f32[40,128]{1,0:T(8,128)S(1)}, f32[40,128]{1,0:T(8,128)S(1)}, u32[]{:S(2)}, u32[]{:S(2)}) %collective-permute-start.2) | collective-permute-done | bytes 20512 | tf_op jit(solution)/shard_map/ppermute | solution.py:608
  9.6 1.7 %collective-permute-done.last_x_ref = f32[40,128]{1,0:T(8,128)S(1)} collective-permute-done((f32[40,128]{1,0:T(8,128)S(1)}, f32[40,128]{1,0:T(8,128)S(1)}, u32[]{:S(2)}, u32[]{:S(2)}) %collective-permute-start) | collective-permute-done | bytes 20512 | tf_op jit(solution)/shard_map/ppermute | solution.py:608
  11.3 0.0 collective-permute-done.1.refs_0_
  11.3 0.1 collective-permute-start.3
  11.4 1.3 %fetch_weights.1 = (f32[128,128]{1,0:T(8,128)S(1)}, f32[128,128]{1,0:T(8,128)S(1)}, f32[8,128]{1,0:T(8,128)S(1)}, f32[3,128]{1,0:T(4,128)S(1)}, f32[128,256]{1,0...) custom-call(s32[2,1,2,8]{3,2,1,0:T(2,128)} %species_hbm.3, s32[1,32]{1,0:T(1,128)} %bitcast.6, ...), custom_call_target="tpu_custom_call" | custom-call | tf_op jit(solution)/shard_map/fetch_weights/pallas_call | solution.py:649
  12.7 0.7 %collective-permute-done.3.refs_2_ = f32[160,128]{1,0:T(8,128)S(1)} collective-permute-done((f32[160,128]{1,0:T(8,128)S(1)}, f32[160,128]{1,0:T(8,128)S(1)}, u32[]{:S(2)}, u32[]{:S(2)}) %collective-permute-start.3) | collective-permute-done | bytes 81952 | tf_op jit(solution)/shard_map/ppermute | solution.py:608
  13.4 5.5 %pair_forces.1 = (f32[16,64]{1,0:T(8,128)S(1)}, f32[16,64]{1,0:T(8,128)S(1)}) custom-call(f32[40,128]{1,0:T(8,128)S(1)} %get-tuple-element.18.here_ref, f32[40,128]{1,0:T(8,128)S(1)} %collective-permute-done.last_x_ref, f32[40,128]{1,0:T(8,128)S(1)} %collective-permute-done.1.refs_0_, f32[40,128]{1,0:T(8,128)S(1)} %collective-permute-done.2.refs_1_, ...), custom_call_target="tpu_custom_call" | custom-call | tf_op jit(solution)/shard_map/pair_forces/pallas_call | solution.py:674
  18.9 2.0 %collective-permute-start.4 = (f32[16,64]{1,0:T(8,128)S(1)}, f32[16,64]{1,0:T(8,128)S(1)}, u32[]{:S(2)}, u32[]{:S(2)}) collective-permute-start(f32[16,64]{1,0:T(8,128)S(1)} %get-tuple-element.28), channel_id=1, source_target_pairs={{0,24},{8,0},{16,8},{24,16},{1,25},{9,1},{17,9},{25,17},{2,26},{10... | collective-permute-start | bytes 12296 | tf_op jit(solution)/shard_map/ppermute | solution.py:608
  20.9 1.7 %collective-permute-done.4 = f32[16,64]{1,0:T(8,128)S(1)} collective-permute-done((f32[16,64]{1,0:T(8,128)S(1)}, f32[16,64]{1,0:T(8,128)S(1)}, u32[]{:S(2)}, u32[]{:S(2)}) %collective-permute-start.4) | collective-permute-done | bytes 4128 | tf_op jit(solution)/shard_map/ppermute | solution.py:608
  22.6 0.6 %collective-permute-start.5 = (f32[16,64]{1,0:T(8,128)S(1)}, f32[16,64]{1,0:T(8,128)S(1)}, u32[]{:S(2)}, u32[]{:S(2)}) collective-permute-start(f32[16,64]{1,0:T(8,128)S(1)} %add.23.mine_ref), channel_id=1, source_target_pairs={{0,1},{1,2},{2,3},{3,0},{4,5},{5,6},{6,7},{7,4},{8,9},{9,10},{10,1... | collective-permute-start | bytes 12296 | tf_op jit(solution)/shard_map/ppermute | solution.py:608
  23.1 2.5 %collective-permute-done.5.refs_0_ = f32[16,64]{1,0:T(8,128)S(1)} collective-permute-done((f32[16,64]{1,0:T(8,128)S(1)}, f32[16,64]{1,0:T(8,128)S(1)}, u32[]{:S(2)}, u32[]{:S(2)}) %collective-permute-start.5) | collective-permute-done | bytes 4128 | tf_op jit(solution)/shard_map/ppermute | solution.py:608
  25.6 0.8 %write_outputs.1 = (f32[2,1,2,8]{3,2,1,0:T(2,128)}, f32[3,2,1,2,8]{4,3,2,1,0:T(2,128)}, f32[2,1,2,8,9]{4,3,2,1,0:T(8,128)}) custom-call(f32[16,64]{1,0:T(8,128)S(1)} %add.23.mine_ref, f32[1,32]{1,0:T(1,128)S(1)} %get-tuple-element.29.shift_row_ref, f32[16,64]{1,0:T(8,128)S(1)} %collective-permute-done.5.refs_0_), custom_call_target="tpu_custom_call" | custom-call | tf_op jit(solution)/shard_map/write_outputs/pallas_call | solution.py:700
  (2 shorter events, 0.0 us)
Async XLA Ops:
  1.7 7.9 %collective-permute-start.2 = (f32[40,128]{1,0:T(8,128)S(1)}, f32[40,128]{1,0:T(8,128)S(1)}, u32[]{:S(2)}, u32[]{:S(2)}) collective-permute-start(f32[40,128]{1,0:T(8,128)S(1)} %get-tuple-element.19), channel_id=1, source_target_pairs={{0,12},{4,8},{8,20},{12,16},{16,28},{20,24},{24,4},{28,0},{1,13},{... | collective-permute-start | bytes 61448 | tf_op jit(solution)/shard_map/ppermute | solution.py:608
  5.7 5.6 %collective-permute-start = (f32[40,128]{1,0:T(8,128)S(1)}, f32[40,128]{1,0:T(8,128)S(1)}, u32[]{:S(2)}, u32[]{:S(2)}) collective-permute-start(f32[40,128]{1,0:T(8,128)S(1)} %get-tuple-element.19), channel_id=1, source_target_pairs={{0,8},{8,16},{16,24},{24,0},{1,9},{9,17},{17,25},{25,1},{2,10},{10... | collective-permute-start | bytes 61448 | tf_op jit(solution)/shard_map/ppermute | solution.py:608
  7.3 4.0 %collective-permute-start.1 = (f32[40,128]{1,0:T(8,128)S(1)}, f32[40,128]{1,0:T(8,128)S(1)}, u32[]{:S(2)}, u32[]{:S(2)}) collective-permute-start(f32[40,128]{1,0:T(8,128)S(1)} %get-tuple-element.18.here_ref), channel_id=1, source_target_pairs={{0,4},{4,0},{1,5},{5,1},{2,6},{6,2},{3,7},{7,3},{8,12},{12,8},{9,1... | collective-permute-start | bytes 61448 | tf_op jit(solution)/shard_map/ppermute | solution.py:608
  11.3 2.1 %collective-permute-start.3 = (f32[160,128]{1,0:T(8,128)S(1)}, f32[160,128]{1,0:T(8,128)S(1)}, u32[]{:S(2)}, u32[]{:S(2)}) collective-permute-start(f32[160,128]{1,0:T(8,128)S(1)} %pad_add_fusion), channel_id=1, source_target_pairs={{0,3},{1,0},{2,1},{3,2},{4,7},{5,4},{6,5},{7,6},{8,11},{9,8},{10,9... | collective-permute-start | bytes 245768 | tf_op jit(solution)/shard_map/ppermute | solution.py:608
  18.9 3.7 %collective-permute-start.4 = (f32[16,64]{1,0:T(8,128)S(1)}, f32[16,64]{1,0:T(8,128)S(1)}, u32[]{:S(2)}, u32[]{:S(2)}) collective-permute-start(f32[16,64]{1,0:T(8,128)S(1)} %get-tuple-element.28), channel_id=1, source_target_pairs={{0,24},{8,0},{16,8},{24,16},{1,25},{9,1},{17,9},{25,17},{2,26},{10... | collective-permute-start | bytes 12296 | tf_op jit(solution)/shard_map/ppermute | solution.py:608
  22.6 3.1 %collective-permute-start.5 = (f32[16,64]{1,0:T(8,128)S(1)}, f32[16,64]{1,0:T(8,128)S(1)}, u32[]{:S(2)}, u32[]{:S(2)}) collective-permute-start(f32[16,64]{1,0:T(8,128)S(1)} %add.23.mine_ref), channel_id=1, source_target_pairs={{0,1},{1,2},{2,3},{3,0},{4,5},{5,6},{6,7},{7,4},{8,9},{9,10},{10,1... | collective-permute-start | bytes 12296 | tf_op jit(solution)/shard_map/ppermute | solution.py:608

commit v24 on v22

--- a/solution.py
+++ b/solution.py
@@ -346,7 +346,7 @@
     out_column = jnp.transpose(jnp.broadcast_to(out_weight_ref[...], (width, width)))
     out_column = jnp.concatenate([out_column] * (pairs // width), axis=1)
 
-    slot_ids = lax.broadcasted_iota(jnp.int32, (centers, pairs), 0)
+    slot_ids = lax.broadcasted_iota(jnp.int32, (centers, 128), 0)
     slot_row = lax.broadcasted_iota(jnp.int32, (1, pairs), 1) // nbr
     group_lane = lax.broadcasted_iota(jnp.int32, (GROUP, pairs), 1) // nbr % GROUP
     group_mask = group_lane == lax.broadcasted_iota(jnp.int32, (GROUP, pairs), 0)
@@ -366,7 +366,11 @@
         one, zero = 1.0, 0.0
     site_ids = jnp.concatenate([site_ids] * (pairs // 128), axis=1)
     pick_half = jnp.where(site_ids == wanted, one, zero).astype(BF16)
-    slot_half = jnp.where(slot_ids == slot_row, 1.0, 0.0).astype(BF16)
+    slot_ids = slot_ids.astype(F32).astype(BF16)
+    slot_ids = jnp.concatenate([slot_ids] * (pairs // 128), axis=1)
+    slot_row = jnp.broadcast_to(slot_row.astype(F32), (16, pairs)).astype(BF16)
+    slot_row = jnp.concatenate([slot_row] * (centers // 16), axis=0)
+    slot_half = jnp.where(slot_ids == slot_row, jnp.ones((), BF16), jnp.zeros((), BF16))
 
     moved = mm(
         jnp.concatenate([place_parts, -center_parts], axis=1),
@@ -412,7 +416,8 @@
     angular_low = angular_low.astype(BF16).astype(F32)
     block_high = [angular_high[m : m + 1] * group_mask for m in range(len(LEVELS))]
     block_low = [angular_low[m : m + 1] * group_mask for m in range(len(LEVELS))]
-    blocks = jnp.concatenate(block_high + block_low + block_high, axis=0).astype(BF16)
+    blocks = jnp.concatenate(block_high + block_low, axis=0).astype(BF16)
+    blocks = jnp.concatenate([blocks, blocks[:tall]], axis=0)
     lane_ids = lax.broadcasted_iota(jnp.int32, (128, span), 0)
     lane_slot = lax.broadcasted_iota(jnp.int32, (128, span), 1) // nbr + 3 * sites
     scale = mm(scale_parts, jnp.where(lane_ids == lane_slot, 1.0, 0.0).astype(BF16))

time: 26.7 us -> 26.7 us (level)
  no operation moved by 1% of the time
where the time goes in v24:
time: 26.7 us; the launch traced here: 26.4 us
  starting transfers between devices  8.69 us (33%)
  Pallas kernels  8.67 us (32%)
  waiting for transfers between devices  8.38 us (31%)
  between operations  0.67 us (3%)
    ppermute x6, starting transfers between devices, moved(): return lax.ppermute(array, names, route)  8.69 us
    ppermute x6, waiting for transfers between devices, moved(): return lax.ppermute(array, names, route)  8.38 us
    pallas_call x1, Pallas kernels, local(): pl.pallas_call(functools.partial(force_kernel, kind, nbr), out_shape=(jax...  5.42 us
    pallas_call x1, Pallas kernels, local(): pl.pallas_call(fetch_kernel, out_shape=(*(jax.ShapeDtypeStruct(w.shape, F...  1.35 us
    pallas_call x1, Pallas kernels, local(): pl.pallas_call(functools.partial(pack_kernel, kind), out_shape=(payload,...  1.08 us
    pallas_call x1, Pallas kernels, local(): pl.pallas_call(finish_kernel, out_shape=(jax.ShapeDtypeStruct(species.sha...  0.82 us
  transfers between devices with their start and end apart: 6, of which 5 were waited for; matrix products, arithmetic and copies ran while one was open for 0% of the time, Pallas kernels for 5%

profile of v24, /device:TPU:0, one launch (start us, length us, event | category | flops | bytes accessed | tf_op | source)
XLA Modules:
  0.0 26.4 jit_solution(7441541293547501385)
XLA Ops:
  0.6 1.1 %pack_payload.1 = (f32[40,128]{1,0:T(8,128)S(1)}, f32[40,128]{1,0:T(8,128)S(1)}) custom-call(f32[3,2,1,2,8]{4,3,2,1,0:T(2,128)} %positions_hbm.1, f32[32,128]{1,0:T(8,128)} %bitcast.4, s32[2,1,2,8]{3,2,1,0:T(2,128)} %species_hbm.3, s32[1,32]{1,0:T(1,128)} %bitcast.5, s32[32,32]{1,0:T(8,128)} %neighbours_hbm.1, f32[5]{0:T(128)} %scale_hbm.1), custom_call_target="tpu_custom_call" | custom-call | tf_op jit(solution)/shard_map/pack_payload/pallas_call | solution.py:615
  1.7 4.0 %collective-permute-start.2 = (f32[40,128]{1,0:T(8,128)S(1)}, f32[40,128]{1,0:T(8,128)S(1)}, u32[]{:S(2)}, u32[]{:S(2)}) collective-permute-start(f32[40,128]{1,0:T(8,128)S(1)} %get-tuple-element.19), channel_id=1, source_target_pairs={{0,12},{4,8},{8,20},{12,16},{16,28},{20,24},{24,4},{28,0},{1,13},{... | collective-permute-start | bytes 61448 | tf_op jit(solution)/shard_map/ppermute | solution.py:609
  5.7 1.6 %collective-permute-start = (f32[40,128]{1,0:T(8,128)S(1)}, f32[40,128]{1,0:T(8,128)S(1)}, u32[]{:S(2)}, u32[]{:S(2)}) collective-permute-start(f32[40,128]{1,0:T(8,128)S(1)} %get-tuple-element.19), channel_id=1, source_target_pairs={{0,8},{8,16},{16,24},{24,0},{1,9},{9,17},{17,25},{25,1},{2,10},{10... | collective-permute-start | bytes 61448 | tf_op jit(solution)/shard_map/ppermute | solution.py:609
  7.3 0.5 %collective-permute-start.1 = (f32[40,128]{1,0:T(8,128)S(1)}, f32[40,128]{1,0:T(8,128)S(1)}, u32[]{:S(2)}, u32[]{:S(2)}) collective-permute-start(f32[40,128]{1,0:T(8,128)S(1)} %get-tuple-element.18.here_ref), channel_id=1, source_target_pairs={{0,4},{4,0},{1,5},{5,1},{2,6},{6,2},{3,7},{7,3},{8,12},{12,8},{9,1... | collective-permute-start | bytes 61448 | tf_op jit(solution)/shard_map/ppermute | solution.py:609
  7.8 1.8 %collective-permute-done.2.refs_1_ = f32[40,128]{1,0:T(8,128)S(1)} collective-permute-done((f32[40,128]{1,0:T(8,128)S(1)}, f32[40,128]{1,0:T(8,128)S(1)}, u32[]{:S(2)}, u32[]{:S(2)}) %collective-permute-start.2) | collective-permute-done | bytes 20512 | tf_op jit(solution)/shard_map/ppermute | solution.py:609
  9.6 1.7 %collective-permute-done.last_x_ref = f32[40,128]{1,0:T(8,128)S(1)} collective-permute-done((f32[40,128]{1,0:T(8,128)S(1)}, f32[40,128]{1,0:T(8,128)S(1)}, u32[]{:S(2)}, u32[]{:S(2)}) %collective-permute-start) | collective-permute-done | bytes 20512 | tf_op jit(solution)/shard_map/ppermute | solution.py:609
  11.3 0.0 collective-permute-done.1.refs_0_
  11.3 0.1 collective-permute-start.3
  11.4 1.3 %fetch_weights.1 = (f32[128,128]{1,0:T(8,128)S(1)}, f32[128,128]{1,0:T(8,128)S(1)}, f32[8,128]{1,0:T(8,128)S(1)}, f32[3,128]{1,0:T(4,128)S(1)}, f32[128,256]{1,0...) custom-call(s32[2,1,2,8]{3,2,1,0:T(2,128)} %species_hbm.3, s32[1,32]{1,0:T(1,128)} %bitcast.6, ...), custom_call_target="tpu_custom_call" | custom-call | tf_op jit(solution)/shard_map/fetch_weights/pallas_call | solution.py:650
  12.7 0.7 %collective-permute-done.3.refs_2_ = f32[160,128]{1,0:T(8,128)S(1)} collective-permute-done((f32[160,128]{1,0:T(8,128)S(1)}, f32[160,128]{1,0:T(8,128)S(1)}, u32[]{:S(2)}, u32[]{:S(2)}) %collective-permute-start.3) | collective-permute-done | bytes 81952 | tf_op jit(solution)/shard_map/ppermute | solution.py:609
  13.4 5.4 %pair_forces.1 = (f32[16,64]{1,0:T(8,128)S(1)}, f32[16,64]{1,0:T(8,128)S(1)}) custom-call(f32[40,128]{1,0:T(8,128)S(1)} %get-tuple-element.18.here_ref, f32[40,128]{1,0:T(8,128)S(1)} %collective-permute-done.last_x_ref, f32[40,128]{1,0:T(8,128)S(1)} %collective-permute-done.1.refs_0_, f32[40,128]{1,0:T(8,128)S(1)} %collective-permute-done.2.refs_1_, ...), custom_call_target="tpu_custom_call" | custom-call | tf_op jit(solution)/shard_map/pair_forces/pallas_call | solution.py:675
  18.9 2.0 %collective-permute-start.4 = (f32[16,64]{1,0:T(8,128)S(1)}, f32[16,64]{1,0:T(8,128)S(1)}, u32[]{:S(2)}, u32[]{:S(2)}) collective-permute-start(f32[16,64]{1,0:T(8,128)S(1)} %get-tuple-element.28), channel_id=1, source_target_pairs={{0,24},{8,0},{16,8},{24,16},{1,25},{9,1},{17,9},{25,17},{2,26},{10... | collective-permute-start | bytes 12296 | tf_op jit(solution)/shard_map/ppermute | solution.py:609
  20.8 1.7 %collective-permute-done.4 = f32[16,64]{1,0:T(8,128)S(1)} collective-permute-done((f32[16,64]{1,0:T(8,128)S(1)}, f32[16,64]{1,0:T(8,128)S(1)}, u32[]{:S(2)}, u32[]{:S(2)}) %collective-permute-start.4) | collective-permute-done | bytes 4128 | tf_op jit(solution)/shard_map/ppermute | solution.py:609
  22.5 0.5 %collective-permute-start.5 = (f32[16,64]{1,0:T(8,128)S(1)}, f32[16,64]{1,0:T(8,128)S(1)}, u32[]{:S(2)}, u32[]{:S(2)}) collective-permute-start(f32[16,64]{1,0:T(8,128)S(1)} %add.23.mine_ref), channel_id=1, source_target_pairs={{0,1},{1,2},{2,3},{3,0},{4,5},{5,6},{6,7},{7,4},{8,9},{9,10},{10,1... | collective-permute-start | bytes 12296 | tf_op jit(solution)/shard_map/ppermute | solution.py:609
  23.1 2.5 %collective-permute-done.5.refs_0_ = f32[16,64]{1,0:T(8,128)S(1)} collective-permute-done((f32[16,64]{1,0:T(8,128)S(1)}, f32[16,64]{1,0:T(8,128)S(1)}, u32[]{:S(2)}, u32[]{:S(2)}) %collective-permute-start.5) | collective-permute-done | bytes 4128 | tf_op jit(solution)/shard_map/ppermute | solution.py:609
  25.6 0.8 %write_outputs.1 = (f32[2,1,2,8]{3,2,1,0:T(2,128)}, f32[3,2,1,2,8]{4,3,2,1,0:T(2,128)}, f32[2,1,2,8,9]{4,3,2,1,0:T(8,128)}) custom-call(f32[16,64]{1,0:T(8,128)S(1)} %add.23.mine_ref, f32[1,32]{1,0:T(1,128)S(1)} %get-tuple-element.29.shift_row_ref, f32[16,64]{1,0:T(8,128)S(1)} %collective-permute-done.5.refs_0_), custom_call_target="tpu_custom_call" | custom-call | tf_op jit(solution)/shard_map/write_outputs/pallas_call | solution.py:701
  (2 shorter events, 0.0 us)
Async XLA Ops:
  1.7 7.9 %collective-permute-start.2 = (f32[40,128]{1,0:T(8,128)S(1)}, f32[40,128]{1,0:T(8,128)S(1)}, u32[]{:S(2)}, u32[]{:S(2)}) collective-permute-start(f32[40,128]{1,0:T(8,128)S(1)} %get-tuple-element.19), channel_id=1, source_target_pairs={{0,12},{4,8},{8,20},{12,16},{16,28},{20,24},{24,4},{28,0},{1,13},{... | collective-permute-start | bytes 61448 | tf_op jit(solution)/shard_map/ppermute | solution.py:609
  5.7 5.6 %collective-permute-start = (f32[40,128]{1,0:T(8,128)S(1)}, f32[40,128]{1,0:T(8,128)S(1)}, u32[]{:S(2)}, u32[]{:S(2)}) collective-permute-start(f32[40,128]{1,0:T(8,128)S(1)} %get-tuple-element.19), channel_id=1, source_target_pairs={{0,8},{8,16},{16,24},{24,0},{1,9},{9,17},{17,25},{25,1},{2,10},{10... | collective-permute-start | bytes 61448 | tf_op jit(solution)/shard_map/ppermute | solution.py:609
  7.3 4.0 %collective-permute-start.1 = (f32[40,128]{1,0:T(8,128)S(1)}, f32[40,128]{1,0:T(8,128)S(1)}, u32[]{:S(2)}, u32[]{:S(2)}) collective-permute-start(f32[40,128]{1,0:T(8,128)S(1)} %get-tuple-element.18.here_ref), channel_id=1, source_target_pairs={{0,4},{4,0},{1,5},{5,1},{2,6},{6,2},{3,7},{7,3},{8,12},{12,8},{9,1... | collective-permute-start | bytes 61448 | tf_op jit(solution)/shard_map/ppermute | solution.py:609
  11.3 2.1 %collective-permute-start.3 = (f32[160,128]{1,0:T(8,128)S(1)}, f32[160,128]{1,0:T(8,128)S(1)}, u32[]{:S(2)}, u32[]{:S(2)}) collective-permute-start(f32[160,128]{1,0:T(8,128)S(1)} %pad_add_fusion), channel_id=1, source_target_pairs={{0,3},{1,0},{2,1},{3,2},{4,7},{5,4},{6,5},{7,6},{8,11},{9,8},{10,9... | collective-permute-start | bytes 245768 | tf_op jit(solution)/shard_map/ppermute | solution.py:609
  18.9 3.7 %collective-permute-start.4 = (f32[16,64]{1,0:T(8,128)S(1)}, f32[16,64]{1,0:T(8,128)S(1)}, u32[]{:S(2)}, u32[]{:S(2)}) collective-permute-start(f32[16,64]{1,0:T(8,128)S(1)} %get-tuple-element.28), channel_id=1, source_target_pairs={{0,24},{8,0},{16,8},{24,16},{1,25},{9,1},{17,9},{25,17},{2,26},{10... | collective-permute-start | bytes 12296 | tf_op jit(solution)/shard_map/ppermute | solution.py:609
  22.5 3.1 %collective-permute-start.5 = (f32[16,64]{1,0:T(8,128)S(1)}, f32[16,64]{1,0:T(8,128)S(1)}, u32[]{:S(2)}, u32[]{:S(2)}) collective-permute-start(f32[16,64]{1,0:T(8,128)S(1)} %add.23.mine_ref), channel_id=1, source_target_pairs={{0,1},{1,2},{2,3},{3,0},{4,5},{5,6},{6,7},{7,4},{8,9},{9,10},{10,1... | collective-permute-start | bytes 12296 | tf_op jit(solution)/shard_map/ppermute | solution.py:609
